TPU v7x, 32 devices: a whole 2x2x4 slice. The times are simulated.
32 devices in a mesh: group: 2 (over x), space: 16 (over z, y, core).
Axes of the slice: x: 2, y: 2, z: 4, core: 2. Of those that a mesh axis runs over, the one named last changes fastest.
Arguments:
- probes: float32 [32, 64, 32, 128], P('group', 'space'), parts along dimension 0, may hold values from -4 to 4
- sources: float32 [3, 128, 32, 128], P(None, ('group', 'space')), parts along dimension 1, may hold values from -6 to 6
- kappa: float32 [128, 32, 128], P(('group', 'space')), parts along dimension 0, may hold values from 0.05 to 0.3
- prior: float32 [128, 32, 128], P(('group', 'space')), parts along dimension 0, may hold values from 0.1 to 1
- basis: float32 [128, 64, 32, 128], P('group', 'space'), parts along dimension 0, may hold values from -0.0078125 to 0.0078125
- entry_cell: int32 [16384], P(('group', 'space')), parts along dimension 0, may hold values from 0 to 16383
- entry_owner: int32 [16384], P(('group', 'space')), parts along dimension 0, may hold values from 0 to 15, as said below
- entry_slot: int32 [16384], P(('group', 'space')), parts along dimension 0, may hold values from 0 to 127
- entry_weight: float32 [16384], P(('group', 'space')), parts along dimension 0, may hold values from 0.05 to 1
- entry_count: int32 [32], P(('group', 'space')), parts along dimension 0, may hold values from 384 to 512, as said below
- trace_weight: float32 [4096], P(('group', 'space')), parts along dimension 0, may hold values from 0.3 to 3
Outputs:
- hess_probe: float32 [32, 64, 32, 128], P('group', 'space'), parts along dimension 0
- coeffs: float32 [128, 16], P('group'), parts along dimension 0
There are 2 independent parts, one for each index of `group`. A program takes and returns all parts, laid end to end along the dimension named above; each array names one. Nothing has to cross between parts.
Inputs may be any that keep to these rules, and one draw needn't show every extreme that they name: `entry_owner`: among the entries of one tile at most 64 name the same owner, and the first 64 entries of every tile name one owner. `entry_count`: some tile has all 512 entries live.
All inputs are finite; a program needn't handle non-finite values.
Results may differ from a plain program's by a relative error of at most 0.00012.
Values sent between devices are 32-bit elements; how exact they have to be, the bound alone decides.
No kernel may reach another device: no remote copies, remote signals or barrier semaphores. Data moves between devices by JAX's collectives and lax.ppermute only.
A program may use at most 64 MiB of HBM per device.

v0:
```python
import jax
import jax.numpy as jnp
from jax import lax
from jax.sharding import PartitionSpec as P

STENCIL = (-205.0 / 72.0, 8.0 / 5.0, -1.0 / 5.0, 8.0 / 315.0, -1.0 / 560.0)


def extended_2(array, sides, width):
    for axis, dim in sides:
        devices, length = (lax.axis_size(axis), array.shape[dim])
        up = [(i, (i + 1) % devices) for i in range(devices - 1)]
        down = [(j, i) for i, j in up]
        last = lax.slice_in_dim(array, length - width, length, axis=dim)
        leading = lax.slice_in_dim(array, 0, width, axis=dim)
        before = lax.ppermute(last, axis, up)
        after = lax.ppermute(leading, axis, down)
        array = jnp.concatenate([before, array, after], axis=dim)
    return array


def second_difference(padded, length_x, length_y, length_z):

    def part(shift_x, shift_y, shift_z):
        return padded[
            :,
            4 + shift_x : 4 + shift_x + length_x,
            4 + shift_y : 4 + shift_y + length_y,
            4 + shift_z : 4 + shift_z + length_z,
        ]

    total = 3.0 * STENCIL[0] * part(0, 0, 0)
    for reach in range(1, 5):
        pair = part(reach, 0, 0) + part(-reach, 0, 0) + part(0, reach, 0) + part(0, -reach, 0)
        pair = pair + part(0, 0, reach) + part(0, 0, -reach)
        total = total + STENCIL[reach] * pair
    return total


def stencil(field):
    extended = extended_2(field, (("space", 1),), 4)
    padded = jnp.pad(extended, ((0, 0), (0, 0), (4, 4), (4, 4)))
    return second_difference(padded, field.shape[1], field.shape[2], field.shape[3])


def local(
    probes,
    sources,
    kappa,
    prior,
    basis,
    entry_cell,
    entry_owner,
    entry_slot,
    entry_weight,
    entry_count,
    trace_weight,
):
    first = probes * sources[0]
    second = 2.0 * first + kappa * stencil(first) + probes * sources[1]
    third = 2.0 * second - first + kappa * stencil(second) + probes * sources[2]
    fields = probes.shape[0]
    entries = entry_cell.shape[0]
    owned = trace_weight.shape[0]
    peers = lax.axis_size("space")
    live = jnp.arange(entries, dtype=jnp.int32) < entry_count[0]
    weight = jnp.where(live, entry_weight, jnp.zeros_like(entry_weight))
    flat = third.reshape(fields, -1)
    values = flat[:, entry_cell] * weight[None, :]
    trace_id = entry_owner * owned + entry_slot
    table = jnp.zeros((fields, peers * owned), jnp.float32).at[:, trace_id].add(values)
    traces = lax.psum_scatter(table, "space", scatter_dimension=1, tiled=True)
    weighted = traces * trace_weight[None, :]
    copies = lax.all_gather(weighted, "space", axis=1, tiled=True)
    returned = copies[:, trace_id]
    injected = returned * weight[None, :]
    adjoint_two = jnp.zeros_like(flat).at[:, entry_cell].add(injected).reshape(third.shape)
    adjoint_one = 2.0 * adjoint_two + stencil(kappa * adjoint_two)
    adjoint_zero = 2.0 * adjoint_one - adjoint_two + stencil(kappa * adjoint_one)
    image = (
        sources[0] * adjoint_zero
        + sources[1] * adjoint_one
        + sources[2] * adjoint_two
        + prior * probes
    )
    partial_coeffs = jnp.einsum("rxyz,pxyz->rp", basis, image, precision=lax.Precision.HIGHEST)
    coeffs = lax.psum(partial_coeffs, "space")
    hess_probe = image - jnp.einsum("rxyz,rp->pxyz", basis, coeffs, precision=lax.Precision.HIGHEST)
    return (hess_probe, coeffs)


def solution(mesh):
    return jax.shard_map(
        local,
        mesh=mesh,
        in_specs=(
            P("group", "space", None, None),
            P(None, ("group", "space"), None, None),
            P(("group", "space"), None, None),
            P(("group", "space"), None, None),
            P("group", "space", None, None),
            P(("group", "space")),
            P(("group", "space")),
            P(("group", "space")),
            P(("group", "space")),
            P(("group", "space")),
            P(("group", "space")),
        ),
        out_specs=(P("group", "space", None, None), P("group", None)),
        check_vma=False,
    )
```

profile of v0, /device:TPU:0, one launch (start us, length us, event | category | flops | bytes accessed | tf_op | source)
XLA Modules:
  0.0 345.3 jit_solution(2974060112535257835)
XLA Ops:
  10.0 2.4 collective-permute-start.1
  14.7 4.4 %collective-permute-done = f32[16,4,32,128]{3,0,2,1:T(8,128)S(1)} collective-permute-done((f32[16,4,32,128]{3,0,2,1:T(8,128)S(1)}, f32[16,4,32,128]{3,0,2,1:T(8,128)S(1)}, u32[]{:S(2)}, u32[]{:S(2)}) %collective-permute-start) | collective-permute-done | bytes 1048608 | tf_op jit(solution)/shard_map/ppermute | solution.py:17
  19.1 3.9 %select_maximum_fusion.6 = f32[16,12,40,136]{3,0,2,1:T(8,128)S(1)} fusion(f32[16,4,32,128]{3,0,2,1:T(8,128)S(1)} %collective-permute-done, f32[16,4,32,128]{3,0,2,1:T(8,128)S(1)} %copy_multiply_fusion, f32[16,4,32,128]{3,0,2,1:T(8,128)S(1)} %collective-permute-done.1), kind=kLoop, calls=%fused_computation.14 | loop fusion | flops 15667200 | bytes 7323648 | tf_op jit(solution)/shard_map/concatenate | solution.py:18
  23.1 8.2 %fusion.96 = f32[16,4,32,128]{3,0,2,1:T(8,128)} fusion(f32[16,4,32,128]{3,0,2,1:T(8,128)} %copy-done.12, f32[16,4,32,128]{3,0,2,1:T(8,128)} %copy-done.5, f32[16,4,32,128]{3,0,2,1:T(8,128)} %copy-done.13, f32[16,12,40,136]{3,0,2,1:T(8,128)S(1)} %select_maximum_fusion.6, f32[16,4,32,128]{3,2,1,0:T(8,128)} %param.11, f32[4,32,128]{2,1,0:T(8,128)S(1)} %get-tuple-element.10, ...), kind=kLoop, calls=%fused_computation.140 | loop fusion | flops 10485760 | bytes 22151168 | tf_op jit(solution)/shard_map/add | solution.py:60
  32.6 21.5 %collective-permute-start.3 = (f32[16,4,32,128]{3,0,2,1:T(8,128)}, f32[16,4,32,128]{3,0,2,1:T(8,128)S(1)}, u32[]{:S(2)}, u32[]{:S(2)}) collective-permute-start(f32[16,4,32,128]{3,0,2,1:T(8,128)} %fusion.96), channel_id=1, source_target_pairs={{0,1},{1,2},{2,3},{3,4},{4,5},{5,6},{6,7},{7,8},{8,9},{9,10},{10,1... | collective-permute-start | bytes 3145736 | tf_op jit(solution)/shard_map/ppermute | solution.py:16
  56.6 5.1 %select_maximum_fusion.4 = f32[16,12,40,136]{3,0,2,1:T(8,128)S(1)} fusion(f32[16,4,32,128]{3,0,2,1:T(8,128)S(1)} %collective-permute-done.2, f32[16,4,32,128]{3,0,2,1:T(8,128)} %fusion.96, f32[16,4,32,128]{3,0,2,1:T(8,128)S(1)} %collective-permute-done.3), kind=kLoop, calls=%fused_computation.12 | loop fusion | flops 15667200 | bytes 7323648 | tf_op jit(solution)/shard_map/concatenate | solution.py:18
  61.7 8.2 %fusion.73 = f32[16,4,32,128]{3,0,2,1:T(8,128)} fusion(f32[16,4,32,128]{3,0,2,1:T(8,128)} %copy-done.11, f32[16,4,32,128]{3,0,2,1:T(8,128)} %fusion.96, f32[16,4,32,128]{3,0,2,1:T(8,128)} %copy-done.10, f32[16,12,40,136]{3,0,2,1:T(8,128)S(1)} %select_maximum_fusion.4, f32[16,4,32,128]{3,2,1,0:T(8,128)} %param.11, f32[4,32,128]{2,1,0:T(8,128)S(1)} %get-tuple-element.8, ...), kind=kLoop, calls=%fused_computation.117 | loop fusion | flops 11010048 | bytes 22216704 | tf_op jit(solution)/shard_map/add | solution.py:61
  70.0 6.0 %copy.36 = f32[16,4,32,128]{0,3,2,1:T(8,128)} copy(f32[16,4,32,128]{3,0,2,1:T(8,128)} %fusion.73) | data formatting | bytes 2097152 | tf_op jit(solution)/shard_map/reshape | solution.py:68
  76.0 6.3 %scatter_custom_fusion = f32[16,2048]{0,1:T(8,128)} fusion(s32[512]{0:T(512)S(1)} %compare_select_fusion, f32[]{:T(128)} %constant.11.clone.1, f32[512]{0:T(512)S(1)} %fusion.126, f32[16,16384]{0,1:T(8,128)} %bitcast.23, s32[1024]{0:T(1024)S(1)} %pad_clamp_fusion.1), kind=kCustom, calls=%fused_computation.206 | custom fusion | flops 16384 | bytes 1185796 | tf_op jit(solution)/shard_map/scatter-add | solution.py:71
  82.3 81.2 %reduce-scatter.2.cloned.1.call-done = f32[16,128]{0,1:T(8,128)} async-done(((f32[16,2048]{0,1:T(8,128)}), f32[16,128]{0,1:T(8,128)}) %reduce-scatter.2.cloned.1.call-update) | async-done | bytes 8208 | tf_op jit(solution)/shard_map/reduce_scatter | solution.py:72
  164.3 22.6 %all_gather.3 = f32[16,2048]{0,1:T(8,128)S(1)} all-gather(f32[16,128]{0,1:T(8,128)S(1)} %broadcast_multiply_fusion.2), channel_id=1, replica_groups=mesh['group'=2,'space'=16] {'space'}, dimensions={1}, use_global_device_ids=true | all-gather | bytes 139264 | tf_op jit(solution)/shard_map/all_gather | solution.py:74
  186.9 7.9 %scatter_custom_fusion.1 = f32[16,16384]{0,1:T(8,128)} fusion(s32[512]{0:T(512)S(1)} %compare_select_fusion.1, f32[]{:T(128)} %constant.11.clone.1, f32[512]{0:T(512)S(1)} %fusion.126, f32[16,2048]{0,1:T(8,128)S(1)} %all_gather.3, s32[1024]{0:T(1024)S(1)} %pad_clamp_fusion), kind=kCustom, calls=%fused_computation.19 | custom fusion | flops 16384 | bytes 2103300 | tf_op jit(solution)/shard_map/scatter-add | solution.py:77
  194.8 5.1 %copy.26 = f32[16,4,32,128]{3,0,2,1:T(8,128)S(1)} copy(f32[16,4,32,128]{0,3,2,1:T(8,128)} %bitcast.22) | data formatting | bytes 2097152 | tf_op jit(solution)/shard_map/reshape | solution.py:77
  200.1 2.3 collective-permute-start.5
  204.6 2.3 collective-permute-done.4
  208.0 3.9 %select_maximum_fusion.2 = f32[16,12,40,136]{3,0,2,1:T(8,128)S(1)} fusion(f32[16,4,32,128]{3,0,2,1:T(8,128)S(1)} %collective-permute-done.4, f32[16,4,32,128]{3,0,2,1:T(8,128)S(1)} %broadcast_multiply_fusion.1, f32[16,4,32,128]{3,0,2,1:T(8,128)S(1)} %collective-permute-done.5), kind=kLoop, calls=%fused_computation.10 | loop fusion | flops 15667200 | bytes 7323648 | tf_op jit(solution)/shard_map/concatenate | solution.py:18
  211.9 8.3 %broadcast_multiply_fusion = (f32[16,4,32,128]{3,0,2,1:T(8,128)}, f32[16,4,32,128]{3,0,2,1:T(8,128)}) fusion(f32[4,32,128]{2,1,0:T(8,128)S(1)} %copy-done.14, f32[16,12,40,136]{3,0,2,1:T(8,128)S(1)} %select_maximum_fusion.2, f32[16,4,32,128]{3,0,2,1:T(8,128)} %copy-done.9, f32[16,4,32,128]{3,0,2,1:T(8,128)} %copy-done.8, f32[16,4,32,128]{3,0,2,1:T(8,128)} %copy-done.4, ...), kind=kLoop, calls=%fused_computation.204 | loop fusion | flops 9961472 | bytes 23134208 | tf_op jit(solution)/shard_map/mul | solution.py:79
  220.3 21.4 %collective-permute-start.7 = (f32[16,4,32,128]{3,0,2,1:T(8,128)}, f32[16,4,32,128]{3,0,2,1:T(8,128)S(1)}, u32[]{:S(2)}, u32[]{:S(2)}) collective-permute-start(f32[16,4,32,128]{3,0,2,1:T(8,128)} %get-tuple-element.6), channel_id=1, source_target_pairs={{0,1},{1,2},{2,3},{3,4},{4,5},{5,6},{6,7},{7,8},{8,9},{9,10},{10,1... | collective-permute-start | bytes 3145736 | tf_op jit(solution)/shard_map/ppermute | solution.py:16
  244.1 4.3 %collective-permute-done.6 = f32[16,4,32,128]{3,0,2,1:T(8,128)S(1)} collective-permute-done((f32[16,4,32,128]{3,0,2,1:T(8,128)}, f32[16,4,32,128]{3,0,2,1:T(8,128)S(1)}, u32[]{:S(2)}, u32[]{:S(2)}) %collective-permute-start.6) | collective-permute-done | bytes 1048608 | tf_op jit(solution)/shard_map/ppermute | solution.py:17
  248.4 6.0 %select_maximum_fusion = f32[16,12,40,136]{3,0,2,1:T(8,128)} fusion(f32[16,4,32,128]{3,0,2,1:T(8,128)S(1)} %collective-permute-done.6, f32[16,4,32,128]{3,0,2,1:T(8,128)} %get-tuple-element.6, f32[16,4,32,128]{3,0,2,1:T(8,128)S(1)} %collective-permute-done.7), kind=kLoop, calls=%fused_computation.8 | loop fusion | flops 15667200 | bytes 7323648 | tf_op jit(solution)/shard_map/concatenate | solution.py:18
  254.5 20.3 %fusion.29 = f32[16,4,32,128]{3,0,2,1:T(8,128)} fusion(f32[16,4,32,128]{3,0,2,1:T(8,128)} %copy-done.6, f32[16,4,32,128]{3,0,2,1:T(8,128)} %get-tuple-element.6, f32[16,4,32,128]{3,0,2,1:T(8,128)} %copy-done.7, f32[16,12,40,136]{3,0,2,1:T(8,128)} %select_maximum_fusion, f32[16,4,32,128]{3,0,2,1:T(8,128)S(1)} %copy-done.1, ...), kind=kLoop, calls=%fused_computation.73 | loop fusion | flops 11796480 | bytes 24379392 | tf_op jit(solution)/shard_map/add | solution.py:81
  274.8 6.3 %fusion.12 = f32[64,16]{0,1:T(8,128)S(1)} fusion(f32[16,4,32,128]{3,0,2,1:T(8,128)} %fusion.29, f32[64,4,32,128]{3,2,1,0:T(8,128)S(1)} %copy-done.2), kind=kOutput, calls=%fused_computation.58 | convolution fusion | flops 201326592 | bytes 5246976 | tf_op jit(solution)/shard_map/rxyz,pxyz->rp/dot_general | solution.py:86
  281.1 49.3 %psum.7 = f32[64,16]{0,1:T(8,128)S(1)} all-reduce(f32[64,16]{0,1:T(8,128)S(1)} %fusion.12), channel_id=1, replica_groups=mesh['group'=2,'space'=16] {'space'}, use_global_device_ids=true, to_apply=%region_3.4 | all-reduce | flops 1024 | bytes 8192 | tf_op jit(solution)/shard_map/psum | solution.py:87
  330.4 6.8 %fusion.9 = f32[16,4,32,128]{3,0,2,1:T(8,128)S(1)} fusion(f32[16,4,32,128]{3,0,2,1:T(8,128)} %fusion.29, f32[64,4,32,128]{3,2,1,0:T(8,128)} %param.15, f32[64,16]{0,1:T(8,128)S(1)} %psum.7), kind=kOutput, calls=%fused_computation.57 | convolution fusion | flops 201588736 | bytes 6295552 | tf_op jit(solution)/shard_map/rxyz,rp->pxyz/dot_general | solution.py:88
  (65 shorter events, 16.0 us)
Async XLA Ops:
  7.2 15.9 %copy-start.14 = (f32[4,32,128]{2,1,0:T(8,128)S(1)}, f32[4,32,128]{2,1,0:T(8,128)}, u32[]{:S(2)}) copy-start(f32[4,32,128]{2,1,0:T(8,128)} %param.13) | copy-start | bytes 196612
  7.2 156.2 %reduce-scatter.2.cloned.1.call-start = ((), (), s32[]{:S(2)}) async-start(), calls=%async_computation.1 | async-start | bytes 1114112 | tf_op jit(solution)/shard_map/reduce_scatter | solution.py:72
  10.0 9.1 %copy-start.5 = (f32[16,4,32,128]{3,0,2,1:T(8,128)}, f32[16,4,32,128]{3,0,2,1:T(8,128)S(1)}, u32[]{:S(2)}) copy-start(f32[16,4,32,128]{3,0,2,1:T(8,128)S(1)} %copy_multiply_fusion) | copy-start | bytes 3145732
  10.0 4.6 %collective-permute-start.1 = (f32[16,4,32,128]{3,0,2,1:T(8,128)S(1)}, f32[16,4,32,128]{3,0,2,1:T(8,128)S(1)}, u32[]{:S(2)}, u32[]{:S(2)}) collective-permute-start(f32[16,4,32,128]{3,0,2,1:T(8,128)S(1)} %copy_multiply_fusion), channel_id=1, source_target_pairs={{0,1},{1,2},{2,3},{3,4},{4,5},{5,6},{6,7},{7,8},{8,9},{9,10},{10,1... | collective-permute-start | bytes 3145736 | tf_op jit(solution)/shard_map/ppermute | solution.py:16
  12.5 6.6 %collective-permute-start = (f32[16,4,32,128]{3,0,2,1:T(8,128)S(1)}, f32[16,4,32,128]{3,0,2,1:T(8,128)S(1)}, u32[]{:S(2)}, u32[]{:S(2)}) collective-permute-start(f32[16,4,32,128]{3,0,2,1:T(8,128)S(1)} %copy_multiply_fusion), channel_id=1, source_target_pairs={{1,0},{2,1},{3,2},{4,3},{5,4},{6,5},{7,6},{8,7},{9,8},{10,9},{11,1... | collective-permute-start | bytes 3145736 | tf_op jit(solution)/shard_map/ppermute | solution.py:17
  14.7 8.4 %copy-start.12 = (f32[16,4,32,128]{3,0,2,1:T(8,128)}, f32[16,4,32,128]{3,0,2,1:T(8,128)S(1)}, u32[]{:S(2)}) copy-start(f32[16,4,32,128]{3,0,2,1:T(8,128)S(1)} %collective-permute-done.1) | copy-start | bytes 3145732
  23.1 31.8 %copy-start.19 = (s32[512]{0:T(512)S(1)}, s32[512]{0:T(512)}, u32[]{:S(2)}) copy-start(s32[512]{0:T(512)} %param.16) | copy-start | bytes 6148
  23.1 31.8 %copy-start.20 = (f32[512]{0:T(512)S(1)}, f32[512]{0:T(512)}, u32[]{:S(2)}) copy-start(f32[512]{0:T(512)} %param.19) | copy-start | bytes 6148
  23.1 31.8 %copy-start.17 = (s32[512]{0:T(512)S(1)}, s32[512]{0:T(512)}, u32[]{:S(2)}) copy-start(s32[512]{0:T(512)} %param.18) | copy-start | bytes 6148
  23.1 31.8 %copy-start.18 = (s32[512]{0:T(512)S(1)}, s32[512]{0:T(512)}, u32[]{:S(2)}) copy-start(s32[512]{0:T(512)} %param.17) | copy-start | bytes 6148
  31.3 23.6 %collective-permute-start.2 = (f32[16,4,32,128]{3,0,2,1:T(8,128)}, f32[16,4,32,128]{3,0,2,1:T(8,128)S(1)}, u32[]{:S(2)}, u32[]{:S(2)}) collective-permute-start(f32[16,4,32,128]{3,0,2,1:T(8,128)} %fusion.96), channel_id=1, source_target_pairs={{1,0},{2,1},{3,2},{4,3},{5,4},{6,5},{7,6},{8,7},{9,8},{10,9},{11,1... | collective-permute-start | bytes 3145736 | tf_op jit(solution)/shard_map/ppermute | solution.py:17
  32.6 24.0 %collective-permute-start.3 = (f32[16,4,32,128]{3,0,2,1:T(8,128)}, f32[16,4,32,128]{3,0,2,1:T(8,128)S(1)}, u32[]{:S(2)}, u32[]{:S(2)}) collective-permute-start(f32[16,4,32,128]{3,0,2,1:T(8,128)} %fusion.96), channel_id=1, source_target_pairs={{0,1},{1,2},{2,3},{3,4},{4,5},{5,6},{6,7},{7,8},{8,9},{9,10},{10,1... | collective-permute-start | bytes 3145736 | tf_op jit(solution)/shard_map/ppermute | solution.py:16
  70.0 93.5 %copy-start.21 = (f32[128]{0:T(128)S(1)}, f32[128]{0:T(128)}, u32[]{:S(2)}) copy-start(f32[128]{0:T(128)} %param.21) | copy-start | bytes 1540
  200.1 6.9 %copy-start.4 = (f32[16,4,32,128]{3,0,2,1:T(8,128)}, f32[16,4,32,128]{3,0,2,1:T(8,128)S(1)}, u32[]{:S(2)}) copy-start(f32[16,4,32,128]{3,0,2,1:T(8,128)S(1)} %broadcast_multiply_fusion.1) | copy-start | bytes 3145732
  200.1 4.5 %collective-permute-start.5 = (f32[16,4,32,128]{3,0,2,1:T(8,128)S(1)}, f32[16,4,32,128]{3,0,2,1:T(8,128)S(1)}, u32[]{:S(2)}, u32[]{:S(2)}) collective-permute-start(f32[16,4,32,128]{3,0,2,1:T(8,128)S(1)} %broadcast_multiply_fusion.1), channel_id=1, source_target_pairs={{0,1},{1,2},{2,3},{3,4},{4,5},{5,6},{6,7},{7,8},{8,9},{9,10},{10,1... | collective-permute-start | bytes 3145736 | tf_op jit(solution)/shard_map/ppermute | solution.py:16
  202.4 4.6 %collective-permute-start.4 = (f32[16,4,32,128]{3,0,2,1:T(8,128)S(1)}, f32[16,4,32,128]{3,0,2,1:T(8,128)S(1)}, u32[]{:S(2)}, u32[]{:S(2)}) collective-permute-start(f32[16,4,32,128]{3,0,2,1:T(8,128)S(1)} %broadcast_multiply_fusion.1), channel_id=1, source_target_pairs={{1,0},{2,1},{3,2},{4,3},{5,4},{6,5},{7,6},{8,7},{9,8},{10,9},{11,1... | collective-permute-start | bytes 3145736 | tf_op jit(solution)/shard_map/ppermute | solution.py:17
  220.2 34.2 %copy-start.1 = (f32[16,4,32,128]{3,0,2,1:T(8,128)S(1)}, f32[16,4,32,128]{3,0,2,1:T(8,128)}, u32[]{:S(2)}) copy-start(f32[16,4,32,128]{3,0,2,1:T(8,128)} %copy-done) | copy-start | bytes 3145732
  220.2 34.2 %copy-start.3 = (f32[16,4,32,128]{3,2,1,0:T(8,128)S(1)}, f32[16,4,32,128]{3,2,1,0:T(8,128)}, u32[]{:S(2)}) copy-start(f32[16,4,32,128]{3,2,1,0:T(8,128)} %param.11) | copy-start | bytes 3145732
  220.2 34.2 %copy-start.15 = (f32[4,32,128]{2,1,0:T(8,128)S(1)}, f32[4,32,128]{2,1,0:T(8,128)}, u32[]{:S(2)}) copy-start(f32[4,32,128]{2,1,0:T(8,128)} %param.14) | copy-start | bytes 196612
  220.3 23.9 %collective-permute-start.7 = (f32[16,4,32,128]{3,0,2,1:T(8,128)}, f32[16,4,32,128]{3,0,2,1:T(8,128)S(1)}, u32[]{:S(2)}, u32[]{:S(2)}) collective-permute-start(f32[16,4,32,128]{3,0,2,1:T(8,128)} %get-tuple-element.6), channel_id=1, source_target_pairs={{0,1},{1,2},{2,3},{3,4},{4,5},{5,6},{6,7},{7,8},{8,9},{9,10},{10,1... | collective-permute-start | bytes 3145736 | tf_op jit(solution)/shard_map/ppermute | solution.py:16
  241.7 6.7 %collective-permute-start.6 = (f32[16,4,32,128]{3,0,2,1:T(8,128)}, f32[16,4,32,128]{3,0,2,1:T(8,128)S(1)}, u32[]{:S(2)}, u32[]{:S(2)}) collective-permute-start(f32[16,4,32,128]{3,0,2,1:T(8,128)} %get-tuple-element.6), channel_id=1, source_target_pairs={{1,0},{2,1},{3,2},{4,3},{5,4},{6,5},{7,6},{8,7},{9,8},{10,9},{11,1... | collective-permute-start | bytes 3145736 | tf_op jit(solution)/shard_map/ppermute | solution.py:17
  244.1 10.3 %copy-start.6 = (f32[16,4,32,128]{3,0,2,1:T(8,128)}, f32[16,4,32,128]{3,0,2,1:T(8,128)S(1)}, u32[]{:S(2)}) copy-start(f32[16,4,32,128]{3,0,2,1:T(8,128)S(1)} %collective-permute-done.7) | copy-start | bytes 3145732
  254.5 20.3 %copy-start.2 = (f32[64,4,32,128]{3,2,1,0:T(8,128)S(1)}, f32[64,4,32,128]{3,2,1,0:T(8,128)}, u32[]{:S(2)}) copy-start(f32[64,4,32,128]{3,2,1,0:T(8,128)} %param.15) | copy-start | bytes 12582916
  330.4 8.1 %copy-start.16 = (f32[64,16]{0,1:T(8,128)}, f32[64,16]{0,1:T(8,128)S(1)}, u32[]{:S(2)}) copy-start(f32[64,16]{0,1:T(8,128)S(1)} %psum.7) | copy-start | bytes 12292
  (7 other events, 24.8 us)
Sparse Core Ops, SparseCore 0:
  82.4 81.0 reduce-scatter.1
where the time goes:
time: 346 us; the launch traced here: 345 us
  waiting for transfers between devices  96.6 us (28%)
  other arithmetic  81.2 us (23%)
  blocking collectives  71.9 us (21%)
  starting transfers between devices  53.1 us (15%)
  between operations  15.1 us (4%)
  local copies, waits for them, and re-layouts  14.4 us (4%)
  matrix products  13 us (4%)
    reduce_scatter x1, waiting for transfers between devices, local(): traces = lax.psum_scatter(table, 'space', scatter_dimension=1, tiled=True)  81.2 us
    psum x1, blocking collectives, local(): coeffs = lax.psum(partial_coeffs, 'space')  49.3 us
    ppermute x4, starting transfers between devices, extended_2(): before = lax.ppermute(last, axis, up)  47.7 us
    all_gather x1, blocking collectives, local(): copies = lax.all_gather(weighted, 'space', axis=1, tiled=True)  22.6 us
    add x1, other arithmetic, local(): sources[0] * adjoint_zero + sources[1] * adjoint_one  20.3 us
    concatenate x4, other arithmetic, extended_2(): array = jnp.concatenate([before, array, after], axis=dim)  19 us
    ppermute x4, waiting for transfers between devices, extended_2(): after = lax.ppermute(leading, axis, down)  11 us
    mul x1, other arithmetic, local(): kappa * adjoint_one  8.31 us
  transfers between devices with their start and end apart: 9, of which 8 were waited for; matrix products, arithmetic and copies ran while one was open for 0% of the time, Pallas kernels for 0%

commit v1 on v0

v1 whole, which is shorter than its diff:
```python
import functools

import jax
import jax.numpy as jnp
import ml_dtypes
import numpy as np
from jax import lax
from jax.experimental import pallas as pl
from jax.experimental.pallas import tpu as pltpu
from jax.sharding import PartitionSpec as P

STENCIL = (-205.0 / 72.0, 8.0 / 5.0, -1.0 / 5.0, 8.0 / 315.0, -1.0 / 560.0)
CENTER = 3.0 * STENCIL[0]
REACH = 4
LAYERS = 4
PADDED = 40
HALF = 128
F32 = jnp.float32
BF16 = jnp.bfloat16
NT = (((1,), (1,)), ((), ()))


def band():
    place = np.arange(HALF)
    apart = np.abs(place[:, None] - place[None, :])
    full = np.zeros((HALF, HALF), np.float32)
    for reach in range(1, REACH + 1):
        full[apart == reach] = STENCIL[reach]
    high = full.astype(ml_dtypes.bfloat16)
    low = (full - high.astype(np.float32)).astype(ml_dtypes.bfloat16)
    return np.block([[high, low], [high, np.zeros_like(low)]])


def split(value):
    high = value.astype(BF16)
    low = (value - high.astype(F32)).astype(BF16)
    return high, low


def at(row, count=16):
    return pl.ds(pl.multiple_of(row, 16), count)


def spread(ref, row, fields):
    return jnp.broadcast_to(ref[pl.ds(row, 1), :], (fields, HALF))


def clear_margins(ref, layers, fields):
    margin = jnp.zeros((REACH * fields, HALF), F32)
    for layer in range(layers):
        start = layer * PADDED * fields
        ref[start : start + REACH * fields, :] = margin
        start += (PADDED - REACH) * fields
        ref[start : start + REACH * fields, :] = margin


def along_z(ref, first, chunk, fields, band_ref, out_ref):
    count = 8 * fields
    pieces = [ref[at(((first + x) * PADDED + REACH + chunk * 8) * fields, count), :] for x in range(LAYERS)]
    high, low = split(jnp.concatenate(pieces, axis=0))
    both = jnp.dot(jnp.concatenate([high, low], axis=1), band_ref[...], preferred_element_type=F32)
    out_ref[...] = both[:, :HALF] + both[:, HALF:]


def laplacian(get, x, y, z_term, lowest, highest):
    total = CENTER * get(x, y) + z_term
    for k in range(1, REACH + 1):
        ring = get(x, y + k) + get(x, y - k)
        if x + k <= highest:
            ring = ring + get(x + k, y)
        if x - k >= lowest:
            ring = ring + get(x - k, y)
        total = total + STENCIL[k] * ring
    return total


def forward_own(fields, probes, sources, kappa, band_ref, turned, first, second, third, z_term):
    clear_margins(first, LAYERS, fields)
    clear_margins(second, LAYERS, fields)

    def load(chunk, carry):
        for x in range(LAYERS):
            for step in range(8):
                y = chunk * 8 + step
                cell = x * 32 + y
                value = probes[pl.ds(cell, fields, stride=HALF), :]
                turned[at(cell * fields, fields), :] = value
                first[at((x * PADDED + REACH + y) * fields, fields), :] = value * spread(sources, cell, fields)
        return carry

    lax.fori_loop(0, 4, load, 0)

    def sweep(field, chunk, emit):
        along_z(field, 0, chunk, fields, band_ref, z_term)
        for x in range(LAYERS):
            for step in range(8):
                y = chunk * 8 + step

                def get(layer, row):
                    return field[at((layer * PADDED + REACH + row) * fields, fields), :]

                z_part = z_term[at((x * 8 + step) * fields, fields), :]
                total = laplacian(get, x, y, z_part, 0, LAYERS - 1)
                emit(x, y, get(x, y), spread(kappa, x * 32 + y, fields) * total)

    def step_one(chunk, carry):
        def emit(x, y, now, change):
            cell = x * 32 + y
            push = turned[at(cell * fields, fields), :] * spread(sources, 128 + cell, fields)
            second[at((x * PADDED + REACH + y) * fields, fields), :] = 2.0 * now + change + push

        sweep(first, chunk, emit)
        return carry

    lax.fori_loop(0, 4, step_one, 0)

    def step_two(chunk, carry):
        def emit(x, y, now, change):
            cell = x * 32 + y
            push = turned[at(cell * fields, fields), :] * spread(sources, 256 + cell, fields)
            before = first[at((x * PADDED + REACH + y) * fields, fields), :]
            third[at(cell * fields, fields), :] = 2.0 * now - before + change + push

        sweep(second, chunk, emit)
        return carry

    lax.fori_loop(0, 4, step_two, 0)


def entry_row(ref, row):
    return jnp.concatenate([ref[row + i : row + i + 1, :] for i in range(4)], axis=1)


def describe(statics, fields, pair, cell_ref, line_ref, owner_ref, slot_ref, weight_ref):
    entries = pair.shape[1]
    place = lax.broadcasted_iota(jnp.int32, (256, entries), 0)
    slot_place = lax.broadcasted_iota(jnp.int32, (HALF, entries), 0)
    for tile, ref in enumerate(statics):
        cell = entry_row(ref, 128).astype(jnp.int32)
        owner = entry_row(ref, 132).astype(jnp.int32)
        slot = entry_row(ref, 136).astype(jnp.int32)
        weight = entry_row(ref, 140)
        hot = jnp.where(place == jnp.bitwise_and(cell, 255), 1.0, 0.0)
        cell_ref[tile * 256 : (tile + 1) * 256, :] = hot.astype(BF16)
        hot = jnp.where(slot_place == slot, 1.0, 0.0)
        slot_ref[tile * HALF : (tile + 1) * HALF, :] = hot.astype(BF16)
        rows = slice(tile * fields, (tile + 1) * fields)
        line_ref[rows, :] = jnp.broadcast_to(lax.shift_right_logical(cell, 8), (fields, entries))
        owner_ref[rows, :] = jnp.broadcast_to(owner, (fields, entries))
        weight_ref[rows, :] = jnp.broadcast_to(weight, (fields, entries))


def forward_window(
    fields, peers, me, first, second, third, kappa_mm, kappa_m, kappa, kappa_p, kappa_pp, band_ref, own_scale,
    table, cell_ref, slot_ref, below, above, z_term, sample, total_ref, line_ref, owner_ref, weight_ref,
):
    statics = (kappa_mm, kappa_m, kappa, kappa_p, kappa_pp)
    entries = line_ref.shape[1]
    describe(statics, fields, cell_ref, cell_ref, line_ref, owner_ref, slot_ref, weight_ref)
    clear_margins(below, LAYERS, fields)
    clear_margins(above, LAYERS, fields)
    total_ref[...] = jnp.zeros_like(total_ref)

    def outward(chunk, carry):
        for step in range(8):
            y = chunk * 8 + step
            own = [first[at((x * PADDED + REACH + y) * fields, fields), :] for x in range(LAYERS)]
            for x in range(LAYERS):
                up = sum(STENCIL[4 + x - other] * own[other] for other in range(x, LAYERS))
                down = sum(STENCIL[4 + other - x] * own[other] for other in range(x + 1))
                row = at((x * PADDED + REACH + y) * fields, fields)
                above[row, :] = spread(kappa_p, x * 32 + y, fields) * up
                below[row, :] = spread(kappa_m, x * 32 + y, fields) * down
        return carry

    lax.fori_loop(0, 4, outward, 0)

    def read(layer, y):
        ref = (below, second, above)[(layer + LAYERS) // LAYERS]
        return ref[at((layer % LAYERS * PADDED + REACH + y) * fields, fields), :]

    def far(x, y, lowest, highest):
        total = None
        for other in range(lowest, highest + 1):
            if 1 <= abs(x - other) <= REACH:
                term = STENCIL[abs(x - other)] * read(other, y)
                total = term if total is None else total + term
        return total

    def sampling(chunk, carry):
        for tile in range(5):
            if tile in (1, 3):
                along_z((below, above)[tile // 2], 0, chunk, fields, band_ref, z_term)
            for x in range(LAYERS):
                for step in range(8):
                    y = chunk * 8 + step
                    cell = x * 32 + y
                    layer = (tile - 2) * LAYERS + x
                    speed = spread(statics[tile], cell, fields)
                    if tile in (0, 4):
                        value = speed * far(layer, y, -4, 7)
                    elif tile == 2:
                        outside = far(layer, y, -4, -1) + far(layer, y, 4, 7)
                        value = third[at(cell * fields, fields), :] + speed * outside
                    else:
                        z_part = z_term[at((x * 8 + step) * fields, fields), :]
                        value = 2.0 * read(layer, y) + speed * laplacian(read, layer, y, z_part, -4, 7)
                    row = (x * 4 + step // 2) * fields
                    side = step % 2 * HALF
                    sample[row : row + fields, side : side + HALF] = value
            high, low = split(sample[...])
            hot = cell_ref[tile * 256 : (tile + 1) * 256, :]
            picked = jnp.dot(high, hot, preferred_element_type=F32) + jnp.dot(low, hot, preferred_element_type=F32)
            rows = slice(tile * fields, (tile + 1) * fields)
            line = line_ref[rows, :]
            total = total_ref[rows, :]
            for x in range(LAYERS):
                for pair in range(4):
                    row = (x * 4 + pair) * fields
                    chosen = line == x * 16 + chunk * 4 + pair
                    total = total + jnp.where(chosen, picked[row : row + fields, :], 0.0)
            total_ref[rows, :] = total
        return carry

    lax.fori_loop(0, 4, sampling, 0)

    for group in range(peers // 16):
        result = jnp.zeros((16 * fields, HALF), F32)
        for tile in range(5):
            rows = slice(tile * fields, (tile + 1) * fields)
            high, low = split(total_ref[rows, :] * weight_ref[rows, :])
            high, low = high.astype(F32), low.astype(F32)
            owner = owner_ref[rows, :]
            hot = slot_ref[tile * HALF : (tile + 1) * HALF, :]
            for part in (high, low):
                pieces = [jnp.where(owner == group * 16 + i, part, 0.0).astype(BF16) for i in range(16)]
                result = result + lax.dot_general(
                    jnp.concatenate(pieces, axis=0), hot, NT, preferred_element_type=F32
                )
        table[group * 16 * fields : (group + 1) * 16 * fields, :] = result
    place = lax.broadcasted_iota(jnp.int32, (peers, HALF), 0)
    own = jnp.broadcast_to(own_scale[...], (peers, HALF))
    table[peers * fields : peers * fields + peers, :] = jnp.where(place == me[0], own, 0.0)


def basis_parts(basis, out):
    rank = basis.shape[0] // HALF

    def body(group, carry):
        for step in range(8):
            high, low = split(basis[pl.ds(group * 8 + step, rank, stride=HALF), :])
            rows = at(group * rank, rank)
            out[rows, step * 256 : step * 256 + HALF] = high
            out[rows, step * 256 + HALF : (step + 1) * 256] = low
        return carry

    lax.fori_loop(0, 16, body, 0)


def adjoint(
    fields, peers, table, statics_mm, statics_m, statics, statics_p, statics_pp, cell_ref, slot_ref, turned, sources,
    prior, band_ref, basis, image, coeffs, speed_ref, line_ref, high_ref, low_ref, left, inner_two, outer_two,
    inner_one, outer_one, z_term, image_parts, scaled,
):
    tiles = (statics_mm, statics_m, statics, statics_p, statics_pp)
    entries = line_ref.shape[1]
    clear_margins(inner_two, 5 * LAYERS, fields)
    clear_margins(inner_one, 3 * LAYERS, fields)
    for owner in range(peers):
        rows = slice(owner * fields, (owner + 1) * fields)
        scaled[rows, :] = table[rows, :] * table[peers * fields + owner : peers * fields + owner + 1, :]
    for tile, ref in enumerate(tiles):
        speed_ref[tile * HALF : (tile + 1) * HALF, :] = ref[0:HALF, :]
        rows = slice(tile * fields, (tile + 1) * fields)
        cell = entry_row(ref, 128).astype(jnp.int32)
        owner = jnp.broadcast_to(entry_row(ref, 132).astype(jnp.int32), (fields, entries))
        line_ref[rows, :] = jnp.broadcast_to(lax.shift_right_logical(cell, 8), (fields, entries))
        hot = slot_ref[tile * HALF : (tile + 1) * HALF, :]
        total = jnp.zeros((fields, entries), F32)
        for group in range(peers // 16):
            high, low = split(scaled[group * 16 * fields : (group + 1) * 16 * fields, :])
            read = jnp.dot(high, hot, preferred_element_type=F32) + jnp.dot(low, hot, preferred_element_type=F32)
            for i in range(16):
                total = total + jnp.where(owner == group * 16 + i, read[i * fields : (i + 1) * fields, :], 0.0)
        high, low = split(total * entry_row(ref, 140))
        high_ref[rows, :] = high.astype(F32)
        low_ref[rows, :] = low.astype(F32)

    def inject(index, carry):
        tile, chunk = index // 4, index % 4
        rows = at(tile * fields, fields)
        line, high, low = line_ref[rows, :], high_ref[rows, :], low_ref[rows, :]
        for x in range(LAYERS):
            for pair in range(4):
                row = (x * 4 + pair) * fields
                chosen = line == x * 16 + chunk * 4 + pair
                left[row : row + fields, :entries] = jnp.where(chosen, high, 0.0).astype(BF16)
                left[row : row + fields, entries:] = jnp.where(chosen, low, 0.0).astype(BF16)
        hot = cell_ref[pl.ds(pl.multiple_of(tile * 256, 256), 256), :]
        value = lax.dot_general(left[:, :entries], hot, NT, preferred_element_type=F32)
        value = value + lax.dot_general(left[:, entries:], hot, NT, preferred_element_type=F32)
        for x in range(LAYERS):
            for step in range(8):
                y = chunk * 8 + step
                row = (x * 4 + step // 2) * fields
                side = step % 2 * HALF
                now = value[row : row + fields, side : side + HALF]
                layer = tile * LAYERS + x
                outer_two[at((layer * 32 + y) * fields, fields), :] = now
                speed = spread(speed_ref, layer * 32 + y, fields)
                inner_two[at((layer * PADDED + REACH + y) * fields, fields), :] = speed * now
        return carry

    lax.fori_loop(0, 20, inject, 0)

    def step_one(index, carry):
        tile, chunk = index // 4 + 1, index % 4
        along_z(inner_two, tile * LAYERS, chunk, fields, band_ref, z_term)
        for x in range(LAYERS):
            for step in range(8):
                y = chunk * 8 + step

                def get(layer, row):
                    return inner_two[at(((tile * LAYERS + layer) * PADDED + REACH + row) * fields, fields), :]

                z_part = z_term[at((x * 8 + step) * fields, fields), :]
                layer = tile * LAYERS + x
                now = 2.0 * outer_two[at((layer * 32 + y) * fields, fields), :]
                now = now + laplacian(get, x, y, z_part, -4, 7)
                speed = spread(speed_ref, layer * 32 + y, fields)
                layer = layer - LAYERS
                outer_one[at((layer * 32 + y) * fields, fields), :] = now
                inner_one[at((layer * PADDED + REACH + y) * fields, fields), :] = speed * now
        return carry

    lax.fori_loop(0, 12, step_one, 0)

    def get_one(layer, row):
        return inner_one[at(((LAYERS + layer) * PADDED + REACH + row) * fields, fields), :]

    def step_two(chunk, total):
        along_z(inner_one, LAYERS, chunk, fields, band_ref, z_term)
        for x in range(LAYERS):
            for step in range(8):
                y = chunk * 8 + step
                cell = x * 32 + y
                z_part = z_term[at((x * 8 + step) * fields, fields), :]
                two = outer_two[at((2 * LAYERS * 32 + cell) * fields, fields), :]
                one = outer_one[at((LAYERS * 32 + cell) * fields, fields), :]
                zero = 2.0 * one - two + laplacian(get_one, x, y, z_part, -4, 7)
                value = spread(sources, cell, fields) * zero
                value = value + spread(sources, 128 + cell, fields) * one
                value = value + spread(sources, 256 + cell, fields) * two
                value = value + spread(prior, cell, fields) * turned[at(cell * fields, fields), :]
                image[at(cell * fields, fields), :] = value
                high, low = split(value)
                side = step * 256
                image_parts[0:fields, side : side + HALF] = high
                image_parts[0:fields, side + HALF : side + 256] = high
                image_parts[fields : 2 * fields, side : side + HALF] = low
                image_parts[fields : 2 * fields, side + HALF : side + 256] = jnp.zeros_like(low)
            rank = coeffs.shape[1]
            columns = basis[at((x * 4 + chunk) * rank, rank), :]
            total = total + lax.dot_general(image_parts[...], columns, NT, preferred_element_type=F32)
        return total

    total = lax.fori_loop(0, 4, step_two, jnp.zeros((2 * fields, coeffs.shape[1]), F32))
    coeffs[...] = total[:fields, :] + total[fields:, :]


def remainder(fields, image, basis, coeffs, out):
    rank = coeffs.shape[1]
    high, low = split(coeffs[...])
    parts = jnp.concatenate([high, low], axis=0)

    def body(group, carry):
        columns = basis[at(group * rank, rank), :]
        both = jnp.dot(parts, columns, preferred_element_type=F32)
        for step in range(8):
            cell = group * 8 + step
            side = step * 256
            along = both[:fields, side : side + HALF] + both[:fields, side + HALF : side + 256]
            along = along + both[fields:, side : side + HALF]
            out[pl.ds(cell, fields, stride=HALF), :] = image[at(cell * fields, fields), :] - along
        return carry

    lax.fori_loop(0, 16, body, 0)


def call(kernel, inputs, out_shape, scratch, flops, size, scalars=0):
    smem = pl.BlockSpec(memory_space=pltpu.SMEM)
    vmem = pl.BlockSpec(memory_space=pltpu.VMEM)
    return pl.pallas_call(
        kernel,
        out_shape=out_shape,
        in_specs=[smem] * scalars + [vmem] * (len(inputs) - scalars),
        out_specs=[vmem] * len(out_shape),
        scratch_shapes=scratch,
        cost_estimate=pl.CostEstimate(flops=flops, bytes_accessed=size, transcendentals=0),
        compiler_params=pltpu.CompilerParams(vmem_limit_bytes=44 * 2**20),
    )(*inputs)


def struct(*shape, dtype=F32):
    return jax.ShapeDtypeStruct(shape, dtype)


def shifted(array, axis, by):
    count = lax.axis_size(axis)
    pairs = [(i, i + by) for i in range(count) if 0 <= i + by < count]
    return lax.ppermute(array, axis, pairs)


def summed(array, axis):
    count = lax.axis_size(axis)
    if count & (count - 1):
        return lax.psum(array, axis)
    bit = 1
    while bit < count:
        array = array + lax.ppermute(array, axis, [(i, i ^ bit) for i in range(count)])
        bit *= 2
    return array


def local(
    probes,
    sources,
    kappa,
    prior,
    basis,
    entry_cell,
    entry_owner,
    entry_slot,
    entry_weight,
    entry_count,
    trace_weight,
):
    fields, rank = probes.shape[0], basis.shape[0]
    entries = entry_cell.shape[0]
    peers = lax.axis_size("space")
    padded = LAYERS * PADDED * fields
    cells = LAYERS * 32
    live = jnp.arange(entries, dtype=jnp.int32) < entry_count[0]
    weight = jnp.where(live, entry_weight, jnp.zeros_like(entry_weight))
    numbers = [array.astype(F32).reshape(-1, HALF) for array in (entry_cell, entry_owner, entry_slot)]
    own = jnp.concatenate([kappa.reshape(cells, HALF)] + numbers + [weight.reshape(-1, HALF)], axis=0)
    near = [shifted(own, "space", by) for by in (2, 1, -1, -2)]
    statics = [near[0], near[1], own, near[2], near[3]]
    matrix = jnp.asarray(band())
    sources = sources.reshape(3 * cells, HALF)

    turned, first, second, third = call(
        functools.partial(forward_own, fields),
        (probes.reshape(fields * cells, HALF), sources, kappa.reshape(cells, HALF), matrix),
        [struct(cells * fields, HALF), struct(padded, HALF), struct(padded, HALF), struct(cells * fields, HALF)],
        [pltpu.VMEM((32 * fields, HALF), F32)],
        600_000_000,
        6 * 2**20,
    )
    me = lax.axis_index("space").astype(jnp.int32).reshape(1)
    table, cell_hot, slot_hot = call(
        functools.partial(forward_window, fields, peers),
        (me, first, second, third, *statics, matrix, trace_weight.reshape(1, HALF)),
        [
            struct(peers * (fields + 1), HALF),
            struct(5 * 256, entries, dtype=BF16),
            struct(5 * HALF, entries, dtype=BF16),
        ],
        [
            pltpu.VMEM((padded, HALF), F32),
            pltpu.VMEM((padded, HALF), F32),
            pltpu.VMEM((32 * fields, HALF), F32),
            pltpu.VMEM((16 * fields, 256), F32),
            pltpu.VMEM((5 * fields, entries), F32),
            pltpu.VMEM((5 * fields, entries), jnp.int32),
            pltpu.VMEM((5 * fields, entries), jnp.int32),
            pltpu.VMEM((5 * fields, entries), F32),
        ],
        3_000_000_000,
        6 * 2**20,
        scalars=1,
    )
    table = summed(table, "space")
    (columns,) = call(
        basis_parts,
        (basis.reshape(rank * cells, HALF),),
        [struct(16 * rank, 2048, dtype=BF16)],
        [],
        10_000_000,
        8 * 2**20,
    )
    image, coeffs = call(
        functools.partial(adjoint, fields, peers),
        (table, *statics, cell_hot, slot_hot, turned, sources, prior.reshape(cells, HALF), matrix, columns),
        [struct(cells * fields, HALF), struct(fields, rank)],
        [
            pltpu.VMEM((5 * HALF, HALF), F32),
            pltpu.VMEM((5 * fields, entries), jnp.int32),
            pltpu.VMEM((5 * fields, entries), F32),
            pltpu.VMEM((5 * fields, entries), F32),
            pltpu.VMEM((16 * fields, 2 * entries), BF16),
            pltpu.VMEM((5 * padded, HALF), F32),
            pltpu.VMEM((5 * cells * fields, HALF), F32),
            pltpu.VMEM((3 * padded, HALF), F32),
            pltpu.VMEM((3 * cells * fields, HALF), F32),
            pltpu.VMEM((32 * fields, HALF), F32),
            pltpu.VMEM((2 * fields, 2048), BF16),
            pltpu.VMEM((peers * fields, HALF), F32),
        ],
        5_000_000_000,
        10 * 2**20,
    )
    coeffs = summed(coeffs, "space")
    (hess_probe,) = call(
        functools.partial(remainder, fields),
        (image, columns, coeffs),
        [struct(fields * cells, HALF)],
        [],
        200_000_000,
        6 * 2**20,
    )
    return hess_probe.reshape(probes.shape), coeffs.T


def solution(mesh):
    return jax.shard_map(
        local,
        mesh=mesh,
        in_specs=(
            P("group", "space", None, None),
            P(None, ("group", "space"), None, None),
            P(("group", "space"), None, None),
            P(("group", "space"), None, None),
            P("group", "space", None, None),
            P(("group", "space")),
            P(("group", "space")),
            P(("group", "space")),
            P(("group", "space")),
            P(("group", "space")),
            P(("group", "space")),
        ),
        out_specs=(P("group", "space", None, None), P("group", None)),
        check_vma=False,
    )
```

time: 346 us -> 87.4 us (0.25)
  other arithmetic: 81.2 us -> 2.16 us
  waiting for transfers between devices: 96.6 us -> 19.4 us
  blocking collectives: 71.9 us -> 0 us
  Pallas kernels: 0 us -> 34.7 us
  starting transfers between devices: 53.1 us -> 24.4 us
  between operations: 15.1 us -> 1.5 us
  matrix products: 13 us -> 0 us
  local copies, waits for them, and re-layouts: 14.4 us -> 4.8 us
    reduce_scatter x1 -> x0, waiting for transfers between devices: 81.2 us -> none  [local(): traces = lax.psum_scatter(table, 'space', scatter_dimension=1, tiled=True)]
    psum x1 -> x0, blocking collectives: 49.3 us -> none  [local(): coeffs = lax.psum(partial_coeffs, 'space')]
    add x3 -> x8, other arithmetic: 36.8 us -> 0.09 us  [summed(): array + lax.ppermute(array, axis, [(i, i ^ bit) for i in range(count)])]
    pallas_call x0 -> x5, Pallas kernels: none -> 34.7 us  [call(): pl.pallas_call(kernel, out_shape=out_shape, in_specs=[smem] * scalars + [...]
    ppermute x8 -> x12, starting transfers between devices: 53.1 us -> 24.4 us  [the longest x8 15.5 us: summed(): lax.ppermute(array, axis, [(i, i ^ bit) for i in range(count)])]
    all_gather x1 -> x0, blocking collectives: 22.6 us -> none  [local(): copies = lax.all_gather(weighted, 'space', axis=1, tiled=True)]
    concatenate x4 -> x0, other arithmetic: 19 us -> none  [extended_2(): array = jnp.concatenate([before, array, after], axis=dim)]
    scatter-add x2 -> x0, other arithmetic: 14.2 us -> none  [the longest x1 7.9 us: local(): jnp.zeros_like(flat).at[:, entry_cell].add(injected).reshape(third.shape)]
  transfers between devices with their start and end apart: 9 -> 12, of which waited for: 8 -> 8; matrix products, arithmetic and copies ran while one was open for 0% -> 0% of each run, Pallas kernels for 0% -> 8%
where the time goes in v1:
time: 87.4 us; the launch traced here: 87 us
  Pallas kernels  34.7 us (40%)
  starting transfers between devices  24.4 us (28%)
  waiting for transfers between devices  19.4 us (22%)
  local copies, waits for them, and re-layouts  4.8 us (5%)
  other arithmetic  2.16 us (2%)
  between operations  1.5 us (2%)
    pallas_call x5, Pallas kernels, call(): pl.pallas_call(kernel, out_shape=out_shape, in_specs=[smem] * scalars + [...  34.7 us
    ppermute x8, waiting for transfers between devices, summed(): lax.ppermute(array, axis, [(i, i ^ bit) for i in range(count)])  19.4 us
    ppermute x8, starting transfers between devices, summed(): lax.ppermute(array, axis, [(i, i ^ bit) for i in range(count)])  15.5 us
    ppermute x4, starting transfers between devices, shifted(): return lax.ppermute(array, axis, pairs)  8.91 us
    unnamed x20, local copies, waits for them, and re-layouts  3.92 us
  transfers between devices with their start and end apart: 12, of which 8 were waited for; matrix products, arithmetic and copies ran while one was open for 0% of the time, Pallas kernels for 8%

profile of v1, /device:TPU:0, one launch (start us, length us, event | category | flops | bytes accessed | tf_op | source)
XLA Modules:
  0.0 87.0 jit_solution(3592012488608921767)
XLA Ops:
  4.3 4.9 %collective-permute-start = (f32[144,128]{1,0:T(8,128)S(1)}, f32[144,128]{1,0:T(8,128)S(1)}, u32[]{:S(2)}, u32[]{:S(2)}) collective-permute-start(f32[144,128]{1,0:T(8,128)S(1)} %concatenate.3.kappa.statics), channel_id=1, source_target_pairs={{0,2},{1,3},{2,4},{3,5},{4,6},{5,7},{6,8},{7,9},{8,10},{9,11},{10,... | collective-permute-start | bytes 221192 | tf_op jit(solution)/shard_map/ppermute | solution.py:411
  9.2 1.5 %collective-permute-start.1 = (f32[144,128]{1,0:T(8,128)S(1)}, f32[144,128]{1,0:T(8,128)S(1)}, u32[]{:S(2)}, u32[]{:S(2)}) collective-permute-start(f32[144,128]{1,0:T(8,128)S(1)} %concatenate.3.kappa.statics), channel_id=1, source_target_pairs={{0,1},{1,2},{2,3},{3,4},{4,5},{5,6},{6,7},{7,8},{8,9},{9,10},{10,1... | collective-permute-start | bytes 221192 | tf_op jit(solution)/shard_map/ppermute | solution.py:411
  10.6 1.3 %collective-permute-start.2 = (f32[144,128]{1,0:T(8,128)S(1)}, f32[144,128]{1,0:T(8,128)S(1)}, u32[]{:S(2)}, u32[]{:S(2)}) collective-permute-start(f32[144,128]{1,0:T(8,128)S(1)} %concatenate.3.kappa.statics), channel_id=1, source_target_pairs={{1,0},{2,1},{3,2},{4,3},{5,4},{6,5},{7,6},{8,7},{9,8},{10,9},{11,1... | collective-permute-start | bytes 221192 | tf_op jit(solution)/shard_map/ppermute | solution.py:411
  11.9 1.3 %collective-permute-start.3 = (f32[144,128]{1,0:T(8,128)S(1)}, f32[144,128]{1,0:T(8,128)S(1)}, u32[]{:S(2)}, u32[]{:S(2)}) collective-permute-start(f32[144,128]{1,0:T(8,128)S(1)} %concatenate.3.kappa.statics), channel_id=1, source_target_pairs={{2,0},{3,1},{4,2},{5,3},{6,4},{7,5},{8,6},{9,7},{10,8},{11,9},{12,... | collective-permute-start | bytes 221192 | tf_op jit(solution)/shard_map/ppermute | solution.py:411
  14.1 1.2 %copy-done.3 = f32[16,4,32,128]{3,2,1,0:T(8,128)S(1)} copy-done((f32[16,4,32,128]{3,2,1,0:T(8,128)S(1)}, f32[16,4,32,128]{3,2,1,0:T(8,128)}, u32[]{:S(2)}) %copy-start.3) | copy-done | bytes 1048600
  17.1 3.6 %shard_map.131 = (f32[2048,128]{1,0:T(8,128)S(1)}, f32[2560,128]{1,0:T(8,128)S(1)}, f32[2560,128]{1,0:T(8,128)S(1)}, f32[2048,128]{1,0:T(8,128)S(1)}) custom-call(f32[2048,128]{1,0:T(8,128)S(1)} %bitcast.23, f32[384,128]{1,0:T(8,128)S(1)} %bitcast.24, f32[128,128]{1,0:T(8,128)S(1)} %bitcast.21, bf16[256,256]{1,0:T(8,128)(2,1)S(1)} %copy-done.8), custom_call_target="tpu_custom_call" | custom-call | flops 600000000 | bytes 6291456 | tf_op jit(solution)/shard_map/pallas_call | solution.py:393
  20.8 8.0 %shard_map.132 = (f32[272,128]{1,0:T(8,128)S(1)}, bf16[1280,512]{1,0:T(8,128)(2,1)S(1)}, bf16[640,512]{1,0:T(8,128)(2,1)S(1)}) custom-call(s32[1]{0:T(128)} %bitcast.me, f32[2560,128]{1,0:T(8,128)S(1)} %get-tuple-element.11.first, f32[2560,128]{1,0:T(8,128)S(1)} %get-tuple-element.12.second, f32[2048,128]{1,0:T(8,128)S(1)} %get-tuple-element.13.third, ...), custom_call_target="tpu_custom_call" | custom-call | flops 3000000000 | bytes 6291456 | tf_op jit(solution)/shard_map/pallas_call | solution.py:393
  28.8 2.8 %collective-permute-start.4 = (f32[272,128]{1,0:T(8,128)S(1)}, f32[272,128]{1,0:T(8,128)S(1)}, u32[]{:S(2)}, u32[]{:S(2)}) collective-permute-start(f32[272,128]{1,0:T(8,128)S(1)} %get-tuple-element.14), channel_id=1, source_target_pairs={{0,1},{1,0},{2,3},{3,2},{4,5},{5,4},{6,7},{7,6},{8,9},{9,8},{10,11... | collective-permute-start | bytes 417800 | tf_op jit(solution)/shard_map/ppermute | solution.py:420
  31.6 1.0 %collective-permute-done.4 = f32[272,128]{1,0:T(8,128)S(1)} collective-permute-done((f32[272,128]{1,0:T(8,128)S(1)}, f32[272,128]{1,0:T(8,128)S(1)}, u32[]{:S(2)}, u32[]{:S(2)}) %collective-permute-start.4) | collective-permute-done | bytes 139296 | tf_op jit(solution)/shard_map/ppermute | solution.py:420
  32.6 2.7 %collective-permute-start.5 = (f32[272,128]{1,0:T(8,128)S(1)}, f32[272,128]{1,0:T(8,128)S(1)}, u32[]{:S(2)}, u32[]{:S(2)}) collective-permute-start(f32[272,128]{1,0:T(8,128)S(1)} %add.24), channel_id=1, source_target_pairs={{0,2},{1,3},{2,0},{3,1},{4,6},{5,7},{6,4},{7,5},{8,10},{9,11},{10,... | collective-permute-start | bytes 417800 | tf_op jit(solution)/shard_map/ppermute | solution.py:420
  35.3 4.0 %collective-permute-done.5 = f32[272,128]{1,0:T(8,128)S(1)} collective-permute-done((f32[272,128]{1,0:T(8,128)S(1)}, f32[272,128]{1,0:T(8,128)S(1)}, u32[]{:S(2)}, u32[]{:S(2)}) %collective-permute-start.5) | collective-permute-done | bytes 139296 | tf_op jit(solution)/shard_map/ppermute | solution.py:420
  39.3 3.3 %collective-permute-start.6 = (f32[272,128]{1,0:T(8,128)S(1)}, f32[272,128]{1,0:T(8,128)S(1)}, u32[]{:S(2)}, u32[]{:S(2)}) collective-permute-start(f32[272,128]{1,0:T(8,128)S(1)} %add.25), channel_id=1, source_target_pairs={{0,4},{1,5},{2,6},{3,7},{4,0},{5,1},{6,2},{7,3},{8,12},{9,13},{10,... | collective-permute-start | bytes 417800 | tf_op jit(solution)/shard_map/ppermute | solution.py:420
  42.6 3.2 %collective-permute-done.6 = f32[272,128]{1,0:T(8,128)S(1)} collective-permute-done((f32[272,128]{1,0:T(8,128)S(1)}, f32[272,128]{1,0:T(8,128)S(1)}, u32[]{:S(2)}, u32[]{:S(2)}) %collective-permute-start.6) | collective-permute-done | bytes 139296 | tf_op jit(solution)/shard_map/ppermute | solution.py:420
  45.7 3.0 %collective-permute-start.7 = (f32[272,128]{1,0:T(8,128)S(1)}, f32[272,128]{1,0:T(8,128)S(1)}, u32[]{:S(2)}, u32[]{:S(2)}) collective-permute-start(f32[272,128]{1,0:T(8,128)S(1)} %add.26), channel_id=1, source_target_pairs={{0,8},{1,9},{2,10},{3,11},{4,12},{5,13},{6,14},{7,15},{8,0},{9,1},... | collective-permute-start | bytes 417800 | tf_op jit(solution)/shard_map/ppermute | solution.py:420
  48.7 3.2 %shard_map.133.basis = bf16[1024,2048]{1,0:T(8,128)(2,1)S(1)} custom-call(f32[8192,128]{1,0:T(8,128)S(1)} %bitcast.19), custom_call_target="tpu_custom_call" | custom-call | flops 10000000 | bytes 8388608 | tf_op jit(solution)/shard_map/pallas_call | solution.py:393
  51.9 2.0 %collective-permute-done.7 = f32[272,128]{1,0:T(8,128)S(1)} collective-permute-done((f32[272,128]{1,0:T(8,128)S(1)}, f32[272,128]{1,0:T(8,128)S(1)}, u32[]{:S(2)}, u32[]{:S(2)}) %collective-permute-start.7) | collective-permute-done | bytes 139296 | tf_op jit(solution)/shard_map/ppermute | solution.py:420
  54.0 15.8 %shard_map.134 = (f32[2048,128]{1,0:T(8,128)S(1)}, f32[16,64]{1,0:T(8,128)S(1)}) custom-call(f32[272,128]{1,0:T(8,128)S(1)} %add.27.table, f32[144,128]{1,0:T(8,128)S(1)} %collective-permute-done.kappa_mm.statics_mm, f32[144,128]{1,0:T(8,128)S(1)} %collective-permute-done.1.kappa_m.statics_m, f32[144,128]{1,0:T(8,128)S(1)} %concatenate.3.kappa.statics, ...), custom_call_target="tpu_custom_call" | custom-call | flops 5000000000 | bytes 10485760 | tf_op jit(solution)/shard_map/pallas_call | solution.py:393
  69.8 1.2 %collective-permute-done.8 = f32[16,64]{1,0:T(8,128)S(1)} collective-permute-done((f32[16,64]{1,0:T(8,128)S(1)}, f32[16,64]{1,0:T(8,128)S(1)}, u32[]{:S(2)}, u32[]{:S(2)}) %collective-permute-start.8) | collective-permute-done | bytes 4128 | tf_op jit(solution)/shard_map/ppermute | solution.py:420
  71.0 1.5 %collective-permute-start.9 = (f32[16,64]{1,0:T(8,128)S(1)}, f32[16,64]{1,0:T(8,128)S(1)}, u32[]{:S(2)}, u32[]{:S(2)}) collective-permute-start(f32[16,64]{1,0:T(8,128)S(1)} %add.28), channel_id=1, source_target_pairs={{0,2},{1,3},{2,0},{3,1},{4,6},{5,7},{6,4},{7,5},{8,10},{9,11},{10,... | collective-permute-start | bytes 12296 | tf_op jit(solution)/shard_map/ppermute | solution.py:420
  72.5 2.1 %collective-permute-done.9 = f32[16,64]{1,0:T(8,128)S(1)} collective-permute-done((f32[16,64]{1,0:T(8,128)S(1)}, f32[16,64]{1,0:T(8,128)S(1)}, u32[]{:S(2)}, u32[]{:S(2)}) %collective-permute-start.9) | collective-permute-done | bytes 4128 | tf_op jit(solution)/shard_map/ppermute | solution.py:420
  75.1 3.2 %collective-permute-done.10 = f32[16,64]{1,0:T(8,128)S(1)} collective-permute-done((f32[16,64]{1,0:T(8,128)S(1)}, f32[16,64]{1,0:T(8,128)S(1)}, u32[]{:S(2)}, u32[]{:S(2)}) %collective-permute-start.10) | collective-permute-done | bytes 4128 | tf_op jit(solution)/shard_map/ppermute | solution.py:420
  78.4 1.9 %collective-permute-start.11 = (f32[16,64]{1,0:T(8,128)S(1)}, f32[16,64]{1,0:T(8,128)S(1)}, u32[]{:S(2)}, u32[]{:S(2)}) collective-permute-start(f32[16,64]{1,0:T(8,128)S(1)} %add.30), channel_id=1, source_target_pairs={{0,8},{1,9},{2,10},{3,11},{4,12},{5,13},{6,14},{7,15},{8,0},{9,1},... | collective-permute-start | bytes 12296 | tf_op jit(solution)/shard_map/ppermute | solution.py:420
  80.2 2.7 %collective-permute-done.11 = f32[16,64]{1,0:T(8,128)S(1)} collective-permute-done((f32[16,64]{1,0:T(8,128)S(1)}, f32[16,64]{1,0:T(8,128)S(1)}, u32[]{:S(2)}, u32[]{:S(2)}) %collective-permute-start.11) | collective-permute-done | bytes 4128 | tf_op jit(solution)/shard_map/ppermute | solution.py:420
  82.9 4.0 %shard_map.135 = f32[2048,128]{1,0:T(8,128)} custom-call(f32[2048,128]{1,0:T(8,128)S(1)} %get-tuple-element.18.image, bf16[1024,2048]{1,0:T(8,128)(2,1)S(1)} %shard_map.133.basis, f32[16,64]{1,0:T(8,128)S(1)} %add.31.coeffs), custom_call_target="tpu_custom_call" | custom-call | flops 200000000 | bytes 6291456 | tf_op jit(solution)/shard_map/pallas_call | solution.py:393
  (37 shorter events, 6.2 us)
Async XLA Ops:
  0.6 20.2 %copy-start.9 = (bf16[256,256]{1,0:T(8,128)(2,1)S(1)}, bf16[256,256]{1,0:T(8,128)(2,1)}, u32[]{:S(2)}) copy-start(bf16[256,256]{1,0:T(8,128)(2,1)} %constant.8.clone.band_ref) | copy-start | bytes 393220
  0.6 20.2 %copy-start.7 = (f32[128]{0:T(128)S(1)}, f32[128]{0:T(128)}, u32[]{:S(2)}) copy-start(f32[128]{0:T(128)} %param.22) | copy-start | bytes 1540
  4.3 16.5 %collective-permute-start = (f32[144,128]{1,0:T(8,128)S(1)}, f32[144,128]{1,0:T(8,128)S(1)}, u32[]{:S(2)}, u32[]{:S(2)}) collective-permute-start(f32[144,128]{1,0:T(8,128)S(1)} %concatenate.3.kappa.statics), channel_id=1, source_target_pairs={{0,2},{1,3},{2,4},{3,5},{4,6},{5,7},{6,8},{7,9},{8,10},{9,11},{10,... | collective-permute-start | bytes 221192 | tf_op jit(solution)/shard_map/ppermute | solution.py:411
  9.2 11.6 %collective-permute-start.1 = (f32[144,128]{1,0:T(8,128)S(1)}, f32[144,128]{1,0:T(8,128)S(1)}, u32[]{:S(2)}, u32[]{:S(2)}) collective-permute-start(f32[144,128]{1,0:T(8,128)S(1)} %concatenate.3.kappa.statics), channel_id=1, source_target_pairs={{0,1},{1,2},{2,3},{3,4},{4,5},{5,6},{6,7},{7,8},{8,9},{9,10},{10,1... | collective-permute-start | bytes 221192 | tf_op jit(solution)/shard_map/ppermute | solution.py:411
  10.6 10.2 %collective-permute-start.2 = (f32[144,128]{1,0:T(8,128)S(1)}, f32[144,128]{1,0:T(8,128)S(1)}, u32[]{:S(2)}, u32[]{:S(2)}) collective-permute-start(f32[144,128]{1,0:T(8,128)S(1)} %concatenate.3.kappa.statics), channel_id=1, source_target_pairs={{1,0},{2,1},{3,2},{4,3},{5,4},{6,5},{7,6},{8,7},{9,8},{10,9},{11,1... | collective-permute-start | bytes 221192 | tf_op jit(solution)/shard_map/ppermute | solution.py:411
  11.9 8.9 %collective-permute-start.3 = (f32[144,128]{1,0:T(8,128)S(1)}, f32[144,128]{1,0:T(8,128)S(1)}, u32[]{:S(2)}, u32[]{:S(2)}) collective-permute-start(f32[144,128]{1,0:T(8,128)S(1)} %concatenate.3.kappa.statics), channel_id=1, source_target_pairs={{2,0},{3,1},{4,2},{5,3},{6,4},{7,5},{8,6},{9,7},{10,8},{11,9},{12,... | collective-permute-start | bytes 221192 | tf_op jit(solution)/shard_map/ppermute | solution.py:411
  13.2 0.8 copy-start.1
  14.1 1.2 %copy-start.3 = (f32[16,4,32,128]{3,2,1,0:T(8,128)S(1)}, f32[16,4,32,128]{3,2,1,0:T(8,128)}, u32[]{:S(2)}) copy-start(f32[16,4,32,128]{3,2,1,0:T(8,128)} %param.12) | copy-start | bytes 3145732
  15.3 0.9 %copy-start.4 = (f32[3,4,32,128]{3,2,1,0:T(8,128)S(1)}, f32[3,4,32,128]{3,2,1,0:T(8,128)}, u32[]{:S(2)}) copy-start(f32[3,4,32,128]{3,2,1,0:T(8,128)} %param.13) | copy-start | bytes 589828
  16.2 0.9 %copy-start.8 = (bf16[256,256]{1,0:T(8,128)(2,1)S(1)}, bf16[256,256]{1,0:T(8,128)(2,1)}, u32[]{:S(2)}) copy-start(bf16[256,256]{1,0:T(8,128)(2,1)} %constant.8.clone.band_ref) | copy-start | bytes 393220
  20.8 27.9 %copy-start = (f32[64,4,32,128]{3,2,1,0:T(8,128)S(1)}, f32[64,4,32,128]{3,2,1,0:T(8,128)}, u32[]{:S(2)}) copy-start(f32[64,4,32,128]{3,2,1,0:T(8,128)} %param.16) | copy-start | bytes 12582916
  28.8 3.8 %collective-permute-start.4 = (f32[272,128]{1,0:T(8,128)S(1)}, f32[272,128]{1,0:T(8,128)S(1)}, u32[]{:S(2)}, u32[]{:S(2)}) collective-permute-start(f32[272,128]{1,0:T(8,128)S(1)} %get-tuple-element.14), channel_id=1, source_target_pairs={{0,1},{1,0},{2,3},{3,2},{4,5},{5,4},{6,7},{7,6},{8,9},{9,8},{10,11... | collective-permute-start | bytes 417800 | tf_op jit(solution)/shard_map/ppermute | solution.py:420
  32.6 6.7 %collective-permute-start.5 = (f32[272,128]{1,0:T(8,128)S(1)}, f32[272,128]{1,0:T(8,128)S(1)}, u32[]{:S(2)}, u32[]{:S(2)}) collective-permute-start(f32[272,128]{1,0:T(8,128)S(1)} %add.24), channel_id=1, source_target_pairs={{0,2},{1,3},{2,0},{3,1},{4,6},{5,7},{6,4},{7,5},{8,10},{9,11},{10,... | collective-permute-start | bytes 417800 | tf_op jit(solution)/shard_map/ppermute | solution.py:420
  39.3 6.4 %collective-permute-start.6 = (f32[272,128]{1,0:T(8,128)S(1)}, f32[272,128]{1,0:T(8,128)S(1)}, u32[]{:S(2)}, u32[]{:S(2)}) collective-permute-start(f32[272,128]{1,0:T(8,128)S(1)} %add.25), channel_id=1, source_target_pairs={{0,4},{1,5},{2,6},{3,7},{4,0},{5,1},{6,2},{7,3},{8,12},{9,13},{10,... | collective-permute-start | bytes 417800 | tf_op jit(solution)/shard_map/ppermute | solution.py:420
  45.7 8.2 %collective-permute-start.7 = (f32[272,128]{1,0:T(8,128)S(1)}, f32[272,128]{1,0:T(8,128)S(1)}, u32[]{:S(2)}, u32[]{:S(2)}) collective-permute-start(f32[272,128]{1,0:T(8,128)S(1)} %add.26), channel_id=1, source_target_pairs={{0,8},{1,9},{2,10},{3,11},{4,12},{5,13},{6,14},{7,15},{8,0},{9,1},... | collective-permute-start | bytes 417800 | tf_op jit(solution)/shard_map/ppermute | solution.py:420
  48.7 5.3 %copy-start.5 = (f32[3,4,32,128]{3,2,1,0:T(8,128)S(1)}, f32[3,4,32,128]{3,2,1,0:T(8,128)}, u32[]{:S(2)}) copy-start(f32[3,4,32,128]{3,2,1,0:T(8,128)} %param.13) | copy-start | bytes 589828
  48.7 5.3 %copy-start.6 = (f32[4,32,128]{2,1,0:T(8,128)S(1)}, f32[4,32,128]{2,1,0:T(8,128)}, u32[]{:S(2)}) copy-start(f32[4,32,128]{2,1,0:T(8,128)} %param.15) | copy-start | bytes 196612
  69.8 1.2 %collective-permute-start.8 = (f32[16,64]{1,0:T(8,128)S(1)}, f32[16,64]{1,0:T(8,128)S(1)}, u32[]{:S(2)}, u32[]{:S(2)}) collective-permute-start(f32[16,64]{1,0:T(8,128)S(1)} %get-tuple-element.19), channel_id=1, source_target_pairs={{0,1},{1,0},{2,3},{3,2},{4,5},{5,4},{6,7},{7,6},{8,9},{9,8},{10,11... | collective-permute-start | bytes 12296 | tf_op jit(solution)/shard_map/ppermute | solution.py:420
  71.0 3.7 %collective-permute-start.9 = (f32[16,64]{1,0:T(8,128)S(1)}, f32[16,64]{1,0:T(8,128)S(1)}, u32[]{:S(2)}, u32[]{:S(2)}) collective-permute-start(f32[16,64]{1,0:T(8,128)S(1)} %add.28), channel_id=1, source_target_pairs={{0,2},{1,3},{2,0},{3,1},{4,6},{5,7},{6,4},{7,5},{8,10},{9,11},{10,... | collective-permute-start | bytes 12296 | tf_op jit(solution)/shard_map/ppermute | solution.py:420
  74.7 3.7 %collective-permute-start.10 = (f32[16,64]{1,0:T(8,128)S(1)}, f32[16,64]{1,0:T(8,128)S(1)}, u32[]{:S(2)}, u32[]{:S(2)}) collective-permute-start(f32[16,64]{1,0:T(8,128)S(1)} %add.29), channel_id=1, source_target_pairs={{0,4},{1,5},{2,6},{3,7},{4,0},{5,1},{6,2},{7,3},{8,12},{9,13},{10,... | collective-permute-start | bytes 12296 | tf_op jit(solution)/shard_map/ppermute | solution.py:420
  78.4 4.5 %collective-permute-start.11 = (f32[16,64]{1,0:T(8,128)S(1)}, f32[16,64]{1,0:T(8,128)S(1)}, u32[]{:S(2)}, u32[]{:S(2)}) collective-permute-start(f32[16,64]{1,0:T(8,128)S(1)} %add.30), channel_id=1, source_target_pairs={{0,8},{1,9},{2,10},{3,11},{4,12},{5,13},{6,14},{7,15},{8,0},{9,1},... | collective-permute-start | bytes 12296 | tf_op jit(solution)/shard_map/ppermute | solution.py:420
  82.9 4.1 %copy-start.2 = (f32[16,64]{1,0:T(8,128)}, f32[16,64]{1,0:T(8,128)S(1)}, u32[]{:S(2)}) copy-start(f32[16,64]{1,0:T(8,128)S(1)} %add.31.coeffs) | copy-start | bytes 12292

commit v2 on v1

--- a/solution.py
+++ b/solution.py
@@ -151,7 +151,7 @@
 
 
 def forward_window(
-    fields, peers, me, first, second, third, kappa_mm, kappa_m, kappa, kappa_p, kappa_pp, band_ref, own_scale,
+    fields, peers, first, second, third, kappa_mm, kappa_m, kappa, kappa_p, kappa_pp, band_ref,
     table, cell_ref, slot_ref, below, above, z_term, sample, total_ref, line_ref, owner_ref, weight_ref,
 ):
     statics = (kappa_mm, kappa_m, kappa, kappa_p, kappa_pp)
@@ -238,9 +238,6 @@
                     jnp.concatenate(pieces, axis=0), hot, NT, preferred_element_type=F32
                 )
         table[group * 16 * fields : (group + 1) * 16 * fields, :] = result
-    place = lax.broadcasted_iota(jnp.int32, (peers, HALF), 0)
-    own = jnp.broadcast_to(own_scale[...], (peers, HALF))
-    table[peers * fields : peers * fields + peers, :] = jnp.where(place == me[0], own, 0.0)
 
 
 def basis_parts(basis, out):
@@ -260,15 +257,13 @@
 def adjoint(
     fields, peers, table, statics_mm, statics_m, statics, statics_p, statics_pp, cell_ref, slot_ref, turned, sources,
     prior, band_ref, basis, image, coeffs, speed_ref, line_ref, high_ref, low_ref, left, inner_two, outer_two,
-    inner_one, outer_one, z_term, image_parts, scaled,
+    inner_one, outer_one, z_term, image_parts,
 ):
+    rank = basis.shape[0] // 16
     tiles = (statics_mm, statics_m, statics, statics_p, statics_pp)
     entries = line_ref.shape[1]
     clear_margins(inner_two, 5 * LAYERS, fields)
     clear_margins(inner_one, 3 * LAYERS, fields)
-    for owner in range(peers):
-        rows = slice(owner * fields, (owner + 1) * fields)
-        scaled[rows, :] = table[rows, :] * table[peers * fields + owner : peers * fields + owner + 1, :]
     for tile, ref in enumerate(tiles):
         speed_ref[tile * HALF : (tile + 1) * HALF, :] = ref[0:HALF, :]
         rows = slice(tile * fields, (tile + 1) * fields)
@@ -278,7 +273,7 @@
         hot = slot_ref[tile * HALF : (tile + 1) * HALF, :]
         total = jnp.zeros((fields, entries), F32)
         for group in range(peers // 16):
-            high, low = split(scaled[group * 16 * fields : (group + 1) * 16 * fields, :])
+            high, low = split(table[group * 16 * fields : (group + 1) * 16 * fields, :])
             read = jnp.dot(high, hot, preferred_element_type=F32) + jnp.dot(low, hot, preferred_element_type=F32)
             for i in range(16):
                 total = total + jnp.where(owner == group * 16 + i, read[i * fields : (i + 1) * fields, :], 0.0)
@@ -359,18 +354,33 @@
                 image_parts[0:fields, side + HALF : side + 256] = high
                 image_parts[fields : 2 * fields, side : side + HALF] = low
                 image_parts[fields : 2 * fields, side + HALF : side + 256] = jnp.zeros_like(low)
-            rank = coeffs.shape[1]
             columns = basis[at((x * 4 + chunk) * rank, rank), :]
             total = total + lax.dot_general(image_parts[...], columns, NT, preferred_element_type=F32)
         return total
 
-    total = lax.fori_loop(0, 4, step_two, jnp.zeros((2 * fields, coeffs.shape[1]), F32))
-    coeffs[...] = total[:fields, :] + total[fields:, :]
-
-
-def remainder(fields, image, basis, coeffs, out):
+    total = lax.fori_loop(0, 4, step_two, jnp.zeros((2 * fields, rank), F32))
+    part = total[:fields, :] + total[fields:, :]
+    part = jnp.concatenate([part, jnp.zeros((fields, coeffs.shape[1] - rank), F32)], axis=1)
+    for peer in range(peers):
+        coeffs[peer * fields : (peer + 1) * fields, :] = part
+
+
+def weigh(fields, peers, arrived, scale, out):
+    total = arrived[0:fields, :]
+    for peer in range(1, peers):
+        total = total + arrived[peer * fields : (peer + 1) * fields, :]
+    total = total * scale[...]
+    for peer in range(peers):
+        out[peer * fields : (peer + 1) * fields, :] = total
+
+
+def remainder(fields, peers, image, basis, arrived, out, coeffs):
     rank = coeffs.shape[1]
-    high, low = split(coeffs[...])
+    total = arrived[0:fields, :rank]
+    for peer in range(1, peers):
+        total = total + arrived[peer * fields : (peer + 1) * fields, :rank]
+    coeffs[...] = total
+    high, low = split(total)
     parts = jnp.concatenate([high, low], axis=0)
 
     def body(group, carry):
@@ -411,15 +421,8 @@
     return lax.ppermute(array, axis, pairs)
 
 
-def summed(array, axis):
-    count = lax.axis_size(axis)
-    if count & (count - 1):
-        return lax.psum(array, axis)
-    bit = 1
-    while bit < count:
-        array = array + lax.ppermute(array, axis, [(i, i ^ bit) for i in range(count)])
-        bit *= 2
-    return array
+def exchanged(array, axis):
+    return lax.all_to_all(array, axis, split_axis=0, concat_axis=0, tiled=True)
 
 
 def local(
@@ -457,12 +460,11 @@
         600_000_000,
         6 * 2**20,
     )
-    me = lax.axis_index("space").astype(jnp.int32).reshape(1)
     table, cell_hot, slot_hot = call(
         functools.partial(forward_window, fields, peers),
-        (me, first, second, third, *statics, matrix, trace_weight.reshape(1, HALF)),
+        (first, second, third, *statics, matrix),
         [
-            struct(peers * (fields + 1), HALF),
+            struct(peers * fields, HALF),
             struct(5 * 256, entries, dtype=BF16),
             struct(5 * HALF, entries, dtype=BF16),
         ],
@@ -478,9 +480,17 @@
         ],
         3_000_000_000,
         6 * 2**20,
-        scalars=1,
-    )
-    table = summed(table, "space")
+    )
+    arrived = exchanged(table, "space")
+    (weighted,) = call(
+        functools.partial(weigh, fields, peers),
+        (arrived, trace_weight.reshape(1, HALF)),
+        [struct(peers * fields, HALF)],
+        [],
+        1_000_000,
+        2**18,
+    )
+    table = exchanged(weighted, "space")
     (columns,) = call(
         basis_parts,
         (basis.reshape(rank * cells, HALF),),
@@ -492,7 +502,7 @@
     image, coeffs = call(
         functools.partial(adjoint, fields, peers),
         (table, *statics, cell_hot, slot_hot, turned, sources, prior.reshape(cells, HALF), matrix, columns),
-        [struct(cells * fields, HALF), struct(fields, rank)],
+        [struct(cells * fields, HALF), struct(peers * fields, -(-rank // HALF) * HALF)],
         [
             pltpu.VMEM((5 * HALF, HALF), F32),
             pltpu.VMEM((5 * fields, entries), jnp.int32),
@@ -505,16 +515,15 @@
             pltpu.VMEM((3 * cells * fields, HALF), F32),
             pltpu.VMEM((32 * fields, HALF), F32),
             pltpu.VMEM((2 * fields, 2048), BF16),
-            pltpu.VMEM((peers * fields, HALF), F32),
         ],
         5_000_000_000,
         10 * 2**20,
     )
-    coeffs = summed(coeffs, "space")
-    (hess_probe,) = call(
-        functools.partial(remainder, fields),
-        (image, columns, coeffs),
-        [struct(fields * cells, HALF)],
+    arrived = exchanged(coeffs, "space")
+    hess_probe, coeffs = call(
+        functools.partial(remainder, fields, peers),
+        (image, columns, arrived),
+        [struct(fields * cells, HALF), struct(fields, rank)],
         [],
         200_000_000,
         6 * 2**20,

time: 87.4 us -> 97.2 us (1.11)
  blocking collectives: 0 us -> 31.6 us
  waiting for transfers between devices: 19.4 us -> 0.58 us
  starting transfers between devices: 24.4 us -> 12.4 us
  local copies, waits for them, and re-layouts: 4.8 us -> 13 us
    all_to_all x0 -> x2, blocking collectives: none -> 31.6 us  [exchanged(): return lax.all_to_all(array, axis, split_axis=0, concat_axis=0, tiled=True)]
    ppermute x8 -> x0, waiting for transfers between devices: 19.4 us -> none  [summed(): lax.ppermute(array, axis, [(i, i ^ bit) for i in range(count)])]
    ppermute x8 -> x0, starting transfers between devices: 15.5 us -> none  [summed(): lax.ppermute(array, axis, [(i, i ^ bit) for i in range(count)])]
    unnamed x20 -> x28, local copies, waits for them, and re-layouts: 3.92 us -> 12.1 us
    all_to_all x0 -> x1, starting transfers between devices: none -> 3.51 us  [exchanged(): return lax.all_to_all(array, axis, split_axis=0, concat_axis=0, tiled=True)]
    pallas_call x5 -> x6, Pallas kernels: 34.7 us -> 35.3 us  [call(): pl.pallas_call(kernel, out_shape=out_shape, in_specs=[smem] * scalars + [...]
  transfers between devices with their start and end apart: 12 -> 5, of which waited for: 8 -> 1; matrix products, arithmetic and copies ran while one was open for 0% -> 0% of each run, Pallas kernels for 8% -> 7%
where the time goes in v2:
time: 97.2 us; the launch traced here: 96.5 us
  Pallas kernels  35.3 us (36%)
  blocking collectives  31.6 us (33%)
  local copies, waits for them, and re-layouts  13 us (13%)
  starting transfers between devices  12.4 us (13%)
  other arithmetic  2.07 us (2%)
  between operations  1.48 us (2%)
    pallas_call x6, Pallas kernels, call(): pl.pallas_call(kernel, out_shape=out_shape, in_specs=[smem] * scalars + [...  35.3 us
    all_to_all x2, blocking collectives, exchanged(): return lax.all_to_all(array, axis, split_axis=0, concat_axis=0, tiled=True)  31.6 us
    unnamed x28, local copies, waits for them, and re-layouts  12.1 us
    ppermute x4, starting transfers between devices, shifted(): return lax.ppermute(array, axis, pairs)  8.91 us
    all_to_all x1, starting transfers between devices, exchanged(): return lax.all_to_all(array, axis, split_axis=0, concat_axis=0, tiled=True)  3.51 us
  transfers between devices with their start and end apart: 5, of which 1 were waited for; matrix products, arithmetic and copies ran while one was open for 0% of the time, Pallas kernels for 7%

profile of v2, /device:TPU:0, one launch (start us, length us, event | category | flops | bytes accessed | tf_op | source)
XLA Modules:
  0.0 96.5 jit_solution(5464011174830892551)
XLA Ops:
  1.3 0.7 convert_bitcast_fusion.2
  2.0 0.7 convert_bitcast_fusion
  3.4 0.9 concatenate.3.kappa.statics
  4.3 4.9 %collective-permute-start = (f32[144,128]{1,0:T(8,128)S(1)}, f32[144,128]{1,0:T(8,128)S(1)}, u32[]{:S(2)}, u32[]{:S(2)}) collective-permute-start(f32[144,128]{1,0:T(8,128)S(1)} %concatenate.3.kappa.statics), channel_id=1, source_target_pairs={{0,2},{1,3},{2,4},{3,5},{4,6},{5,7},{6,8},{7,9},{8,10},{9,11},{10,... | collective-permute-start | bytes 221192 | tf_op jit(solution)/shard_map/ppermute | solution.py:421
  9.1 1.5 %collective-permute-start.1 = (f32[144,128]{1,0:T(8,128)S(1)}, f32[144,128]{1,0:T(8,128)S(1)}, u32[]{:S(2)}, u32[]{:S(2)}) collective-permute-start(f32[144,128]{1,0:T(8,128)S(1)} %concatenate.3.kappa.statics), channel_id=1, source_target_pairs={{0,1},{1,2},{2,3},{3,4},{4,5},{5,6},{6,7},{7,8},{8,9},{9,10},{10,1... | collective-permute-start | bytes 221192 | tf_op jit(solution)/shard_map/ppermute | solution.py:421
  10.6 1.3 %collective-permute-start.2 = (f32[144,128]{1,0:T(8,128)S(1)}, f32[144,128]{1,0:T(8,128)S(1)}, u32[]{:S(2)}, u32[]{:S(2)}) collective-permute-start(f32[144,128]{1,0:T(8,128)S(1)} %concatenate.3.kappa.statics), channel_id=1, source_target_pairs={{1,0},{2,1},{3,2},{4,3},{5,4},{6,5},{7,6},{8,7},{9,8},{10,9},{11,1... | collective-permute-start | bytes 221192 | tf_op jit(solution)/shard_map/ppermute | solution.py:421
  11.9 1.3 %collective-permute-start.3 = (f32[144,128]{1,0:T(8,128)S(1)}, f32[144,128]{1,0:T(8,128)S(1)}, u32[]{:S(2)}, u32[]{:S(2)}) collective-permute-start(f32[144,128]{1,0:T(8,128)S(1)} %concatenate.3.kappa.statics), channel_id=1, source_target_pairs={{2,0},{3,1},{4,2},{5,3},{6,4},{7,5},{8,6},{9,7},{10,8},{11,9},{12,... | collective-permute-start | bytes 221192 | tf_op jit(solution)/shard_map/ppermute | solution.py:421
  13.2 0.8 copy-done.4
  14.1 1.2 %copy-done.6 = f32[16,4,32,128]{3,2,1,0:T(8,128)S(1)} copy-done((f32[16,4,32,128]{3,2,1,0:T(8,128)S(1)}, f32[16,4,32,128]{3,2,1,0:T(8,128)}, u32[]{:S(2)}) %copy-start.6) | copy-done | bytes 1048600
  15.3 0.9 copy-done.7
  16.2 0.9 copy-done.10
  17.1 3.6 %shard_map.131 = (f32[2048,128]{1,0:T(8,128)S(1)}, f32[2560,128]{1,0:T(8,128)S(1)}, f32[2560,128]{1,0:T(8,128)S(1)}, f32[2048,128]{1,0:T(8,128)S(1)}) custom-call(f32[2048,128]{1,0:T(8,128)S(1)} %bitcast.33, f32[384,128]{1,0:T(8,128)S(1)} %bitcast.34, f32[128,128]{1,0:T(8,128)S(1)} %bitcast.31, bf16[256,256]{1,0:T(8,128)(2,1)S(1)} %copy-done.10), custom_call_target="tpu_custom_call" | custom-call | flops 600000000 | bytes 6291456 | tf_op jit(solution)/shard_map/pallas_call | solution.py:403
  20.8 7.9 %shard_map.132 = (f32[256,128]{1,0:T(8,128)S(1)}, bf16[1280,512]{1,0:T(8,128)(2,1)S(1)}, bf16[640,512]{1,0:T(8,128)(2,1)S(1)}) custom-call(f32[2560,128]{1,0:T(8,128)S(1)} %get-tuple-element.13.first, f32[2560,128]{1,0:T(8,128)S(1)} %get-tuple-element.14.second, f32[2048,128]{1,0:T(8,128)S(1)} %get-tuple-element.15.third, ...), custom_call_target="tpu_custom_call" | custom-call | flops 3000000000 | bytes 6291456 | tf_op jit(solution)/shard_map/pallas_call | solution.py:403
  28.8 0.8 copy-done.12
  29.6 18.5 %all_to_all.33 = f32[16,16,128]{2,1,0:T(8,128)S(1)} all-to-all(f32[16,16,128]{2,1,0:T(8,128)S(1)} %bitcast.29), channel_id=1, replica_groups=mesh['group'=2,'space'=16] {'space'}, dimensions={0} | all-to-all | bytes 262144 | tf_op jit(solution)/shard_map/all_to_all | solution.py:425
  48.8 3.5 %all-to-all-start.1 = ((f32[16,16,128]{2,1,0:T(8,128)}), f32[16,16,128]{2,1,0:T(8,128)S(1)}, u32[]{:S(2)}, u32[]{:S(2)}) async-start(f32[16,16,128]{2,1,0:T(8,128)} %bitcast.11), calls=%async_computation.1 | async-start | bytes 262144 | tf_op jit(solution)/shard_map/all_to_all | solution.py:425
  52.3 2.2 %copy-done.3 = f32[64,4,32,128]{3,2,1,0:T(8,128)S(1)} copy-done((f32[64,4,32,128]{3,2,1,0:T(8,128)S(1)}, f32[64,4,32,128]{3,2,1,0:T(8,128)}, u32[]{:S(2)}) %copy-start.3) | copy-done | bytes 4194328
  54.5 3.2 %shard_map.134.basis = bf16[1024,2048]{1,0:T(8,128)(2,1)S(1)} custom-call(f32[8192,128]{1,0:T(8,128)S(1)} %bitcast.24), custom_call_target="tpu_custom_call" | custom-call | flops 10000000 | bytes 8388608 | tf_op jit(solution)/shard_map/pallas_call | solution.py:403
  57.7 1.9 %copy-done = bf16[1024,2048]{1,0:T(8,128)(2,1)} copy-done((bf16[1024,2048]{1,0:T(8,128)(2,1)}, bf16[1024,2048]{1,0:T(8,128)(2,1)S(1)}, u32[]{:S(2)}) %copy-start) | copy-done | bytes 4194328
  60.2 2.2 %copy-done.1 = bf16[1024,2048]{1,0:T(8,128)(2,1)S(1)} copy-done((bf16[1024,2048]{1,0:T(8,128)(2,1)S(1)}, bf16[1024,2048]{1,0:T(8,128)(2,1)}, u32[]{:S(2)}) %copy-start.1) | copy-done | bytes 4194328
  62.4 1.1 %copy-done.13 = bf16[640,512]{1,0:T(8,128)(2,1)S(1)} copy-done((bf16[640,512]{1,0:T(8,128)(2,1)S(1)}, bf16[640,512]{1,0:T(8,128)(2,1)}, u32[]{:S(2)}) %copy-start.13) | copy-done | bytes 655384
  63.5 15.8 %shard_map.135 = (f32[2048,128]{1,0:T(8,128)S(1)}, f32[256,128]{1,0:T(8,128)S(1)}) custom-call(f32[256,128]{1,0:T(8,128)S(1)} %bitcast.27, f32[144,128]{1,0:T(8,128)S(1)} %collective-permute-done.kappa_mm.statics_mm, f32[144,128]{1,0:T(8,128)S(1)} %collective-permute-done.1.kappa_m.statics_m, f32[144,128]{1,0:T(8,128)S(1)} %concatenate.3.kappa.statics, ...), custom_call_target="tpu_custom_call" | custom-call | flops 5000000000 | bytes 10485760 | tf_op jit(solution)/shard_map/pallas_call | solution.py:403
  79.3 13.1 %all_to_all.34 = f32[16,16,128]{2,1,0:T(8,128)S(1)} all-to-all(f32[16,16,128]{2,1,0:T(8,128)S(1)} %bitcast.28), channel_id=1, replica_groups=mesh['group'=2,'space'=16] {'space'}, dimensions={0} | all-to-all | bytes 262144 | tf_op jit(solution)/shard_map/all_to_all | solution.py:425
  92.5 4.1 %shard_map.136 = (f32[2048,128]{1,0:T(8,128)}, f32[16,64]{1,0:T(8,128)}) custom-call(f32[2048,128]{1,0:T(8,128)S(1)} %get-tuple-element.20.image, bf16[1024,2048]{1,0:T(8,128)(2,1)S(1)} %copy-done.2, f32[256,128]{1,0:T(8,128)S(1)} %bitcast.26), custom_call_target="tpu_custom_call" | custom-call | flops 200000000 | bytes 6291456 | tf_op jit(solution)/shard_map/pallas_call | solution.py:403
  (26 shorter events, 2.0 us)
Async XLA Ops:
  0.6 20.1 %copy-start.11 = (bf16[256,256]{1,0:T(8,128)(2,1)S(1)}, bf16[256,256]{1,0:T(8,128)(2,1)}, u32[]{:S(2)}) copy-start(bf16[256,256]{1,0:T(8,128)(2,1)} %constant.4.clone.band_ref) | copy-start | bytes 393220
  4.3 16.4 %collective-permute-start = (f32[144,128]{1,0:T(8,128)S(1)}, f32[144,128]{1,0:T(8,128)S(1)}, u32[]{:S(2)}, u32[]{:S(2)}) collective-permute-start(f32[144,128]{1,0:T(8,128)S(1)} %concatenate.3.kappa.statics), channel_id=1, source_target_pairs={{0,2},{1,3},{2,4},{3,5},{4,6},{5,7},{6,8},{7,9},{8,10},{9,11},{10,... | collective-permute-start | bytes 221192 | tf_op jit(solution)/shard_map/ppermute | solution.py:421
  9.1 11.6 %collective-permute-start.1 = (f32[144,128]{1,0:T(8,128)S(1)}, f32[144,128]{1,0:T(8,128)S(1)}, u32[]{:S(2)}, u32[]{:S(2)}) collective-permute-start(f32[144,128]{1,0:T(8,128)S(1)} %concatenate.3.kappa.statics), channel_id=1, source_target_pairs={{0,1},{1,2},{2,3},{3,4},{4,5},{5,6},{6,7},{7,8},{8,9},{9,10},{10,1... | collective-permute-start | bytes 221192 | tf_op jit(solution)/shard_map/ppermute | solution.py:421
  10.6 10.1 %collective-permute-start.2 = (f32[144,128]{1,0:T(8,128)S(1)}, f32[144,128]{1,0:T(8,128)S(1)}, u32[]{:S(2)}, u32[]{:S(2)}) collective-permute-start(f32[144,128]{1,0:T(8,128)S(1)} %concatenate.3.kappa.statics), channel_id=1, source_target_pairs={{1,0},{2,1},{3,2},{4,3},{5,4},{6,5},{7,6},{8,7},{9,8},{10,9},{11,1... | collective-permute-start | bytes 221192 | tf_op jit(solution)/shard_map/ppermute | solution.py:421
  11.9 8.8 %collective-permute-start.3 = (f32[144,128]{1,0:T(8,128)S(1)}, f32[144,128]{1,0:T(8,128)S(1)}, u32[]{:S(2)}, u32[]{:S(2)}) collective-permute-start(f32[144,128]{1,0:T(8,128)S(1)} %concatenate.3.kappa.statics), channel_id=1, source_target_pairs={{2,0},{3,1},{4,2},{5,3},{6,4},{7,5},{8,6},{9,7},{10,8},{11,9},{12,... | collective-permute-start | bytes 221192 | tf_op jit(solution)/shard_map/ppermute | solution.py:421
  13.2 0.8 copy-start.4
  14.1 1.2 %copy-start.6 = (f32[16,4,32,128]{3,2,1,0:T(8,128)S(1)}, f32[16,4,32,128]{3,2,1,0:T(8,128)}, u32[]{:S(2)}) copy-start(f32[16,4,32,128]{3,2,1,0:T(8,128)} %param.12) | copy-start | bytes 3145732
  15.3 0.9 copy-start.7
  16.2 0.9 copy-start.10
  20.8 27.3 %copy-start.5 = (f32[128]{0:T(128)S(1)}, f32[128]{0:T(128)}, u32[]{:S(2)}) copy-start(f32[128]{0:T(128)} %param.22) | copy-start | bytes 1540
  28.7 0.8 copy-start.12
  48.8 11.4 %all-to-all-start.1 = ((f32[16,16,128]{2,1,0:T(8,128)}), f32[16,16,128]{2,1,0:T(8,128)S(1)}, u32[]{:S(2)}, u32[]{:S(2)}) async-start(f32[16,16,128]{2,1,0:T(8,128)} %bitcast.11), calls=%async_computation.1 | async-start | bytes 262144 | tf_op jit(solution)/shard_map/all_to_all | solution.py:425
  52.3 2.2 %copy-start.3 = (f32[64,4,32,128]{3,2,1,0:T(8,128)S(1)}, f32[64,4,32,128]{3,2,1,0:T(8,128)}, u32[]{:S(2)}) copy-start(f32[64,4,32,128]{3,2,1,0:T(8,128)} %param.16) | copy-start | bytes 12582916
  54.5 5.7 %copy-start.8 = (f32[3,4,32,128]{3,2,1,0:T(8,128)S(1)}, f32[3,4,32,128]{3,2,1,0:T(8,128)}, u32[]{:S(2)}) copy-start(f32[3,4,32,128]{3,2,1,0:T(8,128)} %param.13) | copy-start | bytes 589828
  54.5 5.7 %copy-start.9 = (f32[4,32,128]{2,1,0:T(8,128)S(1)}, f32[4,32,128]{2,1,0:T(8,128)}, u32[]{:S(2)}) copy-start(f32[4,32,128]{2,1,0:T(8,128)} %param.15) | copy-start | bytes 196612
  57.7 1.9 %copy-start = (bf16[1024,2048]{1,0:T(8,128)(2,1)}, bf16[1024,2048]{1,0:T(8,128)(2,1)S(1)}, u32[]{:S(2)}) copy-start(bf16[1024,2048]{1,0:T(8,128)(2,1)S(1)} %shard_map.134.basis) | copy-start | bytes 12582916
  60.2 2.2 %copy-start.1 = (bf16[1024,2048]{1,0:T(8,128)(2,1)S(1)}, bf16[1024,2048]{1,0:T(8,128)(2,1)}, u32[]{:S(2)}) copy-start(bf16[1024,2048]{1,0:T(8,128)(2,1)} %copy-done) | copy-start | bytes 12582916
  62.4 1.1 %copy-start.13 = (bf16[640,512]{1,0:T(8,128)(2,1)S(1)}, bf16[640,512]{1,0:T(8,128)(2,1)}, u32[]{:S(2)}) copy-start(bf16[640,512]{1,0:T(8,128)(2,1)} %copy-done.12) | copy-start | bytes 1966084
  63.5 29.0 %copy-start.2 = (bf16[1024,2048]{1,0:T(8,128)(2,1)S(1)}, bf16[1024,2048]{1,0:T(8,128)(2,1)}, u32[]{:S(2)}) copy-start(bf16[1024,2048]{1,0:T(8,128)(2,1)} %copy-done) | copy-start | bytes 12582916

commit v3 on v1

v3 whole, which is shorter than its diff:
```python
import functools

import jax
import jax.numpy as jnp
from jax import lax
from jax.experimental import pallas as pl
from jax.experimental.pallas import tpu as pltpu
from jax.sharding import PartitionSpec as P

STENCIL = (-205.0 / 72.0, 8.0 / 5.0, -1.0 / 5.0, 8.0 / 315.0, -1.0 / 560.0)
CENTER = 3.0 * STENCIL[0]
REACH = 4
LAYERS = 4
PADDED = 40
HALF = 128
F32 = jnp.float32
BF16 = jnp.bfloat16
NT = (((1,), (1,)), ((), ()))


def split(value):
    high = value.astype(BF16)
    low = (value - high.astype(F32)).astype(BF16)
    return high, low


def at(row, count=16):
    return pl.ds(pl.multiple_of(row, 16), count)


def spread(ref, row, fields):
    return jnp.broadcast_to(ref[pl.ds(row, 1), :], (fields, HALF))


def clear_margins(ref, layers, fields):
    margin = jnp.zeros((REACH * fields, HALF), F32)
    for layer in range(layers):
        start = layer * PADDED * fields
        ref[start : start + REACH * fields, :] = margin
        start += (PADDED - REACH) * fields
        ref[start : start + REACH * fields, :] = margin


def along_z(ref, first, fields, band_ref, out_ref, row=0):
    pieces = [ref[at(((first + x) * PADDED + REACH) * fields, 32 * fields), :] for x in range(LAYERS)]
    high, low = split(jnp.concatenate(pieces, axis=0))
    both = jnp.dot(jnp.concatenate([high, low], axis=1), band_ref[...], preferred_element_type=F32)
    out_ref[at(row, LAYERS * 32 * fields), :] = both[:, :HALF] + both[:, HALF:]


def laplacian(get, x, y, z_term, lowest, highest):
    total = CENTER * get(x, y) + z_term
    for k in range(1, REACH + 1):
        ring = get(x, y + k) + get(x, y - k)
        if x + k <= highest:
            ring = ring + get(x + k, y)
        if x - k >= lowest:
            ring = ring + get(x - k, y)
        total = total + STENCIL[k] * ring
    return total


def pack(
    count, probes, sources, prior, kappa, cell, owner, slot, weight,
    statics, probes_out, sources_out, prior_out, band_ref, small_int, small_float, sem,
):
    rows = cell.shape[0]
    cells = kappa.shape[0]
    small = [
        pltpu.make_async_copy(kappa, statics.at[pl.ds(0, cells)], sem.at[0]),
        pltpu.make_async_copy(cell, small_int.at[0], sem.at[1]),
        pltpu.make_async_copy(owner, small_int.at[1], sem.at[2]),
        pltpu.make_async_copy(slot, small_int.at[2], sem.at[3]),
        pltpu.make_async_copy(weight, small_float, sem.at[4]),
    ]
    large = [
        pltpu.make_async_copy(probes, probes_out, sem.at[5]),
        pltpu.make_async_copy(sources, sources_out, sem.at[6]),
        pltpu.make_async_copy(prior, prior_out, sem.at[7]),
    ]
    for copy in small + large:
        copy.start()
    apart = lax.broadcasted_iota(jnp.int32, (HALF, HALF), 0) - lax.broadcasted_iota(jnp.int32, (HALF, HALF), 1)
    full = jnp.zeros((HALF, HALF), F32)
    for reach in range(1, REACH + 1):
        full = jnp.where(jnp.abs(apart) == reach, STENCIL[reach], full)
    high, low = split(full)
    band_ref[0:HALF, 0:HALF] = high
    band_ref[HALF:, 0:HALF] = high
    band_ref[0:HALF, HALF:] = low
    band_ref[HALF:, HALF:] = jnp.zeros_like(low)
    for copy in small:
        copy.wait()
    for i in range(3):
        statics[cells + i * rows : cells + (i + 1) * rows, :] = small_int[i].astype(F32)
    place = lax.broadcasted_iota(jnp.int32, (rows, HALF), 0) * HALF
    place = place + lax.broadcasted_iota(jnp.int32, (rows, HALF), 1)
    live = jnp.where(place < count[0], small_float[...], 0.0)
    statics[cells + 3 * rows : cells + 4 * rows, :] = live
    for copy in large:
        copy.wait()


def forward_own(fields, probes, sources, statics, band_ref, turned, first, second, third, z_term):
    clear_margins(first, LAYERS, fields)
    clear_margins(second, LAYERS, fields)

    def load(chunk, carry):
        for x in range(LAYERS):
            for step in range(8):
                y = chunk * 8 + step
                cell = x * 32 + y
                value = probes[pl.ds(cell, fields, stride=HALF), :]
                turned[at(cell * fields, fields), :] = value
                first[at((x * PADDED + REACH + y) * fields, fields), :] = value * spread(sources, cell, fields)
        return carry

    lax.fori_loop(0, 4, load, 0)

    def sweep(field, emit):
        along_z(field, 0, fields, band_ref, z_term)

        def body(chunk, carry):
            for x in range(LAYERS):
                for step in range(8):
                    y = chunk * 8 + step
                    cell = x * 32 + y

                    def get(layer, row):
                        return field[at((layer * PADDED + REACH + row) * fields, fields), :]

                    z_part = z_term[at(cell * fields, fields), :]
                    total = laplacian(get, x, y, z_part, 0, LAYERS - 1)
                    emit(x, y, get(x, y), spread(statics, cell, fields) * total)
            return carry

        lax.fori_loop(0, 4, body, 0)

    def step_one(x, y, now, change):
        cell = x * 32 + y
        push = turned[at(cell * fields, fields), :] * spread(sources, 128 + cell, fields)
        second[at((x * PADDED + REACH + y) * fields, fields), :] = 2.0 * now + change + push

    sweep(first, step_one)

    def step_two(x, y, now, change):
        cell = x * 32 + y
        push = turned[at(cell * fields, fields), :] * spread(sources, 256 + cell, fields)
        before = first[at((x * PADDED + REACH + y) * fields, fields), :]
        third[at(cell * fields, fields), :] = 2.0 * now - before + change + push

    sweep(second, step_two)


def entry_row(value, row):
    return jnp.concatenate([value[row + i : row + i + 1, :] for i in range(4)], axis=1)


def forward_window(
    fields, peers, me, first, second, third, own, partner, before, after, band_ref, own_scale,
    kept, sent, cell_ref, slot_ref, speed_ref, line_ref, owner_ref, weight_ref,
    below, above, z_term, sample, total_ref, table,
):
    entries = line_ref.shape[1]
    cells = LAYERS * 32
    length = own.shape[0]
    odd = me[0] % 2 == 1
    clear_margins(below, LAYERS, fields)
    clear_margins(above, LAYERS, fields)
    total_ref[...] = jnp.zeros_like(total_ref)
    tiles = (
        before[0:length, :],
        jnp.where(odd, partner[...], before[length:, :]),
        own[...],
        jnp.where(odd, after[length:, :], partner[...]),
        after[0:length, :],
    )
    place = lax.broadcasted_iota(jnp.int32, (256, entries), 0)
    slot_place = lax.broadcasted_iota(jnp.int32, (HALF, entries), 0)
    for tile, value in enumerate(tiles):
        speed_ref[tile * cells : (tile + 1) * cells, :] = value[0:cells, :]
        cell = entry_row(value, cells).astype(jnp.int32)
        owner = entry_row(value, cells + 4).astype(jnp.int32)
        slot = entry_row(value, cells + 8).astype(jnp.int32)
        weight = entry_row(value, cells + 12)
        hot = jnp.where(place == jnp.bitwise_and(cell, 255), 1.0, 0.0)
        cell_ref[tile * 256 : (tile + 1) * 256, :] = hot.astype(BF16)
        hot = jnp.where(slot_place == slot, 1.0, 0.0)
        slot_ref[tile * HALF : (tile + 1) * HALF, :] = hot.astype(BF16)
        rows = slice(tile * fields, (tile + 1) * fields)
        line_ref[rows, :] = jnp.broadcast_to(lax.shift_right_logical(cell, 8), (fields, entries))
        owner_ref[rows, :] = jnp.broadcast_to(owner, (fields, entries))
        weight_ref[rows, :] = jnp.broadcast_to(weight, (fields, entries))

    def outward(chunk, carry):
        for step in range(8):
            y = chunk * 8 + step
            mine = [first[at((x * PADDED + REACH + y) * fields, fields), :] for x in range(LAYERS)]
            for x in range(LAYERS):
                up = sum(STENCIL[4 + x - other] * mine[other] for other in range(x, LAYERS))
                down = sum(STENCIL[4 + other - x] * mine[other] for other in range(x + 1))
                row = at((x * PADDED + REACH + y) * fields, fields)
                above[row, :] = spread(speed_ref, 3 * cells + x * 32 + y, fields) * up
                below[row, :] = spread(speed_ref, cells + x * 32 + y, fields) * down
        return carry

    lax.fori_loop(0, 4, outward, 0)
    along_z(below, 0, fields, band_ref, z_term, 0)
    along_z(above, 0, fields, band_ref, z_term, cells * fields)

    def read(layer, y):
        ref = (below, second, above)[(layer + LAYERS) // LAYERS]
        return ref[at((layer % LAYERS * PADDED + REACH + y) * fields, fields), :]

    def far(x, y, lowest, highest):
        total = None
        for other in range(lowest, highest + 1):
            if 1 <= abs(x - other) <= REACH:
                term = STENCIL[abs(x - other)] * read(other, y)
                total = term if total is None else total + term
        return total

    def respond(chunk, carry):
        for tile in range(5):
            for x in range(LAYERS):
                for pair in range(4):
                    halves = []
                    for step in range(2):
                        y = chunk * 8 + pair * 2 + step
                        cell = x * 32 + y
                        layer = (tile - 2) * LAYERS + x
                        speed = spread(speed_ref, tile * cells + cell, fields)
                        if tile in (0, 4):
                            value = speed * far(layer, y, -4, 7)
                        elif tile == 2:
                            outside = far(layer, y, -4, -1) + far(layer, y, 4, 7)
                            value = third[at(cell * fields, fields), :] + speed * outside
                        else:
                            z_part = z_term[at((tile // 2 * cells + cell) * fields, fields), :]
                            value = 2.0 * read(layer, y) + speed * laplacian(read, layer, y, z_part, -4, 7)
                        halves.append(split(value))
                    row = at((tile * 64 + x * 16 + chunk * 4 + pair) * fields, fields)
                    for step, (high, low) in enumerate(halves):
                        sample[row, step * HALF : (step + 1) * HALF] = high
                        sample[row, 256 + step * HALF : 256 + (step + 1) * HALF] = low
        return carry

    lax.fori_loop(0, 4, respond, 0)

    def pick(tile, carry):
        hot = cell_ref[at(tile * 256, 256), :]
        parts = sample[at(tile * 64 * fields, 64 * fields), :]
        picked = jnp.dot(parts, jnp.concatenate([hot, hot], axis=0), preferred_element_type=F32)
        rows = at(tile * fields, fields)
        line = line_ref[rows, :]
        total = jnp.zeros((fields, entries), F32)
        for i in range(64):
            total = total + jnp.where(line == i, picked[i * fields : (i + 1) * fields, :], 0.0)
        total_ref[rows, :] = total
        return carry

    lax.fori_loop(0, 5, pick, 0)

    for group in range(peers // 16):
        lefts, rights = [], []
        for tile in range(5):
            rows = slice(tile * fields, (tile + 1) * fields)
            high, low = split(total_ref[rows, :] * weight_ref[rows, :])
            high, low = high.astype(F32), low.astype(F32)
            owner = owner_ref[rows, :]
            for part in (high, low):
                pieces = [jnp.where(owner == group * 16 + i, part, 0.0).astype(BF16) for i in range(16)]
                lefts.append(jnp.concatenate(pieces, axis=0))
                rights.append(slot_ref[tile * HALF : (tile + 1) * HALF, :])
        result = lax.dot_general(
            jnp.concatenate(lefts, axis=1), jnp.concatenate(rights, axis=1), NT, preferred_element_type=F32
        )
        table[group * 16 * fields : (group + 1) * 16 * fields, :] = result
    count = peers // 2
    mine = me[0] % 2
    place = lax.broadcasted_iota(jnp.int32, (count, HALF), 0)
    scale = jnp.broadcast_to(own_scale[...], (count, HALF))
    for out, side in ((kept, mine), (sent, 1 - mine)):
        out[0 : count * fields, :] = table[at(side * count * fields, count * fields), :]
        out[count * fields :, :] = jnp.where(place == me[0] - side * count, scale, 0.0)


def basis_parts(basis, out):
    rank = basis.shape[0] // HALF

    def body(group, carry):
        for step in range(8):
            high, low = split(basis[pl.ds(group * 8 + step, rank, stride=HALF), :])
            rows = at(group * rank, rank)
            out[rows, step * 256 : step * 256 + HALF] = high
            out[rows, step * 256 + HALF : (step + 1) * 256] = low
        return carry

    lax.fori_loop(0, 16, body, 0)


def adjoint(
    fields, peers, me, half, other, cell_ref, slot_ref, speed_ref, line_ref, owner_ref, weight_ref, turned, sources,
    prior, band_ref, basis, image, coeffs, high_ref, low_ref, left, inner_two, outer_two,
    inner_one, outer_one, z_term, image_parts, scaled,
):
    entries = line_ref.shape[1]
    cells = LAYERS * 32
    rank = basis.shape[0] // 16
    clear_margins(inner_two, 5 * LAYERS, fields)
    clear_margins(inner_one, 3 * LAYERS, fields)
    count = peers // 2
    mine = me[0] % 2
    for ref, side in ((half, mine), (other, 1 - mine)):
        for i in range(count):
            scale = ref[count * fields + i : count * fields + i + 1, :]
            scaled[at((side * count + i) * fields, fields), :] = ref[i * fields : (i + 1) * fields, :] * scale
    for tile in range(5):
        rows = slice(tile * fields, (tile + 1) * fields)
        owner = owner_ref[rows, :]
        hot = slot_ref[tile * HALF : (tile + 1) * HALF, :]
        hot = jnp.concatenate([hot, hot], axis=0)
        total = jnp.zeros((fields, entries), F32)
        for group in range(peers // 16):
            parts = split(scaled[group * 16 * fields : (group + 1) * 16 * fields, :])
            found = jnp.dot(jnp.concatenate(parts, axis=1), hot, preferred_element_type=F32)
            for i in range(16):
                total = total + jnp.where(owner == group * 16 + i, found[i * fields : (i + 1) * fields, :], 0.0)
        high, low = split(total * weight_ref[rows, :])
        high_ref[rows, :] = high.astype(F32)
        low_ref[rows, :] = low.astype(F32)

    def inject(tile, carry):
        rows = at(tile * fields, fields)
        line, high, low = line_ref[rows, :], high_ref[rows, :], low_ref[rows, :]
        for i in range(64):
            chosen = line == i
            left[i * fields : (i + 1) * fields, :entries] = jnp.where(chosen, high, 0.0).astype(BF16)
            left[i * fields : (i + 1) * fields, entries:] = jnp.where(chosen, low, 0.0).astype(BF16)
        hot = cell_ref[at(tile * 256, 256), :]
        value = lax.dot_general(left[...], jnp.concatenate([hot, hot], axis=1), NT, preferred_element_type=F32)
        for i in range(64):
            x, pair = i // 16, i % 16
            for step in range(2):
                y = pair * 2 + step
                now = value[i * fields : (i + 1) * fields, step * HALF : (step + 1) * HALF]
                layer = tile * LAYERS + x
                outer_two[at((layer * 32 + y) * fields, fields), :] = now
                speed = spread(speed_ref, layer * 32 + y, fields)
                inner_two[at((layer * PADDED + REACH + y) * fields, fields), :] = speed * now
        return carry

    lax.fori_loop(0, 5, inject, 0)

    def terms(index, carry):
        along_z(inner_two, (index + 1) * LAYERS, fields, band_ref, z_term, index * cells * fields)
        return carry

    lax.fori_loop(0, 3, terms, 0)

    def step_one(index, carry):
        tile, chunk = index // 4 + 1, index % 4
        for x in range(LAYERS):
            for step in range(8):
                y = chunk * 8 + step

                def get(layer, row):
                    return inner_two[at(((tile * LAYERS + layer) * PADDED + REACH + row) * fields, fields), :]

                layer = tile * LAYERS + x
                speed = spread(speed_ref, layer * 32 + y, fields)
                now = 2.0 * outer_two[at((layer * 32 + y) * fields, fields), :]
                layer = layer - LAYERS
                z_part = z_term[at((layer * 32 + y) * fields, fields), :]
                now = now + laplacian(get, x, y, z_part, -4, 7)
                outer_one[at((layer * 32 + y) * fields, fields), :] = now
                inner_one[at((layer * PADDED + REACH + y) * fields, fields), :] = speed * now
        return carry

    lax.fori_loop(0, 12, step_one, 0)

    def get_one(layer, row):
        return inner_one[at(((LAYERS + layer) * PADDED + REACH + row) * fields, fields), :]

    along_z(inner_one, LAYERS, fields, band_ref, z_term)

    def step_two(chunk, total):
        for x in range(LAYERS):
            for step in range(8):
                y = chunk * 8 + step
                cell = x * 32 + y
                z_part = z_term[at(cell * fields, fields), :]
                two = outer_two[at((2 * LAYERS * 32 + cell) * fields, fields), :]
                one = outer_one[at((LAYERS * 32 + cell) * fields, fields), :]
                zero = 2.0 * one - two + laplacian(get_one, x, y, z_part, -4, 7)
                value = spread(sources, cell, fields) * zero
                value = value + spread(sources, 128 + cell, fields) * one
                value = value + spread(sources, 256 + cell, fields) * two
                value = value + spread(prior, cell, fields) * turned[at(cell * fields, fields), :]
                image[at(cell * fields, fields), :] = value
                high, low = split(value)
                side = step * 256
                rows = slice(x * 2 * fields, x * 2 * fields + fields)
                image_parts[rows, side : side + HALF] = high
                image_parts[rows, side + HALF : side + 256] = high
                rows = slice(x * 2 * fields + fields, (x + 1) * 2 * fields)
                image_parts[rows, side : side + HALF] = low
                image_parts[rows, side + HALF : side + 256] = jnp.zeros_like(low)
        for x in range(LAYERS):
            columns = basis[at((x * 4 + chunk) * rank, rank), :]
            parts = image_parts[x * 2 * fields : (x + 1) * 2 * fields, :]
            total = total + lax.dot_general(parts, columns, NT, preferred_element_type=F32)
        return total

    total = lax.fori_loop(0, 4, step_two, jnp.zeros((2 * fields, rank), F32))
    coeffs[...] = total[:fields, :] + total[fields:, :]


def remainder(fields, image, basis, *rest):
    *shares, out, coeffs, natural, sem = rest
    rank = coeffs.shape[1]
    while len(shares) > 1:
        shares = [shares[i][...] + shares[i + 1][...] for i in range(0, len(shares), 2)]
    total = shares[0][...]
    coeffs[...] = total
    parts = jnp.concatenate(split(total), axis=0)
    whole = natural.reshape(out.shape)

    def leave(x):
        return pltpu.make_async_copy(whole.at[:, x], out.at[:, x], sem.at[x])

    def body(x, carry):
        for part in range(4):
            columns = basis[at((x * 4 + part) * rank, rank), :]
            both = jnp.dot(parts, columns, preferred_element_type=F32)
            for step in range(8):
                cell = x * 32 + part * 8 + step
                side = step * 256
                along = both[:fields, side : side + HALF] + both[:fields, side + HALF : side + 256]
                along = along + both[fields:, side : side + HALF]
                natural[pl.ds(cell, fields, stride=HALF), :] = image[at(cell * fields, fields), :] - along
        leave(x).start()
        return carry

    lax.fori_loop(0, LAYERS, body, 0)
    for x in range(LAYERS):
        leave(x).wait()


def call(kernel, inputs, out_shape, scratch, flops, size, scalars=0, far=0, far_out=0):
    smem = pl.BlockSpec(memory_space=pltpu.SMEM)
    vmem = pl.BlockSpec(memory_space=pltpu.VMEM)
    hbm = pl.BlockSpec(memory_space=pltpu.HBM)
    return pl.pallas_call(
        kernel,
        out_shape=out_shape,
        in_specs=[smem] * scalars + [hbm] * far + [vmem] * (len(inputs) - scalars - far),
        out_specs=[hbm] * far_out + [vmem] * (len(out_shape) - far_out),
        scratch_shapes=scratch,
        cost_estimate=pl.CostEstimate(flops=flops, bytes_accessed=size, transcendentals=0),
        compiler_params=pltpu.CompilerParams(vmem_limit_bytes=44 * 2**20),
    )(*inputs)


def struct(*shape, dtype=F32):
    return jax.ShapeDtypeStruct(shape, dtype)


def shifted(array, axis, by):
    count = lax.axis_size(axis)
    return lax.ppermute(array, axis, [(i, i + by) for i in range(count) if 0 <= i + by < count])


def swapped(array, axis, bits):
    count = lax.axis_size(axis)
    return lax.ppermute(array, axis, [(i, i ^ bits) for i in range(count)])


def local(
    probes,
    sources,
    kappa,
    prior,
    basis,
    entry_cell,
    entry_owner,
    entry_slot,
    entry_weight,
    entry_count,
    trace_weight,
):
    fields, rank = probes.shape[0], basis.shape[0]
    entries = entry_cell.shape[0]
    peers = lax.axis_size("space")
    padded = LAYERS * PADDED * fields
    cells = LAYERS * 32
    rows = entries // HALF
    me = lax.axis_index("space").astype(jnp.int32).reshape(1)

    own, probes_near, sources_near, prior_near, matrix = call(
        pack,
        (
            entry_count,
            probes.reshape(fields * cells, HALF),
            sources.reshape(3 * cells, HALF),
            prior.reshape(cells, HALF),
            kappa.reshape(cells, HALF),
            entry_cell.reshape(rows, HALF),
            entry_owner.reshape(rows, HALF),
            entry_slot.reshape(rows, HALF),
            entry_weight.reshape(rows, HALF),
        ),
        [
            struct(cells + 4 * rows, HALF),
            struct(fields * cells, HALF),
            struct(3 * cells, HALF),
            struct(cells, HALF),
            struct(256, 256, dtype=BF16),
        ],
        [pltpu.VMEM((3, rows, HALF), jnp.int32), pltpu.VMEM((rows, HALF), F32), pltpu.SemaphoreType.DMA((8,))],
        100_000,
        2 * 2**20,
        scalars=1,
        far=8,
    )
    partner = swapped(own, "space", 1)
    both = jnp.concatenate([own, partner], axis=0)
    before = shifted(both, "space", 2)
    after = shifted(both, "space", -2)

    turned, first, second, third = call(
        functools.partial(forward_own, fields),
        (probes_near, sources_near, own, matrix),
        [struct(cells * fields, HALF), struct(padded, HALF), struct(padded, HALF), struct(cells * fields, HALF)],
        [pltpu.VMEM((cells * fields, HALF), F32)],
        600_000_000,
        6 * 2**20,
    )
    half_rows = peers // 2 * (fields + 1)
    kept, sent, cell_hot, slot_hot, speed, line, owner, weight = call(
        functools.partial(forward_window, fields, peers),
        (me, first, second, third, own, partner, before, after, matrix, trace_weight.reshape(1, HALF)),
        [
            struct(half_rows, HALF),
            struct(half_rows, HALF),
            struct(5 * 256, entries, dtype=BF16),
            struct(5 * HALF, entries, dtype=BF16),
            struct(5 * cells, HALF),
            struct(5 * fields, entries, dtype=jnp.int32),
            struct(5 * fields, entries, dtype=jnp.int32),
            struct(5 * fields, entries),
        ],
        [
            pltpu.VMEM((padded, HALF), F32),
            pltpu.VMEM((padded, HALF), F32),
            pltpu.VMEM((2 * cells * fields, HALF), F32),
            pltpu.VMEM((5 * 64 * fields, 512), BF16),
            pltpu.VMEM((5 * fields, entries), F32),
            pltpu.VMEM((peers * fields, HALF), F32),
        ],
        3_000_000_000,
        6 * 2**20,
        scalars=1,
    )
    half = kept + swapped(sent, "space", 1)
    bits = 2
    while bits < peers:
        half = half + swapped(half, "space", bits)
        bits *= 2
    other = swapped(half, "space", 1)
    (columns,) = call(
        basis_parts,
        (basis.reshape(rank * cells, HALF),),
        [struct(16 * rank, 2048, dtype=BF16)],
        [],
        10_000_000,
        8 * 2**20,
    )
    image, coeffs = call(
        functools.partial(adjoint, fields, peers),
        (
            me, half, other, cell_hot, slot_hot, speed, line, owner, weight,
            turned, sources_near, prior_near, matrix, columns,
        ),
        [struct(cells * fields, HALF), struct(fields, rank)],
        [
            pltpu.VMEM((5 * fields, entries), F32),
            pltpu.VMEM((5 * fields, entries), F32),
            pltpu.VMEM((64 * fields, 2 * entries), BF16),
            pltpu.VMEM((5 * padded, HALF), F32),
            pltpu.VMEM((5 * cells * fields, HALF), F32),
            pltpu.VMEM((3 * padded, HALF), F32),
            pltpu.VMEM((3 * cells * fields, HALF), F32),
            pltpu.VMEM((3 * cells * fields, HALF), F32),
            pltpu.VMEM((8 * fields, 2048), BF16),
            pltpu.VMEM((peers * fields, HALF), F32),
        ],
        5_000_000_000,
        10 * 2**20,
        scalars=1,
    )
    bits = 1
    while bits * 4 < peers:
        coeffs = coeffs + swapped(coeffs, "space", bits)
        bits *= 2
    shares = [coeffs] + [swapped(coeffs, "space", bits * i) for i in range(1, peers // bits)]
    hess_probe, coeffs = call(
        functools.partial(remainder, fields),
        (image, columns, *shares),
        [struct(*probes.shape), struct(fields, rank)],
        [pltpu.VMEM((fields * cells, HALF), F32), pltpu.SemaphoreType.DMA((LAYERS,))],
        200_000_000,
        6 * 2**20,
        far_out=1,
    )
    return hess_probe, coeffs.T


def solution(mesh):
    return jax.shard_map(
        local,
        mesh=mesh,
        in_specs=(
            P("group", "space", None, None),
            P(None, ("group", "space"), None, None),
            P(("group", "space"), None, None),
            P(("group", "space"), None, None),
            P("group", "space", None, None),
            P(("group", "space")),
            P(("group", "space")),
            P(("group", "space")),
            P(("group", "space")),
            P(("group", "space")),
            P(("group", "space")),
        ),
        out_specs=(P("group", "space", None, None), P("group", None)),
        check_vma=False,
    )
```

time: 87.4 us -> 79.3 us (0.907)
  Pallas kernels: 34.7 us -> 30.9 us
  starting transfers between devices: 24.4 us -> 21.8 us
  other arithmetic: 2.16 us -> 0.04 us
  local copies, waits for them, and re-layouts: 4.8 us -> 6.58 us
  waiting for transfers between devices: 19.4 us -> 18.1 us
    pallas_call x5 -> x6, Pallas kernels: 34.7 us -> 30.9 us  [call(): pl.pallas_call(kernel, out_shape=out_shape, in_specs=[smem] * scalars + [...]
    unnamed x20 -> x25, local copies, waits for them, and re-layouts: 3.92 us -> 6.57 us
    ppermute x12 -> x13, starting transfers between devices: 24.4 us -> 21.8 us  [the longest x11 15.1 us: swapped(): return lax.ppermute(array, axis, [(i, i ^ bits) for i in range(count)])]
    reshape x3 -> x0, other arithmetic: 2.07 us -> none  [the longest x2 1.39 us: local(): array.astype(F32).reshape(-1, HALF)]
    ppermute x12 -> x13, waiting for transfers between devices: 19.4 us -> 18.1 us  [the longest x11 16.3 us: swapped(): return lax.ppermute(array, axis, [(i, i ^ bits) for i in range(count)])]
    concatenate x1, local copies, waits for them, and re-layouts: 0.88 us -> 0.01 us  [local(): both = jnp.concatenate([own, partner], axis=0)]
  transfers between devices with their start and end apart: 12 -> 13, of which waited for: 8 -> 10; matrix products, arithmetic and copies ran while one was open for 0% -> 0% of each run, Pallas kernels for 8% -> 9%
where the time goes in v3:
time: 79.3 us; the launch traced here: 78.9 us
  Pallas kernels  30.9 us (39%)
  starting transfers between devices  21.8 us (27%)
  waiting for transfers between devices  18.1 us (23%)
  local copies, waits for them, and re-layouts  6.58 us (8%)
  between operations  1.43 us (2%)
    pallas_call x6, Pallas kernels, call(): pl.pallas_call(kernel, out_shape=out_shape, in_specs=[smem] * scalars + [...  30.9 us
    ppermute x11, waiting for transfers between devices, swapped(): return lax.ppermute(array, axis, [(i, i ^ bits) for i in range(count)])  16.3 us
    ppermute x11, starting transfers between devices, swapped(): return lax.ppermute(array, axis, [(i, i ^ bits) for i in range(count)])  15.1 us
    ppermute x2, starting transfers between devices, shifted(): lax.ppermute(array, axis, [(i, i + by) for i in range(count) if 0 <= i +...  6.69 us
    unnamed x25, local copies, waits for them, and re-layouts  6.57 us
    ppermute x2, waiting for transfers between devices, shifted(): lax.ppermute(array, axis, [(i, i + by) for i in range(count) if 0 <= i +...  1.77 us
  transfers between devices with their start and end apart: 13, of which 10 were waited for; matrix products, arithmetic and copies ran while one was open for 0% of the time, Pallas kernels for 9%

profile of v3, /device:TPU:0, one launch (start us, length us, event | category | flops | bytes accessed | tf_op | source)
XLA Modules:
  0.0 78.9 jit_solution(515244306226051771)
XLA Ops:
  1.3 1.2 %copy-done.1 = f32[16,4,32,128]{3,2,1,0:T(8,128)S(1)} copy-done((f32[16,4,32,128]{3,2,1,0:T(8,128)S(1)}, f32[16,4,32,128]{3,2,1,0:T(8,128)}, u32[]{:S(2)}) %copy-start.1) | copy-done | bytes 1048600
  2.5 0.9 %copy-done.2 = f32[3,4,32,128]{3,2,1,0:T(8,128)S(1)} copy-done((f32[3,4,32,128]{3,2,1,0:T(8,128)S(1)}, f32[3,4,32,128]{3,2,1,0:T(8,128)}, u32[]{:S(2)}) %copy-start.2) | copy-done | bytes 196632
  3.4 0.8 %copy-done.3 = f32[4,32,128]{2,1,0:T(8,128)S(1)} copy-done((f32[4,32,128]{2,1,0:T(8,128)S(1)}, f32[4,32,128]{2,1,0:T(8,128)}, u32[]{:S(2)}) %copy-start.3) | copy-done | bytes 65560
  9.0 0.9 %collective-permute-done.partner = f32[144,128]{1,0:T(8,128)S(1)} collective-permute-done((f32[144,128]{1,0:T(8,128)S(1)}, f32[144,128]{1,0:T(8,128)S(1)}, u32[]{:S(2)}, u32[]{:S(2)}) %collective-permute-start) | collective-permute-done | bytes 73760 | tf_op jit(solution)/shard_map/ppermute | solution.py:476
  9.9 1.3 %collective-permute-start.2 = (f32[288,128]{1,0:T(8,128)S(1)}, f32[288,128]{1,0:T(8,128)S(1)}, u32[]{:S(2)}, u32[]{:S(2)}) collective-permute-start(f32[288,128]{1,0:T(8,128)S(1)} %constant_dynamic-update-slice_fusion), channel_id=1, source_target_pairs={{2,0},{3,1},{4,2},{5,3},{6,4},{7,5},{8,6},{9,7},{10,8},{11,9},{12,... | collective-permute-start | bytes 442376 | tf_op jit(solution)/shard_map/ppermute | solution.py:471
  11.2 5.4 %collective-permute-start.1 = (f32[288,128]{1,0:T(8,128)S(1)}, f32[288,128]{1,0:T(8,128)S(1)}, u32[]{:S(2)}, u32[]{:S(2)}) collective-permute-start(f32[288,128]{1,0:T(8,128)S(1)} %constant_dynamic-update-slice_fusion), channel_id=1, source_target_pairs={{0,2},{1,3},{2,4},{3,5},{4,6},{5,7},{6,8},{7,9},{8,10},{9,11},{10,... | collective-permute-start | bytes 442376 | tf_op jit(solution)/shard_map/ppermute | solution.py:471
  16.6 3.7 %shard_map.123 = (f32[2048,128]{1,0:T(8,128)S(1)}, f32[2560,128]{1,0:T(8,128)S(1)}, f32[2560,128]{1,0:T(8,128)S(1)}, f32[2048,128]{1,0:T(8,128)S(1)}) custom-call(f32[2048,128]{1,0:T(8,128)S(1)} %get-tuple-element.23.probes, f32[384,128]{1,0:T(8,128)S(1)} %get-tuple-element.24.sources, f32[144,128]{1,0:T(8,128)S(1)} %get-tuple-element.25.statics.own, ...), custom_call_target="tpu_custom_call" | custom-call | flops 600000000 | bytes 6291456 | tf_op jit(solution)/shard_map/pallas_call | solution.py:454
  20.4 1.8 %collective-permute-done.1.before = f32[288,128]{1,0:T(8,128)S(1)} collective-permute-done((f32[288,128]{1,0:T(8,128)S(1)}, f32[288,128]{1,0:T(8,128)S(1)}, u32[]{:S(2)}, u32[]{:S(2)}) %collective-permute-start.1) | collective-permute-done | bytes 147488 | tf_op jit(solution)/shard_map/ppermute | solution.py:471
  22.1 9.0 %shard_map.124 = (f32[136,128]{1,0:T(8,128)S(1)}, f32[136,128]{1,0:T(8,128)S(1)}, bf16[1280,512]{1,0:T(8,128)(2,1)S(1)}, bf16[640,512]{1,0:T(8,128)(2,1)S(1)}, f...) custom-call(s32[1]{0:T(128)} %bitcast.me, ...), custom_call_target="tpu_custom_call" | custom-call | flops 3000000000 | bytes 6291456 | tf_op jit(solution)/shard_map/pallas_call | solution.py:454
  31.3 1.2 %collective-permute-done.3 = f32[136,128]{1,0:T(8,128)S(1)} collective-permute-done((f32[136,128]{1,0:T(8,128)S(1)}, f32[136,128]{1,0:T(8,128)S(1)}, u32[]{:S(2)}, u32[]{:S(2)}) %collective-permute-start.3) | collective-permute-done | bytes 69664 | tf_op jit(solution)/shard_map/ppermute | solution.py:476
  32.5 2.5 %collective-permute-start.4 = (f32[136,128]{1,0:T(8,128)S(1)}, f32[136,128]{1,0:T(8,128)S(1)}, u32[]{:S(2)}, u32[]{:S(2)}) collective-permute-start(f32[136,128]{1,0:T(8,128)S(1)} %add.18), channel_id=1, source_target_pairs={{0,2},{1,3},{2,0},{3,1},{4,6},{5,7},{6,4},{7,5},{8,10},{9,11},{10,... | collective-permute-start | bytes 208904 | tf_op jit(solution)/shard_map/ppermute | solution.py:476
  35.1 2.5 %collective-permute-done.4 = f32[136,128]{1,0:T(8,128)S(1)} collective-permute-done((f32[136,128]{1,0:T(8,128)S(1)}, f32[136,128]{1,0:T(8,128)S(1)}, u32[]{:S(2)}, u32[]{:S(2)}) %collective-permute-start.4) | collective-permute-done | bytes 69664 | tf_op jit(solution)/shard_map/ppermute | solution.py:476
  37.6 1.8 %collective-permute-start.5 = (f32[136,128]{1,0:T(8,128)S(1)}, f32[136,128]{1,0:T(8,128)S(1)}, u32[]{:S(2)}, u32[]{:S(2)}) collective-permute-start(f32[136,128]{1,0:T(8,128)S(1)} %add.19), channel_id=1, source_target_pairs={{0,4},{1,5},{2,6},{3,7},{4,0},{5,1},{6,2},{7,3},{8,12},{9,13},{10,... | collective-permute-start | bytes 208904 | tf_op jit(solution)/shard_map/ppermute | solution.py:476
  39.4 2.6 %collective-permute-done.5 = f32[136,128]{1,0:T(8,128)S(1)} collective-permute-done((f32[136,128]{1,0:T(8,128)S(1)}, f32[136,128]{1,0:T(8,128)S(1)}, u32[]{:S(2)}, u32[]{:S(2)}) %collective-permute-start.5) | collective-permute-done | bytes 69664 | tf_op jit(solution)/shard_map/ppermute | solution.py:476
  42.0 2.8 %collective-permute-start.6 = (f32[136,128]{1,0:T(8,128)S(1)}, f32[136,128]{1,0:T(8,128)S(1)}, u32[]{:S(2)}, u32[]{:S(2)}) collective-permute-start(f32[136,128]{1,0:T(8,128)S(1)} %add.20), channel_id=1, source_target_pairs={{0,8},{1,9},{2,10},{3,11},{4,12},{5,13},{6,14},{7,15},{8,0},{9,1},... | collective-permute-start | bytes 208904 | tf_op jit(solution)/shard_map/ppermute | solution.py:476
  44.8 2.4 %collective-permute-done.6 = f32[136,128]{1,0:T(8,128)S(1)} collective-permute-done((f32[136,128]{1,0:T(8,128)S(1)}, f32[136,128]{1,0:T(8,128)S(1)}, u32[]{:S(2)}, u32[]{:S(2)}) %collective-permute-start.6) | collective-permute-done | bytes 69664 | tf_op jit(solution)/shard_map/ppermute | solution.py:476
  47.4 3.2 %shard_map.125.basis = bf16[1024,2048]{1,0:T(8,128)(2,1)S(1)} custom-call(f32[8192,128]{1,0:T(8,128)S(1)} %bitcast.12), custom_call_target="tpu_custom_call" | custom-call | flops 10000000 | bytes 8388608 | tf_op jit(solution)/shard_map/pallas_call | solution.py:454
  50.6 11.4 %shard_map.126 = (f32[2048,128]{1,0:T(8,128)S(1)}, f32[16,64]{1,0:T(8,128)S(1)}) custom-call(s32[1]{0:T(128)} %bitcast.me, f32[136,128]{1,0:T(8,128)S(1)} %add.21.half, f32[136,128]{1,0:T(8,128)S(1)} %collective-permute-done.7.other, bf16[1280,512]{1,0:T(8,128)(2,1)S(1)} %get-tuple-element.32.cell_ref, bf16[640,512]{1,0:T(8,128)(2,1)S(1)} %get-tuple-element.33.slot_ref, ...), custom_call_target="tpu_custom_call" | custom-call | flops 5000000000 | bytes 10485760 | tf_op jit(solution)/shard_map/pallas_call | solution.py:454
  63.3 1.8 %collective-permute-start.9 = (f32[16,64]{1,0:T(8,128)S(1)}, f32[16,64]{1,0:T(8,128)S(1)}, u32[]{:S(2)}, u32[]{:S(2)}) collective-permute-start(f32[16,64]{1,0:T(8,128)S(1)} %add.22), channel_id=1, source_target_pairs={{0,2},{1,3},{2,0},{3,1},{4,6},{5,7},{6,4},{7,5},{8,10},{9,11},{10,... | collective-permute-start | bytes 12296 | tf_op jit(solution)/shard_map/ppermute | solution.py:476
  65.1 1.9 %collective-permute-done.9 = f32[16,64]{1,0:T(8,128)S(1)} collective-permute-done((f32[16,64]{1,0:T(8,128)S(1)}, f32[16,64]{1,0:T(8,128)S(1)}, u32[]{:S(2)}, u32[]{:S(2)}) %collective-permute-start.9) | collective-permute-done | bytes 4128 | tf_op jit(solution)/shard_map/ppermute | solution.py:476
  67.0 4.4 %collective-permute-start.12 = (f32[16,64]{1,0:T(8,128)S(1)}, f32[16,64]{1,0:T(8,128)S(1)}, u32[]{:S(2)}, u32[]{:S(2)}) collective-permute-start(f32[16,64]{1,0:T(8,128)S(1)} %add.23.rest_0_), channel_id=1, source_target_pairs={{0,12},{1,13},{2,14},{3,15},{4,8},{5,9},{6,10},{7,11},{8,4},{9,5},... | collective-permute-start | bytes 12296 | tf_op jit(solution)/shard_map/ppermute | solution.py:476
  72.0 1.1 %collective-permute-done.12.rest_3_ = f32[16,64]{1,0:T(8,128)S(1)} collective-permute-done((f32[16,64]{1,0:T(8,128)S(1)}, f32[16,64]{1,0:T(8,128)S(1)}, u32[]{:S(2)}, u32[]{:S(2)}) %collective-permute-start.12) | collective-permute-done | bytes 4128 | tf_op jit(solution)/shard_map/ppermute | solution.py:476
  73.1 2.9 %collective-permute-done.11.rest_2_ = f32[16,64]{1,0:T(8,128)S(1)} collective-permute-done((f32[16,64]{1,0:T(8,128)S(1)}, f32[16,64]{1,0:T(8,128)S(1)}, u32[]{:S(2)}, u32[]{:S(2)}) %collective-permute-start.11) | collective-permute-done | bytes 4128 | tf_op jit(solution)/shard_map/ppermute | solution.py:476
  76.0 2.9 %shard_map.127 = (f32[16,4,32,128]{3,2,1,0:T(8,128)}, f32[16,64]{1,0:T(8,128)}) custom-call(f32[2048,128]{1,0:T(8,128)S(1)} %get-tuple-element.40.image, bf16[1024,2048]{1,0:T(8,128)(2,1)S(1)} %shard_map.125.basis, f32[16,64]{1,0:T(8,128)S(1)} %add.23.rest_0_, f32[16,64]{1,0:T(8,128)S(1)} %collective-permute-done.10.rest_1_, ...), custom_call_target="tpu_custom_call" | custom-call | flops 200000000 | bytes 6291456 | tf_op jit(solution)/shard_map/pallas_call | solution.py:454
  (40 shorter events, 6.8 us)
Async XLA Ops:
  1.3 1.2 %copy-start.1 = (f32[16,4,32,128]{3,2,1,0:T(8,128)S(1)}, f32[16,4,32,128]{3,2,1,0:T(8,128)}, u32[]{:S(2)}) copy-start(f32[16,4,32,128]{3,2,1,0:T(8,128)} %param.11) | copy-start | bytes 3145732
  2.5 0.9 %copy-start.2 = (f32[3,4,32,128]{3,2,1,0:T(8,128)S(1)}, f32[3,4,32,128]{3,2,1,0:T(8,128)}, u32[]{:S(2)}) copy-start(f32[3,4,32,128]{3,2,1,0:T(8,128)} %param.12) | copy-start | bytes 589828
  3.4 0.8 %copy-start.3 = (f32[4,32,128]{2,1,0:T(8,128)S(1)}, f32[4,32,128]{2,1,0:T(8,128)}, u32[]{:S(2)}) copy-start(f32[4,32,128]{2,1,0:T(8,128)} %param.14) | copy-start | bytes 196612
  4.3 0.8 %copy-start.4 = (f32[4,32,128]{2,1,0:T(8,128)S(1)}, f32[4,32,128]{2,1,0:T(8,128)}, u32[]{:S(2)}) copy-start(f32[4,32,128]{2,1,0:T(8,128)} %param.13) | copy-start | bytes 196612
  5.1 0.7 copy-start.5
  5.8 0.7 copy-start.6
  6.5 0.7 copy-start.7
  8.4 13.7 %copy-start.9 = (f32[128]{0:T(128)S(1)}, f32[128]{0:T(128)}, u32[]{:S(2)}) copy-start(f32[128]{0:T(128)} %param.21) | copy-start | bytes 1540
  8.4 1.4 %collective-permute-start = (f32[144,128]{1,0:T(8,128)S(1)}, f32[144,128]{1,0:T(8,128)S(1)}, u32[]{:S(2)}, u32[]{:S(2)}) collective-permute-start(f32[144,128]{1,0:T(8,128)S(1)} %get-tuple-element.25.statics.own), channel_id=1, source_target_pairs={{0,1},{1,0},{2,3},{3,2},{4,5},{5,4},{6,7},{7,6},{8,9},{9,8},{10,11... | collective-permute-start | bytes 221192 | tf_op jit(solution)/shard_map/ppermute | solution.py:476
  9.9 10.5 %collective-permute-start.2 = (f32[288,128]{1,0:T(8,128)S(1)}, f32[288,128]{1,0:T(8,128)S(1)}, u32[]{:S(2)}, u32[]{:S(2)}) collective-permute-start(f32[288,128]{1,0:T(8,128)S(1)} %constant_dynamic-update-slice_fusion), channel_id=1, source_target_pairs={{2,0},{3,1},{4,2},{5,3},{6,4},{7,5},{8,6},{9,7},{10,8},{11,9},{12,... | collective-permute-start | bytes 442376 | tf_op jit(solution)/shard_map/ppermute | solution.py:471
  11.2 11.0 %collective-permute-start.1 = (f32[288,128]{1,0:T(8,128)S(1)}, f32[288,128]{1,0:T(8,128)S(1)}, u32[]{:S(2)}, u32[]{:S(2)}) collective-permute-start(f32[288,128]{1,0:T(8,128)S(1)} %constant_dynamic-update-slice_fusion), channel_id=1, source_target_pairs={{0,2},{1,3},{2,4},{3,5},{4,6},{5,7},{6,8},{7,9},{8,10},{9,11},{10,... | collective-permute-start | bytes 442376 | tf_op jit(solution)/shard_map/ppermute | solution.py:471
  20.3 10.8 %copy-start.10 = (f32[2048,128]{1,0:T(8,128)}, f32[2048,128]{1,0:T(8,128)S(1)}, u32[]{:S(2)}) copy-start(f32[2048,128]{1,0:T(8,128)S(1)} %get-tuple-element.38.turned) | copy-start | bytes 3145732
  22.1 25.2 %copy-start = (f32[64,4,32,128]{3,2,1,0:T(8,128)S(1)}, f32[64,4,32,128]{3,2,1,0:T(8,128)}, u32[]{:S(2)}) copy-start(f32[64,4,32,128]{3,2,1,0:T(8,128)} %param.15) | copy-start | bytes 12582916
  31.2 1.3 %collective-permute-start.3 = (f32[136,128]{1,0:T(8,128)S(1)}, f32[136,128]{1,0:T(8,128)S(1)}, u32[]{:S(2)}, u32[]{:S(2)}) collective-permute-start(f32[136,128]{1,0:T(8,128)S(1)} %get-tuple-element.31), channel_id=1, source_target_pairs={{0,1},{1,0},{2,3},{3,2},{4,5},{5,4},{6,7},{7,6},{8,9},{9,8},{10,11... | collective-permute-start | bytes 208904 | tf_op jit(solution)/shard_map/ppermute | solution.py:476
  32.5 5.0 %collective-permute-start.4 = (f32[136,128]{1,0:T(8,128)S(1)}, f32[136,128]{1,0:T(8,128)S(1)}, u32[]{:S(2)}, u32[]{:S(2)}) collective-permute-start(f32[136,128]{1,0:T(8,128)S(1)} %add.18), channel_id=1, source_target_pairs={{0,2},{1,3},{2,0},{3,1},{4,6},{5,7},{6,4},{7,5},{8,10},{9,11},{10,... | collective-permute-start | bytes 208904 | tf_op jit(solution)/shard_map/ppermute | solution.py:476
  37.6 4.4 %collective-permute-start.5 = (f32[136,128]{1,0:T(8,128)S(1)}, f32[136,128]{1,0:T(8,128)S(1)}, u32[]{:S(2)}, u32[]{:S(2)}) collective-permute-start(f32[136,128]{1,0:T(8,128)S(1)} %add.19), channel_id=1, source_target_pairs={{0,4},{1,5},{2,6},{3,7},{4,0},{5,1},{6,2},{7,3},{8,12},{9,13},{10,... | collective-permute-start | bytes 208904 | tf_op jit(solution)/shard_map/ppermute | solution.py:476
  42.0 5.3 %collective-permute-start.6 = (f32[136,128]{1,0:T(8,128)S(1)}, f32[136,128]{1,0:T(8,128)S(1)}, u32[]{:S(2)}, u32[]{:S(2)}) collective-permute-start(f32[136,128]{1,0:T(8,128)S(1)} %add.20), channel_id=1, source_target_pairs={{0,8},{1,9},{2,10},{3,11},{4,12},{5,13},{6,14},{7,15},{8,0},{9,1},... | collective-permute-start | bytes 208904 | tf_op jit(solution)/shard_map/ppermute | solution.py:476
  47.3 3.3 %collective-permute-start.7 = (f32[136,128]{1,0:T(8,128)S(1)}, f32[136,128]{1,0:T(8,128)S(1)}, u32[]{:S(2)}, u32[]{:S(2)}) collective-permute-start(f32[136,128]{1,0:T(8,128)S(1)} %add.21.half), channel_id=1, source_target_pairs={{0,1},{1,0},{2,3},{3,2},{4,5},{5,4},{6,7},{7,6},{8,9},{9,8},{10,11... | collective-permute-start | bytes 208904 | tf_op jit(solution)/shard_map/ppermute | solution.py:476
  47.3 3.2 %copy-start.11 = (f32[2048,128]{1,0:T(8,128)S(1)}, f32[2048,128]{1,0:T(8,128)}, u32[]{:S(2)}) copy-start(f32[2048,128]{1,0:T(8,128)} %copy-done.10) | copy-start | bytes 3145732
  62.0 1.3 %collective-permute-start.8 = (f32[16,64]{1,0:T(8,128)S(1)}, f32[16,64]{1,0:T(8,128)S(1)}, u32[]{:S(2)}, u32[]{:S(2)}) collective-permute-start(f32[16,64]{1,0:T(8,128)S(1)} %get-tuple-element.41), channel_id=1, source_target_pairs={{0,1},{1,0},{2,3},{3,2},{4,5},{5,4},{6,7},{7,6},{8,9},{9,8},{10,11... | collective-permute-start | bytes 12296 | tf_op jit(solution)/shard_map/ppermute | solution.py:476
  63.3 3.7 %collective-permute-start.9 = (f32[16,64]{1,0:T(8,128)S(1)}, f32[16,64]{1,0:T(8,128)S(1)}, u32[]{:S(2)}, u32[]{:S(2)}) collective-permute-start(f32[16,64]{1,0:T(8,128)S(1)} %add.22), channel_id=1, source_target_pairs={{0,2},{1,3},{2,0},{3,1},{4,6},{5,7},{6,4},{7,5},{8,10},{9,11},{10,... | collective-permute-start | bytes 12296 | tf_op jit(solution)/shard_map/ppermute | solution.py:476
  67.0 6.1 %collective-permute-start.12 = (f32[16,64]{1,0:T(8,128)S(1)}, f32[16,64]{1,0:T(8,128)S(1)}, u32[]{:S(2)}, u32[]{:S(2)}) collective-permute-start(f32[16,64]{1,0:T(8,128)S(1)} %add.23.rest_0_), channel_id=1, source_target_pairs={{0,12},{1,13},{2,14},{3,15},{4,8},{5,9},{6,10},{7,11},{8,4},{9,5},... | collective-permute-start | bytes 12296 | tf_op jit(solution)/shard_map/ppermute | solution.py:476
  71.4 4.5 %collective-permute-start.11 = (f32[16,64]{1,0:T(8,128)S(1)}, f32[16,64]{1,0:T(8,128)S(1)}, u32[]{:S(2)}, u32[]{:S(2)}) collective-permute-start(f32[16,64]{1,0:T(8,128)S(1)} %add.23.rest_0_), channel_id=1, source_target_pairs={{0,8},{1,9},{2,10},{3,11},{4,12},{5,13},{6,14},{7,15},{8,0},{9,1},... | collective-permute-start | bytes 12296 | tf_op jit(solution)/shard_map/ppermute | solution.py:476
  71.4 4.5 %collective-permute-start.10 = (f32[16,64]{1,0:T(8,128)S(1)}, f32[16,64]{1,0:T(8,128)S(1)}, u32[]{:S(2)}, u32[]{:S(2)}) collective-permute-start(f32[16,64]{1,0:T(8,128)S(1)} %add.23.rest_0_), channel_id=1, source_target_pairs={{0,4},{1,5},{2,6},{3,7},{4,0},{5,1},{6,2},{7,3},{8,12},{9,13},{10,... | collective-permute-start | bytes 12296 | tf_op jit(solution)/shard_map/ppermute | solution.py:476
  (1 other events, 0.7 us)

commit v4 on v3

--- a/solution.py
+++ b/solution.py
@@ -13,6 +13,7 @@
 LAYERS = 4
 PADDED = 40
 HALF = 128
+PLACES = 512
 F32 = jnp.float32
 BF16 = jnp.bfloat16
 NT = (((1,), (1,)), ((), ()))
@@ -49,7 +50,7 @@
 
 
 def laplacian(get, x, y, z_term, lowest, highest):
-    total = CENTER * get(x, y) + z_term
+    total = z_term
     for k in range(1, REACH + 1):
         ring = get(x, y + k) + get(x, y - k)
         if x + k <= highest:
@@ -81,7 +82,7 @@
     for copy in small + large:
         copy.start()
     apart = lax.broadcasted_iota(jnp.int32, (HALF, HALF), 0) - lax.broadcasted_iota(jnp.int32, (HALF, HALF), 1)
-    full = jnp.zeros((HALF, HALF), F32)
+    full = jnp.where(apart == 0, CENTER, jnp.zeros((HALF, HALF), F32))
     for reach in range(1, REACH + 1):
         full = jnp.where(jnp.abs(apart) == reach, STENCIL[reach], full)
     high, low = split(full)
@@ -159,7 +160,7 @@
 def forward_window(
     fields, peers, me, first, second, third, own, partner, before, after, band_ref, own_scale,
     kept, sent, cell_ref, slot_ref, speed_ref, line_ref, owner_ref, weight_ref,
-    below, above, z_term, sample, total_ref, table,
+    below, above, z_term, total_ref, table, *samples,
 ):
     entries = line_ref.shape[1]
     cells = LAYERS * 32
@@ -169,13 +170,13 @@
     clear_margins(above, LAYERS, fields)
     total_ref[...] = jnp.zeros_like(total_ref)
     tiles = (
-        before[0:length, :],
-        jnp.where(odd, partner[...], before[length:, :]),
+        before[...],
+        jnp.where(odd, partner[0:length, :], partner[length:, :]),
         own[...],
-        jnp.where(odd, after[length:, :], partner[...]),
-        after[0:length, :],
-    )
-    place = lax.broadcasted_iota(jnp.int32, (256, entries), 0)
+        jnp.where(odd, partner[length:, :], partner[0:length, :]),
+        after[...],
+    )
+    place = lax.broadcasted_iota(jnp.int32, (PLACES, entries), 0)
     slot_place = lax.broadcasted_iota(jnp.int32, (HALF, entries), 0)
     for tile, value in enumerate(tiles):
         speed_ref[tile * cells : (tile + 1) * cells, :] = value[0:cells, :]
@@ -183,12 +184,12 @@
         owner = entry_row(value, cells + 4).astype(jnp.int32)
         slot = entry_row(value, cells + 8).astype(jnp.int32)
         weight = entry_row(value, cells + 12)
-        hot = jnp.where(place == jnp.bitwise_and(cell, 255), 1.0, 0.0)
-        cell_ref[tile * 256 : (tile + 1) * 256, :] = hot.astype(BF16)
+        hot = jnp.where(place == jnp.bitwise_and(cell, PLACES - 1), 1.0, 0.0)
+        cell_ref[tile * PLACES : (tile + 1) * PLACES, :] = hot.astype(BF16)
         hot = jnp.where(slot_place == slot, 1.0, 0.0)
         slot_ref[tile * HALF : (tile + 1) * HALF, :] = hot.astype(BF16)
         rows = slice(tile * fields, (tile + 1) * fields)
-        line_ref[rows, :] = jnp.broadcast_to(lax.shift_right_logical(cell, 8), (fields, entries))
+        line_ref[rows, :] = jnp.broadcast_to(lax.shift_right_logical(cell, 9), (fields, entries))
         owner_ref[rows, :] = jnp.broadcast_to(owner, (fields, entries))
         weight_ref[rows, :] = jnp.broadcast_to(weight, (fields, entries))
 
@@ -222,44 +223,42 @@
 
     def respond(chunk, carry):
         for tile in range(5):
+            sample = samples[tile]
             for x in range(LAYERS):
-                for pair in range(4):
-                    halves = []
-                    for step in range(2):
-                        y = chunk * 8 + pair * 2 + step
-                        cell = x * 32 + y
-                        layer = (tile - 2) * LAYERS + x
-                        speed = spread(speed_ref, tile * cells + cell, fields)
-                        if tile in (0, 4):
-                            value = speed * far(layer, y, -4, 7)
-                        elif tile == 2:
-                            outside = far(layer, y, -4, -1) + far(layer, y, 4, 7)
-                            value = third[at(cell * fields, fields), :] + speed * outside
-                        else:
-                            z_part = z_term[at((tile // 2 * cells + cell) * fields, fields), :]
-                            value = 2.0 * read(layer, y) + speed * laplacian(read, layer, y, z_part, -4, 7)
-                        halves.append(split(value))
-                    row = at((tile * 64 + x * 16 + chunk * 4 + pair) * fields, fields)
-                    for step, (high, low) in enumerate(halves):
-                        sample[row, step * HALF : (step + 1) * HALF] = high
-                        sample[row, 256 + step * HALF : 256 + (step + 1) * HALF] = low
+                for step in range(8):
+                    y = chunk * 8 + step
+                    cell = x * 32 + y
+                    layer = (tile - 2) * LAYERS + x
+                    speed = spread(speed_ref, tile * cells + cell, fields)
+                    if tile in (0, 4):
+                        value = speed * far(layer, y, -4, 7)
+                    elif tile == 2:
+                        outside = far(layer, y, -4, -1) + far(layer, y, 4, 7)
+                        value = third[at(cell * fields, fields), :] + speed * outside
+                    else:
+                        z_part = z_term[at((tile // 2 * cells + cell) * fields, fields), :]
+                        value = 2.0 * read(layer, y) + speed * laplacian(read, layer, y, z_part, -4, 7)
+                    row = (x * 2 + step // 4) * fields
+                    side = step % 4 * HALF
+                    high, low = split(value)
+                    sample[row : row + fields, side : side + HALF] = high
+                    row = row + 8 * fields
+                    sample[row : row + fields, side : side + HALF] = low
+            hot = cell_ref[tile * PLACES : (tile + 1) * PLACES, :]
+            picked = jnp.dot(sample[...], hot, preferred_element_type=F32)
+            picked = picked[: 8 * fields, :] + picked[8 * fields :, :]
+            for part in range(fields // 8):
+                rows = slice(tile * fields + part * 8, tile * fields + part * 8 + 8)
+                line = line_ref[rows, :]
+                total = total_ref[rows, :]
+                for i in range(8):
+                    chosen = line == i // 2 * 8 + chunk * 2 + i % 2
+                    row = i * fields + part * 8
+                    total = total + jnp.where(chosen, picked[row : row + 8, :], 0.0)
+                total_ref[rows, :] = total
         return carry
 
     lax.fori_loop(0, 4, respond, 0)
-
-    def pick(tile, carry):
-        hot = cell_ref[at(tile * 256, 256), :]
-        parts = sample[at(tile * 64 * fields, 64 * fields), :]
-        picked = jnp.dot(parts, jnp.concatenate([hot, hot], axis=0), preferred_element_type=F32)
-        rows = at(tile * fields, fields)
-        line = line_ref[rows, :]
-        total = jnp.zeros((fields, entries), F32)
-        for i in range(64):
-            total = total + jnp.where(line == i, picked[i * fields : (i + 1) * fields, :], 0.0)
-        total_ref[rows, :] = total
-        return carry
-
-    lax.fori_loop(0, 5, pick, 0)
 
     for group in range(peers // 16):
         lefts, rights = [], []
@@ -285,7 +284,7 @@
         out[count * fields :, :] = jnp.where(place == me[0] - side * count, scale, 0.0)
 
 
-def basis_parts(basis, out):
+def basis_parts(basis, when, out):
     rank = basis.shape[0] // HALF
 
     def body(group, carry):
@@ -301,8 +300,8 @@
 
 def adjoint(
     fields, peers, me, half, other, cell_ref, slot_ref, speed_ref, line_ref, owner_ref, weight_ref, turned, sources,
-    prior, band_ref, basis, image, coeffs, high_ref, low_ref, left, inner_two, outer_two,
-    inner_one, outer_one, z_term, image_parts, scaled,
+    prior, band_ref, basis, image, coeffs, high_ref, low_ref, inner_two, outer_two,
+    inner_one, outer_one, z_term, image_parts, scaled, *lefts,
 ):
     entries = line_ref.shape[1]
     cells = LAYERS * 32
@@ -330,27 +329,26 @@
         high_ref[rows, :] = high.astype(F32)
         low_ref[rows, :] = low.astype(F32)
 
-    def inject(tile, carry):
-        rows = at(tile * fields, fields)
-        line, high, low = line_ref[rows, :], high_ref[rows, :], low_ref[rows, :]
-        for i in range(64):
-            chosen = line == i
-            left[i * fields : (i + 1) * fields, :entries] = jnp.where(chosen, high, 0.0).astype(BF16)
-            left[i * fields : (i + 1) * fields, entries:] = jnp.where(chosen, low, 0.0).astype(BF16)
-        hot = cell_ref[at(tile * 256, 256), :]
+    for tile in range(5):
+        left = lefts[tile]
+        for part in range(fields // 16):
+            rows = slice(tile * fields + part * 16, tile * fields + part * 16 + 16)
+            line, high, low = line_ref[rows, :], high_ref[rows, :], low_ref[rows, :]
+            for i in range(32):
+                chosen = line == i
+                row = i * fields + part * 16
+                left[row : row + 16, :entries] = jnp.where(chosen, high, 0.0).astype(BF16)
+                left[row : row + 16, entries:] = jnp.where(chosen, low, 0.0).astype(BF16)
+        hot = cell_ref[tile * PLACES : (tile + 1) * PLACES, :]
         value = lax.dot_general(left[...], jnp.concatenate([hot, hot], axis=1), NT, preferred_element_type=F32)
-        for i in range(64):
-            x, pair = i // 16, i % 16
-            for step in range(2):
-                y = pair * 2 + step
+        for i in range(32):
+            for step in range(4):
+                layer, y = tile * LAYERS + i // 8, i % 8 * 4 + step
                 now = value[i * fields : (i + 1) * fields, step * HALF : (step + 1) * HALF]
-                layer = tile * LAYERS + x
-                outer_two[at((layer * 32 + y) * fields, fields), :] = now
+                if 1 <= tile <= 3:
+                    outer_two[at(((layer - LAYERS) * 32 + y) * fields, fields), :] = now
                 speed = spread(speed_ref, layer * 32 + y, fields)
                 inner_two[at((layer * PADDED + REACH + y) * fields, fields), :] = speed * now
-        return carry
-
-    lax.fori_loop(0, 5, inject, 0)
 
     def terms(index, carry):
         along_z(inner_two, (index + 1) * LAYERS, fields, band_ref, z_term, index * cells * fields)
@@ -369,8 +367,8 @@
 
                 layer = tile * LAYERS + x
                 speed = spread(speed_ref, layer * 32 + y, fields)
+                layer = layer - LAYERS
                 now = 2.0 * outer_two[at((layer * 32 + y) * fields, fields), :]
-                layer = layer - LAYERS
                 z_part = z_term[at((layer * 32 + y) * fields, fields), :]
                 now = now + laplacian(get, x, y, z_part, -4, 7)
                 outer_one[at((layer * 32 + y) * fields, fields), :] = now
@@ -390,7 +388,7 @@
                 y = chunk * 8 + step
                 cell = x * 32 + y
                 z_part = z_term[at(cell * fields, fields), :]
-                two = outer_two[at((2 * LAYERS * 32 + cell) * fields, fields), :]
+                two = outer_two[at((LAYERS * 32 + cell) * fields, fields), :]
                 one = outer_one[at((LAYERS * 32 + cell) * fields, fields), :]
                 zero = 2.0 * one - two + laplacian(get_one, x, y, z_part, -4, 7)
                 value = spread(sources, cell, fields) * zero
@@ -447,10 +445,14 @@
         leave(x).wait()
 
 
-def call(kernel, inputs, out_shape, scratch, flops, size, scalars=0, far=0, far_out=0):
+def call(kernel, inputs, out_shape, scratch, flops, size, scalars=0, far=0, far_out=0, room=16):
     smem = pl.BlockSpec(memory_space=pltpu.SMEM)
     vmem = pl.BlockSpec(memory_space=pltpu.VMEM)
     hbm = pl.BlockSpec(memory_space=pltpu.HBM)
+    inputs = [
+        pltpu.with_memory_space_constraint(array, pltpu.HBM) if scalars <= i < scalars + far else array
+        for i, array in enumerate(inputs)
+    ]
     return pl.pallas_call(
         kernel,
         out_shape=out_shape,
@@ -458,7 +460,7 @@
         out_specs=[hbm] * far_out + [vmem] * (len(out_shape) - far_out),
         scratch_shapes=scratch,
         cost_estimate=pl.CostEstimate(flops=flops, bytes_accessed=size, transcendentals=0),
-        compiler_params=pltpu.CompilerParams(vmem_limit_bytes=44 * 2**20),
+        compiler_params=pltpu.CompilerParams(vmem_limit_bytes=room * 2**20),
     )(*inputs)
 
 
@@ -523,10 +525,8 @@
         scalars=1,
         far=8,
     )
-    partner = swapped(own, "space", 1)
-    both = jnp.concatenate([own, partner], axis=0)
-    before = shifted(both, "space", 2)
-    after = shifted(both, "space", -2)
+    before = shifted(own, "space", 2)
+    after = shifted(own, "space", -2)
 
     turned, first, second, third = call(
         functools.partial(forward_own, fields),
@@ -537,13 +537,16 @@
         6 * 2**20,
     )
     half_rows = peers // 2 * (fields + 1)
+    before, after, second = lax.optimization_barrier((before, after, second))
+    relayed = jnp.where(jnp.bitwise_and(me, 1)[0] == 1, before, after)
+    partner = swapped(jnp.concatenate([own, relayed], axis=0), "space", 1)
     kept, sent, cell_hot, slot_hot, speed, line, owner, weight = call(
         functools.partial(forward_window, fields, peers),
         (me, first, second, third, own, partner, before, after, matrix, trace_weight.reshape(1, HALF)),
         [
             struct(half_rows, HALF),
             struct(half_rows, HALF),
-            struct(5 * 256, entries, dtype=BF16),
+            struct(5 * PLACES, entries, dtype=BF16),
             struct(5 * HALF, entries, dtype=BF16),
             struct(5 * cells, HALF),
             struct(5 * fields, entries, dtype=jnp.int32),
@@ -554,28 +557,32 @@
             pltpu.VMEM((padded, HALF), F32),
             pltpu.VMEM((padded, HALF), F32),
             pltpu.VMEM((2 * cells * fields, HALF), F32),
-            pltpu.VMEM((5 * 64 * fields, 512), BF16),
             pltpu.VMEM((5 * fields, entries), F32),
             pltpu.VMEM((peers * fields, HALF), F32),
-        ],
+        ]
+        + [pltpu.VMEM((16 * fields, PLACES), BF16)] * 5,
         3_000_000_000,
         6 * 2**20,
         scalars=1,
+        room=20,
     )
     half = kept + swapped(sent, "space", 1)
     bits = 2
-    while bits < peers:
+    while bits * 2 < peers:
         half = half + swapped(half, "space", bits)
         bits *= 2
-    other = swapped(half, "space", 1)
+    arrived = swapped(half, "space", bits)
     (columns,) = call(
         basis_parts,
-        (basis.reshape(rank * cells, HALF),),
+        (basis.reshape(rank * cells, HALF), half),
         [struct(16 * rank, 2048, dtype=BF16)],
         [],
         10_000_000,
         8 * 2**20,
     )
+    arrived, columns = lax.optimization_barrier((arrived, columns))
+    half = half + arrived
+    other = swapped(half, "space", 1)
     image, coeffs = call(
         functools.partial(adjoint, fields, peers),
         (
@@ -586,18 +593,19 @@
         [
             pltpu.VMEM((5 * fields, entries), F32),
             pltpu.VMEM((5 * fields, entries), F32),
-            pltpu.VMEM((64 * fields, 2 * entries), BF16),
             pltpu.VMEM((5 * padded, HALF), F32),
-            pltpu.VMEM((5 * cells * fields, HALF), F32),
+            pltpu.VMEM((3 * cells * fields, HALF), F32),
             pltpu.VMEM((3 * padded, HALF), F32),
             pltpu.VMEM((3 * cells * fields, HALF), F32),
             pltpu.VMEM((3 * cells * fields, HALF), F32),
             pltpu.VMEM((8 * fields, 2048), BF16),
             pltpu.VMEM((peers * fields, HALF), F32),
-        ],
+        ]
+        + [pltpu.VMEM((32 * fields, 2 * entries), BF16)] * 5,
         5_000_000_000,
         10 * 2**20,
         scalars=1,
+        room=34,
     )
     bits = 1
     while bits * 4 < peers:

time: 79.3 us -> 68.1 us (0.86)
  local copies, waits for them, and re-layouts: 6.58 us -> 0.01 us
  waiting for transfers between devices: 18.1 us -> 15.6 us
  Pallas kernels: 30.9 us -> 29.7 us
    unnamed x25 -> x4, local copies, waits for them, and re-layouts: 6.57 us -> 0.01 us
    ppermute x2, waiting for transfers between devices: 1.77 us -> 0.01 us  [shifted(): lax.ppermute(array, axis, [(i, i + by) for i in range(count) if 0 <= i +...]
    pallas_call x6, Pallas kernels: 30.9 us -> 29.7 us  [call(): pl.pallas_call(kernel, out_shape=out_shape, in_specs=[smem] * scalars + [...]
    ppermute x11, starting transfers between devices: 15.1 us -> 14.3 us  [swapped(): return lax.ppermute(array, axis, [(i, i ^ bits) for i in range(count)])]
  transfers between devices with their start and end apart: 13 -> 13, of which waited for: 10 -> 9; matrix products, arithmetic and copies ran while one was open for 0% -> 0% of each run, Pallas kernels for 9% -> 10%
where the time goes in v4:
time: 68.1 us; the launch traced here: 67.9 us
  Pallas kernels  29.7 us (44%)
  starting transfers between devices  21.1 us (31%)
  waiting for transfers between devices  15.6 us (23%)
  between operations  1.42 us (2%)
    pallas_call x6, Pallas kernels, call(): pl.pallas_call(kernel, out_shape=out_shape, in_specs=[smem] * scalars + [...  29.7 us
    ppermute x11, waiting for transfers between devices, swapped(): return lax.ppermute(array, axis, [(i, i ^ bits) for i in range(count)])  15.6 us
    ppermute x11, starting transfers between devices, swapped(): return lax.ppermute(array, axis, [(i, i ^ bits) for i in range(count)])  14.3 us
    ppermute x2, starting transfers between devices, shifted(): lax.ppermute(array, axis, [(i, i + by) for i in range(count) if 0 <= i +...  6.8 us
  transfers between devices with their start and end apart: 13, of which 9 were waited for; matrix products, arithmetic and copies ran while one was open for 0% of the time, Pallas kernels for 10%

profile of v4, /device:TPU:0, one launch (start us, length us, event | category | flops | bytes accessed | tf_op | source)
XLA Modules:
  0.0 67.9 jit_solution(4409848114358228768)
XLA Ops:
  1.3 1.4 %shard_map.122 = (f32[144,128]{1,0:T(8,128)S(1)}, f32[2048,128]{1,0:T(8,128)S(1)}, f32[384,128]{1,0:T(8,128)S(1)}, f32[128,128]{1,0:T(8,128)S(1)}, bf16[256,256]{1,0:T(8,128)(2,1)S(1)}) custom-call(s32[1]{0:T(128)S(6)} %copy.13.count, f32[2048,128]{1,0:T(8,128)} %bitcast.15, f32[384,128]{1,0:T(8,128)} %bitcast.16, f32[128,128]{1,0:T(8,128)} %bitcast.17, ...), custom_call_target="tpu_custom_call" | custom-call | flops 100000 | bytes 2097152 | tf_op jit(solution)/shard_map/pallas_call | solution.py:456
  2.7 1.3 %collective-permute-start.1 = (f32[144,128]{1,0:T(8,128)S(1)}, f32[144,128]{1,0:T(8,128)S(1)}, u32[]{:S(2)}, u32[]{:S(2)}) collective-permute-start(f32[144,128]{1,0:T(8,128)S(1)} %get-tuple-element.30.statics.own), channel_id=1, source_target_pairs={{2,0},{3,1},{4,2},{5,3},{6,4},{7,5},{8,6},{9,7},{10,8},{11,9},{12,... | collective-permute-start | bytes 221192 | tf_op jit(solution)/shard_map/ppermute | solution.py:473
  4.0 5.5 %collective-permute-start = (f32[144,128]{1,0:T(8,128)S(1)}, f32[144,128]{1,0:T(8,128)S(1)}, u32[]{:S(2)}, u32[]{:S(2)}) collective-permute-start(f32[144,128]{1,0:T(8,128)S(1)} %get-tuple-element.30.statics.own), channel_id=1, source_target_pairs={{0,2},{1,3},{2,4},{3,5},{4,6},{5,7},{6,8},{7,9},{8,10},{9,11},{10,... | collective-permute-start | bytes 221192 | tf_op jit(solution)/shard_map/ppermute | solution.py:473
  9.5 3.6 %shard_map.123 = (f32[2048,128]{1,0:T(8,128)S(1)}, f32[2560,128]{1,0:T(8,128)S(1)}, f32[2560,128]{1,0:T(8,128)S(1)}, f32[2048,128]{1,0:T(8,128)S(1)}) custom-call(f32[2048,128]{1,0:T(8,128)S(1)} %get-tuple-element.28.probes, f32[384,128]{1,0:T(8,128)S(1)} %get-tuple-element.29.sources, f32[144,128]{1,0:T(8,128)S(1)} %get-tuple-element.30.statics.own, ...), custom_call_target="tpu_custom_call" | custom-call | flops 600000000 | bytes 6291456 | tf_op jit(solution)/shard_map/pallas_call | solution.py:456
  13.3 1.4 %collective-permute-done.2.partner = f32[288,128]{1,0:T(8,128)S(1)} collective-permute-done((f32[288,128]{1,0:T(8,128)S(1)}, f32[288,128]{1,0:T(8,128)S(1)}, u32[]{:S(2)}, u32[]{:S(2)}) %collective-permute-start.2) | collective-permute-done | bytes 147488 | tf_op jit(solution)/shard_map/ppermute | solution.py:478
  14.7 8.3 %shard_map.124 = (f32[136,128]{1,0:T(8,128)S(1)}, f32[136,128]{1,0:T(8,128)S(1)}, bf16[2560,512]{1,0:T(8,128)(2,1)S(1)}, bf16[640,512]{1,0:T(8,128)(2,1)S(1)}, f...) custom-call(s32[1]{0:T(128)} %bitcast.me, ...), custom_call_target="tpu_custom_call" | custom-call | flops 3000000000 | bytes 6291456 | tf_op jit(solution)/shard_map/pallas_call | solution.py:456
  23.0 0.2 collective-permute-start.3
  23.2 1.1 %collective-permute-done.3 = f32[136,128]{1,0:T(8,128)S(1)} collective-permute-done((f32[136,128]{1,0:T(8,128)S(1)}, f32[136,128]{1,0:T(8,128)S(1)}, u32[]{:S(2)}, u32[]{:S(2)}) %collective-permute-start.3) | collective-permute-done | bytes 69664 | tf_op jit(solution)/shard_map/ppermute | solution.py:478
  24.3 3.0 %collective-permute-start.4 = (f32[136,128]{1,0:T(8,128)S(1)}, f32[136,128]{1,0:T(8,128)S(1)}, u32[]{:S(2)}, u32[]{:S(2)}) collective-permute-start(f32[136,128]{1,0:T(8,128)S(1)} %add.18), channel_id=1, source_target_pairs={{0,2},{1,3},{2,0},{3,1},{4,6},{5,7},{6,4},{7,5},{8,10},{9,11},{10,... | collective-permute-start | bytes 208904 | tf_op jit(solution)/shard_map/ppermute | solution.py:478
  27.3 2.5 %collective-permute-done.4 = f32[136,128]{1,0:T(8,128)S(1)} collective-permute-done((f32[136,128]{1,0:T(8,128)S(1)}, f32[136,128]{1,0:T(8,128)S(1)}, u32[]{:S(2)}, u32[]{:S(2)}) %collective-permute-start.4) | collective-permute-done | bytes 69664 | tf_op jit(solution)/shard_map/ppermute | solution.py:478
  29.8 2.0 %collective-permute-start.5 = (f32[136,128]{1,0:T(8,128)S(1)}, f32[136,128]{1,0:T(8,128)S(1)}, u32[]{:S(2)}, u32[]{:S(2)}) collective-permute-start(f32[136,128]{1,0:T(8,128)S(1)} %add.19), channel_id=1, source_target_pairs={{0,4},{1,5},{2,6},{3,7},{4,0},{5,1},{6,2},{7,3},{8,12},{9,13},{10,... | collective-permute-start | bytes 208904 | tf_op jit(solution)/shard_map/ppermute | solution.py:478
  31.8 2.4 %collective-permute-done.5 = f32[136,128]{1,0:T(8,128)S(1)} collective-permute-done((f32[136,128]{1,0:T(8,128)S(1)}, f32[136,128]{1,0:T(8,128)S(1)}, u32[]{:S(2)}, u32[]{:S(2)}) %collective-permute-start.5) | collective-permute-done | bytes 69664 | tf_op jit(solution)/shard_map/ppermute | solution.py:478
  34.2 3.0 %collective-permute-start.6 = (f32[136,128]{1,0:T(8,128)S(1)}, f32[136,128]{1,0:T(8,128)S(1)}, u32[]{:S(2)}, u32[]{:S(2)}) collective-permute-start(f32[136,128]{1,0:T(8,128)S(1)} %add.20.when), channel_id=1, source_target_pairs={{0,8},{1,9},{2,10},{3,11},{4,12},{5,13},{6,14},{7,15},{8,0},{9,1},... | collective-permute-start | bytes 208904 | tf_op jit(solution)/shard_map/ppermute | solution.py:478
  37.2 3.2 %shard_map.125.basis = bf16[1024,2048]{1,0:T(8,128)(2,1)S(1)} custom-call(f32[8192,128]{1,0:T(8,128)S(1)} %bitcast.13, f32[136,128]{1,0:T(8,128)S(1)} %add.20.when), custom_call_target="tpu_custom_call" | custom-call | flops 10000000 | bytes 8388608 | tf_op jit(solution)/shard_map/pallas_call | solution.py:456
  40.5 1.2 %collective-permute-done.7.other = f32[136,128]{1,0:T(8,128)S(1)} collective-permute-done((f32[136,128]{1,0:T(8,128)S(1)}, f32[136,128]{1,0:T(8,128)S(1)}, u32[]{:S(2)}, u32[]{:S(2)}) %collective-permute-start.7) | collective-permute-done | bytes 69664 | tf_op jit(solution)/shard_map/ppermute | solution.py:478
  41.7 10.2 %shard_map.126 = (f32[2048,128]{1,0:T(8,128)S(1)}, f32[16,64]{1,0:T(8,128)S(1)}) custom-call(s32[1]{0:T(128)} %bitcast.me, f32[136,128]{1,0:T(8,128)S(1)} %add.21.half, f32[136,128]{1,0:T(8,128)S(1)} %collective-permute-done.7.other, bf16[2560,512]{1,0:T(8,128)(2,1)S(1)} %get-tuple-element.41.cell_ref, bf16[640,512]{1,0:T(8,128)(2,1)S(1)} %get-tuple-element.42.slot_ref, ...), custom_call_target="tpu_custom_call" | custom-call | flops 5000000000 | bytes 10485760 | tf_op jit(solution)/shard_map/pallas_call | solution.py:456
  52.1 1.0 %collective-permute-done.8 = f32[16,64]{1,0:T(8,128)S(1)} collective-permute-done((f32[16,64]{1,0:T(8,128)S(1)}, f32[16,64]{1,0:T(8,128)S(1)}, u32[]{:S(2)}, u32[]{:S(2)}) %collective-permute-start.8) | collective-permute-done | bytes 4128 | tf_op jit(solution)/shard_map/ppermute | solution.py:478
  53.1 1.5 %collective-permute-start.9 = (f32[16,64]{1,0:T(8,128)S(1)}, f32[16,64]{1,0:T(8,128)S(1)}, u32[]{:S(2)}, u32[]{:S(2)}) collective-permute-start(f32[16,64]{1,0:T(8,128)S(1)} %add.22), channel_id=1, source_target_pairs={{0,2},{1,3},{2,0},{3,1},{4,6},{5,7},{6,4},{7,5},{8,10},{9,11},{10,... | collective-permute-start | bytes 12296 | tf_op jit(solution)/shard_map/ppermute | solution.py:478
  54.6 2.2 %collective-permute-done.9 = f32[16,64]{1,0:T(8,128)S(1)} collective-permute-done((f32[16,64]{1,0:T(8,128)S(1)}, f32[16,64]{1,0:T(8,128)S(1)}, u32[]{:S(2)}, u32[]{:S(2)}) %collective-permute-start.9) | collective-permute-done | bytes 4128 | tf_op jit(solution)/shard_map/ppermute | solution.py:478
  56.8 3.6 %collective-permute-start.12 = (f32[16,64]{1,0:T(8,128)S(1)}, f32[16,64]{1,0:T(8,128)S(1)}, u32[]{:S(2)}, u32[]{:S(2)}) collective-permute-start(f32[16,64]{1,0:T(8,128)S(1)} %add.23.rest_0_), channel_id=1, source_target_pairs={{0,12},{1,13},{2,14},{3,15},{4,8},{5,9},{6,10},{7,11},{8,4},{9,5},... | collective-permute-start | bytes 12296 | tf_op jit(solution)/shard_map/ppermute | solution.py:478
  60.4 0.8 %collective-permute-start.10 = (f32[16,64]{1,0:T(8,128)S(1)}, f32[16,64]{1,0:T(8,128)S(1)}, u32[]{:S(2)}, u32[]{:S(2)}) collective-permute-start(f32[16,64]{1,0:T(8,128)S(1)} %add.23.rest_0_), channel_id=1, source_target_pairs={{0,4},{1,5},{2,6},{3,7},{4,0},{5,1},{6,2},{7,3},{8,12},{9,13},{10,... | collective-permute-start | bytes 12296 | tf_op jit(solution)/shard_map/ppermute | solution.py:478
  61.2 1.1 %collective-permute-done.12.rest_3_ = f32[16,64]{1,0:T(8,128)S(1)} collective-permute-done((f32[16,64]{1,0:T(8,128)S(1)}, f32[16,64]{1,0:T(8,128)S(1)}, u32[]{:S(2)}, u32[]{:S(2)}) %collective-permute-start.12) | collective-permute-done | bytes 4128 | tf_op jit(solution)/shard_map/ppermute | solution.py:478
  62.2 2.7 %collective-permute-done.11.rest_2_ = f32[16,64]{1,0:T(8,128)S(1)} collective-permute-done((f32[16,64]{1,0:T(8,128)S(1)}, f32[16,64]{1,0:T(8,128)S(1)}, u32[]{:S(2)}, u32[]{:S(2)}) %collective-permute-start.11) | collective-permute-done | bytes 4128 | tf_op jit(solution)/shard_map/ppermute | solution.py:478
  65.0 2.9 %shard_map.127 = (f32[16,4,32,128]{3,2,1,0:T(8,128)}, f32[16,64]{1,0:T(8,128)}) custom-call(f32[2048,128]{1,0:T(8,128)S(1)} %get-tuple-element.50.image, bf16[1024,2048]{1,0:T(8,128)(2,1)S(1)} %shard_map.125.basis, f32[16,64]{1,0:T(8,128)S(1)} %add.23.rest_0_, f32[16,64]{1,0:T(8,128)S(1)} %collective-permute-done.10.rest_1_, ...), custom_call_target="tpu_custom_call" | custom-call | flops 200000000 | bytes 6291456 | tf_op jit(solution)/shard_map/pallas_call | solution.py:456
  (20 shorter events, 0.4 us)
Async XLA Ops:
  0.6 14.0 %copy-start.1 = (f32[128]{0:T(128)S(1)}, f32[128]{0:T(128)}, u32[]{:S(2)}) copy-start(f32[128]{0:T(128)} %param.21) | copy-start | bytes 1540
  2.7 10.4 %collective-permute-start.1 = (f32[144,128]{1,0:T(8,128)S(1)}, f32[144,128]{1,0:T(8,128)S(1)}, u32[]{:S(2)}, u32[]{:S(2)}) collective-permute-start(f32[144,128]{1,0:T(8,128)S(1)} %get-tuple-element.30.statics.own), channel_id=1, source_target_pairs={{2,0},{3,1},{4,2},{5,3},{6,4},{7,5},{8,6},{9,7},{10,8},{11,9},{12,... | collective-permute-start | bytes 221192 | tf_op jit(solution)/shard_map/ppermute | solution.py:473
  4.0 9.2 %collective-permute-start = (f32[144,128]{1,0:T(8,128)S(1)}, f32[144,128]{1,0:T(8,128)S(1)}, u32[]{:S(2)}, u32[]{:S(2)}) collective-permute-start(f32[144,128]{1,0:T(8,128)S(1)} %get-tuple-element.30.statics.own), channel_id=1, source_target_pairs={{0,2},{1,3},{2,4},{3,5},{4,6},{5,7},{6,8},{7,9},{8,10},{9,11},{10,... | collective-permute-start | bytes 221192 | tf_op jit(solution)/shard_map/ppermute | solution.py:473
  13.2 1.4 %collective-permute-start.2 = (f32[288,128]{1,0:T(8,128)S(1)}, f32[288,128]{1,0:T(8,128)S(1)}, u32[]{:S(2)}, u32[]{:S(2)}) collective-permute-start(f32[288,128]{1,0:T(8,128)S(1)} %pad_maximum_fusion), channel_id=1, source_target_pairs={{0,1},{1,0},{2,3},{3,2},{4,5},{5,4},{6,7},{7,6},{8,9},{9,8},{10,11... | collective-permute-start | bytes 442376 | tf_op jit(solution)/shard_map/ppermute | solution.py:478
  14.7 22.5 %copy-start = (f32[64,4,32,128]{3,2,1,0:T(8,128)S(1)}, f32[64,4,32,128]{3,2,1,0:T(8,128)}, u32[]{:S(2)}) copy-start(f32[64,4,32,128]{3,2,1,0:T(8,128)} %param.15) | copy-start | bytes 12582916
  23.0 1.3 %collective-permute-start.3 = (f32[136,128]{1,0:T(8,128)S(1)}, f32[136,128]{1,0:T(8,128)S(1)}, u32[]{:S(2)}, u32[]{:S(2)}) collective-permute-start(f32[136,128]{1,0:T(8,128)S(1)} %get-tuple-element.39), channel_id=1, source_target_pairs={{0,1},{1,0},{2,3},{3,2},{4,5},{5,4},{6,7},{7,6},{8,9},{9,8},{10,11... | collective-permute-start | bytes 208904 | tf_op jit(solution)/shard_map/ppermute | solution.py:478
  24.3 5.5 %collective-permute-start.4 = (f32[136,128]{1,0:T(8,128)S(1)}, f32[136,128]{1,0:T(8,128)S(1)}, u32[]{:S(2)}, u32[]{:S(2)}) collective-permute-start(f32[136,128]{1,0:T(8,128)S(1)} %add.18), channel_id=1, source_target_pairs={{0,2},{1,3},{2,0},{3,1},{4,6},{5,7},{6,4},{7,5},{8,10},{9,11},{10,... | collective-permute-start | bytes 208904 | tf_op jit(solution)/shard_map/ppermute | solution.py:478
  29.8 4.4 %collective-permute-start.5 = (f32[136,128]{1,0:T(8,128)S(1)}, f32[136,128]{1,0:T(8,128)S(1)}, u32[]{:S(2)}, u32[]{:S(2)}) collective-permute-start(f32[136,128]{1,0:T(8,128)S(1)} %add.19), channel_id=1, source_target_pairs={{0,4},{1,5},{2,6},{3,7},{4,0},{5,1},{6,2},{7,3},{8,12},{9,13},{10,... | collective-permute-start | bytes 208904 | tf_op jit(solution)/shard_map/ppermute | solution.py:478
  34.2 6.2 %collective-permute-start.6 = (f32[136,128]{1,0:T(8,128)S(1)}, f32[136,128]{1,0:T(8,128)S(1)}, u32[]{:S(2)}, u32[]{:S(2)}) collective-permute-start(f32[136,128]{1,0:T(8,128)S(1)} %add.20.when), channel_id=1, source_target_pairs={{0,8},{1,9},{2,10},{3,11},{4,12},{5,13},{6,14},{7,15},{8,0},{9,1},... | collective-permute-start | bytes 208904 | tf_op jit(solution)/shard_map/ppermute | solution.py:478
  40.4 1.3 %collective-permute-start.7 = (f32[136,128]{1,0:T(8,128)S(1)}, f32[136,128]{1,0:T(8,128)S(1)}, u32[]{:S(2)}, u32[]{:S(2)}) collective-permute-start(f32[136,128]{1,0:T(8,128)S(1)} %add.21.half), channel_id=1, source_target_pairs={{0,1},{1,0},{2,3},{3,2},{4,5},{5,4},{6,7},{7,6},{8,9},{9,8},{10,11... | collective-permute-start | bytes 208904 | tf_op jit(solution)/shard_map/ppermute | solution.py:478
  52.0 1.2 %collective-permute-start.8 = (f32[16,64]{1,0:T(8,128)S(1)}, f32[16,64]{1,0:T(8,128)S(1)}, u32[]{:S(2)}, u32[]{:S(2)}) collective-permute-start(f32[16,64]{1,0:T(8,128)S(1)} %get-tuple-element.51), channel_id=1, source_target_pairs={{0,1},{1,0},{2,3},{3,2},{4,5},{5,4},{6,7},{7,6},{8,9},{9,8},{10,11... | collective-permute-start | bytes 12296 | tf_op jit(solution)/shard_map/ppermute | solution.py:478
  53.1 3.7 %collective-permute-start.9 = (f32[16,64]{1,0:T(8,128)S(1)}, f32[16,64]{1,0:T(8,128)S(1)}, u32[]{:S(2)}, u32[]{:S(2)}) collective-permute-start(f32[16,64]{1,0:T(8,128)S(1)} %add.22), channel_id=1, source_target_pairs={{0,2},{1,3},{2,0},{3,1},{4,6},{5,7},{6,4},{7,5},{8,10},{9,11},{10,... | collective-permute-start | bytes 12296 | tf_op jit(solution)/shard_map/ppermute | solution.py:478
  56.8 5.4 %collective-permute-start.12 = (f32[16,64]{1,0:T(8,128)S(1)}, f32[16,64]{1,0:T(8,128)S(1)}, u32[]{:S(2)}, u32[]{:S(2)}) collective-permute-start(f32[16,64]{1,0:T(8,128)S(1)} %add.23.rest_0_), channel_id=1, source_target_pairs={{0,12},{1,13},{2,14},{3,15},{4,8},{5,9},{6,10},{7,11},{8,4},{9,5},... | collective-permute-start | bytes 12296 | tf_op jit(solution)/shard_map/ppermute | solution.py:478
  60.4 4.5 %collective-permute-start.11 = (f32[16,64]{1,0:T(8,128)S(1)}, f32[16,64]{1,0:T(8,128)S(1)}, u32[]{:S(2)}, u32[]{:S(2)}) collective-permute-start(f32[16,64]{1,0:T(8,128)S(1)} %add.23.rest_0_), channel_id=1, source_target_pairs={{0,8},{1,9},{2,10},{3,11},{4,12},{5,13},{6,14},{7,15},{8,0},{9,1},... | collective-permute-start | bytes 12296 | tf_op jit(solution)/shard_map/ppermute | solution.py:478
  60.4 4.5 %collective-permute-start.10 = (f32[16,64]{1,0:T(8,128)S(1)}, f32[16,64]{1,0:T(8,128)S(1)}, u32[]{:S(2)}, u32[]{:S(2)}) collective-permute-start(f32[16,64]{1,0:T(8,128)S(1)} %add.23.rest_0_), channel_id=1, source_target_pairs={{0,4},{1,5},{2,6},{3,7},{4,0},{5,1},{6,2},{7,3},{8,12},{9,13},{10,... | collective-permute-start | bytes 12296 | tf_op jit(solution)/shard_map/ppermute | solution.py:478

commit v5 on v4

--- a/solution.py
+++ b/solution.py
@@ -26,7 +26,18 @@
 
 
 def at(row, count=16):
-    return pl.ds(pl.multiple_of(row, 16), count)
+    return pl.ds(pl.multiple_of(row, 8), count)
+
+
+def kept_rows(load):
+    rows = {}
+
+    def get(layer, y):
+        if (layer, y) not in rows:
+            rows[layer, y] = load(layer, y)
+        return rows[layer, y]
+
+    return get
 
 
 def spread(ref, row, fields):
@@ -122,33 +133,34 @@
         along_z(field, 0, fields, band_ref, z_term)
 
         def body(chunk, carry):
-            for x in range(LAYERS):
-                for step in range(8):
-                    y = chunk * 8 + step
-                    cell = x * 32 + y
-
-                    def get(layer, row):
-                        return field[at((layer * PADDED + REACH + row) * fields, fields), :]
-
-                    z_part = z_term[at(cell * fields, fields), :]
-                    total = laplacian(get, x, y, z_part, 0, LAYERS - 1)
-                    emit(x, y, get(x, y), spread(statics, cell, fields) * total)
+            for part in range(0, fields, 8):
+
+                def load(layer, y):
+                    return field[at((layer * PADDED + REACH + chunk * 8 + y) * fields + part, 8), :]
+
+                get = kept_rows(load)
+                for y in range(8):
+                    for x in range(LAYERS):
+                        cell = x * 32 + chunk * 8 + y
+                        z_part = z_term[at(cell * fields + part, 8), :]
+                        total = laplacian(get, x, y, z_part, 0, LAYERS - 1)
+                        emit(x, chunk * 8 + y, part, get(x, y), spread(statics, cell, 8) * total)
             return carry
 
         lax.fori_loop(0, 4, body, 0)
 
-    def step_one(x, y, now, change):
+    def step_one(x, y, part, now, change):
         cell = x * 32 + y
-        push = turned[at(cell * fields, fields), :] * spread(sources, 128 + cell, fields)
-        second[at((x * PADDED + REACH + y) * fields, fields), :] = 2.0 * now + change + push
+        push = turned[at(cell * fields + part, 8), :] * spread(sources, 128 + cell, 8)
+        second[at((x * PADDED + REACH + y) * fields + part, 8), :] = 2.0 * now + change + push
 
     sweep(first, step_one)
 
-    def step_two(x, y, now, change):
+    def step_two(x, y, part, now, change):
         cell = x * 32 + y
-        push = turned[at(cell * fields, fields), :] * spread(sources, 256 + cell, fields)
-        before = first[at((x * PADDED + REACH + y) * fields, fields), :]
-        third[at(cell * fields, fields), :] = 2.0 * now - before + change + push
+        push = turned[at(cell * fields + part, 8), :] * spread(sources, 256 + cell, 8)
+        before = first[at((x * PADDED + REACH + y) * fields + part, 8), :]
+        third[at(cell * fields + part, 8), :] = 2.0 * now - before + change + push
 
     sweep(second, step_two)
 
@@ -158,7 +170,7 @@
 
 
 def forward_window(
-    fields, peers, me, first, second, third, own, partner, before, after, band_ref, own_scale,
+    fields, peers, me, first, second, third, own, partner, passed, across, band_ref, own_scale,
     kept, sent, cell_ref, slot_ref, speed_ref, line_ref, owner_ref, weight_ref,
     below, above, z_term, total_ref, table, *samples,
 ):
@@ -169,12 +181,13 @@
     clear_margins(below, LAYERS, fields)
     clear_margins(above, LAYERS, fields)
     total_ref[...] = jnp.zeros_like(total_ref)
+    near, next_one, far_one, side_one = passed[0:length, :], passed[length:, :], across[...], partner[...]
     tiles = (
-        before[...],
-        jnp.where(odd, partner[0:length, :], partner[length:, :]),
+        jnp.where(odd, far_one, next_one),
+        jnp.where(odd, side_one, near),
         own[...],
-        jnp.where(odd, partner[length:, :], partner[0:length, :]),
-        after[...],
+        jnp.where(odd, near, side_one),
+        jnp.where(odd, next_one, far_one),
     )
     place = lax.broadcasted_iota(jnp.int32, (PLACES, entries), 0)
     slot_place = lax.broadcasted_iota(jnp.int32, (HALF, entries), 0)
@@ -209,11 +222,7 @@
     along_z(below, 0, fields, band_ref, z_term, 0)
     along_z(above, 0, fields, band_ref, z_term, cells * fields)
 
-    def read(layer, y):
-        ref = (below, second, above)[(layer + LAYERS) // LAYERS]
-        return ref[at((layer % LAYERS * PADDED + REACH + y) * fields, fields), :]
-
-    def far(x, y, lowest, highest):
+    def far(read, x, y, lowest, highest):
         total = None
         for other in range(lowest, highest + 1):
             if 1 <= abs(x - other) <= REACH:
@@ -224,28 +233,31 @@
     def respond(chunk, carry):
         for tile in range(5):
             sample = samples[tile]
-            for x in range(LAYERS):
-                for step in range(8):
-                    y = chunk * 8 + step
-                    cell = x * 32 + y
-                    layer = (tile - 2) * LAYERS + x
-                    speed = spread(speed_ref, tile * cells + cell, fields)
-                    if tile in (0, 4):
-                        value = speed * far(layer, y, -4, 7)
-                    elif tile == 2:
-                        outside = far(layer, y, -4, -1) + far(layer, y, 4, 7)
-                        value = third[at(cell * fields, fields), :] + speed * outside
-                    else:
-                        z_part = z_term[at((tile // 2 * cells + cell) * fields, fields), :]
-                        value = 2.0 * read(layer, y) + speed * laplacian(read, layer, y, z_part, -4, 7)
-                    row = (x * 2 + step // 4) * fields
-                    side = step % 4 * HALF
-                    high, low = split(value)
-                    sample[row : row + fields, side : side + HALF] = high
-                    row = row + 8 * fields
-                    sample[row : row + fields, side : side + HALF] = low
+            for part in range(0, fields, 8):
+
+                def load(layer, y):
+                    ref = (below, second, above)[(layer + LAYERS) // LAYERS]
+                    return ref[at((layer % LAYERS * PADDED + REACH + chunk * 8 + y) * fields + part, 8), :]
+
+                read = kept_rows(load)
+                for y in range(8):
+                    for x in range(LAYERS):
+                        cell = x * 32 + chunk * 8 + y
+                        layer = (tile - 2) * LAYERS + x
+                        speed = spread(speed_ref, tile * cells + cell, 8)
+                        if tile in (0, 4):
+                            value = speed * far(read, layer, y, -4, 7)
+                        elif tile == 2:
+                            outside = far(read, layer, y, -4, -1) + far(read, layer, y, 4, 7)
+                            value = third[at(cell * fields + part, 8), :] + speed * outside
+                        else:
+                            z_part = z_term[at((tile // 2 * cells + cell) * fields + part, 8), :]
+                            value = 2.0 * read(layer, y) + speed * laplacian(read, layer, y, z_part, -4, 7)
+                        row = (x * 2 + y // 4) * fields + part
+                        side = y % 4 * HALF
+                        sample[row : row + 8, side : side + HALF] = value
             hot = cell_ref[tile * PLACES : (tile + 1) * PLACES, :]
-            picked = jnp.dot(sample[...], hot, preferred_element_type=F32)
+            picked = jnp.dot(jnp.concatenate(split(sample[...]), axis=0), hot, preferred_element_type=F32)
             picked = picked[: 8 * fields, :] + picked[8 * fields :, :]
             for part in range(fields // 8):
                 rows = slice(tile * fields + part * 8, tile * fields + part * 8 + 8)
@@ -358,46 +370,51 @@
 
     def step_one(index, carry):
         tile, chunk = index // 4 + 1, index % 4
+        for part in range(0, fields, 8):
+
+            def load(layer, y):
+                row = (tile * LAYERS + layer) * PADDED + REACH + chunk * 8 + y
+                return inner_two[at(row * fields + part, 8), :]
+
+            get = kept_rows(load)
+            for y in range(8):
+                for x in range(LAYERS):
+                    layer = tile * LAYERS + x
+                    speed = spread(speed_ref, layer * 32 + chunk * 8 + y, 8)
+                    layer = layer - LAYERS
+                    row = at((layer * 32 + chunk * 8 + y) * fields + part, 8)
+                    now = 2.0 * outer_two[row, :] + laplacian(get, x, y, z_term[row, :], -4, 7)
+                    outer_one[row, :] = now
+                    inner_one[at((layer * PADDED + REACH + chunk * 8 + y) * fields + part, 8), :] = speed * now
+        return carry
+
+    lax.fori_loop(0, 12, step_one, 0)
+    along_z(inner_one, LAYERS, fields, band_ref, z_term)
+
+    def step_two(chunk, total):
+        for part in range(0, fields, 8):
+
+            def load(layer, y):
+                row = (LAYERS + layer) * PADDED + REACH + chunk * 8 + y
+                return inner_one[at(row * fields + part, 8), :]
+
+            get = kept_rows(load)
+            for y in range(8):
+                for x in range(LAYERS):
+                    cell = x * 32 + chunk * 8 + y
+                    row = at(cell * fields + part, 8)
+                    own_row = at((cells + cell) * fields + part, 8)
+                    two = outer_two[own_row, :]
+                    one = outer_one[own_row, :]
+                    zero = 2.0 * one - two + laplacian(get, x, y, z_term[row, :], -4, 7)
+                    value = spread(sources, cell, 8) * zero
+                    value = value + spread(sources, 128 + cell, 8) * one
+                    value = value + spread(sources, 256 + cell, 8) * two
+                    image[row, :] = value + spread(prior, cell, 8) * turned[row, :]
         for x in range(LAYERS):
-            for step in range(8):
-                y = chunk * 8 + step
-
-                def get(layer, row):
-                    return inner_two[at(((tile * LAYERS + layer) * PADDED + REACH + row) * fields, fields), :]
-
-                layer = tile * LAYERS + x
-                speed = spread(speed_ref, layer * 32 + y, fields)
-                layer = layer - LAYERS
-                now = 2.0 * outer_two[at((layer * 32 + y) * fields, fields), :]
-                z_part = z_term[at((layer * 32 + y) * fields, fields), :]
-                now = now + laplacian(get, x, y, z_part, -4, 7)
-                outer_one[at((layer * 32 + y) * fields, fields), :] = now
-                inner_one[at((layer * PADDED + REACH + y) * fields, fields), :] = speed * now
-        return carry
-
-    lax.fori_loop(0, 12, step_one, 0)
-
-    def get_one(layer, row):
-        return inner_one[at(((LAYERS + layer) * PADDED + REACH + row) * fields, fields), :]
-
-    along_z(inner_one, LAYERS, fields, band_ref, z_term)
-
-    def step_two(chunk, total):
-        for x in range(LAYERS):
-            for step in range(8):
-                y = chunk * 8 + step
-                cell = x * 32 + y
-                z_part = z_term[at(cell * fields, fields), :]
-                two = outer_two[at((LAYERS * 32 + cell) * fields, fields), :]
-                one = outer_one[at((LAYERS * 32 + cell) * fields, fields), :]
-                zero = 2.0 * one - two + laplacian(get_one, x, y, z_part, -4, 7)
-                value = spread(sources, cell, fields) * zero
-                value = value + spread(sources, 128 + cell, fields) * one
-                value = value + spread(sources, 256 + cell, fields) * two
-                value = value + spread(prior, cell, fields) * turned[at(cell * fields, fields), :]
-                image[at(cell * fields, fields), :] = value
-                high, low = split(value)
-                side = step * 256
+            for y in range(8):
+                high, low = split(image[at((x * 32 + chunk * 8 + y) * fields, fields), :])
+                side = y * 256
                 rows = slice(x * 2 * fields, x * 2 * fields + fields)
                 image_parts[rows, side : side + HALF] = high
                 image_parts[rows, side + HALF : side + 256] = high
@@ -427,20 +444,17 @@
     def leave(x):
         return pltpu.make_async_copy(whole.at[:, x], out.at[:, x], sem.at[x])
 
-    def body(x, carry):
+    for x in range(LAYERS):
         for part in range(4):
-            columns = basis[at((x * 4 + part) * rank, rank), :]
+            columns = basis[(x * 4 + part) * rank : (x * 4 + part + 1) * rank, :]
             both = jnp.dot(parts, columns, preferred_element_type=F32)
             for step in range(8):
                 cell = x * 32 + part * 8 + step
                 side = step * 256
                 along = both[:fields, side : side + HALF] + both[:fields, side + HALF : side + 256]
                 along = along + both[fields:, side : side + HALF]
-                natural[pl.ds(cell, fields, stride=HALF), :] = image[at(cell * fields, fields), :] - along
+                natural[pl.ds(cell, fields, stride=HALF), :] = image[cell * fields : (cell + 1) * fields, :] - along
         leave(x).start()
-        return carry
-
-    lax.fori_loop(0, LAYERS, body, 0)
     for x in range(LAYERS):
         leave(x).wait()
 
@@ -466,11 +480,6 @@
 
 def struct(*shape, dtype=F32):
     return jax.ShapeDtypeStruct(shape, dtype)
-
-
-def shifted(array, axis, by):
-    count = lax.axis_size(axis)
-    return lax.ppermute(array, axis, [(i, i + by) for i in range(count) if 0 <= i + by < count])
 
 
 def swapped(array, axis, bits):
@@ -525,8 +534,12 @@
         scalars=1,
         far=8,
     )
-    before = shifted(own, "space", 2)
-    after = shifted(own, "space", -2)
+    partner = swapped(own, "space", 1)
+    passed = lax.ppermute(
+        jnp.concatenate([own, partner], axis=0),
+        "space",
+        [pair for i in range(1, peers - 1, 2) for pair in ((i, i + 1), (i + 1, i))],
+    )
 
     turned, first, second, third = call(
         functools.partial(forward_own, fields),
@@ -537,12 +550,11 @@
         6 * 2**20,
     )
     half_rows = peers // 2 * (fields + 1)
-    before, after, second = lax.optimization_barrier((before, after, second))
-    relayed = jnp.where(jnp.bitwise_and(me, 1)[0] == 1, before, after)
-    partner = swapped(jnp.concatenate([own, relayed], axis=0), "space", 1)
+    passed, second = lax.optimization_barrier((passed, second))
+    across = swapped(passed[: own.shape[0]], "space", 1)
     kept, sent, cell_hot, slot_hot, speed, line, owner, weight = call(
         functools.partial(forward_window, fields, peers),
-        (me, first, second, third, own, partner, before, after, matrix, trace_weight.reshape(1, HALF)),
+        (me, first, second, third, own, partner, passed, across, matrix, trace_weight.reshape(1, HALF)),
         [
             struct(half_rows, HALF),
             struct(half_rows, HALF),
@@ -560,7 +572,7 @@
             pltpu.VMEM((5 * fields, entries), F32),
             pltpu.VMEM((peers * fields, HALF), F32),
         ]
-        + [pltpu.VMEM((16 * fields, PLACES), BF16)] * 5,
+        + [pltpu.VMEM((8 * fields, PLACES), F32)] * 5,
         3_000_000_000,
         6 * 2**20,
         scalars=1,

time: 68.1 us -> 68.4 us (level)
  starting transfers between devices: 21.1 us -> 17.9 us
  local copies, waits for them, and re-layouts: 0.01 us -> 3.2 us
  waiting for transfers between devices: 15.6 us -> 16.6 us
  Pallas kernels: 29.7 us -> 29 us
    ppermute x2 -> x1, starting transfers between devices: 6.8 us -> 0.67 us  [local(): lax.ppermute(jnp.concatenate([own, partner], axis=0), 'space', [pair for...]
    unnamed x4 -> x12, local copies, waits for them, and re-layouts: 0.01 us -> 3.19 us
    ppermute x11 -> x12, starting transfers between devices: 14.3 us -> 17.2 us  [swapped(): return lax.ppermute(array, axis, [(i, i ^ bits) for i in range(count)])]
    ppermute x11 -> x12, waiting for transfers between devices: 15.6 us -> 16.6 us  [swapped(): return lax.ppermute(array, axis, [(i, i ^ bits) for i in range(count)])]
  transfers between devices with their start and end apart: 13 -> 13, of which waited for: 9 -> 10; matrix products, arithmetic and copies ran while one was open for 0% -> 0% of each run, Pallas kernels for 10% -> 10%
where the time goes in v5:
time: 68.4 us; the launch traced here: 68.2 us
  Pallas kernels  29 us (42%)
  starting transfers between devices  17.9 us (26%)
  waiting for transfers between devices  16.6 us (24%)
  local copies, waits for them, and re-layouts  3.2 us (5%)
  between operations  1.4 us (2%)
    pallas_call x6, Pallas kernels, call(): pl.pallas_call(kernel, out_shape=out_shape, in_specs=[smem] * scalars + [...  29 us
    ppermute x12, starting transfers between devices, swapped(): return lax.ppermute(array, axis, [(i, i ^ bits) for i in range(count)])  17.2 us
    ppermute x12, waiting for transfers between devices, swapped(): return lax.ppermute(array, axis, [(i, i ^ bits) for i in range(count)])  16.6 us
    unnamed x12, local copies, waits for them, and re-layouts  3.19 us
  transfers between devices with their start and end apart: 13, of which 10 were waited for; matrix products, arithmetic and copies ran while one was open for 0% of the time, Pallas kernels for 10%

profile of v5, /device:TPU:0, one launch (start us, length us, event | category | flops | bytes accessed | tf_op | source)
XLA Modules:
  0.0 68.2 jit_solution(17831644717345465502)
XLA Ops:
  1.3 1.4 %shard_map.122 = (f32[144,128]{1,0:T(8,128)S(1)}, f32[2048,128]{1,0:T(8,128)S(1)}, f32[384,128]{1,0:T(8,128)S(1)}, f32[128,128]{1,0:T(8,128)S(1)}, bf16[256,256]{1,0:T(8,128)(2,1)S(1)}) custom-call(s32[1]{0:T(128)S(6)} %copy.13.count, f32[2048,128]{1,0:T(8,128)} %bitcast.14, f32[384,128]{1,0:T(8,128)} %bitcast.15, f32[128,128]{1,0:T(8,128)} %bitcast.16, ...), custom_call_target="tpu_custom_call" | custom-call | flops 100000 | bytes 2097152 | tf_op jit(solution)/shard_map/pallas_call | solution.py:470
  3.2 0.9 %collective-permute-done.partner = f32[144,128]{1,0:T(8,128)S(1)} collective-permute-done((f32[144,128]{1,0:T(8,128)S(1)}, f32[144,128]{1,0:T(8,128)S(1)}, u32[]{:S(2)}, u32[]{:S(2)}) %collective-permute-start) | collective-permute-done | bytes 73760 | tf_op jit(solution)/shard_map/ppermute | solution.py:487
  4.9 3.7 %shard_map.123 = (f32[2048,128]{1,0:T(8,128)S(1)}, f32[2560,128]{1,0:T(8,128)S(1)}, f32[2560,128]{1,0:T(8,128)S(1)}, f32[2048,128]{1,0:T(8,128)S(1)}) custom-call(f32[2048,128]{1,0:T(8,128)S(1)} %get-tuple-element.27.probes, f32[384,128]{1,0:T(8,128)S(1)} %get-tuple-element.28.sources, f32[144,128]{1,0:T(8,128)S(1)} %get-tuple-element.29.statics.own, ...), custom_call_target="tpu_custom_call" | custom-call | flops 600000000 | bytes 6291456 | tf_op jit(solution)/shard_map/pallas_call | solution.py:470
  8.6 1.0 %copy-done.2 = f32[2048,128]{1,0:T(8,128)} copy-done((f32[2048,128]{1,0:T(8,128)}, f32[2048,128]{1,0:T(8,128)S(1)}, u32[]{:S(2)}) %copy-start.2) | copy-done | bytes 1048600
  9.6 1.0 %copy-done.4 = f32[2048,128]{1,0:T(8,128)} copy-done((f32[2048,128]{1,0:T(8,128)}, f32[2048,128]{1,0:T(8,128)S(1)}, u32[]{:S(2)}) %copy-start.4) | copy-done | bytes 1048600
  10.5 4.3 %collective-permute-start.2 = (f32[144,128]{1,0:T(8,128)S(1)}, f32[144,128]{1,0:T(8,128)S(1)}, u32[]{:S(2)}, u32[]{:S(2)}) collective-permute-start(f32[144,128]{1,0:T(8,128)S(1)} %slice.3), channel_id=1, source_target_pairs={{0,1},{1,0},{2,3},{3,2},{4,5},{5,4},{6,7},{7,6},{8,9},{9,8},{10,11... | collective-permute-start | bytes 221192 | tf_op jit(solution)/shard_map/ppermute | solution.py:487
  14.8 0.9 %collective-permute-done.2.across = f32[144,128]{1,0:T(8,128)S(1)} collective-permute-done((f32[144,128]{1,0:T(8,128)S(1)}, f32[144,128]{1,0:T(8,128)S(1)}, u32[]{:S(2)}, u32[]{:S(2)}) %collective-permute-start.2) | collective-permute-done | bytes 73760 | tf_op jit(solution)/shard_map/ppermute | solution.py:487
  15.7 1.2 %copy-done.5 = f32[2048,128]{1,0:T(8,128)S(1)} copy-done((f32[2048,128]{1,0:T(8,128)S(1)}, f32[2048,128]{1,0:T(8,128)}, u32[]{:S(2)}) %copy-start.5) | copy-done | bytes 1048600
  17.0 7.9 %shard_map.124 = (f32[136,128]{1,0:T(8,128)S(1)}, f32[136,128]{1,0:T(8,128)S(1)}, bf16[2560,512]{1,0:T(8,128)(2,1)S(1)}, bf16[640,512]{1,0:T(8,128)(2,1)S(1)}, f...) custom-call(s32[1]{0:T(128)} %bitcast.me, ...), custom_call_target="tpu_custom_call" | custom-call | flops 3000000000 | bytes 6291456 | tf_op jit(solution)/shard_map/pallas_call | solution.py:470
  26.2 1.6 %collective-permute-start.4 = (f32[136,128]{1,0:T(8,128)S(1)}, f32[136,128]{1,0:T(8,128)S(1)}, u32[]{:S(2)}, u32[]{:S(2)}) collective-permute-start(f32[136,128]{1,0:T(8,128)S(1)} %add.18), channel_id=1, source_target_pairs={{0,2},{1,3},{2,0},{3,1},{4,6},{5,7},{6,4},{7,5},{8,10},{9,11},{10,... | collective-permute-start | bytes 208904 | tf_op jit(solution)/shard_map/ppermute | solution.py:487
  27.8 2.9 %collective-permute-done.4 = f32[136,128]{1,0:T(8,128)S(1)} collective-permute-done((f32[136,128]{1,0:T(8,128)S(1)}, f32[136,128]{1,0:T(8,128)S(1)}, u32[]{:S(2)}, u32[]{:S(2)}) %collective-permute-start.4) | collective-permute-done | bytes 69664 | tf_op jit(solution)/shard_map/ppermute | solution.py:487
  30.7 1.6 %collective-permute-start.5 = (f32[136,128]{1,0:T(8,128)S(1)}, f32[136,128]{1,0:T(8,128)S(1)}, u32[]{:S(2)}, u32[]{:S(2)}) collective-permute-start(f32[136,128]{1,0:T(8,128)S(1)} %add.19), channel_id=1, source_target_pairs={{0,4},{1,5},{2,6},{3,7},{4,0},{5,1},{6,2},{7,3},{8,12},{9,13},{10,... | collective-permute-start | bytes 208904 | tf_op jit(solution)/shard_map/ppermute | solution.py:487
  32.4 2.7 %collective-permute-done.5 = f32[136,128]{1,0:T(8,128)S(1)} collective-permute-done((f32[136,128]{1,0:T(8,128)S(1)}, f32[136,128]{1,0:T(8,128)S(1)}, u32[]{:S(2)}, u32[]{:S(2)}) %collective-permute-start.5) | collective-permute-done | bytes 69664 | tf_op jit(solution)/shard_map/ppermute | solution.py:487
  35.1 2.6 %collective-permute-start.6 = (f32[136,128]{1,0:T(8,128)S(1)}, f32[136,128]{1,0:T(8,128)S(1)}, u32[]{:S(2)}, u32[]{:S(2)}) collective-permute-start(f32[136,128]{1,0:T(8,128)S(1)} %add.20.when), channel_id=1, source_target_pairs={{0,8},{1,9},{2,10},{3,11},{4,12},{5,13},{6,14},{7,15},{8,0},{9,1},... | collective-permute-start | bytes 208904 | tf_op jit(solution)/shard_map/ppermute | solution.py:487
  37.8 3.2 %shard_map.125.basis = bf16[1024,2048]{1,0:T(8,128)(2,1)S(1)} custom-call(f32[8192,128]{1,0:T(8,128)S(1)} %bitcast.12, f32[136,128]{1,0:T(8,128)S(1)} %add.20.when), custom_call_target="tpu_custom_call" | custom-call | flops 10000000 | bytes 8388608 | tf_op jit(solution)/shard_map/pallas_call | solution.py:470
  41.1 1.2 %collective-permute-done.7.other = f32[136,128]{1,0:T(8,128)S(1)} collective-permute-done((f32[136,128]{1,0:T(8,128)S(1)}, f32[136,128]{1,0:T(8,128)S(1)}, u32[]{:S(2)}, u32[]{:S(2)}) %collective-permute-start.7) | collective-permute-done | bytes 69664 | tf_op jit(solution)/shard_map/ppermute | solution.py:487
  42.3 10.4 %shard_map.126 = (f32[2048,128]{1,0:T(8,128)S(1)}, f32[16,64]{1,0:T(8,128)S(1)}) custom-call(s32[1]{0:T(128)} %bitcast.me, f32[136,128]{1,0:T(8,128)S(1)} %add.21.half, f32[136,128]{1,0:T(8,128)S(1)} %collective-permute-done.7.other, bf16[2560,512]{1,0:T(8,128)(2,1)S(1)} %get-tuple-element.39.cell_ref, bf16[640,512]{1,0:T(8,128)(2,1)S(1)} %get-tuple-element.40.slot_ref, ...), custom_call_target="tpu_custom_call" | custom-call | flops 5000000000 | bytes 10485760 | tf_op jit(solution)/shard_map/pallas_call | solution.py:470
  52.9 1.0 %collective-permute-done.8 = f32[16,64]{1,0:T(8,128)S(1)} collective-permute-done((f32[16,64]{1,0:T(8,128)S(1)}, f32[16,64]{1,0:T(8,128)S(1)}, u32[]{:S(2)}, u32[]{:S(2)}) %collective-permute-start.8) | collective-permute-done | bytes 4128 | tf_op jit(solution)/shard_map/ppermute | solution.py:487
  53.9 1.5 %collective-permute-start.9 = (f32[16,64]{1,0:T(8,128)S(1)}, f32[16,64]{1,0:T(8,128)S(1)}, u32[]{:S(2)}, u32[]{:S(2)}) collective-permute-start(f32[16,64]{1,0:T(8,128)S(1)} %add.22), channel_id=1, source_target_pairs={{0,2},{1,3},{2,0},{3,1},{4,6},{5,7},{6,4},{7,5},{8,10},{9,11},{10,... | collective-permute-start | bytes 12296 | tf_op jit(solution)/shard_map/ppermute | solution.py:487
  55.4 2.1 %collective-permute-done.9 = f32[16,64]{1,0:T(8,128)S(1)} collective-permute-done((f32[16,64]{1,0:T(8,128)S(1)}, f32[16,64]{1,0:T(8,128)S(1)}, u32[]{:S(2)}, u32[]{:S(2)}) %collective-permute-start.9) | collective-permute-done | bytes 4128 | tf_op jit(solution)/shard_map/ppermute | solution.py:487
  57.5 3.7 %collective-permute-start.12 = (f32[16,64]{1,0:T(8,128)S(1)}, f32[16,64]{1,0:T(8,128)S(1)}, u32[]{:S(2)}, u32[]{:S(2)}) collective-permute-start(f32[16,64]{1,0:T(8,128)S(1)} %add.23.rest_0_), channel_id=1, source_target_pairs={{0,12},{1,13},{2,14},{3,15},{4,8},{5,9},{6,10},{7,11},{8,4},{9,5},... | collective-permute-start | bytes 12296 | tf_op jit(solution)/shard_map/ppermute | solution.py:487
  61.9 1.1 %collective-permute-done.12.rest_3_ = f32[16,64]{1,0:T(8,128)S(1)} collective-permute-done((f32[16,64]{1,0:T(8,128)S(1)}, f32[16,64]{1,0:T(8,128)S(1)}, u32[]{:S(2)}, u32[]{:S(2)}) %collective-permute-start.12) | collective-permute-done | bytes 4128 | tf_op jit(solution)/shard_map/ppermute | solution.py:487
  63.0 2.8 %collective-permute-done.11.rest_2_ = f32[16,64]{1,0:T(8,128)S(1)} collective-permute-done((f32[16,64]{1,0:T(8,128)S(1)}, f32[16,64]{1,0:T(8,128)S(1)}, u32[]{:S(2)}, u32[]{:S(2)}) %collective-permute-start.11) | collective-permute-done | bytes 4128 | tf_op jit(solution)/shard_map/ppermute | solution.py:487
  65.7 2.4 %shard_map.127 = (f32[16,4,32,128]{3,2,1,0:T(8,128)}, f32[16,64]{1,0:T(8,128)}) custom-call(f32[2048,128]{1,0:T(8,128)S(1)} %get-tuple-element.48.image, bf16[1024,2048]{1,0:T(8,128)(2,1)S(1)} %shard_map.125.basis, f32[16,64]{1,0:T(8,128)S(1)} %add.23.rest_0_, f32[16,64]{1,0:T(8,128)S(1)} %collective-permute-done.10.rest_1_, ...), custom_call_target="tpu_custom_call" | custom-call | flops 200000000 | bytes 6291456 | tf_op jit(solution)/shard_map/pallas_call | solution.py:470
  (28 shorter events, 3.6 us)
Async XLA Ops:
  0.6 15.1 %copy-start.1 = (f32[128]{0:T(128)S(1)}, f32[128]{0:T(128)}, u32[]{:S(2)}) copy-start(f32[128]{0:T(128)} %param.21) | copy-start | bytes 1540
  2.7 1.4 %collective-permute-start = (f32[144,128]{1,0:T(8,128)S(1)}, f32[144,128]{1,0:T(8,128)S(1)}, u32[]{:S(2)}, u32[]{:S(2)}) collective-permute-start(f32[144,128]{1,0:T(8,128)S(1)} %get-tuple-element.29.statics.own), channel_id=1, source_target_pairs={{0,1},{1,0},{2,3},{3,2},{4,5},{5,4},{6,7},{7,6},{8,9},{9,8},{10,11... | collective-permute-start | bytes 221192 | tf_op jit(solution)/shard_map/ppermute | solution.py:487
  4.2 6.4 %collective-permute-start.1 = (f32[288,128]{1,0:T(8,128)S(1)}, f32[288,128]{1,0:T(8,128)S(1)}, u32[]{:S(2)}, u32[]{:S(2)}) collective-permute-start(f32[288,128]{1,0:T(8,128)S(1)} %pad_maximum_fusion), channel_id=1, source_target_pairs={{1,2},{2,1},{3,4},{4,3},{5,6},{6,5},{7,8},{8,7},{9,10},{10,9},{11,... | collective-permute-start | bytes 442376 | tf_op jit(solution)/shard_map/ppermute | solution.py:538
  8.6 1.0 %copy-start.2 = (f32[2048,128]{1,0:T(8,128)}, f32[2048,128]{1,0:T(8,128)S(1)}, u32[]{:S(2)}) copy-start(f32[2048,128]{1,0:T(8,128)S(1)} %get-tuple-element.45.turned) | copy-start | bytes 3145732
  9.6 1.0 %copy-start.4 = (f32[2048,128]{1,0:T(8,128)}, f32[2048,128]{1,0:T(8,128)S(1)}, u32[]{:S(2)}) copy-start(f32[2048,128]{1,0:T(8,128)S(1)} %get-tuple-element.34.third) | copy-start | bytes 3145732
  10.5 5.2 %collective-permute-start.2 = (f32[144,128]{1,0:T(8,128)S(1)}, f32[144,128]{1,0:T(8,128)S(1)}, u32[]{:S(2)}, u32[]{:S(2)}) collective-permute-start(f32[144,128]{1,0:T(8,128)S(1)} %slice.3), channel_id=1, source_target_pairs={{0,1},{1,0},{2,3},{3,2},{4,5},{5,4},{6,7},{7,6},{8,9},{9,8},{10,11... | collective-permute-start | bytes 221192 | tf_op jit(solution)/shard_map/ppermute | solution.py:487
  15.7 1.2 %copy-start.5 = (f32[2048,128]{1,0:T(8,128)S(1)}, f32[2048,128]{1,0:T(8,128)}, u32[]{:S(2)}) copy-start(f32[2048,128]{1,0:T(8,128)} %copy-done.4) | copy-start | bytes 3145732
  17.0 20.8 %copy-start = (f32[64,4,32,128]{3,2,1,0:T(8,128)S(1)}, f32[64,4,32,128]{3,2,1,0:T(8,128)}, u32[]{:S(2)}) copy-start(f32[64,4,32,128]{3,2,1,0:T(8,128)} %param.15) | copy-start | bytes 12582916
  24.9 1.3 %collective-permute-start.3 = (f32[136,128]{1,0:T(8,128)S(1)}, f32[136,128]{1,0:T(8,128)S(1)}, u32[]{:S(2)}, u32[]{:S(2)}) collective-permute-start(f32[136,128]{1,0:T(8,128)S(1)} %get-tuple-element.37), channel_id=1, source_target_pairs={{0,1},{1,0},{2,3},{3,2},{4,5},{5,4},{6,7},{7,6},{8,9},{9,8},{10,11... | collective-permute-start | bytes 208904 | tf_op jit(solution)/shard_map/ppermute | solution.py:487
  26.2 4.5 %collective-permute-start.4 = (f32[136,128]{1,0:T(8,128)S(1)}, f32[136,128]{1,0:T(8,128)S(1)}, u32[]{:S(2)}, u32[]{:S(2)}) collective-permute-start(f32[136,128]{1,0:T(8,128)S(1)} %add.18), channel_id=1, source_target_pairs={{0,2},{1,3},{2,0},{3,1},{4,6},{5,7},{6,4},{7,5},{8,10},{9,11},{10,... | collective-permute-start | bytes 208904 | tf_op jit(solution)/shard_map/ppermute | solution.py:487
  30.7 4.4 %collective-permute-start.5 = (f32[136,128]{1,0:T(8,128)S(1)}, f32[136,128]{1,0:T(8,128)S(1)}, u32[]{:S(2)}, u32[]{:S(2)}) collective-permute-start(f32[136,128]{1,0:T(8,128)S(1)} %add.19), channel_id=1, source_target_pairs={{0,4},{1,5},{2,6},{3,7},{4,0},{5,1},{6,2},{7,3},{8,12},{9,13},{10,... | collective-permute-start | bytes 208904 | tf_op jit(solution)/shard_map/ppermute | solution.py:487
  35.1 5.8 %collective-permute-start.6 = (f32[136,128]{1,0:T(8,128)S(1)}, f32[136,128]{1,0:T(8,128)S(1)}, u32[]{:S(2)}, u32[]{:S(2)}) collective-permute-start(f32[136,128]{1,0:T(8,128)S(1)} %add.20.when), channel_id=1, source_target_pairs={{0,8},{1,9},{2,10},{3,11},{4,12},{5,13},{6,14},{7,15},{8,0},{9,1},... | collective-permute-start | bytes 208904 | tf_op jit(solution)/shard_map/ppermute | solution.py:487
  37.8 4.5 %copy-start.3 = (f32[2048,128]{1,0:T(8,128)S(1)}, f32[2048,128]{1,0:T(8,128)}, u32[]{:S(2)}) copy-start(f32[2048,128]{1,0:T(8,128)} %copy-done.2) | copy-start | bytes 3145732
  41.0 1.3 %collective-permute-start.7 = (f32[136,128]{1,0:T(8,128)S(1)}, f32[136,128]{1,0:T(8,128)S(1)}, u32[]{:S(2)}, u32[]{:S(2)}) collective-permute-start(f32[136,128]{1,0:T(8,128)S(1)} %add.21.half), channel_id=1, source_target_pairs={{0,1},{1,0},{2,3},{3,2},{4,5},{5,4},{6,7},{7,6},{8,9},{9,8},{10,11... | collective-permute-start | bytes 208904 | tf_op jit(solution)/shard_map/ppermute | solution.py:487
  52.7 1.2 %collective-permute-start.8 = (f32[16,64]{1,0:T(8,128)S(1)}, f32[16,64]{1,0:T(8,128)S(1)}, u32[]{:S(2)}, u32[]{:S(2)}) collective-permute-start(f32[16,64]{1,0:T(8,128)S(1)} %get-tuple-element.49), channel_id=1, source_target_pairs={{0,1},{1,0},{2,3},{3,2},{4,5},{5,4},{6,7},{7,6},{8,9},{9,8},{10,11... | collective-permute-start | bytes 12296 | tf_op jit(solution)/shard_map/ppermute | solution.py:487
  53.9 3.7 %collective-permute-start.9 = (f32[16,64]{1,0:T(8,128)S(1)}, f32[16,64]{1,0:T(8,128)S(1)}, u32[]{:S(2)}, u32[]{:S(2)}) collective-permute-start(f32[16,64]{1,0:T(8,128)S(1)} %add.22), channel_id=1, source_target_pairs={{0,2},{1,3},{2,0},{3,1},{4,6},{5,7},{6,4},{7,5},{8,10},{9,11},{10,... | collective-permute-start | bytes 12296 | tf_op jit(solution)/shard_map/ppermute | solution.py:487
  57.5 5.4 %collective-permute-start.12 = (f32[16,64]{1,0:T(8,128)S(1)}, f32[16,64]{1,0:T(8,128)S(1)}, u32[]{:S(2)}, u32[]{:S(2)}) collective-permute-start(f32[16,64]{1,0:T(8,128)S(1)} %add.23.rest_0_), channel_id=1, source_target_pairs={{0,12},{1,13},{2,14},{3,15},{4,8},{5,9},{6,10},{7,11},{8,4},{9,5},... | collective-permute-start | bytes 12296 | tf_op jit(solution)/shard_map/ppermute | solution.py:487
  61.2 4.5 %collective-permute-start.11 = (f32[16,64]{1,0:T(8,128)S(1)}, f32[16,64]{1,0:T(8,128)S(1)}, u32[]{:S(2)}, u32[]{:S(2)}) collective-permute-start(f32[16,64]{1,0:T(8,128)S(1)} %add.23.rest_0_), channel_id=1, source_target_pairs={{0,8},{1,9},{2,10},{3,11},{4,12},{5,13},{6,14},{7,15},{8,0},{9,1},... | collective-permute-start | bytes 12296 | tf_op jit(solution)/shard_map/ppermute | solution.py:487
  61.2 4.5 %collective-permute-start.10 = (f32[16,64]{1,0:T(8,128)S(1)}, f32[16,64]{1,0:T(8,128)S(1)}, u32[]{:S(2)}, u32[]{:S(2)}) collective-permute-start(f32[16,64]{1,0:T(8,128)S(1)} %add.23.rest_0_), channel_id=1, source_target_pairs={{0,4},{1,5},{2,6},{3,7},{4,0},{5,1},{6,2},{7,3},{8,12},{9,13},{10,... | collective-permute-start | bytes 12296 | tf_op jit(solution)/shard_map/ppermute | solution.py:487

commit v6 on v5

--- a/solution.py
+++ b/solution.py
@@ -27,6 +27,10 @@
 
 def at(row, count=16):
     return pl.ds(pl.multiple_of(row, 8), count)
+
+
+def window(ref, start, size):
+    return ref.at[pl.ds(pl.multiple_of(start, 8), size)]
 
 
 def kept_rows(load):
@@ -117,14 +121,21 @@
     clear_margins(first, LAYERS, fields)
     clear_margins(second, LAYERS, fields)
 
+    slab, flat = PADDED * fields, 32 * fields
+    ahead = 24 * fields
+
     def load(chunk, carry):
+        there = window(turned, chunk * 8 * fields, LAYERS * flat - ahead)
+        padded = window(first, chunk * 8 * fields, LAYERS * slab - ahead)
+        here = window(probes, chunk * 8, LAYERS * flat - 24)
+        push = window(sources, chunk * 8, 3 * LAYERS * 32 - 24)
         for x in range(LAYERS):
-            for step in range(8):
-                y = chunk * 8 + step
+            for y in range(8):
                 cell = x * 32 + y
-                value = probes[pl.ds(cell, fields, stride=HALF), :]
-                turned[at(cell * fields, fields), :] = value
-                first[at((x * PADDED + REACH + y) * fields, fields), :] = value * spread(sources, cell, fields)
+                value = here[pl.ds(cell, fields, stride=HALF), :]
+                there[cell * fields : (cell + 1) * fields, :] = value
+                row = x * slab + (REACH + y) * fields
+                padded[row : row + fields, :] = value * spread(push, cell, fields)
         return carry
 
     lax.fori_loop(0, 4, load, 0)
@@ -133,34 +144,58 @@
         along_z(field, 0, fields, band_ref, z_term)
 
         def body(chunk, carry):
+            padded = window(field, chunk * 8 * fields, LAYERS * slab - ahead)
+            z_part = window(z_term, chunk * 8 * fields, LAYERS * flat - ahead)
+            speed = window(statics, chunk * 8, LAYERS * 32 - 24)
+            put = emit(chunk)
             for part in range(0, fields, 8):
 
                 def load(layer, y):
-                    return field[at((layer * PADDED + REACH + chunk * 8 + y) * fields + part, 8), :]
+                    row = layer * slab + (REACH + y) * fields + part
+                    return padded[row : row + 8, :]
 
                 get = kept_rows(load)
                 for y in range(8):
                     for x in range(LAYERS):
-                        cell = x * 32 + chunk * 8 + y
-                        z_part = z_term[at(cell * fields + part, 8), :]
-                        total = laplacian(get, x, y, z_part, 0, LAYERS - 1)
-                        emit(x, chunk * 8 + y, part, get(x, y), spread(statics, cell, 8) * total)
+                        cell = x * 32 + y
+                        row = cell * fields + part
+                        total = laplacian(get, x, y, z_part[row : row + 8, :], 0, LAYERS - 1)
+                        put(x, y, part, get(x, y), spread(speed, cell, 8) * total)
             return carry
 
         lax.fori_loop(0, 4, body, 0)
 
-    def step_one(x, y, part, now, change):
-        cell = x * 32 + y
-        push = turned[at(cell * fields + part, 8), :] * spread(sources, 128 + cell, 8)
-        second[at((x * PADDED + REACH + y) * fields + part, 8), :] = 2.0 * now + change + push
+    def step_one(chunk):
+        push = window(sources, chunk * 8, 3 * LAYERS * 32 - 24)
+        there = window(turned, chunk * 8 * fields, LAYERS * flat - ahead)
+        out = window(second, chunk * 8 * fields, LAYERS * slab - ahead)
+
+        def put(x, y, part, now, change):
+            cell = x * 32 + y
+            row = cell * fields + part
+            change = change + there[row : row + 8, :] * spread(push, 128 + cell, 8)
+            row = x * slab + (REACH + y) * fields + part
+            out[row : row + 8, :] = 2.0 * now + change
+
+        return put
 
     sweep(first, step_one)
 
-    def step_two(x, y, part, now, change):
-        cell = x * 32 + y
-        push = turned[at(cell * fields + part, 8), :] * spread(sources, 256 + cell, 8)
-        before = first[at((x * PADDED + REACH + y) * fields + part, 8), :]
-        third[at(cell * fields + part, 8), :] = 2.0 * now - before + change + push
+    def step_two(chunk):
+        push = window(sources, chunk * 8, 3 * LAYERS * 32 - 24)
+        there = window(turned, chunk * 8 * fields, LAYERS * flat - ahead)
+        before = window(first, chunk * 8 * fields, LAYERS * slab - ahead)
+        out = window(third, chunk * 8 * fields, LAYERS * flat - ahead)
+
+        def put(x, y, part, now, change):
+            cell = x * 32 + y
+            row = x * slab + (REACH + y) * fields + part
+            change = change - before[row : row + 8, :]
+            row = cell * fields + part
+            change = change + there[row : row + 8, :] * spread(push, 256 + cell, 8)
+            out[row : row + 8, :] = 2.0 * now + change
+
+        return put
 
     sweep(second, step_two)
 
@@ -181,7 +216,7 @@
     clear_margins(below, LAYERS, fields)
     clear_margins(above, LAYERS, fields)
     total_ref[...] = jnp.zeros_like(total_ref)
-    near, next_one, far_one, side_one = passed[0:length, :], passed[length:, :], across[...], partner[...]
+    near, next_one, far_one, side_one = passed[0:length, :], passed[length:, :], across[0:length, :], partner[...]
     tiles = (
         jnp.where(odd, far_one, next_one),
         jnp.where(odd, side_one, near),
@@ -206,16 +241,20 @@
         owner_ref[rows, :] = jnp.broadcast_to(owner, (fields, entries))
         weight_ref[rows, :] = jnp.broadcast_to(weight, (fields, entries))
 
+    slab, flat = PADDED * fields, 32 * fields
+    ahead = 24 * fields
+
     def outward(chunk, carry):
-        for step in range(8):
-            y = chunk * 8 + step
-            mine = [first[at((x * PADDED + REACH + y) * fields, fields), :] for x in range(LAYERS)]
+        speed = window(speed_ref, chunk * 8, 5 * cells - 24)
+        here, low, high = (window(ref, chunk * 8 * fields, LAYERS * slab - ahead) for ref in (first, below, above))
+        for y in range(8):
+            rows = [slice(x * slab + (REACH + y) * fields, x * slab + (REACH + y + 1) * fields) for x in range(LAYERS)]
+            mine = [here[row, :] for row in rows]
             for x in range(LAYERS):
                 up = sum(STENCIL[4 + x - other] * mine[other] for other in range(x, LAYERS))
                 down = sum(STENCIL[4 + other - x] * mine[other] for other in range(x + 1))
-                row = at((x * PADDED + REACH + y) * fields, fields)
-                above[row, :] = spread(speed_ref, 3 * cells + x * 32 + y, fields) * up
-                below[row, :] = spread(speed_ref, cells + x * 32 + y, fields) * down
+                high[rows[x], :] = spread(speed, 3 * cells + x * 32 + y, fields) * up
+                low[rows[x], :] = spread(speed, cells + x * 32 + y, fields) * down
         return carry
 
     lax.fori_loop(0, 4, outward, 0)
@@ -231,27 +270,33 @@
         return total
 
     def respond(chunk, carry):
+        speeds = window(speed_ref, chunk * 8, 5 * cells - 24)
+        sides = [window(ref, chunk * 8 * fields, LAYERS * slab - ahead) for ref in (below, second, above)]
+        base = window(third, chunk * 8 * fields, LAYERS * flat - ahead)
+        z_parts = window(z_term, chunk * 8 * fields, 2 * LAYERS * flat - ahead)
         for tile in range(5):
             sample = samples[tile]
             for part in range(0, fields, 8):
 
                 def load(layer, y):
-                    ref = (below, second, above)[(layer + LAYERS) // LAYERS]
-                    return ref[at((layer % LAYERS * PADDED + REACH + chunk * 8 + y) * fields + part, 8), :]
+                    row = layer % LAYERS * slab + (REACH + y) * fields + part
+                    return sides[(layer + LAYERS) // LAYERS][row : row + 8, :]
 
                 read = kept_rows(load)
                 for y in range(8):
                     for x in range(LAYERS):
-                        cell = x * 32 + chunk * 8 + y
+                        cell = x * 32 + y
+                        row = cell * fields + part
                         layer = (tile - 2) * LAYERS + x
-                        speed = spread(speed_ref, tile * cells + cell, 8)
+                        speed = spread(speeds, tile * cells + cell, 8)
                         if tile in (0, 4):
                             value = speed * far(read, layer, y, -4, 7)
                         elif tile == 2:
                             outside = far(read, layer, y, -4, -1) + far(read, layer, y, 4, 7)
-                            value = third[at(cell * fields + part, 8), :] + speed * outside
+                            value = base[row : row + 8, :] + speed * outside
                         else:
-                            z_part = z_term[at((tile // 2 * cells + cell) * fields + part, 8), :]
+                            row = row + tile // 2 * cells * fields
+                            z_part = z_parts[row : row + 8, :]
                             value = 2.0 * read(layer, y) + speed * laplacian(read, layer, y, z_part, -4, 7)
                         row = (x * 2 + y // 4) * fields + part
                         side = y % 4 * HALF
@@ -296,28 +341,29 @@
         out[count * fields :, :] = jnp.where(place == me[0] - side * count, scale, 0.0)
 
 
-def basis_parts(basis, when, out):
+def basis_parts(first, basis, when, out):
     rank = basis.shape[0] // HALF
 
     def body(group, carry):
+        here = window(basis, (first + group) * 8, basis.shape[0] - 15 * 8)
+        there = window(out, group * rank, rank)
         for step in range(8):
-            high, low = split(basis[pl.ds(group * 8 + step, rank, stride=HALF), :])
-            rows = at(group * rank, rank)
-            out[rows, step * 256 : step * 256 + HALF] = high
-            out[rows, step * 256 + HALF : (step + 1) * 256] = low
+            high, low = split(here[pl.ds(step, rank, stride=HALF), :])
+            there[:, step * 256 : step * 256 + HALF] = high
+            there[:, step * 256 + HALF : (step + 1) * 256] = low
         return carry
 
-    lax.fori_loop(0, 16, body, 0)
+    lax.fori_loop(0, 8, body, 0)
 
 
 def adjoint(
     fields, peers, me, half, other, cell_ref, slot_ref, speed_ref, line_ref, owner_ref, weight_ref, turned, sources,
-    prior, band_ref, basis, image, coeffs, high_ref, low_ref, inner_two, outer_two,
+    prior, band_ref, basis, basis_two, image, coeffs, high_ref, low_ref, inner_two, outer_two,
     inner_one, outer_one, z_term, image_parts, scaled, *lefts,
 ):
     entries = line_ref.shape[1]
     cells = LAYERS * 32
-    rank = basis.shape[0] // 16
+    rank = basis.shape[0] // 8
     clear_margins(inner_two, 5 * LAYERS, fields)
     clear_margins(inner_one, 3 * LAYERS, fields)
     count = peers // 2
@@ -368,52 +414,64 @@
 
     lax.fori_loop(0, 3, terms, 0)
 
+    slab, flat = PADDED * fields, 32 * fields
+    ahead = 24 * fields
+
     def step_one(index, carry):
-        tile, chunk = index // 4 + 1, index % 4
+        tile, chunk = index // 4, index % 4
+        start, skip = tile * LAYERS * slab + chunk * 8 * fields, tile * LAYERS * flat + chunk * 8 * fields
+        here = window(inner_two, start, 3 * LAYERS * slab - ahead)
+        two, one, z_part = (window(ref, skip, LAYERS * flat - ahead) for ref in (outer_two, outer_one, z_term))
+        out = window(inner_one, start, LAYERS * slab - ahead)
+        speed = window(speed_ref, (tile + 1) * cells + chunk * 8, cells - 24)
         for part in range(0, fields, 8):
 
             def load(layer, y):
-                row = (tile * LAYERS + layer) * PADDED + REACH + chunk * 8 + y
-                return inner_two[at(row * fields + part, 8), :]
+                row = (layer + LAYERS) * slab + (REACH + y) * fields + part
+                return here[row : row + 8, :]
 
             get = kept_rows(load)
             for y in range(8):
                 for x in range(LAYERS):
-                    layer = tile * LAYERS + x
-                    speed = spread(speed_ref, layer * 32 + chunk * 8 + y, 8)
-                    layer = layer - LAYERS
-                    row = at((layer * 32 + chunk * 8 + y) * fields + part, 8)
-                    now = 2.0 * outer_two[row, :] + laplacian(get, x, y, z_term[row, :], -4, 7)
-                    outer_one[row, :] = now
-                    inner_one[at((layer * PADDED + REACH + chunk * 8 + y) * fields + part, 8), :] = speed * now
+                    cell = x * 32 + y
+                    row = slice(cell * fields + part, cell * fields + part + 8)
+                    now = 2.0 * two[row, :] + laplacian(get, x, y, z_part[row, :], -4, 7)
+                    one[row, :] = now
+                    row = x * slab + (REACH + y) * fields + part
+                    out[row : row + 8, :] = spread(speed, cell, 8) * now
         return carry
 
     lax.fori_loop(0, 12, step_one, 0)
     along_z(inner_one, LAYERS, fields, band_ref, z_term)
 
     def step_two(chunk, total):
+        skip = chunk * 8 * fields
+        here = window(inner_one, skip, 3 * LAYERS * slab - ahead)
+        two_rows, one_rows = (window(ref, LAYERS * flat + skip, LAYERS * flat - ahead) for ref in (outer_two, outer_one))
+        z_part, there, out = (window(ref, skip, LAYERS * flat - ahead) for ref in (z_term, turned, image))
+        push = window(sources, chunk * 8, 3 * cells - 24)
+        damping = window(prior, chunk * 8, cells - 24)
         for part in range(0, fields, 8):
 
             def load(layer, y):
-                row = (LAYERS + layer) * PADDED + REACH + chunk * 8 + y
-                return inner_one[at(row * fields + part, 8), :]
+                row = (layer + LAYERS) * slab + (REACH + y) * fields + part
+                return here[row : row + 8, :]
 
             get = kept_rows(load)
             for y in range(8):
                 for x in range(LAYERS):
-                    cell = x * 32 + chunk * 8 + y
-                    row = at(cell * fields + part, 8)
-                    own_row = at((cells + cell) * fields + part, 8)
-                    two = outer_two[own_row, :]
-                    one = outer_one[own_row, :]
-                    zero = 2.0 * one - two + laplacian(get, x, y, z_term[row, :], -4, 7)
-                    value = spread(sources, cell, 8) * zero
-                    value = value + spread(sources, 128 + cell, 8) * one
-                    value = value + spread(sources, 256 + cell, 8) * two
-                    image[row, :] = value + spread(prior, cell, 8) * turned[row, :]
+                    cell = x * 32 + y
+                    row = slice(cell * fields + part, cell * fields + part + 8)
+                    two, one = two_rows[row, :], one_rows[row, :]
+                    zero = 2.0 * one - two + laplacian(get, x, y, z_part[row, :], -4, 7)
+                    value = spread(push, cell, 8) * zero
+                    value = value + spread(push, 128 + cell, 8) * one
+                    value = value + spread(push, 256 + cell, 8) * two
+                    out[row, :] = value + spread(damping, cell, 8) * there[row, :]
         for x in range(LAYERS):
             for y in range(8):
-                high, low = split(image[at((x * 32 + chunk * 8 + y) * fields, fields), :])
+                cell = x * 32 + y
+                high, low = split(out[cell * fields : (cell + 1) * fields, :])
                 side = y * 256
                 rows = slice(x * 2 * fields, x * 2 * fields + fields)
                 image_parts[rows, side : side + HALF] = high
@@ -422,7 +480,7 @@
                 image_parts[rows, side : side + HALF] = low
                 image_parts[rows, side + HALF : side + 256] = jnp.zeros_like(low)
         for x in range(LAYERS):
-            columns = basis[at((x * 4 + chunk) * rank, rank), :]
+            columns = (basis, basis_two)[x // 2][at((x % 2 * 4 + chunk) * rank, rank), :]
             parts = image_parts[x * 2 * fields : (x + 1) * 2 * fields, :]
             total = total + lax.dot_general(parts, columns, NT, preferred_element_type=F32)
         return total
@@ -431,7 +489,7 @@
     coeffs[...] = total[:fields, :] + total[fields:, :]
 
 
-def remainder(fields, image, basis, *rest):
+def remainder(fields, image, basis, basis_two, *rest):
     *shares, out, coeffs, natural, sem = rest
     rank = coeffs.shape[1]
     while len(shares) > 1:
@@ -446,7 +504,7 @@
 
     for x in range(LAYERS):
         for part in range(4):
-            columns = basis[(x * 4 + part) * rank : (x * 4 + part + 1) * rank, :]
+            columns = (basis, basis_two)[x // 2][(x % 2 * 4 + part) * rank : (x % 2 * 4 + part + 1) * rank, :]
             both = jnp.dot(parts, columns, preferred_element_type=F32)
             for step in range(8):
                 cell = x * 32 + part * 8 + step
@@ -551,7 +609,7 @@
     )
     half_rows = peers // 2 * (fields + 1)
     passed, second = lax.optimization_barrier((passed, second))
-    across = swapped(passed[: own.shape[0]], "space", 1)
+    across = swapped(passed, "space", 1)
     kept, sent, cell_hot, slot_hot, speed, line, owner, weight = call(
         functools.partial(forward_window, fields, peers),
         (me, first, second, third, own, partner, passed, across, matrix, trace_weight.reshape(1, HALF)),
@@ -579,27 +637,29 @@
         room=20,
     )
     half = kept + swapped(sent, "space", 1)
+    columns = []
     bits = 2
-    while bits * 2 < peers:
-        half = half + swapped(half, "space", bits)
+    while bits < peers:
+        arrived = swapped(half, "space", bits)
+        if len(columns) < 2:
+            (some,) = call(
+                functools.partial(basis_parts, 8 * len(columns)),
+                (basis.reshape(rank * cells, HALF), half),
+                [struct(8 * rank, 2048, dtype=BF16)],
+                [],
+                10_000_000,
+                4 * 2**20,
+            )
+            arrived, some = lax.optimization_barrier((arrived, some))
+            columns.append(some)
+        half = half + arrived
         bits *= 2
-    arrived = swapped(half, "space", bits)
-    (columns,) = call(
-        basis_parts,
-        (basis.reshape(rank * cells, HALF), half),
-        [struct(16 * rank, 2048, dtype=BF16)],
-        [],
-        10_000_000,
-        8 * 2**20,
-    )
-    arrived, columns = lax.optimization_barrier((arrived, columns))
-    half = half + arrived
     other = swapped(half, "space", 1)
     image, coeffs = call(
         functools.partial(adjoint, fields, peers),
         (
             me, half, other, cell_hot, slot_hot, speed, line, owner, weight,
-            turned, sources_near, prior_near, matrix, columns,
+            turned, sources_near, prior_near, matrix, *columns,
         ),
         [struct(cells * fields, HALF), struct(fields, rank)],
         [
@@ -626,7 +686,7 @@
     shares = [coeffs] + [swapped(coeffs, "space", bits * i) for i in range(1, peers // bits)]
     hess_probe, coeffs = call(
         functools.partial(remainder, fields),
-        (image, columns, *shares),
+        (image, *columns, *shares),
         [struct(*probes.shape), struct(fields, rank)],
         [pltpu.VMEM((fields * cells, HALF), F32), pltpu.SemaphoreType.DMA((LAYERS,))],
         200_000_000,

time: 68.4 us -> 68.4 us (level)
    pallas_call x6 -> x7, Pallas kernels: 29 us -> 29 us  [call(): pl.pallas_call(kernel, out_shape=out_shape, in_specs=[smem] * scalars + [...]
  transfers between devices with their start and end apart: 13 -> 13, of which waited for: 10 -> 11; matrix products, arithmetic and copies ran while one was open for 0% -> 0% of each run, Pallas kernels for 10% -> 10%
where the time goes in v6:
time: 68.4 us; the launch traced here: 68.2 us
  Pallas kernels  29 us (42%)
  starting transfers between devices  18.3 us (27%)
  waiting for transfers between devices  16.3 us (24%)
  local copies, waits for them, and re-layouts  3.19 us (5%)
  between operations  1.39 us (2%)
    pallas_call x7, Pallas kernels, call(): pl.pallas_call(kernel, out_shape=out_shape, in_specs=[smem] * scalars + [...  29 us
    ppermute x12, starting transfers between devices, swapped(): return lax.ppermute(array, axis, [(i, i ^ bits) for i in range(count)])  17.6 us
    ppermute x12, waiting for transfers between devices, swapped(): return lax.ppermute(array, axis, [(i, i ^ bits) for i in range(count)])  16.3 us
    unnamed x12, local copies, waits for them, and re-layouts  3.19 us
  transfers between devices with their start and end apart: 13, of which 11 were waited for; matrix products, arithmetic and copies ran while one was open for 0% of the time, Pallas kernels for 10%

profile of v6, /device:TPU:0, one launch (start us, length us, event | category | flops | bytes accessed | tf_op | source)
XLA Modules:
  0.0 68.2 jit_solution(3463676822567601561)
XLA Ops:
  1.3 1.4 %shard_map.122 = (f32[144,128]{1,0:T(8,128)S(1)}, f32[2048,128]{1,0:T(8,128)S(1)}, f32[384,128]{1,0:T(8,128)S(1)}, f32[128,128]{1,0:T(8,128)S(1)}, bf16[256,256]{1,0:T(8,128)(2,1)S(1)}) custom-call(s32[1]{0:T(128)S(6)} %copy.13.count, f32[2048,128]{1,0:T(8,128)} %bitcast.15, f32[384,128]{1,0:T(8,128)} %bitcast.16, f32[128,128]{1,0:T(8,128)} %bitcast.17, ...), custom_call_target="tpu_custom_call" | custom-call | flops 100000 | bytes 2097152 | tf_op jit(solution)/shard_map/pallas_call | solution.py:528
  4.9 3.7 %shard_map.123 = (f32[2048,128]{1,0:T(8,128)S(1)}, f32[2560,128]{1,0:T(8,128)S(1)}, f32[2560,128]{1,0:T(8,128)S(1)}, f32[2048,128]{1,0:T(8,128)S(1)}) custom-call(f32[2048,128]{1,0:T(8,128)S(1)} %get-tuple-element.29.probes, f32[384,128]{1,0:T(8,128)S(1)} %get-tuple-element.30.sources, f32[144,128]{1,0:T(8,128)S(1)} %get-tuple-element.31.statics.own, ...), custom_call_target="tpu_custom_call" | custom-call | flops 600000000 | bytes 6291456 | tf_op jit(solution)/shard_map/pallas_call | solution.py:528
  8.6 1.0 %copy-done.2 = f32[2048,128]{1,0:T(8,128)} copy-done((f32[2048,128]{1,0:T(8,128)}, f32[2048,128]{1,0:T(8,128)S(1)}, u32[]{:S(2)}) %copy-start.2) | copy-done | bytes 1048600
  10.5 4.2 %collective-permute-start.2 = (f32[288,128]{1,0:T(8,128)S(1)}, f32[288,128]{1,0:T(8,128)S(1)}, u32[]{:S(2)}, u32[]{:S(2)}) collective-permute-start(f32[288,128]{1,0:T(8,128)S(1)} %collective-permute-done.1.passed), channel_id=1, source_target_pairs={{0,1},{1,0},{2,3},{3,2},{4,5},{5,4},{6,7},{7,6},{8,9},{9,8},{10,11... | collective-permute-start | bytes 442376 | tf_op jit(solution)/shard_map/ppermute | solution.py:545
  14.7 1.0 %collective-permute-done.2.across = f32[288,128]{1,0:T(8,128)S(1)} collective-permute-done((f32[288,128]{1,0:T(8,128)S(1)}, f32[288,128]{1,0:T(8,128)S(1)}, u32[]{:S(2)}, u32[]{:S(2)}) %collective-permute-start.2) | collective-permute-done | bytes 147488 | tf_op jit(solution)/shard_map/ppermute | solution.py:545
  15.8 1.2 %copy-done.5 = f32[2048,128]{1,0:T(8,128)S(1)} copy-done((f32[2048,128]{1,0:T(8,128)S(1)}, f32[2048,128]{1,0:T(8,128)}, u32[]{:S(2)}) %copy-start.5) | copy-done | bytes 1048600
  17.0 7.9 %shard_map.124 = (f32[136,128]{1,0:T(8,128)S(1)}, f32[136,128]{1,0:T(8,128)S(1)}, bf16[2560,512]{1,0:T(8,128)(2,1)S(1)}, bf16[640,512]{1,0:T(8,128)(2,1)S(1)}, f...) custom-call(s32[1]{0:T(128)} %bitcast.me, ...), custom_call_target="tpu_custom_call" | custom-call | flops 3000000000 | bytes 6291456 | tf_op jit(solution)/shard_map/pallas_call | solution.py:528
  26.2 1.6 %collective-permute-start.4 = (f32[136,128]{1,0:T(8,128)S(1)}, f32[136,128]{1,0:T(8,128)S(1)}, u32[]{:S(2)}, u32[]{:S(2)}) collective-permute-start(f32[136,128]{1,0:T(8,128)S(1)} %add.18.when), channel_id=1, source_target_pairs={{0,2},{1,3},{2,0},{3,1},{4,6},{5,7},{6,4},{7,5},{8,10},{9,11},{10,... | collective-permute-start | bytes 208904 | tf_op jit(solution)/shard_map/ppermute | solution.py:545
  27.8 1.6 %shard_map.125.basis = bf16[512,2048]{1,0:T(8,128)(2,1)S(1)} custom-call(f32[8192,128]{1,0:T(8,128)S(1)} %bitcast.12, f32[136,128]{1,0:T(8,128)S(1)} %add.18.when), custom_call_target="tpu_custom_call" | custom-call | flops 10000000 | bytes 4194304 | tf_op jit(solution)/shard_map/pallas_call | solution.py:528
  29.4 1.3 %collective-permute-done.4 = f32[136,128]{1,0:T(8,128)S(1)} collective-permute-done((f32[136,128]{1,0:T(8,128)S(1)}, f32[136,128]{1,0:T(8,128)S(1)}, u32[]{:S(2)}, u32[]{:S(2)}) %collective-permute-start.4) | collective-permute-done | bytes 69664 | tf_op jit(solution)/shard_map/ppermute | solution.py:545
  30.7 1.6 %collective-permute-start.5 = (f32[136,128]{1,0:T(8,128)S(1)}, f32[136,128]{1,0:T(8,128)S(1)}, u32[]{:S(2)}, u32[]{:S(2)}) collective-permute-start(f32[136,128]{1,0:T(8,128)S(1)} %add.19.when), channel_id=1, source_target_pairs={{0,4},{1,5},{2,6},{3,7},{4,0},{5,1},{6,2},{7,3},{8,12},{9,13},{10,... | collective-permute-start | bytes 208904 | tf_op jit(solution)/shard_map/ppermute | solution.py:545
  32.4 1.6 %shard_map.126.basis_two = bf16[512,2048]{1,0:T(8,128)(2,1)S(1)} custom-call(f32[8192,128]{1,0:T(8,128)S(1)} %bitcast.13, f32[136,128]{1,0:T(8,128)S(1)} %add.19.when), custom_call_target="tpu_custom_call" | custom-call | flops 10000000 | bytes 4194304 | tf_op jit(solution)/shard_map/pallas_call | solution.py:528
  34.0 1.1 %collective-permute-done.5 = f32[136,128]{1,0:T(8,128)S(1)} collective-permute-done((f32[136,128]{1,0:T(8,128)S(1)}, f32[136,128]{1,0:T(8,128)S(1)}, u32[]{:S(2)}, u32[]{:S(2)}) %collective-permute-start.5) | collective-permute-done | bytes 69664 | tf_op jit(solution)/shard_map/ppermute | solution.py:545
  35.1 2.7 %collective-permute-start.6 = (f32[136,128]{1,0:T(8,128)S(1)}, f32[136,128]{1,0:T(8,128)S(1)}, u32[]{:S(2)}, u32[]{:S(2)}) collective-permute-start(f32[136,128]{1,0:T(8,128)S(1)} %add.20), channel_id=1, source_target_pairs={{0,8},{1,9},{2,10},{3,11},{4,12},{5,13},{6,14},{7,15},{8,0},{9,1},... | collective-permute-start | bytes 208904 | tf_op jit(solution)/shard_map/ppermute | solution.py:545
  37.8 2.6 %collective-permute-done.6 = f32[136,128]{1,0:T(8,128)S(1)} collective-permute-done((f32[136,128]{1,0:T(8,128)S(1)}, f32[136,128]{1,0:T(8,128)S(1)}, u32[]{:S(2)}, u32[]{:S(2)}) %collective-permute-start.6) | collective-permute-done | bytes 69664 | tf_op jit(solution)/shard_map/ppermute | solution.py:545
  40.5 1.2 %collective-permute-done.7.other = f32[136,128]{1,0:T(8,128)S(1)} collective-permute-done((f32[136,128]{1,0:T(8,128)S(1)}, f32[136,128]{1,0:T(8,128)S(1)}, u32[]{:S(2)}, u32[]{:S(2)}) %collective-permute-start.7) | collective-permute-done | bytes 69664 | tf_op jit(solution)/shard_map/ppermute | solution.py:545
  41.7 10.3 %shard_map.127 = (f32[2048,128]{1,0:T(8,128)S(1)}, f32[16,64]{1,0:T(8,128)S(1)}) custom-call(s32[1]{0:T(128)} %bitcast.me, f32[136,128]{1,0:T(8,128)S(1)} %add.21.half, f32[136,128]{1,0:T(8,128)S(1)} %collective-permute-done.7.other, bf16[2560,512]{1,0:T(8,128)(2,1)S(1)} %get-tuple-element.42.cell_ref, bf16[640,512]{1,0:T(8,128)(2,1)S(1)} %get-tuple-element.43.slot_ref, ...), custom_call_target="tpu_custom_call" | custom-call | flops 5000000000 | bytes 10485760 | tf_op jit(solution)/shard_map/pallas_call | solution.py:528
  52.2 1.0 %collective-permute-done.8 = f32[16,64]{1,0:T(8,128)S(1)} collective-permute-done((f32[16,64]{1,0:T(8,128)S(1)}, f32[16,64]{1,0:T(8,128)S(1)}, u32[]{:S(2)}, u32[]{:S(2)}) %collective-permute-start.8) | collective-permute-done | bytes 4128 | tf_op jit(solution)/shard_map/ppermute | solution.py:545
  53.3 1.5 %collective-permute-start.9 = (f32[16,64]{1,0:T(8,128)S(1)}, f32[16,64]{1,0:T(8,128)S(1)}, u32[]{:S(2)}, u32[]{:S(2)}) collective-permute-start(f32[16,64]{1,0:T(8,128)S(1)} %add.22), channel_id=1, source_target_pairs={{0,2},{1,3},{2,0},{3,1},{4,6},{5,7},{6,4},{7,5},{8,10},{9,11},{10,... | collective-permute-start | bytes 12296 | tf_op jit(solution)/shard_map/ppermute | solution.py:545
  54.8 2.1 %collective-permute-done.9 = f32[16,64]{1,0:T(8,128)S(1)} collective-permute-done((f32[16,64]{1,0:T(8,128)S(1)}, f32[16,64]{1,0:T(8,128)S(1)}, u32[]{:S(2)}, u32[]{:S(2)}) %collective-permute-start.9) | collective-permute-done | bytes 4128 | tf_op jit(solution)/shard_map/ppermute | solution.py:545
  56.9 4.2 %collective-permute-start.12 = (f32[16,64]{1,0:T(8,128)S(1)}, f32[16,64]{1,0:T(8,128)S(1)}, u32[]{:S(2)}, u32[]{:S(2)}) collective-permute-start(f32[16,64]{1,0:T(8,128)S(1)} %add.23.rest_0_), channel_id=1, source_target_pairs={{0,12},{1,13},{2,14},{3,15},{4,8},{5,9},{6,10},{7,11},{8,4},{9,5},... | collective-permute-start | bytes 12296 | tf_op jit(solution)/shard_map/ppermute | solution.py:545
  61.7 1.1 %collective-permute-done.12.rest_3_ = f32[16,64]{1,0:T(8,128)S(1)} collective-permute-done((f32[16,64]{1,0:T(8,128)S(1)}, f32[16,64]{1,0:T(8,128)S(1)}, u32[]{:S(2)}, u32[]{:S(2)}) %collective-permute-start.12) | collective-permute-done | bytes 4128 | tf_op jit(solution)/shard_map/ppermute | solution.py:545
  62.8 2.9 %collective-permute-done.11.rest_2_ = f32[16,64]{1,0:T(8,128)S(1)} collective-permute-done((f32[16,64]{1,0:T(8,128)S(1)}, f32[16,64]{1,0:T(8,128)S(1)}, u32[]{:S(2)}, u32[]{:S(2)}) %collective-permute-start.11) | collective-permute-done | bytes 4128 | tf_op jit(solution)/shard_map/ppermute | solution.py:545
  65.7 2.4 %shard_map.128 = (f32[16,4,32,128]{3,2,1,0:T(8,128)}, f32[16,64]{1,0:T(8,128)}) custom-call(f32[2048,128]{1,0:T(8,128)S(1)} %get-tuple-element.52.image, bf16[512,2048]{1,0:T(8,128)(2,1)S(1)} %shard_map.125.basis, bf16[512,2048]{1,0:T(8,128)(2,1)S(1)} %shard_map.126.basis_two, f32[16,64]{1,0:T(8,128)S(1)} %add.23.rest_0_, ...), custom_call_target="tpu_custom_call" | custom-call | flops 200000000 | bytes 6291456 | tf_op jit(solution)/shard_map/pallas_call | solution.py:528
  (28 shorter events, 5.3 us)
Async XLA Ops:
  0.6 15.1 %copy-start.1 = (f32[128]{0:T(128)S(1)}, f32[128]{0:T(128)}, u32[]{:S(2)}) copy-start(f32[128]{0:T(128)} %param.21) | copy-start | bytes 1540
  2.7 1.4 %collective-permute-start = (f32[144,128]{1,0:T(8,128)S(1)}, f32[144,128]{1,0:T(8,128)S(1)}, u32[]{:S(2)}, u32[]{:S(2)}) collective-permute-start(f32[144,128]{1,0:T(8,128)S(1)} %get-tuple-element.31.statics.own), channel_id=1, source_target_pairs={{0,1},{1,0},{2,3},{3,2},{4,5},{5,4},{6,7},{7,6},{8,9},{9,8},{10,11... | collective-permute-start | bytes 221192 | tf_op jit(solution)/shard_map/ppermute | solution.py:545
  4.2 6.3 %collective-permute-start.1 = (f32[288,128]{1,0:T(8,128)S(1)}, f32[288,128]{1,0:T(8,128)S(1)}, u32[]{:S(2)}, u32[]{:S(2)}) collective-permute-start(f32[288,128]{1,0:T(8,128)S(1)} %pad_maximum_fusion), channel_id=1, source_target_pairs={{1,2},{2,1},{3,4},{4,3},{5,6},{6,5},{7,8},{8,7},{9,10},{10,9},{11,... | collective-permute-start | bytes 442376 | tf_op jit(solution)/shard_map/ppermute | solution.py:596
  8.6 1.0 %copy-start.2 = (f32[2048,128]{1,0:T(8,128)}, f32[2048,128]{1,0:T(8,128)S(1)}, u32[]{:S(2)}) copy-start(f32[2048,128]{1,0:T(8,128)S(1)} %get-tuple-element.48.turned) | copy-start | bytes 3145732
  9.6 1.0 %copy-start.4 = (f32[2048,128]{1,0:T(8,128)}, f32[2048,128]{1,0:T(8,128)S(1)}, u32[]{:S(2)}) copy-start(f32[2048,128]{1,0:T(8,128)S(1)} %get-tuple-element.36.third) | copy-start | bytes 3145732
  10.5 5.2 %collective-permute-start.2 = (f32[288,128]{1,0:T(8,128)S(1)}, f32[288,128]{1,0:T(8,128)S(1)}, u32[]{:S(2)}, u32[]{:S(2)}) collective-permute-start(f32[288,128]{1,0:T(8,128)S(1)} %collective-permute-done.1.passed), channel_id=1, source_target_pairs={{0,1},{1,0},{2,3},{3,2},{4,5},{5,4},{6,7},{7,6},{8,9},{9,8},{10,11... | collective-permute-start | bytes 442376 | tf_op jit(solution)/shard_map/ppermute | solution.py:545
  15.8 1.2 %copy-start.5 = (f32[2048,128]{1,0:T(8,128)S(1)}, f32[2048,128]{1,0:T(8,128)}, u32[]{:S(2)}) copy-start(f32[2048,128]{1,0:T(8,128)} %copy-done.4) | copy-start | bytes 3145732
  17.0 10.8 %copy-start = (f32[64,4,32,128]{3,2,1,0:T(8,128)S(1)}, f32[64,4,32,128]{3,2,1,0:T(8,128)}, u32[]{:S(2)}) copy-start(f32[64,4,32,128]{3,2,1,0:T(8,128)} %param.15) | copy-start | bytes 12582916
  24.9 1.3 %collective-permute-start.3 = (f32[136,128]{1,0:T(8,128)S(1)}, f32[136,128]{1,0:T(8,128)S(1)}, u32[]{:S(2)}, u32[]{:S(2)}) collective-permute-start(f32[136,128]{1,0:T(8,128)S(1)} %get-tuple-element.39), channel_id=1, source_target_pairs={{0,1},{1,0},{2,3},{3,2},{4,5},{5,4},{6,7},{7,6},{8,9},{9,8},{10,11... | collective-permute-start | bytes 208904 | tf_op jit(solution)/shard_map/ppermute | solution.py:545
  26.2 4.5 %collective-permute-start.4 = (f32[136,128]{1,0:T(8,128)S(1)}, f32[136,128]{1,0:T(8,128)S(1)}, u32[]{:S(2)}, u32[]{:S(2)}) collective-permute-start(f32[136,128]{1,0:T(8,128)S(1)} %add.18.when), channel_id=1, source_target_pairs={{0,2},{1,3},{2,0},{3,1},{4,6},{5,7},{6,4},{7,5},{8,10},{9,11},{10,... | collective-permute-start | bytes 208904 | tf_op jit(solution)/shard_map/ppermute | solution.py:545
  30.7 11.0 %copy-start.3 = (f32[2048,128]{1,0:T(8,128)S(1)}, f32[2048,128]{1,0:T(8,128)}, u32[]{:S(2)}) copy-start(f32[2048,128]{1,0:T(8,128)} %copy-done.2) | copy-start | bytes 3145732
  30.7 4.4 %collective-permute-start.5 = (f32[136,128]{1,0:T(8,128)S(1)}, f32[136,128]{1,0:T(8,128)S(1)}, u32[]{:S(2)}, u32[]{:S(2)}) collective-permute-start(f32[136,128]{1,0:T(8,128)S(1)} %add.19.when), channel_id=1, source_target_pairs={{0,4},{1,5},{2,6},{3,7},{4,0},{5,1},{6,2},{7,3},{8,12},{9,13},{10,... | collective-permute-start | bytes 208904 | tf_op jit(solution)/shard_map/ppermute | solution.py:545
  35.1 5.3 %collective-permute-start.6 = (f32[136,128]{1,0:T(8,128)S(1)}, f32[136,128]{1,0:T(8,128)S(1)}, u32[]{:S(2)}, u32[]{:S(2)}) collective-permute-start(f32[136,128]{1,0:T(8,128)S(1)} %add.20), channel_id=1, source_target_pairs={{0,8},{1,9},{2,10},{3,11},{4,12},{5,13},{6,14},{7,15},{8,0},{9,1},... | collective-permute-start | bytes 208904 | tf_op jit(solution)/shard_map/ppermute | solution.py:545
  40.4 1.3 %collective-permute-start.7 = (f32[136,128]{1,0:T(8,128)S(1)}, f32[136,128]{1,0:T(8,128)S(1)}, u32[]{:S(2)}, u32[]{:S(2)}) collective-permute-start(f32[136,128]{1,0:T(8,128)S(1)} %add.21.half), channel_id=1, source_target_pairs={{0,1},{1,0},{2,3},{3,2},{4,5},{5,4},{6,7},{7,6},{8,9},{9,8},{10,11... | collective-permute-start | bytes 208904 | tf_op jit(solution)/shard_map/ppermute | solution.py:545
  52.1 1.2 %collective-permute-start.8 = (f32[16,64]{1,0:T(8,128)S(1)}, f32[16,64]{1,0:T(8,128)S(1)}, u32[]{:S(2)}, u32[]{:S(2)}) collective-permute-start(f32[16,64]{1,0:T(8,128)S(1)} %get-tuple-element.53), channel_id=1, source_target_pairs={{0,1},{1,0},{2,3},{3,2},{4,5},{5,4},{6,7},{7,6},{8,9},{9,8},{10,11... | collective-permute-start | bytes 12296 | tf_op jit(solution)/shard_map/ppermute | solution.py:545
  53.3 3.7 %collective-permute-start.9 = (f32[16,64]{1,0:T(8,128)S(1)}, f32[16,64]{1,0:T(8,128)S(1)}, u32[]{:S(2)}, u32[]{:S(2)}) collective-permute-start(f32[16,64]{1,0:T(8,128)S(1)} %add.22), channel_id=1, source_target_pairs={{0,2},{1,3},{2,0},{3,1},{4,6},{5,7},{6,4},{7,5},{8,10},{9,11},{10,... | collective-permute-start | bytes 12296 | tf_op jit(solution)/shard_map/ppermute | solution.py:545
  56.9 5.9 %collective-permute-start.12 = (f32[16,64]{1,0:T(8,128)S(1)}, f32[16,64]{1,0:T(8,128)S(1)}, u32[]{:S(2)}, u32[]{:S(2)}) collective-permute-start(f32[16,64]{1,0:T(8,128)S(1)} %add.23.rest_0_), channel_id=1, source_target_pairs={{0,12},{1,13},{2,14},{3,15},{4,8},{5,9},{6,10},{7,11},{8,4},{9,5},... | collective-permute-start | bytes 12296 | tf_op jit(solution)/shard_map/ppermute | solution.py:545
  61.2 4.5 %collective-permute-start.11 = (f32[16,64]{1,0:T(8,128)S(1)}, f32[16,64]{1,0:T(8,128)S(1)}, u32[]{:S(2)}, u32[]{:S(2)}) collective-permute-start(f32[16,64]{1,0:T(8,128)S(1)} %add.23.rest_0_), channel_id=1, source_target_pairs={{0,8},{1,9},{2,10},{3,11},{4,12},{5,13},{6,14},{7,15},{8,0},{9,1},... | collective-permute-start | bytes 12296 | tf_op jit(solution)/shard_map/ppermute | solution.py:545
  61.2 4.5 %collective-permute-start.10 = (f32[16,64]{1,0:T(8,128)S(1)}, f32[16,64]{1,0:T(8,128)S(1)}, u32[]{:S(2)}, u32[]{:S(2)}) collective-permute-start(f32[16,64]{1,0:T(8,128)S(1)} %add.23.rest_0_), channel_id=1, source_target_pairs={{0,4},{1,5},{2,6},{3,7},{4,0},{5,1},{6,2},{7,3},{8,12},{9,13},{10,... | collective-permute-start | bytes 12296 | tf_op jit(solution)/shard_map/ppermute | solution.py:545

commit v7 on v6

--- a/solution.py
+++ b/solution.py
@@ -77,7 +77,7 @@
 
 
 def pack(
-    count, probes, sources, prior, kappa, cell, owner, slot, weight,
+    count, me, probes, sources, prior, kappa, cell, owner, slot, weight,
     statics, probes_out, sources_out, prior_out, band_ref, small_int, small_float, sem,
 ):
     rows = cell.shape[0]
@@ -570,6 +570,7 @@
         pack,
         (
             entry_count,
+            me,
             probes.reshape(fields * cells, HALF),
             sources.reshape(3 * cells, HALF),
             prior.reshape(cells, HALF),
@@ -589,7 +590,7 @@
         [pltpu.VMEM((3, rows, HALF), jnp.int32), pltpu.VMEM((rows, HALF), F32), pltpu.SemaphoreType.DMA((8,))],
         100_000,
         2 * 2**20,
-        scalars=1,
+        scalars=2,
         far=8,
     )
     partner = swapped(own, "space", 1)

time: 68.4 us -> 66.2 us (0.968)
  local copies, waits for them, and re-layouts: 3.19 us -> 0.01 us
  starting transfers between devices: 18.3 us -> 20.3 us
  waiting for transfers between devices: 16.3 us -> 15.1 us
    unnamed x12 -> x4, local copies, waits for them, and re-layouts: 3.19 us -> 0.01 us
    ppermute x12, starting transfers between devices: 17.6 us -> 19.7 us  [swapped(): return lax.ppermute(array, axis, [(i, i ^ bits) for i in range(count)])]
    ppermute x12, waiting for transfers between devices: 16.3 us -> 15.1 us  [swapped(): return lax.ppermute(array, axis, [(i, i ^ bits) for i in range(count)])]
  transfers between devices with their start and end apart: 13 -> 13, of which waited for: 11 -> 11; matrix products, arithmetic and copies ran while one was open for 0% -> 0% of each run, Pallas kernels for 10% -> 11%
where the time goes in v7:
time: 66.2 us; the launch traced here: 66 us
  Pallas kernels  29.1 us (44%)
  starting transfers between devices  20.3 us (31%)
  waiting for transfers between devices  15.1 us (23%)
  between operations  1.38 us (2%)
    pallas_call x7, Pallas kernels, call(): pl.pallas_call(kernel, out_shape=out_shape, in_specs=[smem] * scalars + [...  29.1 us
    ppermute x12, starting transfers between devices, swapped(): return lax.ppermute(array, axis, [(i, i ^ bits) for i in range(count)])  19.7 us
    ppermute x12, waiting for transfers between devices, swapped(): return lax.ppermute(array, axis, [(i, i ^ bits) for i in range(count)])  15.1 us
  transfers between devices with their start and end apart: 13, of which 11 were waited for; matrix products, arithmetic and copies ran while one was open for 0% of the time, Pallas kernels for 11%

profile of v7, /device:TPU:0, one launch (start us, length us, event | category | flops | bytes accessed | tf_op | source)
XLA Modules:
  0.0 66.0 jit_solution(12732234789318657203)
XLA Ops:
  1.3 1.4 %shard_map.122 = (f32[144,128]{1,0:T(8,128)S(1)}, f32[2048,128]{1,0:T(8,128)S(1)}, f32[384,128]{1,0:T(8,128)S(1)}, f32[128,128]{1,0:T(8,128)S(1)}, bf16[256,256]{1,0:T(8,128)(2,1)S(1)}) custom-call(s32[1]{0:T(128)S(6)} %copy.13.count, s32[1]{0:T(128)} %bitcast.me, f32[2048,128]{1,0:T(8,128)} %bitcast.15, f32[384,128]{1,0:T(8,128)} %bitcast.16, ...), custom_call_target="tpu_custom_call" | custom-call | flops 100000 | bytes 2097152 | tf_op jit(solution)/shard_map/pallas_call | solution.py:528
  3.2 0.9 %collective-permute-done.partner = f32[144,128]{1,0:T(8,128)S(1)} collective-permute-done((f32[144,128]{1,0:T(8,128)S(1)}, f32[144,128]{1,0:T(8,128)S(1)}, u32[]{:S(2)}, u32[]{:S(2)}) %collective-permute-start) | collective-permute-done | bytes 73760 | tf_op jit(solution)/shard_map/ppermute | solution.py:545
  4.9 3.7 %shard_map.123 = (f32[2048,128]{1,0:T(8,128)S(1)}, f32[2560,128]{1,0:T(8,128)S(1)}, f32[2560,128]{1,0:T(8,128)S(1)}, f32[2048,128]{1,0:T(8,128)S(1)}) custom-call(f32[2048,128]{1,0:T(8,128)S(1)} %get-tuple-element.29.probes, f32[384,128]{1,0:T(8,128)S(1)} %get-tuple-element.30.sources, f32[144,128]{1,0:T(8,128)S(1)} %get-tuple-element.31.statics.own, ...), custom_call_target="tpu_custom_call" | custom-call | flops 600000000 | bytes 6291456 | tf_op jit(solution)/shard_map/pallas_call | solution.py:528
  8.6 4.3 %collective-permute-start.2 = (f32[288,128]{1,0:T(8,128)S(1)}, f32[288,128]{1,0:T(8,128)S(1)}, u32[]{:S(2)}, u32[]{:S(2)}) collective-permute-start(f32[288,128]{1,0:T(8,128)S(1)} %collective-permute-done.1.passed), channel_id=1, source_target_pairs={{0,1},{1,0},{2,3},{3,2},{4,5},{5,4},{6,7},{7,6},{8,9},{9,8},{10,11... | collective-permute-start | bytes 442376 | tf_op jit(solution)/shard_map/ppermute | solution.py:545
  12.9 1.0 %collective-permute-done.2.across = f32[288,128]{1,0:T(8,128)S(1)} collective-permute-done((f32[288,128]{1,0:T(8,128)S(1)}, f32[288,128]{1,0:T(8,128)S(1)}, u32[]{:S(2)}, u32[]{:S(2)}) %collective-permute-start.2) | collective-permute-done | bytes 147488 | tf_op jit(solution)/shard_map/ppermute | solution.py:545
  13.9 7.9 %shard_map.124 = (f32[136,128]{1,0:T(8,128)S(1)}, f32[136,128]{1,0:T(8,128)S(1)}, bf16[2560,512]{1,0:T(8,128)(2,1)S(1)}, bf16[640,512]{1,0:T(8,128)(2,1)S(1)}, f...) custom-call(s32[1]{0:T(128)} %bitcast.me, ...), custom_call_target="tpu_custom_call" | custom-call | flops 3000000000 | bytes 6291456 | tf_op jit(solution)/shard_map/pallas_call | solution.py:528
  22.3 0.9 %collective-permute-done.3 = f32[136,128]{1,0:T(8,128)S(1)} collective-permute-done((f32[136,128]{1,0:T(8,128)S(1)}, f32[136,128]{1,0:T(8,128)S(1)}, u32[]{:S(2)}, u32[]{:S(2)}) %collective-permute-start.3) | collective-permute-done | bytes 69664 | tf_op jit(solution)/shard_map/ppermute | solution.py:545
  23.2 2.6 %collective-permute-start.4 = (f32[136,128]{1,0:T(8,128)S(1)}, f32[136,128]{1,0:T(8,128)S(1)}, u32[]{:S(2)}, u32[]{:S(2)}) collective-permute-start(f32[136,128]{1,0:T(8,128)S(1)} %add.18.when), channel_id=1, source_target_pairs={{0,2},{1,3},{2,0},{3,1},{4,6},{5,7},{6,4},{7,5},{8,10},{9,11},{10,... | collective-permute-start | bytes 208904 | tf_op jit(solution)/shard_map/ppermute | solution.py:545
  25.8 1.6 %shard_map.125.basis = bf16[512,2048]{1,0:T(8,128)(2,1)S(1)} custom-call(f32[8192,128]{1,0:T(8,128)S(1)} %bitcast.12, f32[136,128]{1,0:T(8,128)S(1)} %add.18.when), custom_call_target="tpu_custom_call" | custom-call | flops 10000000 | bytes 4194304 | tf_op jit(solution)/shard_map/pallas_call | solution.py:528
  27.4 0.9 %collective-permute-done.4 = f32[136,128]{1,0:T(8,128)S(1)} collective-permute-done((f32[136,128]{1,0:T(8,128)S(1)}, f32[136,128]{1,0:T(8,128)S(1)}, u32[]{:S(2)}, u32[]{:S(2)}) %collective-permute-start.4) | collective-permute-done | bytes 69664 | tf_op jit(solution)/shard_map/ppermute | solution.py:545
  28.3 1.9 %collective-permute-start.5 = (f32[136,128]{1,0:T(8,128)S(1)}, f32[136,128]{1,0:T(8,128)S(1)}, u32[]{:S(2)}, u32[]{:S(2)}) collective-permute-start(f32[136,128]{1,0:T(8,128)S(1)} %add.19.when), channel_id=1, source_target_pairs={{0,4},{1,5},{2,6},{3,7},{4,0},{5,1},{6,2},{7,3},{8,12},{9,13},{10,... | collective-permute-start | bytes 208904 | tf_op jit(solution)/shard_map/ppermute | solution.py:545
  30.2 1.6 %shard_map.126.basis_two = bf16[512,2048]{1,0:T(8,128)(2,1)S(1)} custom-call(f32[8192,128]{1,0:T(8,128)S(1)} %bitcast.13, f32[136,128]{1,0:T(8,128)S(1)} %add.19.when), custom_call_target="tpu_custom_call" | custom-call | flops 10000000 | bytes 4194304 | tf_op jit(solution)/shard_map/pallas_call | solution.py:528
  31.8 0.9 %collective-permute-done.5 = f32[136,128]{1,0:T(8,128)S(1)} collective-permute-done((f32[136,128]{1,0:T(8,128)S(1)}, f32[136,128]{1,0:T(8,128)S(1)}, u32[]{:S(2)}, u32[]{:S(2)}) %collective-permute-start.5) | collective-permute-done | bytes 69664 | tf_op jit(solution)/shard_map/ppermute | solution.py:545
  32.7 2.9 %collective-permute-start.6 = (f32[136,128]{1,0:T(8,128)S(1)}, f32[136,128]{1,0:T(8,128)S(1)}, u32[]{:S(2)}, u32[]{:S(2)}) collective-permute-start(f32[136,128]{1,0:T(8,128)S(1)} %add.20), channel_id=1, source_target_pairs={{0,8},{1,9},{2,10},{3,11},{4,12},{5,13},{6,14},{7,15},{8,0},{9,1},... | collective-permute-start | bytes 208904 | tf_op jit(solution)/shard_map/ppermute | solution.py:545
  35.6 2.4 %collective-permute-done.6 = f32[136,128]{1,0:T(8,128)S(1)} collective-permute-done((f32[136,128]{1,0:T(8,128)S(1)}, f32[136,128]{1,0:T(8,128)S(1)}, u32[]{:S(2)}, u32[]{:S(2)}) %collective-permute-start.6) | collective-permute-done | bytes 69664 | tf_op jit(solution)/shard_map/ppermute | solution.py:545
  38.1 1.2 %collective-permute-done.7.other = f32[136,128]{1,0:T(8,128)S(1)} collective-permute-done((f32[136,128]{1,0:T(8,128)S(1)}, f32[136,128]{1,0:T(8,128)S(1)}, u32[]{:S(2)}, u32[]{:S(2)}) %collective-permute-start.7) | collective-permute-done | bytes 69664 | tf_op jit(solution)/shard_map/ppermute | solution.py:545
  39.3 10.4 %shard_map.127 = (f32[2048,128]{1,0:T(8,128)S(1)}, f32[16,64]{1,0:T(8,128)S(1)}) custom-call(s32[1]{0:T(128)} %bitcast.me, f32[136,128]{1,0:T(8,128)S(1)} %add.21.half, f32[136,128]{1,0:T(8,128)S(1)} %collective-permute-done.7.other, bf16[2560,512]{1,0:T(8,128)(2,1)S(1)} %get-tuple-element.42.cell_ref, bf16[640,512]{1,0:T(8,128)(2,1)S(1)} %get-tuple-element.43.slot_ref, ...), custom_call_target="tpu_custom_call" | custom-call | flops 5000000000 | bytes 10485760 | tf_op jit(solution)/shard_map/pallas_call | solution.py:528
  49.8 1.0 %collective-permute-done.8 = f32[16,64]{1,0:T(8,128)S(1)} collective-permute-done((f32[16,64]{1,0:T(8,128)S(1)}, f32[16,64]{1,0:T(8,128)S(1)}, u32[]{:S(2)}, u32[]{:S(2)}) %collective-permute-start.8) | collective-permute-done | bytes 4128 | tf_op jit(solution)/shard_map/ppermute | solution.py:545
  50.9 1.8 %collective-permute-start.9 = (f32[16,64]{1,0:T(8,128)S(1)}, f32[16,64]{1,0:T(8,128)S(1)}, u32[]{:S(2)}, u32[]{:S(2)}) collective-permute-start(f32[16,64]{1,0:T(8,128)S(1)} %add.22), channel_id=1, source_target_pairs={{0,2},{1,3},{2,0},{3,1},{4,6},{5,7},{6,4},{7,5},{8,10},{9,11},{10,... | collective-permute-start | bytes 12296 | tf_op jit(solution)/shard_map/ppermute | solution.py:545
  52.7 1.8 %collective-permute-done.9 = f32[16,64]{1,0:T(8,128)S(1)} collective-permute-done((f32[16,64]{1,0:T(8,128)S(1)}, f32[16,64]{1,0:T(8,128)S(1)}, u32[]{:S(2)}, u32[]{:S(2)}) %collective-permute-start.9) | collective-permute-done | bytes 4128 | tf_op jit(solution)/shard_map/ppermute | solution.py:545
  54.5 4.5 %collective-permute-start.12 = (f32[16,64]{1,0:T(8,128)S(1)}, f32[16,64]{1,0:T(8,128)S(1)}, u32[]{:S(2)}, u32[]{:S(2)}) collective-permute-start(f32[16,64]{1,0:T(8,128)S(1)} %add.23.rest_0_), channel_id=1, source_target_pairs={{0,12},{1,13},{2,14},{3,15},{4,8},{5,9},{6,10},{7,11},{8,4},{9,5},... | collective-permute-start | bytes 12296 | tf_op jit(solution)/shard_map/ppermute | solution.py:545
  59.6 1.1 %collective-permute-done.12.rest_3_ = f32[16,64]{1,0:T(8,128)S(1)} collective-permute-done((f32[16,64]{1,0:T(8,128)S(1)}, f32[16,64]{1,0:T(8,128)S(1)}, u32[]{:S(2)}, u32[]{:S(2)}) %collective-permute-start.12) | collective-permute-done | bytes 4128 | tf_op jit(solution)/shard_map/ppermute | solution.py:545
  60.6 2.9 %collective-permute-done.11.rest_2_ = f32[16,64]{1,0:T(8,128)S(1)} collective-permute-done((f32[16,64]{1,0:T(8,128)S(1)}, f32[16,64]{1,0:T(8,128)S(1)}, u32[]{:S(2)}, u32[]{:S(2)}) %collective-permute-start.11) | collective-permute-done | bytes 4128 | tf_op jit(solution)/shard_map/ppermute | solution.py:545
  63.5 2.4 %shard_map.128 = (f32[16,4,32,128]{3,2,1,0:T(8,128)}, f32[16,64]{1,0:T(8,128)}) custom-call(f32[2048,128]{1,0:T(8,128)S(1)} %get-tuple-element.52.image, bf16[512,2048]{1,0:T(8,128)(2,1)S(1)} %shard_map.125.basis, bf16[512,2048]{1,0:T(8,128)(2,1)S(1)} %shard_map.126.basis_two, f32[16,64]{1,0:T(8,128)S(1)} %add.23.rest_0_, ...), custom_call_target="tpu_custom_call" | custom-call | flops 200000000 | bytes 6291456 | tf_op jit(solution)/shard_map/pallas_call | solution.py:528
  (20 shorter events, 2.5 us)
Async XLA Ops:
  0.6 13.3 %copy-start.1 = (f32[128]{0:T(128)S(1)}, f32[128]{0:T(128)}, u32[]{:S(2)}) copy-start(f32[128]{0:T(128)} %param.21) | copy-start | bytes 1540
  2.7 1.4 %collective-permute-start = (f32[144,128]{1,0:T(8,128)S(1)}, f32[144,128]{1,0:T(8,128)S(1)}, u32[]{:S(2)}, u32[]{:S(2)}) collective-permute-start(f32[144,128]{1,0:T(8,128)S(1)} %get-tuple-element.31.statics.own), channel_id=1, source_target_pairs={{0,1},{1,0},{2,3},{3,2},{4,5},{5,4},{6,7},{7,6},{8,9},{9,8},{10,11... | collective-permute-start | bytes 221192 | tf_op jit(solution)/shard_map/ppermute | solution.py:545
  4.2 4.4 %collective-permute-start.1 = (f32[288,128]{1,0:T(8,128)S(1)}, f32[288,128]{1,0:T(8,128)S(1)}, u32[]{:S(2)}, u32[]{:S(2)}) collective-permute-start(f32[288,128]{1,0:T(8,128)S(1)} %pad_maximum_fusion), channel_id=1, source_target_pairs={{1,2},{2,1},{3,4},{4,3},{5,6},{6,5},{7,8},{8,7},{9,10},{10,9},{11,... | collective-permute-start | bytes 442376 | tf_op jit(solution)/shard_map/ppermute | solution.py:597
  8.6 5.3 %collective-permute-start.2 = (f32[288,128]{1,0:T(8,128)S(1)}, f32[288,128]{1,0:T(8,128)S(1)}, u32[]{:S(2)}, u32[]{:S(2)}) collective-permute-start(f32[288,128]{1,0:T(8,128)S(1)} %collective-permute-done.1.passed), channel_id=1, source_target_pairs={{0,1},{1,0},{2,3},{3,2},{4,5},{5,4},{6,7},{7,6},{8,9},{9,8},{10,11... | collective-permute-start | bytes 442376 | tf_op jit(solution)/shard_map/ppermute | solution.py:545
  13.9 11.9 %copy-start = (f32[64,4,32,128]{3,2,1,0:T(8,128)S(1)}, f32[64,4,32,128]{3,2,1,0:T(8,128)}, u32[]{:S(2)}) copy-start(f32[64,4,32,128]{3,2,1,0:T(8,128)} %param.15) | copy-start | bytes 12582916
  21.8 1.3 %collective-permute-start.3 = (f32[136,128]{1,0:T(8,128)S(1)}, f32[136,128]{1,0:T(8,128)S(1)}, u32[]{:S(2)}, u32[]{:S(2)}) collective-permute-start(f32[136,128]{1,0:T(8,128)S(1)} %get-tuple-element.39), channel_id=1, source_target_pairs={{0,1},{1,0},{2,3},{3,2},{4,5},{5,4},{6,7},{7,6},{8,9},{9,8},{10,11... | collective-permute-start | bytes 208904 | tf_op jit(solution)/shard_map/ppermute | solution.py:545
  23.2 5.1 %collective-permute-start.4 = (f32[136,128]{1,0:T(8,128)S(1)}, f32[136,128]{1,0:T(8,128)S(1)}, u32[]{:S(2)}, u32[]{:S(2)}) collective-permute-start(f32[136,128]{1,0:T(8,128)S(1)} %add.18.when), channel_id=1, source_target_pairs={{0,2},{1,3},{2,0},{3,1},{4,6},{5,7},{6,4},{7,5},{8,10},{9,11},{10,... | collective-permute-start | bytes 208904 | tf_op jit(solution)/shard_map/ppermute | solution.py:545
  28.3 4.4 %collective-permute-start.5 = (f32[136,128]{1,0:T(8,128)S(1)}, f32[136,128]{1,0:T(8,128)S(1)}, u32[]{:S(2)}, u32[]{:S(2)}) collective-permute-start(f32[136,128]{1,0:T(8,128)S(1)} %add.19.when), channel_id=1, source_target_pairs={{0,4},{1,5},{2,6},{3,7},{4,0},{5,1},{6,2},{7,3},{8,12},{9,13},{10,... | collective-permute-start | bytes 208904 | tf_op jit(solution)/shard_map/ppermute | solution.py:545
  32.7 5.3 %collective-permute-start.6 = (f32[136,128]{1,0:T(8,128)S(1)}, f32[136,128]{1,0:T(8,128)S(1)}, u32[]{:S(2)}, u32[]{:S(2)}) collective-permute-start(f32[136,128]{1,0:T(8,128)S(1)} %add.20), channel_id=1, source_target_pairs={{0,8},{1,9},{2,10},{3,11},{4,12},{5,13},{6,14},{7,15},{8,0},{9,1},... | collective-permute-start | bytes 208904 | tf_op jit(solution)/shard_map/ppermute | solution.py:545
  38.0 1.3 %collective-permute-start.7 = (f32[136,128]{1,0:T(8,128)S(1)}, f32[136,128]{1,0:T(8,128)S(1)}, u32[]{:S(2)}, u32[]{:S(2)}) collective-permute-start(f32[136,128]{1,0:T(8,128)S(1)} %add.21.half), channel_id=1, source_target_pairs={{0,1},{1,0},{2,3},{3,2},{4,5},{5,4},{6,7},{7,6},{8,9},{9,8},{10,11... | collective-permute-start | bytes 208904 | tf_op jit(solution)/shard_map/ppermute | solution.py:545
  49.7 1.2 %collective-permute-start.8 = (f32[16,64]{1,0:T(8,128)S(1)}, f32[16,64]{1,0:T(8,128)S(1)}, u32[]{:S(2)}, u32[]{:S(2)}) collective-permute-start(f32[16,64]{1,0:T(8,128)S(1)} %get-tuple-element.53), channel_id=1, source_target_pairs={{0,1},{1,0},{2,3},{3,2},{4,5},{5,4},{6,7},{7,6},{8,9},{9,8},{10,11... | collective-permute-start | bytes 12296 | tf_op jit(solution)/shard_map/ppermute | solution.py:545
  50.9 3.7 %collective-permute-start.9 = (f32[16,64]{1,0:T(8,128)S(1)}, f32[16,64]{1,0:T(8,128)S(1)}, u32[]{:S(2)}, u32[]{:S(2)}) collective-permute-start(f32[16,64]{1,0:T(8,128)S(1)} %add.22), channel_id=1, source_target_pairs={{0,2},{1,3},{2,0},{3,1},{4,6},{5,7},{6,4},{7,5},{8,10},{9,11},{10,... | collective-permute-start | bytes 12296 | tf_op jit(solution)/shard_map/ppermute | solution.py:545
  54.5 6.1 %collective-permute-start.12 = (f32[16,64]{1,0:T(8,128)S(1)}, f32[16,64]{1,0:T(8,128)S(1)}, u32[]{:S(2)}, u32[]{:S(2)}) collective-permute-start(f32[16,64]{1,0:T(8,128)S(1)} %add.23.rest_0_), channel_id=1, source_target_pairs={{0,12},{1,13},{2,14},{3,15},{4,8},{5,9},{6,10},{7,11},{8,4},{9,5},... | collective-permute-start | bytes 12296 | tf_op jit(solution)/shard_map/ppermute | solution.py:545
  59.0 4.5 %collective-permute-start.11 = (f32[16,64]{1,0:T(8,128)S(1)}, f32[16,64]{1,0:T(8,128)S(1)}, u32[]{:S(2)}, u32[]{:S(2)}) collective-permute-start(f32[16,64]{1,0:T(8,128)S(1)} %add.23.rest_0_), channel_id=1, source_target_pairs={{0,8},{1,9},{2,10},{3,11},{4,12},{5,13},{6,14},{7,15},{8,0},{9,1},... | collective-permute-start | bytes 12296 | tf_op jit(solution)/shard_map/ppermute | solution.py:545
  59.0 4.5 %collective-permute-start.10 = (f32[16,64]{1,0:T(8,128)S(1)}, f32[16,64]{1,0:T(8,128)S(1)}, u32[]{:S(2)}, u32[]{:S(2)}) collective-permute-start(f32[16,64]{1,0:T(8,128)S(1)} %add.23.rest_0_), channel_id=1, source_target_pairs={{0,4},{1,5},{2,6},{3,7},{4,0},{5,1},{6,2},{7,3},{8,12},{9,13},{10,... | collective-permute-start | bytes 12296 | tf_op jit(solution)/shard_map/ppermute | solution.py:545

commit v8 on v7

v8 whole, which is shorter than its diff:
```python
import functools

import jax
import jax.numpy as jnp
from jax import lax
from jax.experimental import pallas as pl
from jax.experimental.pallas import tpu as pltpu
from jax.sharding import PartitionSpec as P

STENCIL = (-205.0 / 72.0, 8.0 / 5.0, -1.0 / 5.0, 8.0 / 315.0, -1.0 / 560.0)
CENTER = 3.0 * STENCIL[0]
REACH = 4
LAYERS = 4
PAIR = 8
TILES = 6
PADDED = 40
HALF = 128
PLACES = 512
F32 = jnp.float32
BF16 = jnp.bfloat16
NT = (((1,), (1,)), ((), ()))


def split(value):
    high = value.astype(BF16)
    low = (value - high.astype(F32)).astype(BF16)
    return high, low


def at(row, count=16):
    return pl.ds(pl.multiple_of(row, 8), count)


def window(ref, start, size):
    return ref.at[pl.ds(pl.multiple_of(start, 8), size)]


def kept_rows(load):
    rows = {}

    def get(layer, y):
        if (layer, y) not in rows:
            rows[layer, y] = load(layer, y)
        return rows[layer, y]

    return get


def spread(ref, row, fields):
    return jnp.broadcast_to(ref[pl.ds(row, 1), :], (fields, HALF))


def clear_margins(ref, layers, fields):
    margin = jnp.zeros((REACH * fields, HALF), F32)
    for layer in range(layers):
        start = layer * PADDED * fields
        ref[start : start + REACH * fields, :] = margin
        start += (PADDED - REACH) * fields
        ref[start : start + REACH * fields, :] = margin


def along_z(ref, first, layers, fields, band_ref, out_ref, row=0):
    pieces = [ref[at(((first + x) * PADDED + REACH) * fields, 32 * fields), :] for x in range(layers)]
    high, low = split(jnp.concatenate(pieces, axis=0))
    both = jnp.dot(jnp.concatenate([high, low], axis=1), band_ref[...], preferred_element_type=F32)
    out_ref[at(row, layers * 32 * fields), :] = both[:, :HALF] + both[:, HALF:]


def laplacian(get, x, y, z_term, lowest, highest):
    total = z_term
    for k in range(1, REACH + 1):
        ring = get(x, y + k) + get(x, y - k)
        if x + k <= highest:
            ring = ring + get(x + k, y)
        if x - k >= lowest:
            ring = ring + get(x - k, y)
        total = total + STENCIL[k] * ring
    return total


def pack(
    count, me, probes, sources, prior, kappa, cell, owner, slot, weight, scale,
    statics, probes_out, sources_out, prior_out, lent, band_ref, small_int, small_float, sem,
):
    rows = cell.shape[0]
    cells = kappa.shape[0]
    half = probes_out.shape[0]
    mine = me[0] % 2
    other = probes.at[pl.ds(pl.multiple_of((1 - mine) * half, 8), half)]
    small = [
        pltpu.make_async_copy(kappa, statics.at[pl.ds(0, cells)], sem.at[0]),
        pltpu.make_async_copy(cell, small_int.at[0], sem.at[1]),
        pltpu.make_async_copy(owner, small_int.at[1], sem.at[2]),
        pltpu.make_async_copy(slot, small_int.at[2], sem.at[3]),
        pltpu.make_async_copy(weight, small_float.at[pl.ds(0, rows)], sem.at[4]),
        pltpu.make_async_copy(scale, small_float.at[pl.ds(8, 1)], sem.at[5]),
    ]
    large = [
        pltpu.make_async_copy(other, lent.at[pl.ds(0, half)], sem.at[6]),
        pltpu.make_async_copy(sources, lent.at[pl.ds(half, 3 * cells)], sem.at[7]),
        pltpu.make_async_copy(prior, lent.at[pl.ds(half + 3 * cells, cells)], sem.at[8]),
        pltpu.make_async_copy(probes.at[pl.ds(pl.multiple_of(mine * half, 8), half)], probes_out, sem.at[9]),
        pltpu.make_async_copy(sources, sources_out, sem.at[10]),
        pltpu.make_async_copy(prior, prior_out, sem.at[11]),
    ]
    for copy in small + large:
        copy.start()
    apart = lax.broadcasted_iota(jnp.int32, (HALF, HALF), 0) - lax.broadcasted_iota(jnp.int32, (HALF, HALF), 1)
    full = jnp.where(apart == 0, CENTER, jnp.zeros((HALF, HALF), F32))
    for reach in range(1, REACH + 1):
        full = jnp.where(jnp.abs(apart) == reach, STENCIL[reach], full)
    high, low = split(full)
    band_ref[0:HALF, 0:HALF] = high
    band_ref[HALF:, 0:HALF] = high
    band_ref[0:HALF, HALF:] = low
    band_ref[HALF:, HALF:] = jnp.zeros_like(low)
    for copy in small:
        copy.wait()
    for i in range(3):
        statics[cells + i * rows : cells + (i + 1) * rows, :] = small_int[i].astype(F32)
    place = lax.broadcasted_iota(jnp.int32, (rows, HALF), 0) * HALF
    place = place + lax.broadcasted_iota(jnp.int32, (rows, HALF), 1)
    live = jnp.where(place < count[0], small_float[0:rows, :], 0.0)
    statics[cells + 3 * rows : cells + 4 * rows, :] = live
    statics[cells + 4 * rows : cells + 4 * rows + 8, :] = jnp.broadcast_to(small_float[8:9, :], (8, HALF))
    for copy in large:
        copy.wait()


def forward_own(
    fields, me, probes, sources, prior, own, partner, borrowed, band_ref,
    turned, first, second, third, push_ref, prior_ref, z_term, speed_ref,
):
    slab, flat, cells = PADDED * fields, 32 * fields, LAYERS * 32
    ahead = 24 * fields
    half = probes.shape[0]
    mine = me[0] % 2
    clear_margins(first, PAIR, fields)
    clear_margins(second, PAIR, fields)
    lent = borrowed.at[pl.ds(half, 4 * cells)]
    for side, pushes, damping, statics in ((mine, sources, prior, own), (1 - mine, lent, None, partner)):
        for i in range(3):
            push_ref[at(i * 2 * cells + side * cells, cells), :] = pushes[i * cells : (i + 1) * cells, :]
        place = at(side * cells, cells)
        prior_ref[place, :] = lent[3 * cells :, :] if damping is None else damping[...]
        speed_ref[place, :] = statics[0:cells, :]

    def load(chunk, carry):
        for side, ref in ((mine, probes), (1 - mine, borrowed)):
            there = window(turned, side * LAYERS * flat + chunk * 8 * fields, LAYERS * flat - ahead)
            padded = window(first, side * LAYERS * slab + chunk * 8 * fields, LAYERS * slab - ahead)
            here = window(ref, chunk * 8, half - 24)
            push = window(push_ref, side * cells + chunk * 8, cells - 24)
            for x in range(LAYERS):
                for y in range(8):
                    cell = x * 32 + y
                    value = here[pl.ds(cell, fields, stride=HALF), :]
                    there[cell * fields : (cell + 1) * fields, :] = value
                    row = x * slab + (REACH + y) * fields
                    padded[row : row + fields, :] = value * spread(push, cell, fields)
        return carry

    lax.fori_loop(0, 4, load, 0)

    def sweep(field, emit):
        along_z(field, 0, PAIR, fields, band_ref, z_term)

        def body(chunk, carry):
            padded = window(field, chunk * 8 * fields, PAIR * slab - ahead)
            z_part = window(z_term, chunk * 8 * fields, PAIR * flat - ahead)
            speed = window(speed_ref, chunk * 8, 2 * cells - 24)
            push = window(push_ref, chunk * 8, 6 * cells - 24)
            there = window(turned, chunk * 8 * fields, PAIR * flat - ahead)
            put = emit(chunk)

            def load(layer, y):
                row = layer * slab + (REACH + y) * fields
                return padded[row : row + fields, :]

            for side in range(2):
                get = kept_rows(load)
                for y in range(8):
                    for x in range(side * LAYERS, (side + 1) * LAYERS):
                        cell = x * 32 + y
                        row = slice(cell * fields, (cell + 1) * fields)
                        change = spread(speed, cell, fields) * laplacian(get, x, y, z_part[row, :], 0, PAIR - 1)
                        put(x, y, get(x, y), change, there[row, :], push)
            return carry

        lax.fori_loop(0, 4, body, 0)

    def step_one(chunk):
        out = window(second, chunk * 8 * fields, PAIR * slab - ahead)

        def put(x, y, now, change, probe, push):
            change = change + probe * spread(push, 2 * cells + x * 32 + y, fields)
            row = x * slab + (REACH + y) * fields
            out[row : row + fields, :] = 2.0 * now + change

        return put

    sweep(first, step_one)

    def step_two(chunk):
        before = window(first, chunk * 8 * fields, PAIR * slab - ahead)
        out = window(third, chunk * 8 * fields, PAIR * flat - ahead)

        def put(x, y, now, change, probe, push):
            row = x * slab + (REACH + y) * fields
            change = change - before[row : row + fields, :]
            cell = x * 32 + y
            change = change + probe * spread(push, 4 * cells + cell, fields)
            out[cell * fields : (cell + 1) * fields, :] = 2.0 * now + change

        return put

    sweep(second, step_two)


def entry_row(value, row):
    return jnp.concatenate([value[row + i : row + i + 1, :] for i in range(4)], axis=1)


def forward_window(
    fields, peers, me, first, second, third, own, partner, passed, across, band_ref,
    table, cell_ref, slot_ref, speed_ref, line_ref, owner_ref, weight_ref,
    below, above, z_term, total_ref, *samples,
):
    entries = line_ref.shape[1]
    cells = LAYERS * 32
    length = own.shape[0]
    odd = me[0] % 2 == 1
    slab, flat = PADDED * fields, 32 * fields
    clear_margins(below, LAYERS, fields)
    clear_margins(above, LAYERS, fields)
    total_ref[...] = jnp.zeros_like(total_ref)
    mine, theirs = own[...], partner[...]
    low = jnp.where(odd, across[...], passed[...])
    high = jnp.where(odd, passed[...], across[...])
    tiles = (
        low[length:, :],
        low[0:length, :],
        jnp.where(odd, theirs, mine),
        jnp.where(odd, mine, theirs),
        high[0:length, :],
        high[length:, :],
    )
    place = lax.broadcasted_iota(jnp.int32, (PLACES, entries), 0)
    slot_place = lax.broadcasted_iota(jnp.int32, (HALF, entries), 0)
    for tile, value in enumerate(tiles):
        speed_ref[tile * cells : (tile + 1) * cells, :] = value[0:cells, :]
        cell = entry_row(value, cells).astype(jnp.int32)
        owner = entry_row(value, cells + 4).astype(jnp.int32)
        slot = entry_row(value, cells + 8).astype(jnp.int32)
        weight = entry_row(value, cells + 12)
        hot = jnp.where(place == jnp.bitwise_and(cell, PLACES - 1), 1.0, 0.0)
        cell_ref[tile * PLACES : (tile + 1) * PLACES, :] = hot.astype(BF16)
        hot = jnp.where(slot_place == slot, 1.0, 0.0)
        slot_ref[tile * HALF : (tile + 1) * HALF, :] = hot.astype(BF16)
        rows = slice(tile * fields, (tile + 1) * fields)
        line_ref[rows, :] = jnp.broadcast_to(lax.shift_right_logical(cell, 9), (fields, entries))
        owner_ref[rows, :] = jnp.broadcast_to(owner, (fields, entries))
        weight_ref[rows, :] = jnp.broadcast_to(weight, (fields, entries))

    def outward(chunk, carry):
        ahead = 24 * fields
        speed = window(speed_ref, chunk * 8, TILES * cells - 24)
        here = window(first, chunk * 8 * fields, PAIR * slab - ahead)
        down_out, up_out = (window(ref, chunk * 8 * fields, LAYERS * slab - ahead) for ref in (below, above))
        for y in range(8):
            rows = [slice(x * slab + (REACH + y) * fields, x * slab + (REACH + y + 1) * fields) for x in range(PAIR)]
            field = [here[row, :] for row in rows]
            for x in range(LAYERS):
                up = sum(STENCIL[4 + x - other] * field[4 + other] for other in range(x, LAYERS))
                down = sum(STENCIL[4 + other - x] * field[other] for other in range(x + 1))
                up_out[rows[x], :] = spread(speed, 4 * cells + x * 32 + y, fields) * up
                down_out[rows[x], :] = spread(speed, cells + x * 32 + y, fields) * down
        return carry

    lax.fori_loop(0, 4, outward, 0)
    along_z(below, 0, LAYERS, fields, band_ref, z_term, 0)
    along_z(above, 0, LAYERS, fields, band_ref, z_term, cells * fields)

    def far(read, x, y, lowest, highest):
        total = None
        for other in range(lowest, highest + 1):
            if 1 <= abs(x - other) <= REACH:
                term = STENCIL[abs(x - other)] * read(other, y)
                total = term if total is None else total + term
        return total

    def respond(chunk, carry):
        ahead = 16 * fields
        speeds = window(speed_ref, chunk * 16, TILES * cells - 16)
        low_side, high_side = (window(ref, chunk * 16 * fields, LAYERS * slab - ahead) for ref in (below, above))
        inside = window(second, chunk * 16 * fields, PAIR * slab - ahead)
        base = window(third, chunk * 16 * fields, PAIR * flat - ahead)
        z_parts = window(z_term, chunk * 16 * fields, PAIR * flat - ahead)

        def load(layer, y):
            if layer < 0:
                ref, layer = low_side, layer + LAYERS
            elif layer >= PAIR:
                ref, layer = high_side, layer - PAIR
            else:
                ref = inside
            row = layer * slab + (REACH + y) * fields
            return ref[row : row + fields, :]

        for tile in range(TILES):
            sample = samples[tile]
            read = kept_rows(load)
            for y in range(16):
                for x in range(LAYERS):
                    cell = x * 32 + y
                    layer = (tile - 2) * LAYERS + x
                    speed = spread(speeds, tile * cells + cell, fields)
                    if tile in (0, 5):
                        value = speed * far(read, layer, y, -4, 11)
                    elif tile in (2, 3):
                        outside = far(read, layer, y, -4, -1) if tile == 2 else far(read, layer, y, 8, 11)
                        row = ((tile - 2) * cells + cell) * fields
                        value = base[row : row + fields, :] + speed * outside
                    else:
                        row = (tile // 4 * cells + cell) * fields
                        lap = laplacian(read, layer, y, z_parts[row : row + fields, :], -4, 11)
                        value = 2.0 * read(layer, y) + speed * lap
                    row = (x * 4 + y // 4) * fields
                    side = y % 4 * HALF
                    sample[row : row + fields, side : side + HALF] = value
            hot = cell_ref[tile * PLACES : (tile + 1) * PLACES, :]
            picked = jnp.dot(jnp.concatenate(split(sample[...]), axis=0), hot, preferred_element_type=F32)
            picked = picked[: 16 * fields, :] + picked[16 * fields :, :]
            rows = slice(tile * fields, (tile + 1) * fields)
            line = line_ref[rows, :]
            total = total_ref[rows, :]
            for i in range(16):
                chosen = line == i // 4 * 8 + chunk * 4 + i % 4
                total = total + jnp.where(chosen, picked[i * fields : (i + 1) * fields, :], 0.0)
            total_ref[rows, :] = total
        return carry

    lax.fori_loop(0, 2, respond, 0)

    for group in range(peers // 16):
        lefts, rights = [], []
        for tile in range(TILES):
            rows = slice(tile * fields, (tile + 1) * fields)
            value = total_ref[rows, :] * weight_ref[rows, :]
            high = value.astype(BF16).astype(F32)
            owner = owner_ref[rows, :]
            for part in (high, value - high):
                pieces = [jnp.where(owner == group * 16 + i, part, 0.0) for i in range(16)]
                lefts.append(jnp.concatenate(pieces, axis=0).astype(BF16))
                rights.append(slot_ref[tile * HALF : (tile + 1) * HALF, :])
        result = lax.dot_general(
            jnp.concatenate(lefts, axis=1), jnp.concatenate(rights, axis=1), NT, preferred_element_type=F32
        )
        table[group * 16 * fields : (group + 1) * 16 * fields, :] = result
    place = lax.broadcasted_iota(jnp.int32, (peers, HALF), 0)
    scales = jnp.zeros((peers, HALF), F32)
    for position, value in ((me[0], mine), (me[0] + 1 - 2 * (me[0] % 2), theirs)):
        scale = jnp.broadcast_to(value[cells + 16 : cells + 17, :], (peers, HALF))
        scales = jnp.where(place == position, scale, scales)
    table[peers * fields :, :] = scales


def basis_parts(first, basis, when, out):
    rank = basis.shape[0] // HALF

    def body(group, carry):
        here = window(basis, (first + group) * 8, basis.shape[0] - 15 * 8)
        there = window(out, group * rank, rank)
        for step in range(8):
            high, low = split(here[pl.ds(step, rank, stride=HALF), :])
            there[:, step * 256 : step * 256 + HALF] = high
            there[:, step * 256 + HALF : (step + 1) * 256] = low
        return carry

    lax.fori_loop(0, 8, body, 0)


def adjoint(
    fields, peers, me, table, cell_ref, slot_ref, speed_ref, line_ref, owner_ref, weight_ref, turned, push_ref,
    prior_ref, band_ref, own_basis, own_basis_two, other_basis, other_basis_two, kept, lent, coeffs,
    high_ref, low_ref, inner_two, outer_two, inner_one, outer_one, z_term, image, image_parts, scaled, *lefts,
):
    entries = line_ref.shape[1]
    cells = LAYERS * 32
    rank = own_basis.shape[0] // 8
    slab, flat = PADDED * fields, 32 * fields
    ahead = 24 * fields
    clear_margins(inner_two, TILES * LAYERS, fields)
    clear_margins(inner_one, 2 * PAIR, fields)
    for owner in range(peers):
        rows = slice(owner * fields, (owner + 1) * fields)
        scaled[rows, :] = table[rows, :] * table[peers * fields + owner : peers * fields + owner + 1, :]
    for tile in range(TILES):
        rows = slice(tile * fields, (tile + 1) * fields)
        owner = owner_ref[rows, :]
        hot = slot_ref[tile * HALF : (tile + 1) * HALF, :]
        hot = jnp.concatenate([hot, hot], axis=0)
        total = jnp.zeros((fields, entries), F32)
        for group in range(peers // 16):
            parts = split(scaled[group * 16 * fields : (group + 1) * 16 * fields, :])
            found = jnp.dot(jnp.concatenate(parts, axis=1), hot, preferred_element_type=F32)
            for i in range(16):
                total = total + jnp.where(owner == group * 16 + i, found[i * fields : (i + 1) * fields, :], 0.0)
        value = total * weight_ref[rows, :]
        high = value.astype(BF16).astype(F32)
        high_ref[rows, :] = high
        low_ref[rows, :] = value - high

    for tile in range(TILES):
        left = lefts[tile]
        rows = slice(tile * fields, (tile + 1) * fields)
        line, high, low = line_ref[rows, :], high_ref[rows, :], low_ref[rows, :]
        for i in range(0, 32, 2):
            chosen = [line == i, line == i + 1]
            row = slice(i * fields, (i + 2) * fields)
            for part, side in ((high, slice(0, entries)), (low, slice(entries, 2 * entries))):
                both = [jnp.where(which, part, 0.0) for which in chosen]
                left[row, side] = jnp.concatenate(both, axis=0).astype(BF16)
        hot = cell_ref[tile * PLACES : (tile + 1) * PLACES, :]
        value = lax.dot_general(left[...], jnp.concatenate([hot, hot], axis=1), NT, preferred_element_type=F32)
        for i in range(32):
            for step in range(4):
                layer, y = tile * LAYERS + i // 8, i % 8 * 4 + step
                now = value[i * fields : (i + 1) * fields, step * HALF : (step + 1) * HALF]
                if 1 <= tile <= 4:
                    row = ((layer - LAYERS) * 32 + y) * fields
                    outer_two[row : row + fields, :] = now
                speed = spread(speed_ref, layer * 32 + y, fields)
                row = layer * slab + (REACH + y) * fields
                inner_two[row : row + fields, :] = speed * now
        if 1 <= tile <= 4:
            along_z(inner_two, tile * LAYERS, LAYERS, fields, band_ref, z_term, (tile - 1) * cells * fields)

    def step_one(index, carry):
        pair, chunk = index // 4, index % 4
        start, skip = pair * PAIR * slab + chunk * 8 * fields, pair * PAIR * flat + chunk * 8 * fields
        here = window(inner_two, start, 2 * PAIR * slab - ahead)
        two, one, z_part = (window(ref, skip, PAIR * flat - ahead) for ref in (outer_two, outer_one, z_term))
        out = window(inner_one, start, PAIR * slab - ahead)
        speed = window(speed_ref, cells + pair * 2 * cells + chunk * 8, 2 * cells - 24)

        def load(layer, y):
            row = (layer + LAYERS) * slab + (REACH + y) * fields
            return here[row : row + fields, :]

        for side in range(2):
            get = kept_rows(load)
            for y in range(8):
                for x in range(side * LAYERS, (side + 1) * LAYERS):
                    cell = x * 32 + y
                    row = slice(cell * fields, (cell + 1) * fields)
                    now = 2.0 * two[row, :] + laplacian(get, x, y, z_part[row, :], -4, 11)
                    one[row, :] = now
                    row = x * slab + (REACH + y) * fields
                    out[row : row + fields, :] = spread(speed, cell, fields) * now
        return carry

    lax.fori_loop(0, 8, step_one, 0)
    along_z(inner_one, LAYERS, PAIR, fields, band_ref, z_term)
    mine = me[0] % 2

    def step_two(chunk, total):
        skip = chunk * 8 * fields
        here = window(inner_one, skip, 2 * PAIR * slab - ahead)
        two_rows, one_rows = (window(ref, LAYERS * flat + skip, PAIR * flat - ahead) for ref in (outer_two, outer_one))
        z_part, there, out = (window(ref, skip, PAIR * flat - ahead) for ref in (z_term, turned, image))
        push = window(push_ref, chunk * 8, 6 * cells - 24)
        damping = window(prior_ref, chunk * 8, 2 * cells - 24)

        def load(layer, y):
            row = (layer + LAYERS) * slab + (REACH + y) * fields
            return here[row : row + fields, :]

        nothing = jnp.zeros((fields, HALF), F32)
        for side in range(2):
            get = kept_rows(load)
            for y in range(8):
                for x in range(side * LAYERS, (side + 1) * LAYERS):
                    cell = x * 32 + y
                    row = slice(cell * fields, (cell + 1) * fields)
                    two, one = two_rows[row, :], one_rows[row, :]
                    zero = 2.0 * one - two + laplacian(get, x, y, z_part[row, :], -4, 11)
                    value = spread(push, cell, fields) * zero
                    value = value + spread(push, 2 * cells + cell, fields) * one
                    value = value + spread(push, 4 * cells + cell, fields) * two
                    value = value + spread(damping, cell, fields) * there[row, :]
                    out[row, :] = value
                    high = value.astype(BF16).astype(F32)
                    rows, lane = slice(x * 2 * fields, (x + 1) * 2 * fields), y * 256
                    image_parts[rows, lane : lane + HALF] = jnp.concatenate([high, value - high], axis=0).astype(BF16)
                    image_parts[rows, lane + HALF : lane + 256] = jnp.concatenate([high, nothing], axis=0).astype(BF16)
        for side, pieces in ((mine, (own_basis, own_basis_two)), (1 - mine, (other_basis, other_basis_two))):
            for x in range(LAYERS):
                columns = pieces[x // 2][at((x % 2 * 4 + chunk) * rank, rank), :]
                parts = image_parts[at((side * LAYERS + x) * 2 * fields, 2 * fields), :]
                total = total + lax.dot_general(parts, columns, NT, preferred_element_type=F32)
        return total

    total = lax.fori_loop(0, 4, step_two, jnp.zeros((2 * fields, rank), F32))
    coeffs[...] = total[:fields, :] + total[fields:, :]
    kept[...] = image[at(mine * LAYERS * flat, LAYERS * flat), :]
    lent[...] = image[at((1 - mine) * LAYERS * flat, LAYERS * flat), :]


def remainder(fields, me, image, borrowed, basis, basis_two, *rest):
    *shares, out, coeffs, natural, sem = rest
    rank = coeffs.shape[1]
    half = fields // 2
    mine = me[0] % 2
    while len(shares) > 1:
        shares = [shares[i][...] + shares[i + 1][...] for i in range(0, len(shares), 2)]
    total = shares[0][...]
    coeffs[at(mine * half, half), :] = total[:half, :]
    coeffs[at((1 - mine) * half, half), :] = total[half:, :]
    parts = jnp.concatenate(split(total), axis=0)
    whole = natural.reshape(out.shape)
    first, second = (window(natural, side * half * HALF, half * HALF) for side in (mine, 1 - mine))

    def leave(x):
        return pltpu.make_async_copy(whole.at[:, x], out.at[:, x], sem.at[x])

    for x in range(LAYERS):
        for part in range(4):
            columns = (basis, basis_two)[x // 2][(x % 2 * 4 + part) * rank : (x % 2 * 4 + part + 1) * rank, :]
            both = jnp.dot(parts, columns, preferred_element_type=F32)
            for step in range(8):
                cell = x * 32 + part * 8 + step
                side = step * 256
                along = both[:fields, side : side + HALF] + both[:fields, side + HALF : side + 256]
                along = along + both[fields:, side : side + HALF]
                row = slice(cell * half, (cell + 1) * half)
                first[pl.ds(cell, half, stride=HALF), :] = image[row, :] - along[:half, :]
                second[pl.ds(cell, half, stride=HALF), :] = borrowed[row, :] - along[half:, :]
        leave(x).start()
    for x in range(LAYERS):
        leave(x).wait()


def call(kernel, inputs, out_shape, scratch, flops, size, scalars=0, far=0, far_out=0, room=16):
    smem = pl.BlockSpec(memory_space=pltpu.SMEM)
    vmem = pl.BlockSpec(memory_space=pltpu.VMEM)
    hbm = pl.BlockSpec(memory_space=pltpu.HBM)
    inputs = [
        pltpu.with_memory_space_constraint(array, pltpu.HBM) if scalars <= i < scalars + far else array
        for i, array in enumerate(inputs)
    ]
    return pl.pallas_call(
        kernel,
        out_shape=out_shape,
        in_specs=[smem] * scalars + [hbm] * far + [vmem] * (len(inputs) - scalars - far),
        out_specs=[hbm] * far_out + [vmem] * (len(out_shape) - far_out),
        scratch_shapes=scratch,
        cost_estimate=pl.CostEstimate(flops=flops, bytes_accessed=size, transcendentals=0),
        compiler_params=pltpu.CompilerParams(vmem_limit_bytes=room * 2**20),
    )(*inputs)


def struct(*shape, dtype=F32):
    return jax.ShapeDtypeStruct(shape, dtype)


def swapped(array, axis, bits):
    count = lax.axis_size(axis)
    return lax.ppermute(array, axis, [(i, i ^ bits) for i in range(count)])


def local(
    probes,
    sources,
    kappa,
    prior,
    basis,
    entry_cell,
    entry_owner,
    entry_slot,
    entry_weight,
    entry_count,
    trace_weight,
):
    rank = basis.shape[0]
    fields = probes.shape[0] // 2
    entries = entry_cell.shape[0]
    peers = lax.axis_size("space")
    slab, flat = PADDED * fields, 32 * fields
    cells = LAYERS * 32
    rows = entries // HALF
    basis = basis.reshape(rank * cells, HALF)
    me = lax.axis_index("space").astype(jnp.int32).reshape(1)

    own, probes_near, sources_near, prior_near, lent, matrix = call(
        pack,
        (
            entry_count,
            me,
            probes.reshape(2 * fields * cells, HALF),
            sources.reshape(3 * cells, HALF),
            prior.reshape(cells, HALF),
            kappa.reshape(cells, HALF),
            entry_cell.reshape(rows, HALF),
            entry_owner.reshape(rows, HALF),
            entry_slot.reshape(rows, HALF),
            entry_weight.reshape(rows, HALF),
            trace_weight.reshape(1, HALF),
        ),
        [
            struct(cells + 4 * rows + 8, HALF),
            struct(fields * cells, HALF),
            struct(3 * cells, HALF),
            struct(cells, HALF),
            struct((fields + 4) * cells, HALF),
            struct(256, 256, dtype=BF16),
        ],
        [pltpu.VMEM((3, rows, HALF), jnp.int32), pltpu.VMEM((16, HALF), F32), pltpu.SemaphoreType.DMA((12,))],
        100_000,
        2 * 2**20,
        scalars=2,
        far=9,
    )
    partner = swapped(own, "space", 1)
    lent, partner = lax.optimization_barrier((lent, partner))
    borrowed = swapped(lent, "space", 1)
    passed = lax.ppermute(
        jnp.concatenate([own, partner], axis=0),
        "space",
        [pair for i in range(1, peers - 1, 2) for pair in ((i, i + 1), (i + 1, i))],
    )

    turned, first, second, third, push, damping = call(
        functools.partial(forward_own, fields),
        (me, probes_near, sources_near, prior_near, own, partner, borrowed, matrix),
        [
            struct(PAIR * flat, HALF),
            struct(PAIR * slab, HALF),
            struct(PAIR * slab, HALF),
            struct(PAIR * flat, HALF),
            struct(6 * cells, HALF),
            struct(2 * cells, HALF),
        ],
        [pltpu.VMEM((PAIR * flat, HALF), F32), pltpu.VMEM((2 * cells, HALF), F32)],
        600_000_000,
        6 * 2**20,
        scalars=1,
    )
    passed, second = lax.optimization_barrier((passed, second))
    across = swapped(passed, "space", 1)
    across, basis_there = lax.optimization_barrier((across, basis))
    basis_there = swapped(basis_there, "space", 1)
    table, cell_hot, slot_hot, speed, line, owner, weight = call(
        functools.partial(forward_window, fields, peers),
        (me, first, second, third, own, partner, passed, across, matrix),
        [
            struct(peers * (fields + 1), HALF),
            struct(TILES * PLACES, entries, dtype=BF16),
            struct(TILES * HALF, entries, dtype=BF16),
            struct(TILES * cells, HALF),
            struct(TILES * fields, entries, dtype=jnp.int32),
            struct(TILES * fields, entries, dtype=jnp.int32),
            struct(TILES * fields, entries),
        ],
        [
            pltpu.VMEM((LAYERS * slab, HALF), F32),
            pltpu.VMEM((LAYERS * slab, HALF), F32),
            pltpu.VMEM((PAIR * flat, HALF), F32),
            pltpu.VMEM((TILES * fields, entries), F32),
        ]
        + [pltpu.VMEM((16 * fields, PLACES), F32)] * TILES,
        3_000_000_000,
        6 * 2**20,
        scalars=1,
        room=20,
    )
    columns = []
    bits = 2
    while bits < peers:
        arrived = swapped(table, "space", bits)
        for i in ((0,), (1,), (2, 3))[len(columns)] if len(columns) < 3 else ():
            (some,) = call(
                functools.partial(basis_parts, 8 * (i % 2)),
                ((basis, basis_there)[i // 2], table),
                [struct(8 * rank, 2048, dtype=BF16)],
                [],
                10_000_000,
                4 * 2**20,
            )
            columns.append(some)
        arrived, columns = lax.optimization_barrier((arrived, columns))
        table = table + arrived
        bits *= 2
    kept, lent, coeffs = call(
        functools.partial(adjoint, fields, peers),
        (me, table, cell_hot, slot_hot, speed, line, owner, weight, turned, push, damping, matrix, *columns),
        [struct(LAYERS * flat, HALF), struct(LAYERS * flat, HALF), struct(fields, rank)],
        [
            pltpu.VMEM((TILES * fields, entries), F32),
            pltpu.VMEM((TILES * fields, entries), F32),
            pltpu.VMEM((TILES * LAYERS * slab, HALF), F32),
            pltpu.VMEM((2 * PAIR * flat, HALF), F32),
            pltpu.VMEM((2 * PAIR * slab, HALF), F32),
            pltpu.VMEM((2 * PAIR * flat, HALF), F32),
            pltpu.VMEM((2 * PAIR * flat, HALF), F32),
            pltpu.VMEM((PAIR * flat, HALF), F32),
            pltpu.VMEM((2 * PAIR * fields, 2048), BF16),
            pltpu.VMEM((peers * fields, HALF), F32),
        ]
        + [pltpu.VMEM((32 * fields, 2 * entries), BF16)] * TILES,
        5_000_000_000,
        10 * 2**20,
        scalars=1,
        room=30,
    )
    coeffs = jnp.concatenate([coeffs, swapped(coeffs, "space", 1)], axis=0)
    lent, coeffs = lax.optimization_barrier((lent, coeffs))
    borrowed = swapped(lent, "space", 1)
    bits = 2
    while bits * 4 < peers:
        coeffs = coeffs + swapped(coeffs, "space", bits)
        bits *= 2
    shares = [coeffs] + [swapped(coeffs, "space", bits * i) for i in range(1, peers // bits)]
    hess_probe, coeffs = call(
        functools.partial(remainder, 2 * fields),
        (me, kept, borrowed, *columns[:2], *shares),
        [struct(*probes.shape), struct(2 * fields, rank)],
        [pltpu.VMEM((2 * fields * cells, HALF), F32), pltpu.SemaphoreType.DMA((LAYERS,))],
        200_000_000,
        6 * 2**20,
        scalars=1,
        far_out=1,
    )
    return hess_probe, coeffs.T


def solution(mesh):
    return jax.shard_map(
        local,
        mesh=mesh,
        in_specs=(
            P("group", "space", None, None),
            P(None, ("group", "space"), None, None),
            P(("group", "space"), None, None),
            P(("group", "space"), None, None),
            P("group", "space", None, None),
            P(("group", "space")),
            P(("group", "space")),
            P(("group", "space")),
            P(("group", "space")),
            P(("group", "space")),
            P(("group", "space")),
        ),
        out_specs=(P("group", "space", None, None), P("group", None)),
        check_vma=False,
    )
```

time: 66.2 us -> 61.9 us (0.935)
  starting transfers between devices: 20.3 us -> 18 us
  waiting for transfers between devices: 15.1 us -> 14 us
  Pallas kernels: 29.1 us -> 28.3 us
    ppermute x12 -> x13, starting transfers between devices: 19.7 us -> 17.4 us  [swapped(): return lax.ppermute(array, axis, [(i, i ^ bits) for i in range(count)])]
    ppermute x12 -> x13, waiting for transfers between devices: 15.1 us -> 14 us  [swapped(): return lax.ppermute(array, axis, [(i, i ^ bits) for i in range(count)])]
    pallas_call x7 -> x9, Pallas kernels: 29.1 us -> 28.3 us  [call(): pl.pallas_call(kernel, out_shape=out_shape, in_specs=[smem] * scalars + [...]
  transfers between devices with their start and end apart: 13 -> 14, of which waited for: 11 -> 9; matrix products, arithmetic and copies ran while one was open for 0% -> 0% of each run, Pallas kernels for 11% -> 25%
where the time goes in v8:
time: 61.9 us; the launch traced here: 61.8 us
  Pallas kernels  28.3 us (46%)
  starting transfers between devices  18 us (29%)
  waiting for transfers between devices  14 us (23%)
  between operations  1.4 us (2%)
    pallas_call x9, Pallas kernels, call(): pl.pallas_call(kernel, out_shape=out_shape, in_specs=[smem] * scalars + [...  28.3 us
    ppermute x13, starting transfers between devices, swapped(): return lax.ppermute(array, axis, [(i, i ^ bits) for i in range(count)])  17.4 us
    ppermute x13, waiting for transfers between devices, swapped(): return lax.ppermute(array, axis, [(i, i ^ bits) for i in range(count)])  14 us
  transfers between devices with their start and end apart: 14, of which 9 were waited for; matrix products, arithmetic and copies ran while one was open for 0% of the time, Pallas kernels for 25%

profile of v8, /device:TPU:0, one launch (start us, length us, event | category | flops | bytes accessed | tf_op | source)
XLA Modules:
  0.0 61.8 jit_solution(13228278084410929996)
XLA Ops:
  1.3 1.6 %shard_map.122 = (f32[152,128]{1,0:T(8,128)S(1)}, f32[1024,128]{1,0:T(8,128)S(1)}, f32[384,128]{1,0:T(8,128)S(1)}, f32[128,128]{1,0:T(8,128)S(1)}, f32[1536,128]...) custom-call(s32[1]{0:T(128)S(6)} %copy.13.count, s32[1]{0:T(128)} %bitcast.me, f32[2048,128]{1,0:T(8,128)} %bitcast.15, ...), custom_call_target="tpu_custom_call" | custom-call | flops 100000 | bytes 2097152 | tf_op jit(solution)/shard_map/pallas_call | solution.py:552
  5.3 1.2 %collective-permute-done.1.borrowed = f32[1536,128]{1,0:T(8,128)S(1)} collective-permute-done((f32[1536,128]{1,0:T(8,128)S(1)}, f32[1536,128]{1,0:T(8,128)S(1)}, u32[]{:S(2)}, u32[]{:S(2)}) %collective-permute-start.1) | collective-permute-done | bytes 786464 | tf_op jit(solution)/shard_map/ppermute | solution.py:569
  6.6 3.9 %shard_map.123 = (f32[2048,128]{1,0:T(8,128)S(1)}, f32[2560,128]{1,0:T(8,128)S(1)}, f32[2560,128]{1,0:T(8,128)S(1)}, f32[2048,128]{1,0:T(8,128)S(1)}, f32[768,128]{1,0:T(8,128)S(1)}, /*index=5*/f32[256,128]{1,0:T(8,128)S(1)}) custom-call(s32[1]{0:T(128)} %bitcast.me, f32[1024,128]{1,0:T(8,128)S(1)} %get-tuple-element.44.probes, ...), custom_call_target="tpu_custom_call" | custom-call | flops 600000000 | bytes 6291456 | tf_op jit(solution)/shard_map/pallas_call | solution.py:552
  10.5 2.9 %collective-permute-start.3 = (f32[304,128]{1,0:T(8,128)S(1)}, f32[304,128]{1,0:T(8,128)S(1)}, u32[]{:S(2)}, u32[]{:S(2)}) collective-permute-start(f32[304,128]{1,0:T(8,128)S(1)} %collective-permute-done.2.passed), channel_id=1, source_target_pairs={{0,1},{1,0},{2,3},{3,2},{4,5},{5,4},{6,7},{7,6},{8,9},{9,8},{10,11... | collective-permute-start | bytes 466952 | tf_op jit(solution)/shard_map/ppermute | solution.py:569
  13.4 1.0 %collective-permute-done.3.across = f32[304,128]{1,0:T(8,128)S(1)} collective-permute-done((f32[304,128]{1,0:T(8,128)S(1)}, f32[304,128]{1,0:T(8,128)S(1)}, u32[]{:S(2)}, u32[]{:S(2)}) %collective-permute-start.3) | collective-permute-done | bytes 155680 | tf_op jit(solution)/shard_map/ppermute | solution.py:569
  14.8 4.8 %shard_map.124 = (f32[144,128]{1,0:T(8,128)S(1)}, bf16[3072,512]{1,0:T(8,128)(2,1)S(1)}, bf16[768,512]{1,0:T(8,128)(2,1)S(1)}, f32[768,128]{1,0:T(8,128)S(1)}, s...) custom-call(s32[1]{0:T(128)} %bitcast.me, f32[2560,128]{1,0:T(8,128)S(1)} %get-tuple-element.52.first, ...), custom_call_target="tpu_custom_call" | custom-call | flops 3000000000 | bytes 6291456 | tf_op jit(solution)/shard_map/pallas_call | solution.py:552
  19.6 2.4 %collective-permute-start.4 = (f32[144,128]{1,0:T(8,128)S(1)}, f32[144,128]{1,0:T(8,128)S(1)}, u32[]{:S(2)}, u32[]{:S(2)}) collective-permute-start(f32[144,128]{1,0:T(8,128)S(1)} %get-tuple-element.58.when), channel_id=1, source_target_pairs={{0,2},{1,3},{2,0},{3,1},{4,6},{5,7},{6,4},{7,5},{8,10},{9,11},{10,... | collective-permute-start | bytes 221192 | tf_op jit(solution)/shard_map/ppermute | solution.py:569
  22.0 1.6 %shard_map.125.own_basis.basis = bf16[512,2048]{1,0:T(8,128)(2,1)S(1)} custom-call(f32[8192,128]{1,0:T(8,128)S(1)} %bitcast.13, f32[144,128]{1,0:T(8,128)S(1)} %get-tuple-element.58.when), custom_call_target="tpu_custom_call" | custom-call | flops 10000000 | bytes 4194304 | tf_op jit(solution)/shard_map/pallas_call | solution.py:552
  23.6 1.2 %collective-permute-done.4 = f32[144,128]{1,0:T(8,128)S(1)} collective-permute-done((f32[144,128]{1,0:T(8,128)S(1)}, f32[144,128]{1,0:T(8,128)S(1)}, u32[]{:S(2)}, u32[]{:S(2)}) %collective-permute-start.4) | collective-permute-done | bytes 73760 | tf_op jit(solution)/shard_map/ppermute | solution.py:569
  24.8 1.9 %collective-permute-start.5 = (f32[144,128]{1,0:T(8,128)S(1)}, f32[144,128]{1,0:T(8,128)S(1)}, u32[]{:S(2)}, u32[]{:S(2)}) collective-permute-start(f32[144,128]{1,0:T(8,128)S(1)} %add.12.when), channel_id=1, source_target_pairs={{0,4},{1,5},{2,6},{3,7},{4,0},{5,1},{6,2},{7,3},{8,12},{9,13},{10,... | collective-permute-start | bytes 221192 | tf_op jit(solution)/shard_map/ppermute | solution.py:569
  26.7 1.6 %shard_map.126.own_basis_two.basis_two = bf16[512,2048]{1,0:T(8,128)(2,1)S(1)} custom-call(f32[8192,128]{1,0:T(8,128)S(1)} %bitcast.14, f32[144,128]{1,0:T(8,128)S(1)} %add.12.when), custom_call_target="tpu_custom_call" | custom-call | flops 10000000 | bytes 4194304 | tf_op jit(solution)/shard_map/pallas_call | solution.py:552
  28.3 1.0 %collective-permute-done.5 = f32[144,128]{1,0:T(8,128)S(1)} collective-permute-done((f32[144,128]{1,0:T(8,128)S(1)}, f32[144,128]{1,0:T(8,128)S(1)}, u32[]{:S(2)}, u32[]{:S(2)}) %collective-permute-start.5) | collective-permute-done | bytes 73760 | tf_op jit(solution)/shard_map/ppermute | solution.py:569
  29.2 2.9 %collective-permute-start.6 = (f32[144,128]{1,0:T(8,128)S(1)}, f32[144,128]{1,0:T(8,128)S(1)}, u32[]{:S(2)}, u32[]{:S(2)}) collective-permute-start(f32[144,128]{1,0:T(8,128)S(1)} %add.13.when), channel_id=1, source_target_pairs={{0,8},{1,9},{2,10},{3,11},{4,12},{5,13},{6,14},{7,15},{8,0},{9,1},... | collective-permute-start | bytes 221192 | tf_op jit(solution)/shard_map/ppermute | solution.py:569
  32.1 1.6 %shard_map.128.other_basis_two = bf16[512,2048]{1,0:T(8,128)(2,1)S(1)} custom-call(f32[8192,128]{1,0:T(8,128)S(1)} %collective-permute-done.7.basis, f32[144,128]{1,0:T(8,128)S(1)} %add.13.when), custom_call_target="tpu_custom_call" | custom-call | flops 10000000 | bytes 4194304 | tf_op jit(solution)/shard_map/pallas_call | solution.py:552
  33.7 1.6 %shard_map.127.other_basis = bf16[512,2048]{1,0:T(8,128)(2,1)S(1)} custom-call(f32[8192,128]{1,0:T(8,128)S(1)} %collective-permute-done.7.basis, f32[144,128]{1,0:T(8,128)S(1)} %add.13.when), custom_call_target="tpu_custom_call" | custom-call | flops 10000000 | bytes 4194304 | tf_op jit(solution)/shard_map/pallas_call | solution.py:552
  35.4 9.1 %shard_map.129 = (f32[1024,128]{1,0:T(8,128)S(1)}, f32[1024,128]{1,0:T(8,128)S(1)}, f32[8,64]{1,0:T(8,128)S(1)}) custom-call(s32[1]{0:T(128)} %bitcast.me, f32[144,128]{1,0:T(8,128)S(1)} %add.14.table, bf16[3072,512]{1,0:T(8,128)(2,1)S(1)} %get-tuple-element.66.cell_ref, bf16[768,512]{1,0:T(8,128)(2,1)S(1)} %get-tuple-element.67.slot_ref, ...), custom_call_target="tpu_custom_call" | custom-call | flops 5000000000 | bytes 10485760 | tf_op jit(solution)/shard_map/pallas_call | solution.py:552
  44.6 1.2 %collective-permute-done.8 = f32[8,64]{1,0:T(8,128)S(1)} collective-permute-done((f32[8,64]{1,0:T(8,128)S(1)}, f32[8,64]{1,0:T(8,128)S(1)}, u32[]{:S(2)}, u32[]{:S(2)}) %collective-permute-start.8) | collective-permute-done | bytes 2080 | tf_op jit(solution)/shard_map/ppermute | solution.py:569
  45.9 1.5 %collective-permute-start.10 = (f32[16,64]{1,0:T(8,128)S(1)}, f32[16,64]{1,0:T(8,128)S(1)}, u32[]{:S(2)}, u32[]{:S(2)}) collective-permute-start(f32[16,64]{1,0:T(8,128)S(1)} %pad_maximum_fusion.1), channel_id=1, source_target_pairs={{0,2},{1,3},{2,0},{3,1},{4,6},{5,7},{6,4},{7,5},{8,10},{9,11},{10,... | collective-permute-start | bytes 12296 | tf_op jit(solution)/shard_map/ppermute | solution.py:569
  47.4 2.2 %collective-permute-done.10 = f32[16,64]{1,0:T(8,128)S(1)} collective-permute-done((f32[16,64]{1,0:T(8,128)S(1)}, f32[16,64]{1,0:T(8,128)S(1)}, u32[]{:S(2)}, u32[]{:S(2)}) %collective-permute-start.10) | collective-permute-done | bytes 4128 | tf_op jit(solution)/shard_map/ppermute | solution.py:569
  49.6 1.6 %collective-permute-start.11 = (f32[16,64]{1,0:T(8,128)S(1)}, f32[16,64]{1,0:T(8,128)S(1)}, u32[]{:S(2)}, u32[]{:S(2)}) collective-permute-start(f32[16,64]{1,0:T(8,128)S(1)} %add.15.rest_0_), channel_id=1, source_target_pairs={{0,4},{1,5},{2,6},{3,7},{4,0},{5,1},{6,2},{7,3},{8,12},{9,13},{10,... | collective-permute-start | bytes 12296 | tf_op jit(solution)/shard_map/ppermute | solution.py:569
  51.1 2.7 %collective-permute-start.12 = (f32[16,64]{1,0:T(8,128)S(1)}, f32[16,64]{1,0:T(8,128)S(1)}, u32[]{:S(2)}, u32[]{:S(2)}) collective-permute-start(f32[16,64]{1,0:T(8,128)S(1)} %add.15.rest_0_), channel_id=1, source_target_pairs={{0,8},{1,9},{2,10},{3,11},{4,12},{5,13},{6,14},{7,15},{8,0},{9,1},... | collective-permute-start | bytes 12296 | tf_op jit(solution)/shard_map/ppermute | solution.py:569
  54.0 1.7 %collective-permute-done.12.rest_2_ = f32[16,64]{1,0:T(8,128)S(1)} collective-permute-done((f32[16,64]{1,0:T(8,128)S(1)}, f32[16,64]{1,0:T(8,128)S(1)}, u32[]{:S(2)}, u32[]{:S(2)}) %collective-permute-start.12) | collective-permute-done | bytes 4128 | tf_op jit(solution)/shard_map/ppermute | solution.py:569
  55.7 3.6 %collective-permute-done.13.rest_3_ = f32[16,64]{1,0:T(8,128)S(1)} collective-permute-done((f32[16,64]{1,0:T(8,128)S(1)}, f32[16,64]{1,0:T(8,128)S(1)}, u32[]{:S(2)}, u32[]{:S(2)}) %collective-permute-start.13) | collective-permute-done | bytes 4128 | tf_op jit(solution)/shard_map/ppermute | solution.py:569
  59.3 2.5 %shard_map.130 = (f32[16,4,32,128]{3,2,1,0:T(8,128)}, f32[16,64]{1,0:T(8,128)}) custom-call(s32[1]{0:T(128)} %bitcast.me, f32[1024,128]{1,0:T(8,128)S(1)} %get-tuple-element.79.image, f32[1024,128]{1,0:T(8,128)S(1)} %collective-permute-done.9.borrowed, bf16[512,2048]{1,0:T(8,128)(2,1)S(1)} %shard_map.125.own_basis.basis, ...), custom_call_target="tpu_custom_call" | custom-call | flops 200000000 | bytes 6291456 | tf_op jit(solution)/shard_map/pallas_call | solution.py:552
  (21 shorter events, 3.2 us)
Async XLA Ops:
  2.8 1.4 %collective-permute-start = (f32[152,128]{1,0:T(8,128)S(1)}, f32[152,128]{1,0:T(8,128)S(1)}, u32[]{:S(2)}, u32[]{:S(2)}) collective-permute-start(f32[152,128]{1,0:T(8,128)S(1)} %get-tuple-element.47.own), channel_id=1, source_target_pairs={{0,1},{1,0},{2,3},{3,2},{4,5},{5,4},{6,7},{7,6},{8,9},{9,8},{10,11... | collective-permute-start | bytes 233480 | tf_op jit(solution)/shard_map/ppermute | solution.py:569
  4.3 2.3 %collective-permute-start.1 = (f32[1536,128]{1,0:T(8,128)S(1)}, f32[1536,128]{1,0:T(8,128)S(1)}, u32[]{:S(2)}, u32[]{:S(2)}) collective-permute-start(f32[1536,128]{1,0:T(8,128)S(1)} %get-tuple-element.50), channel_id=1, source_target_pairs={{0,1},{1,0},{2,3},{3,2},{4,5},{5,4},{6,7},{7,6},{8,9},{9,8},{10,11... | collective-permute-start | bytes 2359304 | tf_op jit(solution)/shard_map/ppermute | solution.py:569
  4.6 5.9 %collective-permute-start.2 = (f32[304,128]{1,0:T(8,128)S(1)}, f32[304,128]{1,0:T(8,128)S(1)}, u32[]{:S(2)}, u32[]{:S(2)}) collective-permute-start(f32[304,128]{1,0:T(8,128)S(1)} %pad_maximum_fusion), channel_id=1, source_target_pairs={{1,2},{2,1},{3,4},{4,3},{5,6},{6,5},{7,8},{8,7},{9,10},{10,9},{11,... | collective-permute-start | bytes 466952 | tf_op jit(solution)/shard_map/ppermute | solution.py:627
  10.5 3.9 %collective-permute-start.3 = (f32[304,128]{1,0:T(8,128)S(1)}, f32[304,128]{1,0:T(8,128)S(1)}, u32[]{:S(2)}, u32[]{:S(2)}) collective-permute-start(f32[304,128]{1,0:T(8,128)S(1)} %collective-permute-done.2.passed), channel_id=1, source_target_pairs={{0,1},{1,0},{2,3},{3,2},{4,5},{5,4},{6,7},{7,6},{8,9},{9,8},{10,11... | collective-permute-start | bytes 466952 | tf_op jit(solution)/shard_map/ppermute | solution.py:569
  14.4 17.7 %collective-permute-start.7 = (f32[8192,128]{1,0:T(8,128)}, f32[8192,128]{1,0:T(8,128)S(1)}, u32[]{:S(2)}, u32[]{:S(2)}) collective-permute-start(f32[8192,128]{1,0:T(8,128)} %bitcast.12), channel_id=1, source_target_pairs={{0,1},{1,0},{2,3},{3,2},{4,5},{5,4},{6,7},{7,6},{8,9},{9,8},{10,11... | collective-permute-start | bytes 12582920 | tf_op jit(solution)/shard_map/ppermute | solution.py:569
  14.8 7.2 %copy-start = (f32[64,4,32,128]{3,2,1,0:T(8,128)S(1)}, f32[64,4,32,128]{3,2,1,0:T(8,128)}, u32[]{:S(2)}) copy-start(f32[64,4,32,128]{3,2,1,0:T(8,128)} %param.15) | copy-start | bytes 12582916
  19.6 5.2 %collective-permute-start.4 = (f32[144,128]{1,0:T(8,128)S(1)}, f32[144,128]{1,0:T(8,128)S(1)}, u32[]{:S(2)}, u32[]{:S(2)}) collective-permute-start(f32[144,128]{1,0:T(8,128)S(1)} %get-tuple-element.58.when), channel_id=1, source_target_pairs={{0,2},{1,3},{2,0},{3,1},{4,6},{5,7},{6,4},{7,5},{8,10},{9,11},{10,... | collective-permute-start | bytes 221192 | tf_op jit(solution)/shard_map/ppermute | solution.py:569
  24.8 4.4 %collective-permute-start.5 = (f32[144,128]{1,0:T(8,128)S(1)}, f32[144,128]{1,0:T(8,128)S(1)}, u32[]{:S(2)}, u32[]{:S(2)}) collective-permute-start(f32[144,128]{1,0:T(8,128)S(1)} %add.12.when), channel_id=1, source_target_pairs={{0,4},{1,5},{2,6},{3,7},{4,0},{5,1},{6,2},{7,3},{8,12},{9,13},{10,... | collective-permute-start | bytes 221192 | tf_op jit(solution)/shard_map/ppermute | solution.py:569
  29.2 6.1 %collective-permute-start.6 = (f32[144,128]{1,0:T(8,128)S(1)}, f32[144,128]{1,0:T(8,128)S(1)}, u32[]{:S(2)}, u32[]{:S(2)}) collective-permute-start(f32[144,128]{1,0:T(8,128)S(1)} %add.13.when), channel_id=1, source_target_pairs={{0,8},{1,9},{2,10},{3,11},{4,12},{5,13},{6,14},{7,15},{8,0},{9,1},... | collective-permute-start | bytes 221192 | tf_op jit(solution)/shard_map/ppermute | solution.py:569
  44.5 1.2 %collective-permute-start.8 = (f32[8,64]{1,0:T(8,128)S(1)}, f32[8,64]{1,0:T(8,128)S(1)}, u32[]{:S(2)}, u32[]{:S(2)}) collective-permute-start(f32[8,64]{1,0:T(8,128)S(1)} %get-tuple-element.81), channel_id=1, source_target_pairs={{0,1},{1,0},{2,3},{3,2},{4,5},{5,4},{6,7},{7,6},{8,9},{9,8},{10,11... | collective-permute-start | bytes 6152 | tf_op jit(solution)/shard_map/ppermute | solution.py:569
  45.7 13.6 %collective-permute-start.9 = (f32[1024,128]{1,0:T(8,128)S(1)}, f32[1024,128]{1,0:T(8,128)S(1)}, u32[]{:S(2)}, u32[]{:S(2)}) collective-permute-start(f32[1024,128]{1,0:T(8,128)S(1)} %get-tuple-element.82), channel_id=1, source_target_pairs={{0,1},{1,0},{2,3},{3,2},{4,5},{5,4},{6,7},{7,6},{8,9},{9,8},{10,11... | collective-permute-start | bytes 1572872 | tf_op jit(solution)/shard_map/ppermute | solution.py:569
  45.9 3.7 %collective-permute-start.10 = (f32[16,64]{1,0:T(8,128)S(1)}, f32[16,64]{1,0:T(8,128)S(1)}, u32[]{:S(2)}, u32[]{:S(2)}) collective-permute-start(f32[16,64]{1,0:T(8,128)S(1)} %pad_maximum_fusion.1), channel_id=1, source_target_pairs={{0,2},{1,3},{2,0},{3,1},{4,6},{5,7},{6,4},{7,5},{8,10},{9,11},{10,... | collective-permute-start | bytes 12296 | tf_op jit(solution)/shard_map/ppermute | solution.py:569
  49.6 4.4 %collective-permute-start.11 = (f32[16,64]{1,0:T(8,128)S(1)}, f32[16,64]{1,0:T(8,128)S(1)}, u32[]{:S(2)}, u32[]{:S(2)}) collective-permute-start(f32[16,64]{1,0:T(8,128)S(1)} %add.15.rest_0_), channel_id=1, source_target_pairs={{0,4},{1,5},{2,6},{3,7},{4,0},{5,1},{6,2},{7,3},{8,12},{9,13},{10,... | collective-permute-start | bytes 12296 | tf_op jit(solution)/shard_map/ppermute | solution.py:569
  51.1 4.5 %collective-permute-start.12 = (f32[16,64]{1,0:T(8,128)S(1)}, f32[16,64]{1,0:T(8,128)S(1)}, u32[]{:S(2)}, u32[]{:S(2)}) collective-permute-start(f32[16,64]{1,0:T(8,128)S(1)} %add.15.rest_0_), channel_id=1, source_target_pairs={{0,8},{1,9},{2,10},{3,11},{4,12},{5,13},{6,14},{7,15},{8,0},{9,1},... | collective-permute-start | bytes 12296 | tf_op jit(solution)/shard_map/ppermute | solution.py:569
  53.9 5.4 %collective-permute-start.13 = (f32[16,64]{1,0:T(8,128)S(1)}, f32[16,64]{1,0:T(8,128)S(1)}, u32[]{:S(2)}, u32[]{:S(2)}) collective-permute-start(f32[16,64]{1,0:T(8,128)S(1)} %add.15.rest_0_), channel_id=1, source_target_pairs={{0,12},{1,13},{2,14},{3,15},{4,8},{5,9},{6,10},{7,11},{8,4},{9,5},... | collective-permute-start | bytes 12296 | tf_op jit(solution)/shard_map/ppermute | solution.py:569

commit v9 on v8

--- a/solution.py
+++ b/solution.py
@@ -152,12 +152,13 @@
             here = window(ref, chunk * 8, half - 24)
             push = window(push_ref, side * cells + chunk * 8, cells - 24)
             for x in range(LAYERS):
+                rows = [here[p * cells + x * 32 : p * cells + x * 32 + 8, :] for p in range(fields)]
+                values = jnp.swapaxes(jnp.stack(rows, axis=0), 0, 1)
                 for y in range(8):
                     cell = x * 32 + y
-                    value = here[pl.ds(cell, fields, stride=HALF), :]
-                    there[cell * fields : (cell + 1) * fields, :] = value
+                    there[cell * fields : (cell + 1) * fields, :] = values[y]
                     row = x * slab + (REACH + y) * fields
-                    padded[row : row + fields, :] = value * spread(push, cell, fields)
+                    padded[row : row + fields, :] = values[y] * spread(push, cell, fields)
         return carry
 
     lax.fori_loop(0, 4, load, 0)
@@ -383,8 +384,9 @@
 def adjoint(
     fields, peers, me, table, cell_ref, slot_ref, speed_ref, line_ref, owner_ref, weight_ref, turned, push_ref,
     prior_ref, band_ref, own_basis, own_basis_two, other_basis, other_basis_two, kept, lent, coeffs,
-    high_ref, low_ref, inner_two, outer_two, inner_one, outer_one, z_term, image, image_parts, scaled, *lefts,
+    high_ref, low_ref, inner_two, outer_two, inner_one, outer_one, z_term, image, scaled, *scratch,
 ):
+    lefts, image_parts = scratch[:TILES], scratch[TILES:]
     entries = line_ref.shape[1]
     cells = LAYERS * 32
     rank = own_basis.shape[0] // 8
@@ -417,12 +419,12 @@
         line, high, low = line_ref[rows, :], high_ref[rows, :], low_ref[rows, :]
         for i in range(0, 32, 2):
             chosen = [line == i, line == i + 1]
-            row = slice(i * fields, (i + 2) * fields)
-            for part, side in ((high, slice(0, entries)), (low, slice(entries, 2 * entries))):
+            for part, start in ((high, i * fields), (low, (32 + i) * fields)):
                 both = [jnp.where(which, part, 0.0) for which in chosen]
-                left[row, side] = jnp.concatenate(both, axis=0).astype(BF16)
+                left[start : start + 2 * fields, :] = jnp.concatenate(both, axis=0).astype(BF16)
         hot = cell_ref[tile * PLACES : (tile + 1) * PLACES, :]
-        value = lax.dot_general(left[...], jnp.concatenate([hot, hot], axis=1), NT, preferred_element_type=F32)
+        value = lax.dot_general(left[...], hot, NT, preferred_element_type=F32)
+        value = value[: 32 * fields, :] + value[32 * fields :, :]
         for i in range(32):
             for step in range(4):
                 layer, y = tile * LAYERS + i // 8, i % 8 * 4 + step
@@ -464,7 +466,7 @@
     along_z(inner_one, LAYERS, PAIR, fields, band_ref, z_term)
     mine = me[0] % 2
 
-    def step_two(chunk, total):
+    def step_two(chunk, total, image_parts):
         skip = chunk * 8 * fields
         here = window(inner_one, skip, 2 * PAIR * slab - ahead)
         two_rows, one_rows = (window(ref, LAYERS * flat + skip, PAIR * flat - ahead) for ref in (outer_two, outer_one))
@@ -496,12 +498,14 @@
                     image_parts[rows, lane + HALF : lane + 256] = jnp.concatenate([high, nothing], axis=0).astype(BF16)
         for side, pieces in ((mine, (own_basis, own_basis_two)), (1 - mine, (other_basis, other_basis_two))):
             for x in range(LAYERS):
-                columns = pieces[x // 2][at((x % 2 * 4 + chunk) * rank, rank), :]
+                columns = pieces[x // 2][(x % 2 * 4 + chunk) * rank : (x % 2 * 4 + chunk + 1) * rank, :]
                 parts = image_parts[at((side * LAYERS + x) * 2 * fields, 2 * fields), :]
                 total = total + lax.dot_general(parts, columns, NT, preferred_element_type=F32)
         return total
 
-    total = lax.fori_loop(0, 4, step_two, jnp.zeros((2 * fields, rank), F32))
+    total = jnp.zeros((2 * fields, rank), F32)
+    for chunk in range(4):
+        total = step_two(chunk, total, image_parts[chunk])
     coeffs[...] = total[:fields, :] + total[fields:, :]
     kept[...] = image[at(mine * LAYERS * flat, LAYERS * flat), :]
     lent[...] = image[at((1 - mine) * LAYERS * flat, LAYERS * flat), :]
@@ -528,14 +532,19 @@
         for part in range(4):
             columns = (basis, basis_two)[x // 2][(x % 2 * 4 + part) * rank : (x % 2 * 4 + part + 1) * rank, :]
             both = jnp.dot(parts, columns, preferred_element_type=F32)
+            cell = x * 32 + part * 8
+            results = ([], [])
             for step in range(8):
-                cell = x * 32 + part * 8 + step
                 side = step * 256
                 along = both[:fields, side : side + HALF] + both[:fields, side + HALF : side + 256]
                 along = along + both[fields:, side : side + HALF]
-                row = slice(cell * half, (cell + 1) * half)
-                first[pl.ds(cell, half, stride=HALF), :] = image[row, :] - along[:half, :]
-                second[pl.ds(cell, half, stride=HALF), :] = borrowed[row, :] - along[half:, :]
+                row = slice((cell + step) * half, (cell + step + 1) * half)
+                results[0].append(image[row, :] - along[:half, :])
+                results[1].append(borrowed[row, :] - along[half:, :])
+            for ref, values in zip((first, second), results):
+                values = jnp.swapaxes(jnp.stack(values, axis=0), 0, 1)
+                for p in range(half):
+                    ref[p * HALF + cell : p * HALF + cell + 8, :] = values[p]
         leave(x).start()
     for x in range(LAYERS):
         leave(x).wait()
@@ -704,10 +713,10 @@
             pltpu.VMEM((2 * PAIR * flat, HALF), F32),
             pltpu.VMEM((2 * PAIR * flat, HALF), F32),
             pltpu.VMEM((PAIR * flat, HALF), F32),
-            pltpu.VMEM((2 * PAIR * fields, 2048), BF16),
             pltpu.VMEM((peers * fields, HALF), F32),
         ]
-        + [pltpu.VMEM((32 * fields, 2 * entries), BF16)] * TILES,
+        + [pltpu.VMEM((64 * fields, entries), BF16)] * TILES
+        + [pltpu.VMEM((2 * PAIR * fields, 2048), BF16)] * 4,
         5_000_000_000,
         10 * 2**20,
         scalars=1,
@@ -720,7 +729,7 @@
     while bits * 4 < peers:
         coeffs = coeffs + swapped(coeffs, "space", bits)
         bits *= 2
-    shares = [coeffs] + [swapped(coeffs, "space", bits * i) for i in range(1, peers // bits)]
+    shares = [swapped(coeffs, "space", bits * i) for i in (3, 2, 1)] + [coeffs]
     hess_probe, coeffs = call(
         functools.partial(remainder, 2 * fields),
         (me, kept, borrowed, *columns[:2], *shares),

time: 61.9 us -> 63.6 us (1.027)
  Pallas kernels: 28.3 us -> 30.8 us
  waiting for transfers between devices: 14 us -> 12.5 us
    pallas_call x9, Pallas kernels: 28.3 us -> 30.8 us  [call(): pl.pallas_call(kernel, out_shape=out_shape, in_specs=[smem] * scalars + [...]
    ppermute x13, waiting for transfers between devices: 14 us -> 12.5 us  [swapped(): return lax.ppermute(array, axis, [(i, i ^ bits) for i in range(count)])]
  transfers between devices with their start and end apart: 14 -> 14, of which waited for: 9 -> 9; matrix products, arithmetic and copies ran while one was open for 0% -> 0% of each run, Pallas kernels for 25% -> 23%
where the time goes in v9:
time: 63.6 us; the launch traced here: 63.4 us
  Pallas kernels  30.8 us (48%)
  starting transfers between devices  18.5 us (29%)
  waiting for transfers between devices  12.5 us (20%)
  between operations  1.54 us (2%)
    pallas_call x9, Pallas kernels, call(): pl.pallas_call(kernel, out_shape=out_shape, in_specs=[smem] * scalars + [...  30.8 us
    ppermute x13, starting transfers between devices, swapped(): return lax.ppermute(array, axis, [(i, i ^ bits) for i in range(count)])  17.8 us
    ppermute x13, waiting for transfers between devices, swapped(): return lax.ppermute(array, axis, [(i, i ^ bits) for i in range(count)])  12.5 us
  transfers between devices with their start and end apart: 14, of which 9 were waited for; matrix products, arithmetic and copies ran while one was open for 0% of the time, Pallas kernels for 23%

profile of v9, /device:TPU:0, one launch (start us, length us, event | category | flops | bytes accessed | tf_op | source)
XLA Modules:
  0.0 63.4 jit_solution(14922123676800620441)
XLA Ops:
  1.3 1.6 %shard_map.122 = (f32[152,128]{1,0:T(8,128)S(1)}, f32[1024,128]{1,0:T(8,128)S(1)}, f32[384,128]{1,0:T(8,128)S(1)}, f32[128,128]{1,0:T(8,128)S(1)}, f32[1536,128]...) custom-call(s32[1]{0:T(128)S(6)} %copy.13.count, s32[1]{0:T(128)} %bitcast.me, f32[2048,128]{1,0:T(8,128)} %bitcast.15, ...), custom_call_target="tpu_custom_call" | custom-call | flops 100000 | bytes 2097152 | tf_op jit(solution)/shard_map/pallas_call | solution.py:561
  3.4 0.9 %collective-permute-done.partner = f32[152,128]{1,0:T(8,128)S(1)} collective-permute-done((f32[152,128]{1,0:T(8,128)S(1)}, f32[152,128]{1,0:T(8,128)S(1)}, u32[]{:S(2)}, u32[]{:S(2)}) %collective-permute-start) | collective-permute-done | bytes 77856 | tf_op jit(solution)/shard_map/ppermute | solution.py:578
  5.3 1.2 %collective-permute-done.1.borrowed = f32[1536,128]{1,0:T(8,128)S(1)} collective-permute-done((f32[1536,128]{1,0:T(8,128)S(1)}, f32[1536,128]{1,0:T(8,128)S(1)}, u32[]{:S(2)}, u32[]{:S(2)}) %collective-permute-start.1) | collective-permute-done | bytes 786464 | tf_op jit(solution)/shard_map/ppermute | solution.py:578
  6.6 3.5 %shard_map.123 = (f32[2048,128]{1,0:T(8,128)S(1)}, f32[2560,128]{1,0:T(8,128)S(1)}, f32[2560,128]{1,0:T(8,128)S(1)}, f32[2048,128]{1,0:T(8,128)S(1)}, f32[768,128]{1,0:T(8,128)S(1)}, /*index=5*/f32[256,128]{1,0:T(8,128)S(1)}) custom-call(s32[1]{0:T(128)} %bitcast.me, f32[1024,128]{1,0:T(8,128)S(1)} %get-tuple-element.44.probes, ...), custom_call_target="tpu_custom_call" | custom-call | flops 600000000 | bytes 6291456 | tf_op jit(solution)/shard_map/pallas_call | solution.py:561
  10.1 2.9 %collective-permute-start.3 = (f32[304,128]{1,0:T(8,128)S(1)}, f32[304,128]{1,0:T(8,128)S(1)}, u32[]{:S(2)}, u32[]{:S(2)}) collective-permute-start(f32[304,128]{1,0:T(8,128)S(1)} %collective-permute-done.2.passed), channel_id=1, source_target_pairs={{0,1},{1,0},{2,3},{3,2},{4,5},{5,4},{6,7},{7,6},{8,9},{9,8},{10,11... | collective-permute-start | bytes 466952 | tf_op jit(solution)/shard_map/ppermute | solution.py:578
  13.0 1.0 %collective-permute-done.3.across = f32[304,128]{1,0:T(8,128)S(1)} collective-permute-done((f32[304,128]{1,0:T(8,128)S(1)}, f32[304,128]{1,0:T(8,128)S(1)}, u32[]{:S(2)}, u32[]{:S(2)}) %collective-permute-start.3) | collective-permute-done | bytes 155680 | tf_op jit(solution)/shard_map/ppermute | solution.py:578
  14.3 4.8 %shard_map.124 = (f32[144,128]{1,0:T(8,128)S(1)}, bf16[3072,512]{1,0:T(8,128)(2,1)S(1)}, bf16[768,512]{1,0:T(8,128)(2,1)S(1)}, f32[768,128]{1,0:T(8,128)S(1)}, s...) custom-call(s32[1]{0:T(128)} %bitcast.me, f32[2560,128]{1,0:T(8,128)S(1)} %get-tuple-element.52.first, ...), custom_call_target="tpu_custom_call" | custom-call | flops 3000000000 | bytes 6291456 | tf_op jit(solution)/shard_map/pallas_call | solution.py:561
  19.2 2.8 %collective-permute-start.4 = (f32[144,128]{1,0:T(8,128)S(1)}, f32[144,128]{1,0:T(8,128)S(1)}, u32[]{:S(2)}, u32[]{:S(2)}) collective-permute-start(f32[144,128]{1,0:T(8,128)S(1)} %get-tuple-element.58.when), channel_id=1, source_target_pairs={{0,2},{1,3},{2,0},{3,1},{4,6},{5,7},{6,4},{7,5},{8,10},{9,11},{10,... | collective-permute-start | bytes 221192 | tf_op jit(solution)/shard_map/ppermute | solution.py:578
  22.0 1.6 %shard_map.125.own_basis.basis = bf16[512,2048]{1,0:T(8,128)(2,1)S(1)} custom-call(f32[8192,128]{1,0:T(8,128)S(1)} %bitcast.13, f32[144,128]{1,0:T(8,128)S(1)} %get-tuple-element.58.when), custom_call_target="tpu_custom_call" | custom-call | flops 10000000 | bytes 4194304 | tf_op jit(solution)/shard_map/pallas_call | solution.py:561
  23.6 1.2 %collective-permute-done.4 = f32[144,128]{1,0:T(8,128)S(1)} collective-permute-done((f32[144,128]{1,0:T(8,128)S(1)}, f32[144,128]{1,0:T(8,128)S(1)}, u32[]{:S(2)}, u32[]{:S(2)}) %collective-permute-start.4) | collective-permute-done | bytes 73760 | tf_op jit(solution)/shard_map/ppermute | solution.py:578
  24.8 1.9 %collective-permute-start.5 = (f32[144,128]{1,0:T(8,128)S(1)}, f32[144,128]{1,0:T(8,128)S(1)}, u32[]{:S(2)}, u32[]{:S(2)}) collective-permute-start(f32[144,128]{1,0:T(8,128)S(1)} %add.12.when), channel_id=1, source_target_pairs={{0,4},{1,5},{2,6},{3,7},{4,0},{5,1},{6,2},{7,3},{8,12},{9,13},{10,... | collective-permute-start | bytes 221192 | tf_op jit(solution)/shard_map/ppermute | solution.py:578
  26.7 1.6 %shard_map.126.own_basis_two.basis_two = bf16[512,2048]{1,0:T(8,128)(2,1)S(1)} custom-call(f32[8192,128]{1,0:T(8,128)S(1)} %bitcast.14, f32[144,128]{1,0:T(8,128)S(1)} %add.12.when), custom_call_target="tpu_custom_call" | custom-call | flops 10000000 | bytes 4194304 | tf_op jit(solution)/shard_map/pallas_call | solution.py:561
  28.3 0.9 %collective-permute-done.5 = f32[144,128]{1,0:T(8,128)S(1)} collective-permute-done((f32[144,128]{1,0:T(8,128)S(1)}, f32[144,128]{1,0:T(8,128)S(1)}, u32[]{:S(2)}, u32[]{:S(2)}) %collective-permute-start.5) | collective-permute-done | bytes 73760 | tf_op jit(solution)/shard_map/ppermute | solution.py:578
  29.2 2.9 %collective-permute-start.6 = (f32[144,128]{1,0:T(8,128)S(1)}, f32[144,128]{1,0:T(8,128)S(1)}, u32[]{:S(2)}, u32[]{:S(2)}) collective-permute-start(f32[144,128]{1,0:T(8,128)S(1)} %add.13.when), channel_id=1, source_target_pairs={{0,8},{1,9},{2,10},{3,11},{4,12},{5,13},{6,14},{7,15},{8,0},{9,1},... | collective-permute-start | bytes 221192 | tf_op jit(solution)/shard_map/ppermute | solution.py:578
  32.1 1.6 %shard_map.128.other_basis_two = bf16[512,2048]{1,0:T(8,128)(2,1)S(1)} custom-call(f32[8192,128]{1,0:T(8,128)S(1)} %collective-permute-done.7.basis, f32[144,128]{1,0:T(8,128)S(1)} %add.13.when), custom_call_target="tpu_custom_call" | custom-call | flops 10000000 | bytes 4194304 | tf_op jit(solution)/shard_map/pallas_call | solution.py:561
  33.7 1.6 %shard_map.127.other_basis = bf16[512,2048]{1,0:T(8,128)(2,1)S(1)} custom-call(f32[8192,128]{1,0:T(8,128)S(1)} %collective-permute-done.7.basis, f32[144,128]{1,0:T(8,128)S(1)} %add.13.when), custom_call_target="tpu_custom_call" | custom-call | flops 10000000 | bytes 4194304 | tf_op jit(solution)/shard_map/pallas_call | solution.py:561
  35.4 12.4 %shard_map.129 = (f32[1024,128]{1,0:T(8,128)S(1)}, f32[1024,128]{1,0:T(8,128)S(1)}, f32[8,64]{1,0:T(8,128)S(1)}) custom-call(s32[1]{0:T(128)} %bitcast.me, f32[144,128]{1,0:T(8,128)S(1)} %add.14.table, bf16[3072,512]{1,0:T(8,128)(2,1)S(1)} %get-tuple-element.66.cell_ref, bf16[768,512]{1,0:T(8,128)(2,1)S(1)} %get-tuple-element.67.slot_ref, ...), custom_call_target="tpu_custom_call" | custom-call | flops 5000000000 | bytes 10485760 | tf_op jit(solution)/shard_map/pallas_call | solution.py:561
  47.8 1.2 %collective-permute-done.8 = f32[8,64]{1,0:T(8,128)S(1)} collective-permute-done((f32[8,64]{1,0:T(8,128)S(1)}, f32[8,64]{1,0:T(8,128)S(1)}, u32[]{:S(2)}, u32[]{:S(2)}) %collective-permute-start.8) | collective-permute-done | bytes 2080 | tf_op jit(solution)/shard_map/ppermute | solution.py:578
  49.1 1.5 %collective-permute-start.10 = (f32[16,64]{1,0:T(8,128)S(1)}, f32[16,64]{1,0:T(8,128)S(1)}, u32[]{:S(2)}, u32[]{:S(2)}) collective-permute-start(f32[16,64]{1,0:T(8,128)S(1)} %pad_maximum_fusion.1), channel_id=1, source_target_pairs={{0,2},{1,3},{2,0},{3,1},{4,6},{5,7},{6,4},{7,5},{8,10},{9,11},{10,... | collective-permute-start | bytes 12296 | tf_op jit(solution)/shard_map/ppermute | solution.py:578
  50.7 2.1 %collective-permute-done.10 = f32[16,64]{1,0:T(8,128)S(1)} collective-permute-done((f32[16,64]{1,0:T(8,128)S(1)}, f32[16,64]{1,0:T(8,128)S(1)}, u32[]{:S(2)}, u32[]{:S(2)}) %collective-permute-start.10) | collective-permute-done | bytes 4128 | tf_op jit(solution)/shard_map/ppermute | solution.py:578
  52.8 3.7 %collective-permute-start.11 = (f32[16,64]{1,0:T(8,128)S(1)}, f32[16,64]{1,0:T(8,128)S(1)}, u32[]{:S(2)}, u32[]{:S(2)}) collective-permute-start(f32[16,64]{1,0:T(8,128)S(1)} %add.15.rest_3_), channel_id=1, source_target_pairs={{0,12},{1,13},{2,14},{3,15},{4,8},{5,9},{6,10},{7,11},{8,4},{9,5},... | collective-permute-start | bytes 12296 | tf_op jit(solution)/shard_map/ppermute | solution.py:578
  57.2 1.1 %collective-permute-done.11.rest_0_ = f32[16,64]{1,0:T(8,128)S(1)} collective-permute-done((f32[16,64]{1,0:T(8,128)S(1)}, f32[16,64]{1,0:T(8,128)S(1)}, u32[]{:S(2)}, u32[]{:S(2)}) %collective-permute-start.11) | collective-permute-done | bytes 4128 | tf_op jit(solution)/shard_map/ppermute | solution.py:578
  58.3 2.8 %collective-permute-done.12.rest_1_ = f32[16,64]{1,0:T(8,128)S(1)} collective-permute-done((f32[16,64]{1,0:T(8,128)S(1)}, f32[16,64]{1,0:T(8,128)S(1)}, u32[]{:S(2)}, u32[]{:S(2)}) %collective-permute-start.12) | collective-permute-done | bytes 4128 | tf_op jit(solution)/shard_map/ppermute | solution.py:578
  61.1 2.2 %shard_map.130 = (f32[16,4,32,128]{3,2,1,0:T(8,128)}, f32[16,64]{1,0:T(8,128)}) custom-call(s32[1]{0:T(128)} %bitcast.me, f32[1024,128]{1,0:T(8,128)S(1)} %get-tuple-element.79.image, f32[1024,128]{1,0:T(8,128)S(1)} %collective-permute-done.9.borrowed, bf16[512,2048]{1,0:T(8,128)(2,1)S(1)} %shard_map.125.own_basis.basis, ...), custom_call_target="tpu_custom_call" | custom-call | flops 200000000 | bytes 6291456 | tf_op jit(solution)/shard_map/pallas_call | solution.py:561
  (21 shorter events, 2.8 us)
Async XLA Ops:
  2.8 1.4 %collective-permute-start = (f32[152,128]{1,0:T(8,128)S(1)}, f32[152,128]{1,0:T(8,128)S(1)}, u32[]{:S(2)}, u32[]{:S(2)}) collective-permute-start(f32[152,128]{1,0:T(8,128)S(1)} %get-tuple-element.47.own), channel_id=1, source_target_pairs={{0,1},{1,0},{2,3},{3,2},{4,5},{5,4},{6,7},{7,6},{8,9},{9,8},{10,11... | collective-permute-start | bytes 233480 | tf_op jit(solution)/shard_map/ppermute | solution.py:578
  4.3 2.3 %collective-permute-start.1 = (f32[1536,128]{1,0:T(8,128)S(1)}, f32[1536,128]{1,0:T(8,128)S(1)}, u32[]{:S(2)}, u32[]{:S(2)}) collective-permute-start(f32[1536,128]{1,0:T(8,128)S(1)} %get-tuple-element.50), channel_id=1, source_target_pairs={{0,1},{1,0},{2,3},{3,2},{4,5},{5,4},{6,7},{7,6},{8,9},{9,8},{10,11... | collective-permute-start | bytes 2359304 | tf_op jit(solution)/shard_map/ppermute | solution.py:578
  4.6 5.4 %collective-permute-start.2 = (f32[304,128]{1,0:T(8,128)S(1)}, f32[304,128]{1,0:T(8,128)S(1)}, u32[]{:S(2)}, u32[]{:S(2)}) collective-permute-start(f32[304,128]{1,0:T(8,128)S(1)} %pad_maximum_fusion), channel_id=1, source_target_pairs={{1,2},{2,1},{3,4},{4,3},{5,6},{6,5},{7,8},{8,7},{9,10},{10,9},{11,... | collective-permute-start | bytes 466952 | tf_op jit(solution)/shard_map/ppermute | solution.py:636
  10.1 3.9 %collective-permute-start.3 = (f32[304,128]{1,0:T(8,128)S(1)}, f32[304,128]{1,0:T(8,128)S(1)}, u32[]{:S(2)}, u32[]{:S(2)}) collective-permute-start(f32[304,128]{1,0:T(8,128)S(1)} %collective-permute-done.2.passed), channel_id=1, source_target_pairs={{0,1},{1,0},{2,3},{3,2},{4,5},{5,4},{6,7},{7,6},{8,9},{9,8},{10,11... | collective-permute-start | bytes 466952 | tf_op jit(solution)/shard_map/ppermute | solution.py:578
  14.0 18.2 %collective-permute-start.7 = (f32[8192,128]{1,0:T(8,128)}, f32[8192,128]{1,0:T(8,128)S(1)}, u32[]{:S(2)}, u32[]{:S(2)}) collective-permute-start(f32[8192,128]{1,0:T(8,128)} %bitcast.12), channel_id=1, source_target_pairs={{0,1},{1,0},{2,3},{3,2},{4,5},{5,4},{6,7},{7,6},{8,9},{9,8},{10,11... | collective-permute-start | bytes 12582920 | tf_op jit(solution)/shard_map/ppermute | solution.py:578
  14.3 7.7 %copy-start = (f32[64,4,32,128]{3,2,1,0:T(8,128)S(1)}, f32[64,4,32,128]{3,2,1,0:T(8,128)}, u32[]{:S(2)}) copy-start(f32[64,4,32,128]{3,2,1,0:T(8,128)} %param.15) | copy-start | bytes 12582916
  19.2 5.6 %collective-permute-start.4 = (f32[144,128]{1,0:T(8,128)S(1)}, f32[144,128]{1,0:T(8,128)S(1)}, u32[]{:S(2)}, u32[]{:S(2)}) collective-permute-start(f32[144,128]{1,0:T(8,128)S(1)} %get-tuple-element.58.when), channel_id=1, source_target_pairs={{0,2},{1,3},{2,0},{3,1},{4,6},{5,7},{6,4},{7,5},{8,10},{9,11},{10,... | collective-permute-start | bytes 221192 | tf_op jit(solution)/shard_map/ppermute | solution.py:578
  24.8 4.4 %collective-permute-start.5 = (f32[144,128]{1,0:T(8,128)S(1)}, f32[144,128]{1,0:T(8,128)S(1)}, u32[]{:S(2)}, u32[]{:S(2)}) collective-permute-start(f32[144,128]{1,0:T(8,128)S(1)} %add.12.when), channel_id=1, source_target_pairs={{0,4},{1,5},{2,6},{3,7},{4,0},{5,1},{6,2},{7,3},{8,12},{9,13},{10,... | collective-permute-start | bytes 221192 | tf_op jit(solution)/shard_map/ppermute | solution.py:578
  29.2 6.1 %collective-permute-start.6 = (f32[144,128]{1,0:T(8,128)S(1)}, f32[144,128]{1,0:T(8,128)S(1)}, u32[]{:S(2)}, u32[]{:S(2)}) collective-permute-start(f32[144,128]{1,0:T(8,128)S(1)} %add.13.when), channel_id=1, source_target_pairs={{0,8},{1,9},{2,10},{3,11},{4,12},{5,13},{6,14},{7,15},{8,0},{9,1},... | collective-permute-start | bytes 221192 | tf_op jit(solution)/shard_map/ppermute | solution.py:578
  47.8 1.2 %collective-permute-start.8 = (f32[8,64]{1,0:T(8,128)S(1)}, f32[8,64]{1,0:T(8,128)S(1)}, u32[]{:S(2)}, u32[]{:S(2)}) collective-permute-start(f32[8,64]{1,0:T(8,128)S(1)} %get-tuple-element.81), channel_id=1, source_target_pairs={{0,1},{1,0},{2,3},{3,2},{4,5},{5,4},{6,7},{7,6},{8,9},{9,8},{10,11... | collective-permute-start | bytes 6152 | tf_op jit(solution)/shard_map/ppermute | solution.py:578
  49.0 12.1 %collective-permute-start.9 = (f32[1024,128]{1,0:T(8,128)S(1)}, f32[1024,128]{1,0:T(8,128)S(1)}, u32[]{:S(2)}, u32[]{:S(2)}) collective-permute-start(f32[1024,128]{1,0:T(8,128)S(1)} %get-tuple-element.82), channel_id=1, source_target_pairs={{0,1},{1,0},{2,3},{3,2},{4,5},{5,4},{6,7},{7,6},{8,9},{9,8},{10,11... | collective-permute-start | bytes 1572872 | tf_op jit(solution)/shard_map/ppermute | solution.py:578
  49.1 3.7 %collective-permute-start.10 = (f32[16,64]{1,0:T(8,128)S(1)}, f32[16,64]{1,0:T(8,128)S(1)}, u32[]{:S(2)}, u32[]{:S(2)}) collective-permute-start(f32[16,64]{1,0:T(8,128)S(1)} %pad_maximum_fusion.1), channel_id=1, source_target_pairs={{0,2},{1,3},{2,0},{3,1},{4,6},{5,7},{6,4},{7,5},{8,10},{9,11},{10,... | collective-permute-start | bytes 12296 | tf_op jit(solution)/shard_map/ppermute | solution.py:578
  52.8 5.4 %collective-permute-start.11 = (f32[16,64]{1,0:T(8,128)S(1)}, f32[16,64]{1,0:T(8,128)S(1)}, u32[]{:S(2)}, u32[]{:S(2)}) collective-permute-start(f32[16,64]{1,0:T(8,128)S(1)} %add.15.rest_3_), channel_id=1, source_target_pairs={{0,12},{1,13},{2,14},{3,15},{4,8},{5,9},{6,10},{7,11},{8,4},{9,5},... | collective-permute-start | bytes 12296 | tf_op jit(solution)/shard_map/ppermute | solution.py:578
  56.5 4.5 %collective-permute-start.12 = (f32[16,64]{1,0:T(8,128)S(1)}, f32[16,64]{1,0:T(8,128)S(1)}, u32[]{:S(2)}, u32[]{:S(2)}) collective-permute-start(f32[16,64]{1,0:T(8,128)S(1)} %add.15.rest_3_), channel_id=1, source_target_pairs={{0,8},{1,9},{2,10},{3,11},{4,12},{5,13},{6,14},{7,15},{8,0},{9,1},... | collective-permute-start | bytes 12296 | tf_op jit(solution)/shard_map/ppermute | solution.py:578
  56.5 4.5 %collective-permute-start.13 = (f32[16,64]{1,0:T(8,128)S(1)}, f32[16,64]{1,0:T(8,128)S(1)}, u32[]{:S(2)}, u32[]{:S(2)}) collective-permute-start(f32[16,64]{1,0:T(8,128)S(1)} %add.15.rest_3_), channel_id=1, source_target_pairs={{0,4},{1,5},{2,6},{3,7},{4,0},{5,1},{6,2},{7,3},{8,12},{9,13},{10,... | collective-permute-start | bytes 12296 | tf_op jit(solution)/shard_map/ppermute | solution.py:578

commit v10 on v9

--- a/solution.py
+++ b/solution.py
@@ -60,10 +60,17 @@
 
 
 def along_z(ref, first, layers, fields, band_ref, out_ref, row=0):
-    pieces = [ref[at(((first + x) * PADDED + REACH) * fields, 32 * fields), :] for x in range(layers)]
-    high, low = split(jnp.concatenate(pieces, axis=0))
-    both = jnp.dot(jnp.concatenate([high, low], axis=1), band_ref[...], preferred_element_type=F32)
-    out_ref[at(row, layers * 32 * fields), :] = both[:, :HALF] + both[:, HALF:]
+    slab, flat = PADDED * fields, 32 * fields
+
+    def body(index, carry):
+        here = window(ref, (first + index * LAYERS) * slab, LAYERS * slab)
+        pieces = [here[x * slab + REACH * fields : x * slab + REACH * fields + flat, :] for x in range(LAYERS)]
+        high, low = split(jnp.concatenate(pieces, axis=0))
+        both = jnp.dot(jnp.concatenate([high, low], axis=1), band_ref[...], preferred_element_type=F32)
+        out_ref[at(row + index * LAYERS * flat, LAYERS * flat), :] = both[:, :HALF] + both[:, HALF:]
+        return carry
+
+    lax.fori_loop(0, layers // LAYERS, body, 0)
 
 
 def laplacian(get, x, y, z_term, lowest, highest):
@@ -145,56 +152,52 @@
         prior_ref[place, :] = lent[3 * cells :, :] if damping is None else damping[...]
         speed_ref[place, :] = statics[0:cells, :]
 
-    def load(chunk, carry):
+    def load(index, carry):
+        x, chunk = index // 4, index % 4
         for side, ref in ((mine, probes), (1 - mine, borrowed)):
-            there = window(turned, side * LAYERS * flat + chunk * 8 * fields, LAYERS * flat - ahead)
-            padded = window(first, side * LAYERS * slab + chunk * 8 * fields, LAYERS * slab - ahead)
-            here = window(ref, chunk * 8, half - 24)
-            push = window(push_ref, side * cells + chunk * 8, cells - 24)
-            for x in range(LAYERS):
-                rows = [here[p * cells + x * 32 : p * cells + x * 32 + 8, :] for p in range(fields)]
-                values = jnp.swapaxes(jnp.stack(rows, axis=0), 0, 1)
-                for y in range(8):
-                    cell = x * 32 + y
-                    there[cell * fields : (cell + 1) * fields, :] = values[y]
-                    row = x * slab + (REACH + y) * fields
-                    padded[row : row + fields, :] = values[y] * spread(push, cell, fields)
-        return carry
-
-    lax.fori_loop(0, 4, load, 0)
+            there = window(turned, (side * LAYERS + x) * flat + chunk * 8 * fields, 8 * fields)
+            padded = window(first, (side * LAYERS + x) * slab + (REACH + chunk * 8) * fields, 8 * fields)
+            here = window(ref, x * 32 + chunk * 8, half - cells + 8)
+            push = window(push_ref, side * cells + x * 32 + chunk * 8, 8)
+            rows = [here[p * cells : p * cells + 8, :] for p in range(fields)]
+            values = jnp.swapaxes(jnp.stack(rows, axis=0), 0, 1)
+            for y in range(8):
+                there[y * fields : (y + 1) * fields, :] = values[y]
+                padded[y * fields : (y + 1) * fields, :] = values[y] * spread(push, y, fields)
+        return carry
+
+    lax.fori_loop(0, 16, load, 0)
 
     def sweep(field, emit):
         along_z(field, 0, PAIR, fields, band_ref, z_term)
 
         def body(chunk, carry):
-            padded = window(field, chunk * 8 * fields, PAIR * slab - ahead)
-            z_part = window(z_term, chunk * 8 * fields, PAIR * flat - ahead)
-            speed = window(speed_ref, chunk * 8, 2 * cells - 24)
-            push = window(push_ref, chunk * 8, 6 * cells - 24)
-            there = window(turned, chunk * 8 * fields, PAIR * flat - ahead)
-            put = emit(chunk)
+            ahead = 30 * fields
+            padded = window(field, chunk * 2 * fields, PAIR * slab - ahead)
+            z_part = window(z_term, chunk * 2 * fields, PAIR * flat - ahead)
+            there = window(turned, chunk * 2 * fields, PAIR * flat - ahead)
+            put = emit(chunk, ahead)
 
             def load(layer, y):
                 row = layer * slab + (REACH + y) * fields
                 return padded[row : row + fields, :]
 
-            for side in range(2):
-                get = kept_rows(load)
-                for y in range(8):
-                    for x in range(side * LAYERS, (side + 1) * LAYERS):
-                        cell = x * 32 + y
-                        row = slice(cell * fields, (cell + 1) * fields)
-                        change = spread(speed, cell, fields) * laplacian(get, x, y, z_part[row, :], 0, PAIR - 1)
-                        put(x, y, get(x, y), change, there[row, :], push)
+            get = kept_rows(load)
+            for y in range(2):
+                for x in range(PAIR):
+                    row = slice((x * 32 + y) * fields, (x * 32 + y + 1) * fields)
+                    cell = x * 32 + chunk * 2 + y
+                    change = spread(speed_ref, cell, fields) * laplacian(get, x, y, z_part[row, :], 0, PAIR - 1)
+                    put(x, y, get(x, y), change, there[row, :], cell)
             return carry
 
-        lax.fori_loop(0, 4, body, 0)
-
-    def step_one(chunk):
-        out = window(second, chunk * 8 * fields, PAIR * slab - ahead)
-
-        def put(x, y, now, change, probe, push):
-            change = change + probe * spread(push, 2 * cells + x * 32 + y, fields)
+        lax.fori_loop(0, 16, body, 0)
+
+    def step_one(chunk, ahead):
+        out = window(second, chunk * 2 * fields, PAIR * slab - ahead)
+
+        def put(x, y, now, change, probe, cell):
+            change = change + probe * spread(push_ref, 2 * cells + cell, fields)
             row = x * slab + (REACH + y) * fields
             out[row : row + fields, :] = 2.0 * now + change
 
@@ -202,16 +205,16 @@
 
     sweep(first, step_one)
 
-    def step_two(chunk):
-        before = window(first, chunk * 8 * fields, PAIR * slab - ahead)
-        out = window(third, chunk * 8 * fields, PAIR * flat - ahead)
-
-        def put(x, y, now, change, probe, push):
+    def step_two(chunk, ahead):
+        before = window(first, chunk * 2 * fields, PAIR * slab - ahead)
+        out = window(third, chunk * 2 * fields, PAIR * flat - ahead)
+
+        def put(x, y, now, change, probe, cell):
             row = x * slab + (REACH + y) * fields
             change = change - before[row : row + fields, :]
-            cell = x * 32 + y
-            change = change + probe * spread(push, 4 * cells + cell, fields)
-            out[cell * fields : (cell + 1) * fields, :] = 2.0 * now + change
+            change = change + probe * spread(push_ref, 4 * cells + cell, fields)
+            row = (x * 32 + y) * fields
+            out[row : row + fields, :] = 2.0 * now + change
 
         return put
 
@@ -225,7 +228,7 @@
 def forward_window(
     fields, peers, me, first, second, third, own, partner, passed, across, band_ref,
     table, cell_ref, slot_ref, speed_ref, line_ref, owner_ref, weight_ref,
-    below, above, z_term, total_ref, *samples,
+    below, above, z_term, total_ref, sample, statics,
 ):
     entries = line_ref.shape[1]
     cells = LAYERS * 32
@@ -250,35 +253,40 @@
     slot_place = lax.broadcasted_iota(jnp.int32, (HALF, entries), 0)
     for tile, value in enumerate(tiles):
         speed_ref[tile * cells : (tile + 1) * cells, :] = value[0:cells, :]
-        cell = entry_row(value, cells).astype(jnp.int32)
-        owner = entry_row(value, cells + 4).astype(jnp.int32)
-        slot = entry_row(value, cells + 8).astype(jnp.int32)
-        weight = entry_row(value, cells + 12)
+        statics[tile * 16 : (tile + 1) * 16, :] = value[cells : cells + 16, :]
+
+    def describe(tile, carry):
+        value = statics[at(tile * 16), :]
+        cell, owner, slot = (entry_row(value, i * 4).astype(jnp.int32) for i in range(3))
+        weight = entry_row(value, 12)
         hot = jnp.where(place == jnp.bitwise_and(cell, PLACES - 1), 1.0, 0.0)
-        cell_ref[tile * PLACES : (tile + 1) * PLACES, :] = hot.astype(BF16)
+        cell_ref[at(tile * PLACES, PLACES), :] = hot.astype(BF16)
         hot = jnp.where(slot_place == slot, 1.0, 0.0)
-        slot_ref[tile * HALF : (tile + 1) * HALF, :] = hot.astype(BF16)
-        rows = slice(tile * fields, (tile + 1) * fields)
+        slot_ref[at(tile * HALF, HALF), :] = hot.astype(BF16)
+        rows = at(tile * fields, fields)
         line_ref[rows, :] = jnp.broadcast_to(lax.shift_right_logical(cell, 9), (fields, entries))
         owner_ref[rows, :] = jnp.broadcast_to(owner, (fields, entries))
         weight_ref[rows, :] = jnp.broadcast_to(weight, (fields, entries))
+        return carry
+
+    lax.fori_loop(0, TILES, describe, 0)
 
     def outward(chunk, carry):
-        ahead = 24 * fields
-        speed = window(speed_ref, chunk * 8, TILES * cells - 24)
-        here = window(first, chunk * 8 * fields, PAIR * slab - ahead)
-        down_out, up_out = (window(ref, chunk * 8 * fields, LAYERS * slab - ahead) for ref in (below, above))
-        for y in range(8):
+        ahead = 30 * fields
+        here = window(first, chunk * 2 * fields, PAIR * slab - ahead)
+        down_out, up_out = (window(ref, chunk * 2 * fields, LAYERS * slab - ahead) for ref in (below, above))
+        for y in range(2):
             rows = [slice(x * slab + (REACH + y) * fields, x * slab + (REACH + y + 1) * fields) for x in range(PAIR)]
             field = [here[row, :] for row in rows]
             for x in range(LAYERS):
                 up = sum(STENCIL[4 + x - other] * field[4 + other] for other in range(x, LAYERS))
                 down = sum(STENCIL[4 + other - x] * field[other] for other in range(x + 1))
-                up_out[rows[x], :] = spread(speed, 4 * cells + x * 32 + y, fields) * up
-                down_out[rows[x], :] = spread(speed, cells + x * 32 + y, fields) * down
-        return carry
-
-    lax.fori_loop(0, 4, outward, 0)
+                cell = x * 32 + chunk * 2 + y
+                up_out[rows[x], :] = spread(speed_ref, 4 * cells + cell, fields) * up
+                down_out[rows[x], :] = spread(speed_ref, cells + cell, fields) * down
+        return carry
+
+    lax.fori_loop(0, 16, outward, 0)
     along_z(below, 0, LAYERS, fields, band_ref, z_term, 0)
     along_z(above, 0, LAYERS, fields, band_ref, z_term, cells * fields)
 
@@ -291,12 +299,12 @@
         return total
 
     def respond(chunk, carry):
-        ahead = 16 * fields
-        speeds = window(speed_ref, chunk * 16, TILES * cells - 16)
-        low_side, high_side = (window(ref, chunk * 16 * fields, LAYERS * slab - ahead) for ref in (below, above))
-        inside = window(second, chunk * 16 * fields, PAIR * slab - ahead)
-        base = window(third, chunk * 16 * fields, PAIR * flat - ahead)
-        z_parts = window(z_term, chunk * 16 * fields, PAIR * flat - ahead)
+        ahead = 30 * fields
+        low_side, high_side = (window(ref, chunk * 2 * fields, LAYERS * slab - ahead) for ref in (below, above))
+        inside = window(second, chunk * 2 * fields, PAIR * slab - ahead)
+        base = window(third, chunk * 2 * fields, PAIR * flat - ahead)
+        z_parts = window(z_term, chunk * 2 * fields, PAIR * flat - ahead)
+        out = window(sample, chunk % 2 * 2 * flat + chunk // 2 * fields, TILES * 4 * flat - 2 * flat - 7 * fields)
 
         def load(layer, y):
             if layer < 0:
@@ -308,14 +316,13 @@
             row = layer * slab + (REACH + y) * fields
             return ref[row : row + fields, :]
 
+        read = kept_rows(load)
         for tile in range(TILES):
-            sample = samples[tile]
-            read = kept_rows(load)
-            for y in range(16):
+            for y in range(2):
                 for x in range(LAYERS):
                     cell = x * 32 + y
                     layer = (tile - 2) * LAYERS + x
-                    speed = spread(speeds, tile * cells + cell, fields)
+                    speed = spread(speed_ref, tile * cells + x * 32 + chunk * 2 + y, fields)
                     if tile in (0, 5):
                         value = speed * far(read, layer, y, -4, 11)
                     elif tile in (2, 3):
@@ -326,38 +333,48 @@
                         row = (tile // 4 * cells + cell) * fields
                         lap = laplacian(read, layer, y, z_parts[row : row + fields, :], -4, 11)
                         value = 2.0 * read(layer, y) + speed * lap
-                    row = (x * 4 + y // 4) * fields
-                    side = y % 4 * HALF
-                    sample[row : row + fields, side : side + HALF] = value
-            hot = cell_ref[tile * PLACES : (tile + 1) * PLACES, :]
-            picked = jnp.dot(jnp.concatenate(split(sample[...]), axis=0), hot, preferred_element_type=F32)
-            picked = picked[: 16 * fields, :] + picked[16 * fields :, :]
-            rows = slice(tile * fields, (tile + 1) * fields)
-            line = line_ref[rows, :]
-            total = total_ref[rows, :]
-            for i in range(16):
-                chosen = line == i // 4 * 8 + chunk * 4 + i % 4
-                total = total + jnp.where(chosen, picked[i * fields : (i + 1) * fields, :], 0.0)
-            total_ref[rows, :] = total
-        return carry
-
-    lax.fori_loop(0, 2, respond, 0)
+                    row = (tile * 4 + y) * flat + x * 8 * fields
+                    out[row : row + fields, :] = value
+        return carry
+
+    lax.fori_loop(0, 16, respond, 0)
+
+    def pick(index, carry):
+        tile, side = index // 2, index % 2
+        here = window(sample, tile * 4 * flat + side * 16 * fields, 3 * flat + 16 * fields)
+        value = jnp.concatenate([here[i * flat : i * flat + 16 * fields, :] for i in range(4)], axis=1)
+        hot = cell_ref[at(tile * PLACES, PLACES), :]
+        picked = jnp.dot(jnp.concatenate(split(value), axis=0), hot, preferred_element_type=F32)
+        picked = picked[: 16 * fields, :] + picked[16 * fields :, :]
+        rows = at(tile * fields, fields)
+        line = line_ref[rows, :] - side * 16
+        total = total_ref[rows, :]
+        for i in range(16):
+            total = total + jnp.where(line == i, picked[i * fields : (i + 1) * fields, :], 0.0)
+        total_ref[rows, :] = total
+        return carry
+
+    lax.fori_loop(0, 2 * TILES, pick, 0)
 
     for group in range(peers // 16):
-        lefts, rights = [], []
-        for tile in range(TILES):
-            rows = slice(tile * fields, (tile + 1) * fields)
+
+        def gather(tile, result):
+            rows = at(tile * fields, fields)
             value = total_ref[rows, :] * weight_ref[rows, :]
             high = value.astype(BF16).astype(F32)
-            owner = owner_ref[rows, :]
+            owner = owner_ref[rows, :] - group * 16
+            lefts = []
             for part in (high, value - high):
-                pieces = [jnp.where(owner == group * 16 + i, part, 0.0) for i in range(16)]
+                pieces = [jnp.where(owner == i, part, 0.0) for i in range(16)]
                 lefts.append(jnp.concatenate(pieces, axis=0).astype(BF16))
-                rights.append(slot_ref[tile * HALF : (tile + 1) * HALF, :])
-        result = lax.dot_general(
-            jnp.concatenate(lefts, axis=1), jnp.concatenate(rights, axis=1), NT, preferred_element_type=F32
+            hot = slot_ref[at(tile * HALF, HALF), :]
+            left = jnp.concatenate(lefts, axis=1)
+            hots = jnp.concatenate([hot, hot], axis=1)
+            return result + lax.dot_general(left, hots, NT, preferred_element_type=F32)
+
+        table[group * 16 * fields : (group + 1) * 16 * fields, :] = lax.fori_loop(
+            0, TILES, gather, jnp.zeros((16 * fields, HALF), F32)
         )
-        table[group * 16 * fields : (group + 1) * 16 * fields, :] = result
     place = lax.broadcasted_iota(jnp.int32, (peers, HALF), 0)
     scales = jnp.zeros((peers, HALF), F32)
     for position, value in ((me[0], mine), (me[0] + 1 - 2 * (me[0] % 2), theirs)):
@@ -384,9 +401,8 @@
 def adjoint(
     fields, peers, me, table, cell_ref, slot_ref, speed_ref, line_ref, owner_ref, weight_ref, turned, push_ref,
     prior_ref, band_ref, own_basis, own_basis_two, other_basis, other_basis_two, kept, lent, coeffs,
-    high_ref, low_ref, inner_two, outer_two, inner_one, outer_one, z_term, image, scaled, *scratch,
+    high_ref, low_ref, inner_two, outer_two, inner_one, outer_one, z_term, image, scaled, left,
 ):
-    lefts, image_parts = scratch[:TILES], scratch[TILES:]
     entries = line_ref.shape[1]
     cells = LAYERS * 32
     rank = own_basis.shape[0] // 8
@@ -397,10 +413,10 @@
     for owner in range(peers):
         rows = slice(owner * fields, (owner + 1) * fields)
         scaled[rows, :] = table[rows, :] * table[peers * fields + owner : peers * fields + owner + 1, :]
-    for tile in range(TILES):
-        rows = slice(tile * fields, (tile + 1) * fields)
+    def weigh(tile, carry):
+        rows = at(tile * fields, fields)
         owner = owner_ref[rows, :]
-        hot = slot_ref[tile * HALF : (tile + 1) * HALF, :]
+        hot = slot_ref[at(tile * HALF, HALF), :]
         hot = jnp.concatenate([hot, hot], axis=0)
         total = jnp.zeros((fields, entries), F32)
         for group in range(peers // 16):
@@ -412,100 +428,112 @@
         high = value.astype(BF16).astype(F32)
         high_ref[rows, :] = high
         low_ref[rows, :] = value - high
-
-    for tile in range(TILES):
-        left = lefts[tile]
-        rows = slice(tile * fields, (tile + 1) * fields)
-        line, high, low = line_ref[rows, :], high_ref[rows, :], low_ref[rows, :]
-        for i in range(0, 32, 2):
+        return carry
+
+    lax.fori_loop(0, TILES, weigh, 0)
+
+    def inject(index, carry):
+        tile, side = index // 2, index % 2
+        rows = at(tile * fields, fields)
+        line, high, low = line_ref[rows, :] - side * 16, high_ref[rows, :], low_ref[rows, :]
+        for i in range(0, 16, 2):
             chosen = [line == i, line == i + 1]
-            for part, start in ((high, i * fields), (low, (32 + i) * fields)):
+            for part, start in ((high, i * fields), (low, (16 + i) * fields)):
                 both = [jnp.where(which, part, 0.0) for which in chosen]
                 left[start : start + 2 * fields, :] = jnp.concatenate(both, axis=0).astype(BF16)
-        hot = cell_ref[tile * PLACES : (tile + 1) * PLACES, :]
+        hot = cell_ref[at(tile * PLACES, PLACES), :]
         value = lax.dot_general(left[...], hot, NT, preferred_element_type=F32)
-        value = value[: 32 * fields, :] + value[32 * fields :, :]
-        for i in range(32):
+        value = value[: 16 * fields, :] + value[16 * fields :, :]
+        layer = tile * LAYERS + side * 2
+        two = window(outer_two, layer * flat, 2 * flat)
+        out = window(inner_two, layer * slab, 2 * slab)
+        speed = window(speed_ref, layer * 32, 64)
+        for i in range(16):
             for step in range(4):
-                layer, y = tile * LAYERS + i // 8, i % 8 * 4 + step
+                x, y = i // 8, i % 8 * 4 + step
                 now = value[i * fields : (i + 1) * fields, step * HALF : (step + 1) * HALF]
-                if 1 <= tile <= 4:
-                    row = ((layer - LAYERS) * 32 + y) * fields
-                    outer_two[row : row + fields, :] = now
-                speed = spread(speed_ref, layer * 32 + y, fields)
-                row = layer * slab + (REACH + y) * fields
-                inner_two[row : row + fields, :] = speed * now
-        if 1 <= tile <= 4:
-            along_z(inner_two, tile * LAYERS, LAYERS, fields, band_ref, z_term, (tile - 1) * cells * fields)
+                cell = x * 32 + y
+                two[cell * fields : (cell + 1) * fields, :] = now
+                row = x * slab + (REACH + y) * fields
+                out[row : row + fields, :] = spread(speed, cell, fields) * now
+        return carry
+
+    lax.fori_loop(0, 2 * TILES, inject, 0)
+    along_z(inner_two, LAYERS, 2 * PAIR, fields, band_ref, z_term)
 
     def step_one(index, carry):
-        pair, chunk = index // 4, index % 4
-        start, skip = pair * PAIR * slab + chunk * 8 * fields, pair * PAIR * flat + chunk * 8 * fields
+        pair, chunk = index // 16, index % 16
+        ahead = 30 * fields
+        start, skip = pair * PAIR * slab + chunk * 2 * fields, pair * PAIR * flat + chunk * 2 * fields
         here = window(inner_two, start, 2 * PAIR * slab - ahead)
-        two, one, z_part = (window(ref, skip, PAIR * flat - ahead) for ref in (outer_two, outer_one, z_term))
+        two = window(outer_two, LAYERS * flat + skip, PAIR * flat - ahead)
+        one, z_part = (window(ref, skip, PAIR * flat - ahead) for ref in (outer_one, z_term))
         out = window(inner_one, start, PAIR * slab - ahead)
-        speed = window(speed_ref, cells + pair * 2 * cells + chunk * 8, 2 * cells - 24)
 
         def load(layer, y):
             row = (layer + LAYERS) * slab + (REACH + y) * fields
             return here[row : row + fields, :]
 
-        for side in range(2):
-            get = kept_rows(load)
-            for y in range(8):
-                for x in range(side * LAYERS, (side + 1) * LAYERS):
-                    cell = x * 32 + y
-                    row = slice(cell * fields, (cell + 1) * fields)
-                    now = 2.0 * two[row, :] + laplacian(get, x, y, z_part[row, :], -4, 11)
-                    one[row, :] = now
-                    row = x * slab + (REACH + y) * fields
-                    out[row : row + fields, :] = spread(speed, cell, fields) * now
-        return carry
-
-    lax.fori_loop(0, 8, step_one, 0)
+        get = kept_rows(load)
+        for y in range(2):
+            for x in range(PAIR):
+                cell = x * 32 + y
+                row = slice(cell * fields, (cell + 1) * fields)
+                now = 2.0 * two[row, :] + laplacian(get, x, y, z_part[row, :], -4, 11)
+                one[row, :] = now
+                row = x * slab + (REACH + y) * fields
+                speed = spread(speed_ref, (pair * 2 + 1) * cells + x * 32 + chunk * 2 + y, fields)
+                out[row : row + fields, :] = speed * now
+        return carry
+
+    lax.fori_loop(0, 32, step_one, 0)
     along_z(inner_one, LAYERS, PAIR, fields, band_ref, z_term)
     mine = me[0] % 2
 
-    def step_two(chunk, total, image_parts):
-        skip = chunk * 8 * fields
+    def step_two(chunk, carry):
+        ahead = 30 * fields
+        skip = chunk * 2 * fields
         here = window(inner_one, skip, 2 * PAIR * slab - ahead)
-        two_rows, one_rows = (window(ref, LAYERS * flat + skip, PAIR * flat - ahead) for ref in (outer_two, outer_one))
+        two_rows = window(outer_two, 2 * LAYERS * flat + skip, PAIR * flat - ahead)
+        one_rows = window(outer_one, LAYERS * flat + skip, PAIR * flat - ahead)
         z_part, there, out = (window(ref, skip, PAIR * flat - ahead) for ref in (z_term, turned, image))
-        push = window(push_ref, chunk * 8, 6 * cells - 24)
-        damping = window(prior_ref, chunk * 8, 2 * cells - 24)
 
         def load(layer, y):
             row = (layer + LAYERS) * slab + (REACH + y) * fields
             return here[row : row + fields, :]
 
-        nothing = jnp.zeros((fields, HALF), F32)
-        for side in range(2):
-            get = kept_rows(load)
-            for y in range(8):
-                for x in range(side * LAYERS, (side + 1) * LAYERS):
-                    cell = x * 32 + y
-                    row = slice(cell * fields, (cell + 1) * fields)
-                    two, one = two_rows[row, :], one_rows[row, :]
-                    zero = 2.0 * one - two + laplacian(get, x, y, z_part[row, :], -4, 11)
-                    value = spread(push, cell, fields) * zero
-                    value = value + spread(push, 2 * cells + cell, fields) * one
-                    value = value + spread(push, 4 * cells + cell, fields) * two
-                    value = value + spread(damping, cell, fields) * there[row, :]
-                    out[row, :] = value
-                    high = value.astype(BF16).astype(F32)
-                    rows, lane = slice(x * 2 * fields, (x + 1) * 2 * fields), y * 256
-                    image_parts[rows, lane : lane + HALF] = jnp.concatenate([high, value - high], axis=0).astype(BF16)
-                    image_parts[rows, lane + HALF : lane + 256] = jnp.concatenate([high, nothing], axis=0).astype(BF16)
+        get = kept_rows(load)
+        for y in range(2):
+            for x in range(PAIR):
+                cell = x * 32 + chunk * 2 + y
+                row = slice((x * 32 + y) * fields, (x * 32 + y + 1) * fields)
+                two, one = two_rows[row, :], one_rows[row, :]
+                zero = 2.0 * one - two + laplacian(get, x, y, z_part[row, :], -4, 11)
+                value = spread(push_ref, cell, fields) * zero
+                value = value + spread(push_ref, 2 * cells + cell, fields) * one
+                value = value + spread(push_ref, 4 * cells + cell, fields) * two
+                out[row, :] = value + spread(prior_ref, cell, fields) * there[row, :]
+        return carry
+
+    lax.fori_loop(0, 16, step_two, 0)
+    nothing = jnp.zeros((fields, HALF), F32)
+
+    def project(chunk, total):
         for side, pieces in ((mine, (own_basis, own_basis_two)), (1 - mine, (other_basis, other_basis_two))):
             for x in range(LAYERS):
-                columns = pieces[x // 2][(x % 2 * 4 + chunk) * rank : (x % 2 * 4 + chunk + 1) * rank, :]
-                parts = image_parts[at((side * LAYERS + x) * 2 * fields, 2 * fields), :]
+                here = window(image, (side * LAYERS + x) * flat + chunk * 8 * fields, 8 * fields)
+                parts = []
+                for y in range(8):
+                    value = here[y * fields : (y + 1) * fields, :]
+                    high = value.astype(BF16).astype(F32)
+                    parts.append(jnp.concatenate([high, value - high], axis=0))
+                    parts.append(jnp.concatenate([high, nothing], axis=0))
+                parts = jnp.concatenate(parts, axis=1).astype(BF16)
+                columns = pieces[x // 2][at((x % 2 * 4 + chunk) * rank, rank), :]
                 total = total + lax.dot_general(parts, columns, NT, preferred_element_type=F32)
         return total
 
-    total = jnp.zeros((2 * fields, rank), F32)
-    for chunk in range(4):
-        total = step_two(chunk, total, image_parts[chunk])
+    total = lax.fori_loop(0, 4, project, jnp.zeros((2 * fields, rank), F32))
     coeffs[...] = total[:fields, :] + total[fields:, :]
     kept[...] = image[at(mine * LAYERS * flat, LAYERS * flat), :]
     lent[...] = image[at((1 - mine) * LAYERS * flat, LAYERS * flat), :]
@@ -677,7 +705,7 @@
             pltpu.VMEM((PAIR * flat, HALF), F32),
             pltpu.VMEM((TILES * fields, entries), F32),
         ]
-        + [pltpu.VMEM((16 * fields, PLACES), F32)] * TILES,
+        + [pltpu.VMEM((TILES * 4 * flat, HALF), F32), pltpu.VMEM((TILES * 16, HALF), F32)],
         3_000_000_000,
         6 * 2**20,
         scalars=1,
@@ -708,15 +736,14 @@
             pltpu.VMEM((TILES * fields, entries), F32),
             pltpu.VMEM((TILES * fields, entries), F32),
             pltpu.VMEM((TILES * LAYERS * slab, HALF), F32),
-            pltpu.VMEM((2 * PAIR * flat, HALF), F32),
+            pltpu.VMEM((TILES * LAYERS * flat, HALF), F32),
             pltpu.VMEM((2 * PAIR * slab, HALF), F32),
             pltpu.VMEM((2 * PAIR * flat, HALF), F32),
             pltpu.VMEM((2 * PAIR * flat, HALF), F32),
             pltpu.VMEM((PAIR * flat, HALF), F32),
             pltpu.VMEM((peers * fields, HALF), F32),
         ]
-        + [pltpu.VMEM((64 * fields, entries), BF16)] * TILES
-        + [pltpu.VMEM((2 * PAIR * fields, 2048), BF16)] * 4,
+        + [pltpu.VMEM((32 * fields, entries), BF16)],
         5_000_000_000,
         10 * 2**20,
         scalars=1,

time: 63.6 us -> 67.8 us (1.066)
  Pallas kernels: 30.8 us -> 35.7 us
    pallas_call x9, Pallas kernels: 30.8 us -> 35.7 us  [call(): pl.pallas_call(kernel, out_shape=out_shape, in_specs=[smem] * scalars + [...]
  transfers between devices with their start and end apart: 14 -> 14, of which waited for: 9 -> 9; matrix products, arithmetic and copies ran while one was open for 0% -> 0% of each run, Pallas kernels for 23% -> 27%
where the time goes in v10:
time: 67.8 us; the launch traced here: 67.7 us
  Pallas kernels  35.7 us (53%)
  starting transfers between devices  18 us (27%)
  waiting for transfers between devices  12.5 us (18%)
  between operations  1.4 us (2%)
    pallas_call x9, Pallas kernels, call(): pl.pallas_call(kernel, out_shape=out_shape, in_specs=[smem] * scalars + [...  35.7 us
    ppermute x13, starting transfers between devices, swapped(): return lax.ppermute(array, axis, [(i, i ^ bits) for i in range(count)])  17.3 us
    ppermute x13, waiting for transfers between devices, swapped(): return lax.ppermute(array, axis, [(i, i ^ bits) for i in range(count)])  12.5 us
  transfers between devices with their start and end apart: 14, of which 9 were waited for; matrix products, arithmetic and copies ran while one was open for 0% of the time, Pallas kernels for 27%

profile of v10, /device:TPU:0, one launch (start us, length us, event | category | flops | bytes accessed | tf_op | source)
XLA Modules:
  0.0 67.7 jit_solution(5383575978021793927)
XLA Ops:
  1.3 1.6 %shard_map.122 = (f32[152,128]{1,0:T(8,128)S(1)}, f32[1024,128]{1,0:T(8,128)S(1)}, f32[384,128]{1,0:T(8,128)S(1)}, f32[128,128]{1,0:T(8,128)S(1)}, f32[1536,128]...) custom-call(s32[1]{0:T(128)S(6)} %copy.13.count, s32[1]{0:T(128)} %bitcast.me, f32[2048,128]{1,0:T(8,128)} %bitcast.15, ...), custom_call_target="tpu_custom_call" | custom-call | flops 100000 | bytes 2097152 | tf_op jit(solution)/shard_map/pallas_call | solution.py:589
  3.4 0.9 %collective-permute-done.partner = f32[152,128]{1,0:T(8,128)S(1)} collective-permute-done((f32[152,128]{1,0:T(8,128)S(1)}, f32[152,128]{1,0:T(8,128)S(1)}, u32[]{:S(2)}, u32[]{:S(2)}) %collective-permute-start) | collective-permute-done | bytes 77856 | tf_op jit(solution)/shard_map/ppermute | solution.py:606
  5.3 1.2 %collective-permute-done.1.borrowed = f32[1536,128]{1,0:T(8,128)S(1)} collective-permute-done((f32[1536,128]{1,0:T(8,128)S(1)}, f32[1536,128]{1,0:T(8,128)S(1)}, u32[]{:S(2)}, u32[]{:S(2)}) %collective-permute-start.1) | collective-permute-done | bytes 786464 | tf_op jit(solution)/shard_map/ppermute | solution.py:606
  6.6 4.0 %shard_map.123 = (f32[2048,128]{1,0:T(8,128)S(1)}, f32[2560,128]{1,0:T(8,128)S(1)}, f32[2560,128]{1,0:T(8,128)S(1)}, f32[2048,128]{1,0:T(8,128)S(1)}, f32[768,128]{1,0:T(8,128)S(1)}, /*index=5*/f32[256,128]{1,0:T(8,128)S(1)}) custom-call(s32[1]{0:T(128)} %bitcast.me, f32[1024,128]{1,0:T(8,128)S(1)} %get-tuple-element.44.probes, ...), custom_call_target="tpu_custom_call" | custom-call | flops 600000000 | bytes 6291456 | tf_op jit(solution)/shard_map/pallas_call | solution.py:589
  10.5 2.9 %collective-permute-start.3 = (f32[304,128]{1,0:T(8,128)S(1)}, f32[304,128]{1,0:T(8,128)S(1)}, u32[]{:S(2)}, u32[]{:S(2)}) collective-permute-start(f32[304,128]{1,0:T(8,128)S(1)} %collective-permute-done.2.passed), channel_id=1, source_target_pairs={{0,1},{1,0},{2,3},{3,2},{4,5},{5,4},{6,7},{7,6},{8,9},{9,8},{10,11... | collective-permute-start | bytes 466952 | tf_op jit(solution)/shard_map/ppermute | solution.py:606
  13.4 1.0 %collective-permute-done.3.across = f32[304,128]{1,0:T(8,128)S(1)} collective-permute-done((f32[304,128]{1,0:T(8,128)S(1)}, f32[304,128]{1,0:T(8,128)S(1)}, u32[]{:S(2)}, u32[]{:S(2)}) %collective-permute-start.3) | collective-permute-done | bytes 155680 | tf_op jit(solution)/shard_map/ppermute | solution.py:606
  14.8 8.1 %shard_map.124 = (f32[144,128]{1,0:T(8,128)S(1)}, bf16[3072,512]{1,0:T(8,128)(2,1)S(1)}, bf16[768,512]{1,0:T(8,128)(2,1)S(1)}, f32[768,128]{1,0:T(8,128)S(1)}, s...) custom-call(s32[1]{0:T(128)} %bitcast.me, f32[2560,128]{1,0:T(8,128)S(1)} %get-tuple-element.52.first, ...), custom_call_target="tpu_custom_call" | custom-call | flops 3000000000 | bytes 6291456 | tf_op jit(solution)/shard_map/pallas_call | solution.py:589
  22.9 2.3 %collective-permute-start.4 = (f32[144,128]{1,0:T(8,128)S(1)}, f32[144,128]{1,0:T(8,128)S(1)}, u32[]{:S(2)}, u32[]{:S(2)}) collective-permute-start(f32[144,128]{1,0:T(8,128)S(1)} %get-tuple-element.58.when), channel_id=1, source_target_pairs={{0,2},{1,3},{2,0},{3,1},{4,6},{5,7},{6,4},{7,5},{8,10},{9,11},{10,... | collective-permute-start | bytes 221192 | tf_op jit(solution)/shard_map/ppermute | solution.py:606
  25.3 1.6 %shard_map.125.own_basis.basis = bf16[512,2048]{1,0:T(8,128)(2,1)S(1)} custom-call(f32[8192,128]{1,0:T(8,128)S(1)} %bitcast.13, f32[144,128]{1,0:T(8,128)S(1)} %get-tuple-element.58.when), custom_call_target="tpu_custom_call" | custom-call | flops 10000000 | bytes 4194304 | tf_op jit(solution)/shard_map/pallas_call | solution.py:589
  26.9 1.2 %collective-permute-done.4 = f32[144,128]{1,0:T(8,128)S(1)} collective-permute-done((f32[144,128]{1,0:T(8,128)S(1)}, f32[144,128]{1,0:T(8,128)S(1)}, u32[]{:S(2)}, u32[]{:S(2)}) %collective-permute-start.4) | collective-permute-done | bytes 73760 | tf_op jit(solution)/shard_map/ppermute | solution.py:606
  28.1 1.9 %collective-permute-start.5 = (f32[144,128]{1,0:T(8,128)S(1)}, f32[144,128]{1,0:T(8,128)S(1)}, u32[]{:S(2)}, u32[]{:S(2)}) collective-permute-start(f32[144,128]{1,0:T(8,128)S(1)} %add.12.when), channel_id=1, source_target_pairs={{0,4},{1,5},{2,6},{3,7},{4,0},{5,1},{6,2},{7,3},{8,12},{9,13},{10,... | collective-permute-start | bytes 221192 | tf_op jit(solution)/shard_map/ppermute | solution.py:606
  29.9 1.6 %shard_map.126.own_basis_two.basis_two = bf16[512,2048]{1,0:T(8,128)(2,1)S(1)} custom-call(f32[8192,128]{1,0:T(8,128)S(1)} %bitcast.14, f32[144,128]{1,0:T(8,128)S(1)} %add.12.when), custom_call_target="tpu_custom_call" | custom-call | flops 10000000 | bytes 4194304 | tf_op jit(solution)/shard_map/pallas_call | solution.py:589
  31.5 1.0 %collective-permute-done.5 = f32[144,128]{1,0:T(8,128)S(1)} collective-permute-done((f32[144,128]{1,0:T(8,128)S(1)}, f32[144,128]{1,0:T(8,128)S(1)}, u32[]{:S(2)}, u32[]{:S(2)}) %collective-permute-start.5) | collective-permute-done | bytes 73760 | tf_op jit(solution)/shard_map/ppermute | solution.py:606
  32.5 2.9 %collective-permute-start.6 = (f32[144,128]{1,0:T(8,128)S(1)}, f32[144,128]{1,0:T(8,128)S(1)}, u32[]{:S(2)}, u32[]{:S(2)}) collective-permute-start(f32[144,128]{1,0:T(8,128)S(1)} %add.13.when), channel_id=1, source_target_pairs={{0,8},{1,9},{2,10},{3,11},{4,12},{5,13},{6,14},{7,15},{8,0},{9,1},... | collective-permute-start | bytes 221192 | tf_op jit(solution)/shard_map/ppermute | solution.py:606
  35.4 1.6 %shard_map.128.other_basis_two = bf16[512,2048]{1,0:T(8,128)(2,1)S(1)} custom-call(f32[8192,128]{1,0:T(8,128)S(1)} %collective-permute-done.7.basis, f32[144,128]{1,0:T(8,128)S(1)} %add.13.when), custom_call_target="tpu_custom_call" | custom-call | flops 10000000 | bytes 4194304 | tf_op jit(solution)/shard_map/pallas_call | solution.py:589
  37.0 1.6 %shard_map.127.other_basis = bf16[512,2048]{1,0:T(8,128)(2,1)S(1)} custom-call(f32[8192,128]{1,0:T(8,128)S(1)} %collective-permute-done.7.basis, f32[144,128]{1,0:T(8,128)S(1)} %add.13.when), custom_call_target="tpu_custom_call" | custom-call | flops 10000000 | bytes 4194304 | tf_op jit(solution)/shard_map/pallas_call | solution.py:589
  38.6 13.5 %shard_map.129 = (f32[1024,128]{1,0:T(8,128)S(1)}, f32[1024,128]{1,0:T(8,128)S(1)}, f32[8,64]{1,0:T(8,128)S(1)}) custom-call(s32[1]{0:T(128)} %bitcast.me, f32[144,128]{1,0:T(8,128)S(1)} %add.14.table, bf16[3072,512]{1,0:T(8,128)(2,1)S(1)} %get-tuple-element.66.cell_ref, bf16[768,512]{1,0:T(8,128)(2,1)S(1)} %get-tuple-element.67.slot_ref, ...), custom_call_target="tpu_custom_call" | custom-call | flops 5000000000 | bytes 10485760 | tf_op jit(solution)/shard_map/pallas_call | solution.py:589
  52.2 1.2 %collective-permute-done.8 = f32[8,64]{1,0:T(8,128)S(1)} collective-permute-done((f32[8,64]{1,0:T(8,128)S(1)}, f32[8,64]{1,0:T(8,128)S(1)}, u32[]{:S(2)}, u32[]{:S(2)}) %collective-permute-start.8) | collective-permute-done | bytes 2080 | tf_op jit(solution)/shard_map/ppermute | solution.py:606
  53.5 1.5 %collective-permute-start.10 = (f32[16,64]{1,0:T(8,128)S(1)}, f32[16,64]{1,0:T(8,128)S(1)}, u32[]{:S(2)}, u32[]{:S(2)}) collective-permute-start(f32[16,64]{1,0:T(8,128)S(1)} %pad_maximum_fusion.1), channel_id=1, source_target_pairs={{0,2},{1,3},{2,0},{3,1},{4,6},{5,7},{6,4},{7,5},{8,10},{9,11},{10,... | collective-permute-start | bytes 12296 | tf_op jit(solution)/shard_map/ppermute | solution.py:606
  55.0 2.2 %collective-permute-done.10 = f32[16,64]{1,0:T(8,128)S(1)} collective-permute-done((f32[16,64]{1,0:T(8,128)S(1)}, f32[16,64]{1,0:T(8,128)S(1)}, u32[]{:S(2)}, u32[]{:S(2)}) %collective-permute-start.10) | collective-permute-done | bytes 4128 | tf_op jit(solution)/shard_map/ppermute | solution.py:606
  57.2 3.7 %collective-permute-start.11 = (f32[16,64]{1,0:T(8,128)S(1)}, f32[16,64]{1,0:T(8,128)S(1)}, u32[]{:S(2)}, u32[]{:S(2)}) collective-permute-start(f32[16,64]{1,0:T(8,128)S(1)} %add.15.rest_3_), channel_id=1, source_target_pairs={{0,12},{1,13},{2,14},{3,15},{4,8},{5,9},{6,10},{7,11},{8,4},{9,5},... | collective-permute-start | bytes 12296 | tf_op jit(solution)/shard_map/ppermute | solution.py:606
  61.6 1.1 %collective-permute-done.11.rest_0_ = f32[16,64]{1,0:T(8,128)S(1)} collective-permute-done((f32[16,64]{1,0:T(8,128)S(1)}, f32[16,64]{1,0:T(8,128)S(1)}, u32[]{:S(2)}, u32[]{:S(2)}) %collective-permute-start.11) | collective-permute-done | bytes 4128 | tf_op jit(solution)/shard_map/ppermute | solution.py:606
  62.6 2.8 %collective-permute-done.12.rest_1_ = f32[16,64]{1,0:T(8,128)S(1)} collective-permute-done((f32[16,64]{1,0:T(8,128)S(1)}, f32[16,64]{1,0:T(8,128)S(1)}, u32[]{:S(2)}, u32[]{:S(2)}) %collective-permute-start.12) | collective-permute-done | bytes 4128 | tf_op jit(solution)/shard_map/ppermute | solution.py:606
  65.5 2.2 %shard_map.130 = (f32[16,4,32,128]{3,2,1,0:T(8,128)}, f32[16,64]{1,0:T(8,128)}) custom-call(s32[1]{0:T(128)} %bitcast.me, f32[1024,128]{1,0:T(8,128)S(1)} %get-tuple-element.79.image, f32[1024,128]{1,0:T(8,128)S(1)} %collective-permute-done.9.borrowed, bf16[512,2048]{1,0:T(8,128)(2,1)S(1)} %shard_map.125.own_basis.basis, ...), custom_call_target="tpu_custom_call" | custom-call | flops 200000000 | bytes 6291456 | tf_op jit(solution)/shard_map/pallas_call | solution.py:589
  (21 shorter events, 2.9 us)
Async XLA Ops:
  2.8 1.4 %collective-permute-start = (f32[152,128]{1,0:T(8,128)S(1)}, f32[152,128]{1,0:T(8,128)S(1)}, u32[]{:S(2)}, u32[]{:S(2)}) collective-permute-start(f32[152,128]{1,0:T(8,128)S(1)} %get-tuple-element.47.own), channel_id=1, source_target_pairs={{0,1},{1,0},{2,3},{3,2},{4,5},{5,4},{6,7},{7,6},{8,9},{9,8},{10,11... | collective-permute-start | bytes 233480 | tf_op jit(solution)/shard_map/ppermute | solution.py:606
  4.3 2.3 %collective-permute-start.1 = (f32[1536,128]{1,0:T(8,128)S(1)}, f32[1536,128]{1,0:T(8,128)S(1)}, u32[]{:S(2)}, u32[]{:S(2)}) collective-permute-start(f32[1536,128]{1,0:T(8,128)S(1)} %get-tuple-element.50), channel_id=1, source_target_pairs={{0,1},{1,0},{2,3},{3,2},{4,5},{5,4},{6,7},{7,6},{8,9},{9,8},{10,11... | collective-permute-start | bytes 2359304 | tf_op jit(solution)/shard_map/ppermute | solution.py:606
  4.6 5.9 %collective-permute-start.2 = (f32[304,128]{1,0:T(8,128)S(1)}, f32[304,128]{1,0:T(8,128)S(1)}, u32[]{:S(2)}, u32[]{:S(2)}) collective-permute-start(f32[304,128]{1,0:T(8,128)S(1)} %pad_maximum_fusion), channel_id=1, source_target_pairs={{1,2},{2,1},{3,4},{4,3},{5,6},{6,5},{7,8},{8,7},{9,10},{10,9},{11,... | collective-permute-start | bytes 466952 | tf_op jit(solution)/shard_map/ppermute | solution.py:664
  10.5 3.9 %collective-permute-start.3 = (f32[304,128]{1,0:T(8,128)S(1)}, f32[304,128]{1,0:T(8,128)S(1)}, u32[]{:S(2)}, u32[]{:S(2)}) collective-permute-start(f32[304,128]{1,0:T(8,128)S(1)} %collective-permute-done.2.passed), channel_id=1, source_target_pairs={{0,1},{1,0},{2,3},{3,2},{4,5},{5,4},{6,7},{7,6},{8,9},{9,8},{10,11... | collective-permute-start | bytes 466952 | tf_op jit(solution)/shard_map/ppermute | solution.py:606
  14.4 20.9 %collective-permute-start.7 = (f32[8192,128]{1,0:T(8,128)}, f32[8192,128]{1,0:T(8,128)S(1)}, u32[]{:S(2)}, u32[]{:S(2)}) collective-permute-start(f32[8192,128]{1,0:T(8,128)} %bitcast.12), channel_id=1, source_target_pairs={{0,1},{1,0},{2,3},{3,2},{4,5},{5,4},{6,7},{7,6},{8,9},{9,8},{10,11... | collective-permute-start | bytes 12582920 | tf_op jit(solution)/shard_map/ppermute | solution.py:606
  14.8 10.5 %copy-start = (f32[64,4,32,128]{3,2,1,0:T(8,128)S(1)}, f32[64,4,32,128]{3,2,1,0:T(8,128)}, u32[]{:S(2)}) copy-start(f32[64,4,32,128]{3,2,1,0:T(8,128)} %param.15) | copy-start | bytes 12582916
  22.9 5.1 %collective-permute-start.4 = (f32[144,128]{1,0:T(8,128)S(1)}, f32[144,128]{1,0:T(8,128)S(1)}, u32[]{:S(2)}, u32[]{:S(2)}) collective-permute-start(f32[144,128]{1,0:T(8,128)S(1)} %get-tuple-element.58.when), channel_id=1, source_target_pairs={{0,2},{1,3},{2,0},{3,1},{4,6},{5,7},{6,4},{7,5},{8,10},{9,11},{10,... | collective-permute-start | bytes 221192 | tf_op jit(solution)/shard_map/ppermute | solution.py:606
  28.1 4.4 %collective-permute-start.5 = (f32[144,128]{1,0:T(8,128)S(1)}, f32[144,128]{1,0:T(8,128)S(1)}, u32[]{:S(2)}, u32[]{:S(2)}) collective-permute-start(f32[144,128]{1,0:T(8,128)S(1)} %add.12.when), channel_id=1, source_target_pairs={{0,4},{1,5},{2,6},{3,7},{4,0},{5,1},{6,2},{7,3},{8,12},{9,13},{10,... | collective-permute-start | bytes 221192 | tf_op jit(solution)/shard_map/ppermute | solution.py:606
  32.5 6.1 %collective-permute-start.6 = (f32[144,128]{1,0:T(8,128)S(1)}, f32[144,128]{1,0:T(8,128)S(1)}, u32[]{:S(2)}, u32[]{:S(2)}) collective-permute-start(f32[144,128]{1,0:T(8,128)S(1)} %add.13.when), channel_id=1, source_target_pairs={{0,8},{1,9},{2,10},{3,11},{4,12},{5,13},{6,14},{7,15},{8,0},{9,1},... | collective-permute-start | bytes 221192 | tf_op jit(solution)/shard_map/ppermute | solution.py:606
  52.1 1.2 %collective-permute-start.8 = (f32[8,64]{1,0:T(8,128)S(1)}, f32[8,64]{1,0:T(8,128)S(1)}, u32[]{:S(2)}, u32[]{:S(2)}) collective-permute-start(f32[8,64]{1,0:T(8,128)S(1)} %get-tuple-element.81), channel_id=1, source_target_pairs={{0,1},{1,0},{2,3},{3,2},{4,5},{5,4},{6,7},{7,6},{8,9},{9,8},{10,11... | collective-permute-start | bytes 6152 | tf_op jit(solution)/shard_map/ppermute | solution.py:606
  53.4 12.1 %collective-permute-start.9 = (f32[1024,128]{1,0:T(8,128)S(1)}, f32[1024,128]{1,0:T(8,128)S(1)}, u32[]{:S(2)}, u32[]{:S(2)}) collective-permute-start(f32[1024,128]{1,0:T(8,128)S(1)} %get-tuple-element.82), channel_id=1, source_target_pairs={{0,1},{1,0},{2,3},{3,2},{4,5},{5,4},{6,7},{7,6},{8,9},{9,8},{10,11... | collective-permute-start | bytes 1572872 | tf_op jit(solution)/shard_map/ppermute | solution.py:606
  53.5 3.7 %collective-permute-start.10 = (f32[16,64]{1,0:T(8,128)S(1)}, f32[16,64]{1,0:T(8,128)S(1)}, u32[]{:S(2)}, u32[]{:S(2)}) collective-permute-start(f32[16,64]{1,0:T(8,128)S(1)} %pad_maximum_fusion.1), channel_id=1, source_target_pairs={{0,2},{1,3},{2,0},{3,1},{4,6},{5,7},{6,4},{7,5},{8,10},{9,11},{10,... | collective-permute-start | bytes 12296 | tf_op jit(solution)/shard_map/ppermute | solution.py:606
  57.2 5.4 %collective-permute-start.11 = (f32[16,64]{1,0:T(8,128)S(1)}, f32[16,64]{1,0:T(8,128)S(1)}, u32[]{:S(2)}, u32[]{:S(2)}) collective-permute-start(f32[16,64]{1,0:T(8,128)S(1)} %add.15.rest_3_), channel_id=1, source_target_pairs={{0,12},{1,13},{2,14},{3,15},{4,8},{5,9},{6,10},{7,11},{8,4},{9,5},... | collective-permute-start | bytes 12296 | tf_op jit(solution)/shard_map/ppermute | solution.py:606
  60.9 4.5 %collective-permute-start.12 = (f32[16,64]{1,0:T(8,128)S(1)}, f32[16,64]{1,0:T(8,128)S(1)}, u32[]{:S(2)}, u32[]{:S(2)}) collective-permute-start(f32[16,64]{1,0:T(8,128)S(1)} %add.15.rest_3_), channel_id=1, source_target_pairs={{0,8},{1,9},{2,10},{3,11},{4,12},{5,13},{6,14},{7,15},{8,0},{9,1},... | collective-permute-start | bytes 12296 | tf_op jit(solution)/shard_map/ppermute | solution.py:606
  60.9 4.5 %collective-permute-start.13 = (f32[16,64]{1,0:T(8,128)S(1)}, f32[16,64]{1,0:T(8,128)S(1)}, u32[]{:S(2)}, u32[]{:S(2)}) collective-permute-start(f32[16,64]{1,0:T(8,128)S(1)} %add.15.rest_3_), channel_id=1, source_target_pairs={{0,4},{1,5},{2,6},{3,7},{4,0},{5,1},{6,2},{7,3},{8,12},{9,13},{10,... | collective-permute-start | bytes 12296 | tf_op jit(solution)/shard_map/ppermute | solution.py:606

commit v11 on v9

--- a/solution.py
+++ b/solution.py
@@ -224,8 +224,8 @@
 
 def forward_window(
     fields, peers, me, first, second, third, own, partner, passed, across, band_ref,
-    table, cell_ref, slot_ref, speed_ref, line_ref, owner_ref, weight_ref,
-    below, above, z_term, total_ref, *samples,
+    table, place_ref, slot_ref, speed_ref, line_ref, owner_ref, weight_ref,
+    cell_ref, below, above, z_term, total_ref, *samples,
 ):
     entries = line_ref.shape[1]
     cells = LAYERS * 32
@@ -260,6 +260,7 @@
         slot_ref[tile * HALF : (tile + 1) * HALF, :] = hot.astype(BF16)
         rows = slice(tile * fields, (tile + 1) * fields)
         line_ref[rows, :] = jnp.broadcast_to(lax.shift_right_logical(cell, 9), (fields, entries))
+        place_ref[rows, :] = jnp.broadcast_to(jnp.bitwise_and(cell, PLACES - 1), (fields, entries)).astype(F32)
         owner_ref[rows, :] = jnp.broadcast_to(owner, (fields, entries))
         weight_ref[rows, :] = jnp.broadcast_to(weight, (fields, entries))
 
@@ -381,12 +382,23 @@
     lax.fori_loop(0, 8, body, 0)
 
 
+def turn_places(fields, place_ref, when, hot_ref):
+    entries = place_ref.shape[1]
+    lane = lax.broadcasted_iota(jnp.int32, (entries, HALF), 1)
+    for tile in range(TILES):
+        row = place_ref[tile * fields : tile * fields + 1, :]
+        column = jnp.transpose(jnp.broadcast_to(row, (HALF, entries))).astype(jnp.int32)
+        for part in range(PLACES // HALF):
+            hot = jnp.where(column == lane + part * HALF, 1.0, 0.0).astype(BF16)
+            hot_ref[tile * entries : (tile + 1) * entries, part * HALF : (part + 1) * HALF] = hot
+
+
 def adjoint(
-    fields, peers, me, table, cell_ref, slot_ref, speed_ref, line_ref, owner_ref, weight_ref, turned, push_ref,
+    fields, peers, me, table, hot_ref, slot_ref, speed_ref, line_ref, owner_ref, weight_ref, turned, push_ref,
     prior_ref, band_ref, own_basis, own_basis_two, other_basis, other_basis_two, kept, lent, coeffs,
     high_ref, low_ref, inner_two, outer_two, inner_one, outer_one, z_term, image, scaled, *scratch,
 ):
-    lefts, image_parts = scratch[:TILES], scratch[TILES:]
+    *lefts, image_parts = scratch
     entries = line_ref.shape[1]
     cells = LAYERS * 32
     rank = own_basis.shape[0] // 8
@@ -419,12 +431,12 @@
         line, high, low = line_ref[rows, :], high_ref[rows, :], low_ref[rows, :]
         for i in range(0, 32, 2):
             chosen = [line == i, line == i + 1]
-            for part, start in ((high, i * fields), (low, (32 + i) * fields)):
+            row = slice(i * fields, (i + 2) * fields)
+            for part, side in ((high, slice(0, entries)), (low, slice(entries, 2 * entries))):
                 both = [jnp.where(which, part, 0.0) for which in chosen]
-                left[start : start + 2 * fields, :] = jnp.concatenate(both, axis=0).astype(BF16)
-        hot = cell_ref[tile * PLACES : (tile + 1) * PLACES, :]
-        value = lax.dot_general(left[...], hot, NT, preferred_element_type=F32)
-        value = value[: 32 * fields, :] + value[32 * fields :, :]
+                left[row, side] = jnp.concatenate(both, axis=0).astype(BF16)
+        hot = hot_ref[tile * entries : (tile + 1) * entries, :]
+        value = jnp.dot(left[...], jnp.concatenate([hot, hot], axis=0), preferred_element_type=F32)
         for i in range(32):
             for step in range(4):
                 layer, y = tile * LAYERS + i // 8, i % 8 * 4 + step
@@ -466,7 +478,7 @@
     along_z(inner_one, LAYERS, PAIR, fields, band_ref, z_term)
     mine = me[0] % 2
 
-    def step_two(chunk, total, image_parts):
+    def step_two(chunk, total):
         skip = chunk * 8 * fields
         here = window(inner_one, skip, 2 * PAIR * slab - ahead)
         two_rows, one_rows = (window(ref, LAYERS * flat + skip, PAIR * flat - ahead) for ref in (outer_two, outer_one))
@@ -498,15 +510,14 @@
                     image_parts[rows, lane + HALF : lane + 256] = jnp.concatenate([high, nothing], axis=0).astype(BF16)
         for side, pieces in ((mine, (own_basis, own_basis_two)), (1 - mine, (other_basis, other_basis_two))):
             for x in range(LAYERS):
-                columns = pieces[x // 2][(x % 2 * 4 + chunk) * rank : (x % 2 * 4 + chunk + 1) * rank, :]
+                columns = pieces[x // 2][at((x % 2 * 4 + chunk) * rank, rank), :]
                 parts = image_parts[at((side * LAYERS + x) * 2 * fields, 2 * fields), :]
-                total = total + lax.dot_general(parts, columns, NT, preferred_element_type=F32)
+                total = total + lax.dot_general(columns, parts, NT, preferred_element_type=F32)
         return total
 
-    total = jnp.zeros((2 * fields, rank), F32)
-    for chunk in range(4):
-        total = step_two(chunk, total, image_parts[chunk])
-    coeffs[...] = total[:fields, :] + total[fields:, :]
+    total = lax.fori_loop(0, 4, step_two, jnp.zeros((rank, 2 * fields), F32))
+    both = jnp.concatenate([total[:, :fields] + total[:, fields:], jnp.zeros((rank, HALF - fields), F32)], axis=1)
+    coeffs[...] = jnp.transpose(both)[:fields, :]
     kept[...] = image[at(mine * LAYERS * flat, LAYERS * flat), :]
     lent[...] = image[at((1 - mine) * LAYERS * flat, LAYERS * flat), :]
 
@@ -659,12 +670,12 @@
     across = swapped(passed, "space", 1)
     across, basis_there = lax.optimization_barrier((across, basis))
     basis_there = swapped(basis_there, "space", 1)
-    table, cell_hot, slot_hot, speed, line, owner, weight = call(
+    table, place, slot_hot, speed, line, owner, weight = call(
         functools.partial(forward_window, fields, peers),
         (me, first, second, third, own, partner, passed, across, matrix),
         [
             struct(peers * (fields + 1), HALF),
-            struct(TILES * PLACES, entries, dtype=BF16),
+            struct(TILES * fields, entries),
             struct(TILES * HALF, entries, dtype=BF16),
             struct(TILES * cells, HALF),
             struct(TILES * fields, entries, dtype=jnp.int32),
@@ -672,6 +683,7 @@
             struct(TILES * fields, entries),
         ],
         [
+            pltpu.VMEM((TILES * PLACES, entries), BF16),
             pltpu.VMEM((LAYERS * slab, HALF), F32),
             pltpu.VMEM((LAYERS * slab, HALF), F32),
             pltpu.VMEM((PAIR * flat, HALF), F32),
@@ -697,12 +709,22 @@
                 4 * 2**20,
             )
             columns.append(some)
+        if bits == 2:
+            (turned_hot,) = call(
+                functools.partial(turn_places, fields),
+                (place, table),
+                [struct(TILES * entries, PLACES, dtype=BF16)],
+                [],
+                10_000_000,
+                4 * 2**20,
+            )
+            arrived, turned_hot = lax.optimization_barrier((arrived, turned_hot))
         arrived, columns = lax.optimization_barrier((arrived, columns))
         table = table + arrived
         bits *= 2
     kept, lent, coeffs = call(
         functools.partial(adjoint, fields, peers),
-        (me, table, cell_hot, slot_hot, speed, line, owner, weight, turned, push, damping, matrix, *columns),
+        (me, table, turned_hot, slot_hot, speed, line, owner, weight, turned, push, damping, matrix, *columns),
         [struct(LAYERS * flat, HALF), struct(LAYERS * flat, HALF), struct(fields, rank)],
         [
             pltpu.VMEM((TILES * fields, entries), F32),
@@ -715,8 +737,8 @@
             pltpu.VMEM((PAIR * flat, HALF), F32),
             pltpu.VMEM((peers * fields, HALF), F32),
         ]
-        + [pltpu.VMEM((64 * fields, entries), BF16)] * TILES
-        + [pltpu.VMEM((2 * PAIR * fields, 2048), BF16)] * 4,
+        + [pltpu.VMEM((32 * fields, 2 * entries), BF16)] * TILES
+        + [pltpu.VMEM((2 * PAIR * fields, 2048), BF16)],
         5_000_000_000,
         10 * 2**20,
         scalars=1,

time: 63.6 us -> 60.5 us (0.951)
  Pallas kernels: 30.8 us -> 28.7 us
  waiting for transfers between devices: 12.5 us -> 11.7 us
    pallas_call x9 -> x10, Pallas kernels: 30.8 us -> 28.7 us  [call(): pl.pallas_call(kernel, out_shape=out_shape, in_specs=[smem] * scalars + [...]
    ppermute x13, waiting for transfers between devices: 12.5 us -> 11.7 us  [swapped(): return lax.ppermute(array, axis, [(i, i ^ bits) for i in range(count)])]
  transfers between devices with their start and end apart: 14 -> 14, of which waited for: 9 -> 9; matrix products, arithmetic and copies ran while one was open for 0% -> 0% of each run, Pallas kernels for 23% -> 26%
where the time goes in v11:
time: 60.5 us; the launch traced here: 60.3 us
  Pallas kernels  28.7 us (47%)
  starting transfers between devices  18.4 us (30%)
  waiting for transfers between devices  11.7 us (19%)
  between operations  1.4 us (2%)
    pallas_call x10, Pallas kernels, call(): pl.pallas_call(kernel, out_shape=out_shape, in_specs=[smem] * scalars + [...  28.7 us
    ppermute x13, starting transfers between devices, swapped(): return lax.ppermute(array, axis, [(i, i ^ bits) for i in range(count)])  17.8 us
    ppermute x13, waiting for transfers between devices, swapped(): return lax.ppermute(array, axis, [(i, i ^ bits) for i in range(count)])  11.7 us
  transfers between devices with their start and end apart: 14, of which 9 were waited for; matrix products, arithmetic and copies ran while one was open for 0% of the time, Pallas kernels for 26%

profile of v11, /device:TPU:0, one launch (start us, length us, event | category | flops | bytes accessed | tf_op | source)
XLA Modules:
  0.0 60.3 jit_solution(10909476766890486962)
XLA Ops:
  1.3 1.6 %shard_map.122 = (f32[152,128]{1,0:T(8,128)S(1)}, f32[1024,128]{1,0:T(8,128)S(1)}, f32[384,128]{1,0:T(8,128)S(1)}, f32[128,128]{1,0:T(8,128)S(1)}, f32[1536,128]...) custom-call(s32[1]{0:T(128)S(6)} %copy.13.count, s32[1]{0:T(128)} %bitcast.me, f32[2048,128]{1,0:T(8,128)} %bitcast.15, ...), custom_call_target="tpu_custom_call" | custom-call | flops 100000 | bytes 2097152 | tf_op jit(solution)/shard_map/pallas_call | solution.py:572
  3.4 0.9 %collective-permute-done.partner = f32[152,128]{1,0:T(8,128)S(1)} collective-permute-done((f32[152,128]{1,0:T(8,128)S(1)}, f32[152,128]{1,0:T(8,128)S(1)}, u32[]{:S(2)}, u32[]{:S(2)}) %collective-permute-start) | collective-permute-done | bytes 77856 | tf_op jit(solution)/shard_map/ppermute | solution.py:589
  5.3 1.2 %collective-permute-done.1.borrowed = f32[1536,128]{1,0:T(8,128)S(1)} collective-permute-done((f32[1536,128]{1,0:T(8,128)S(1)}, f32[1536,128]{1,0:T(8,128)S(1)}, u32[]{:S(2)}, u32[]{:S(2)}) %collective-permute-start.1) | collective-permute-done | bytes 786464 | tf_op jit(solution)/shard_map/ppermute | solution.py:589
  6.6 3.5 %shard_map.123 = (f32[2048,128]{1,0:T(8,128)S(1)}, f32[2560,128]{1,0:T(8,128)S(1)}, f32[2560,128]{1,0:T(8,128)S(1)}, f32[2048,128]{1,0:T(8,128)S(1)}, f32[768,128]{1,0:T(8,128)S(1)}, /*index=5*/f32[256,128]{1,0:T(8,128)S(1)}) custom-call(s32[1]{0:T(128)} %bitcast.me, f32[1024,128]{1,0:T(8,128)S(1)} %get-tuple-element.46.probes, ...), custom_call_target="tpu_custom_call" | custom-call | flops 600000000 | bytes 6291456 | tf_op jit(solution)/shard_map/pallas_call | solution.py:572
  10.1 2.9 %collective-permute-start.3 = (f32[304,128]{1,0:T(8,128)S(1)}, f32[304,128]{1,0:T(8,128)S(1)}, u32[]{:S(2)}, u32[]{:S(2)}) collective-permute-start(f32[304,128]{1,0:T(8,128)S(1)} %collective-permute-done.2.passed), channel_id=1, source_target_pairs={{0,1},{1,0},{2,3},{3,2},{4,5},{5,4},{6,7},{7,6},{8,9},{9,8},{10,11... | collective-permute-start | bytes 466952 | tf_op jit(solution)/shard_map/ppermute | solution.py:589
  12.9 1.0 %collective-permute-done.3.across = f32[304,128]{1,0:T(8,128)S(1)} collective-permute-done((f32[304,128]{1,0:T(8,128)S(1)}, f32[304,128]{1,0:T(8,128)S(1)}, u32[]{:S(2)}, u32[]{:S(2)}) %collective-permute-start.3) | collective-permute-done | bytes 155680 | tf_op jit(solution)/shard_map/ppermute | solution.py:589
  14.3 4.9 %shard_map.124 = (f32[144,128]{1,0:T(8,128)S(1)}, f32[48,512]{1,0:T(8,128)S(1)}, bf16[768,512]{1,0:T(8,128)(2,1)S(1)}, f32[768,128]{1,0:T(8,128)S(1)}, s32[48,51...) custom-call(s32[1]{0:T(128)} %bitcast.me, f32[2560,128]{1,0:T(8,128)S(1)} %get-tuple-element.54.first, ...), custom_call_target="tpu_custom_call" | custom-call | flops 3000000000 | bytes 6291456 | tf_op jit(solution)/shard_map/pallas_call | solution.py:572
  19.2 2.8 %collective-permute-start.4 = (f32[144,128]{1,0:T(8,128)S(1)}, f32[144,128]{1,0:T(8,128)S(1)}, u32[]{:S(2)}, u32[]{:S(2)}) collective-permute-start(f32[144,128]{1,0:T(8,128)S(1)} %get-tuple-element.60.when), channel_id=1, source_target_pairs={{0,2},{1,3},{2,0},{3,1},{4,6},{5,7},{6,4},{7,5},{8,10},{9,11},{10,... | collective-permute-start | bytes 221192 | tf_op jit(solution)/shard_map/ppermute | solution.py:589
  22.0 1.6 %shard_map.126.own_basis.basis = bf16[512,2048]{1,0:T(8,128)(2,1)S(1)} custom-call(f32[8192,128]{1,0:T(8,128)S(1)} %bitcast.13, f32[144,128]{1,0:T(8,128)S(1)} %get-tuple-element.60.when), custom_call_target="tpu_custom_call" | custom-call | flops 10000000 | bytes 4194304 | tf_op jit(solution)/shard_map/pallas_call | solution.py:572
  23.6 0.8 %shard_map.125.hot_ref = bf16[3072,512]{1,0:T(8,128)(2,1)S(1)} custom-call(f32[48,512]{1,0:T(8,128)S(1)} %get-tuple-element.61.place_ref, f32[144,128]{1,0:T(8,128)S(1)} %get-tuple-element.60.when), custom_call_target="tpu_custom_call" | custom-call | flops 10000000 | bytes 4194304 | tf_op jit(solution)/shard_map/pallas_call | solution.py:572
  24.8 1.9 %collective-permute-start.5 = (f32[144,128]{1,0:T(8,128)S(1)}, f32[144,128]{1,0:T(8,128)S(1)}, u32[]{:S(2)}, u32[]{:S(2)}) collective-permute-start(f32[144,128]{1,0:T(8,128)S(1)} %add.12.when), channel_id=1, source_target_pairs={{0,4},{1,5},{2,6},{3,7},{4,0},{5,1},{6,2},{7,3},{8,12},{9,13},{10,... | collective-permute-start | bytes 221192 | tf_op jit(solution)/shard_map/ppermute | solution.py:589
  26.7 1.6 %shard_map.127.own_basis_two.basis_two = bf16[512,2048]{1,0:T(8,128)(2,1)S(1)} custom-call(f32[8192,128]{1,0:T(8,128)S(1)} %bitcast.14, f32[144,128]{1,0:T(8,128)S(1)} %add.12.when), custom_call_target="tpu_custom_call" | custom-call | flops 10000000 | bytes 4194304 | tf_op jit(solution)/shard_map/pallas_call | solution.py:572
  28.3 0.9 %collective-permute-done.5 = f32[144,128]{1,0:T(8,128)S(1)} collective-permute-done((f32[144,128]{1,0:T(8,128)S(1)}, f32[144,128]{1,0:T(8,128)S(1)}, u32[]{:S(2)}, u32[]{:S(2)}) %collective-permute-start.5) | collective-permute-done | bytes 73760 | tf_op jit(solution)/shard_map/ppermute | solution.py:589
  29.2 2.9 %collective-permute-start.6 = (f32[144,128]{1,0:T(8,128)S(1)}, f32[144,128]{1,0:T(8,128)S(1)}, u32[]{:S(2)}, u32[]{:S(2)}) collective-permute-start(f32[144,128]{1,0:T(8,128)S(1)} %add.13.when), channel_id=1, source_target_pairs={{0,8},{1,9},{2,10},{3,11},{4,12},{5,13},{6,14},{7,15},{8,0},{9,1},... | collective-permute-start | bytes 221192 | tf_op jit(solution)/shard_map/ppermute | solution.py:589
  32.1 1.6 %shard_map.129.other_basis_two = bf16[512,2048]{1,0:T(8,128)(2,1)S(1)} custom-call(f32[8192,128]{1,0:T(8,128)S(1)} %collective-permute-done.7.basis, f32[144,128]{1,0:T(8,128)S(1)} %add.13.when), custom_call_target="tpu_custom_call" | custom-call | flops 10000000 | bytes 4194304 | tf_op jit(solution)/shard_map/pallas_call | solution.py:572
  33.7 1.6 %shard_map.128.other_basis = bf16[512,2048]{1,0:T(8,128)(2,1)S(1)} custom-call(f32[8192,128]{1,0:T(8,128)S(1)} %collective-permute-done.7.basis, f32[144,128]{1,0:T(8,128)S(1)} %add.13.when), custom_call_target="tpu_custom_call" | custom-call | flops 10000000 | bytes 4194304 | tf_op jit(solution)/shard_map/pallas_call | solution.py:572
  35.3 9.5 %shard_map.130 = (f32[1024,128]{1,0:T(8,128)S(1)}, f32[1024,128]{1,0:T(8,128)S(1)}, f32[8,64]{1,0:T(8,128)S(1)}) custom-call(s32[1]{0:T(128)} %bitcast.me, f32[144,128]{1,0:T(8,128)S(1)} %add.14.table, bf16[3072,512]{1,0:T(8,128)(2,1)S(1)} %shard_map.125.hot_ref, bf16[768,512]{1,0:T(8,128)(2,1)S(1)} %get-tuple-element.71.slot_ref, ...), custom_call_target="tpu_custom_call" | custom-call | flops 5000000000 | bytes 10485760 | tf_op jit(solution)/shard_map/pallas_call | solution.py:572
  44.9 1.2 %collective-permute-done.8 = f32[8,64]{1,0:T(8,128)S(1)} collective-permute-done((f32[8,64]{1,0:T(8,128)S(1)}, f32[8,64]{1,0:T(8,128)S(1)}, u32[]{:S(2)}, u32[]{:S(2)}) %collective-permute-start.8) | collective-permute-done | bytes 2080 | tf_op jit(solution)/shard_map/ppermute | solution.py:589
  46.2 1.5 %collective-permute-start.10 = (f32[16,64]{1,0:T(8,128)S(1)}, f32[16,64]{1,0:T(8,128)S(1)}, u32[]{:S(2)}, u32[]{:S(2)}) collective-permute-start(f32[16,64]{1,0:T(8,128)S(1)} %pad_maximum_fusion.1), channel_id=1, source_target_pairs={{0,2},{1,3},{2,0},{3,1},{4,6},{5,7},{6,4},{7,5},{8,10},{9,11},{10,... | collective-permute-start | bytes 12296 | tf_op jit(solution)/shard_map/ppermute | solution.py:589
  47.7 2.2 %collective-permute-done.10 = f32[16,64]{1,0:T(8,128)S(1)} collective-permute-done((f32[16,64]{1,0:T(8,128)S(1)}, f32[16,64]{1,0:T(8,128)S(1)}, u32[]{:S(2)}, u32[]{:S(2)}) %collective-permute-start.10) | collective-permute-done | bytes 4128 | tf_op jit(solution)/shard_map/ppermute | solution.py:589
  49.9 3.7 %collective-permute-start.11 = (f32[16,64]{1,0:T(8,128)S(1)}, f32[16,64]{1,0:T(8,128)S(1)}, u32[]{:S(2)}, u32[]{:S(2)}) collective-permute-start(f32[16,64]{1,0:T(8,128)S(1)} %add.15.rest_3_), channel_id=1, source_target_pairs={{0,12},{1,13},{2,14},{3,15},{4,8},{5,9},{6,10},{7,11},{8,4},{9,5},... | collective-permute-start | bytes 12296 | tf_op jit(solution)/shard_map/ppermute | solution.py:589
  54.3 1.1 %collective-permute-done.11.rest_0_ = f32[16,64]{1,0:T(8,128)S(1)} collective-permute-done((f32[16,64]{1,0:T(8,128)S(1)}, f32[16,64]{1,0:T(8,128)S(1)}, u32[]{:S(2)}, u32[]{:S(2)}) %collective-permute-start.11) | collective-permute-done | bytes 4128 | tf_op jit(solution)/shard_map/ppermute | solution.py:589
  55.3 2.8 %collective-permute-done.12.rest_1_ = f32[16,64]{1,0:T(8,128)S(1)} collective-permute-done((f32[16,64]{1,0:T(8,128)S(1)}, f32[16,64]{1,0:T(8,128)S(1)}, u32[]{:S(2)}, u32[]{:S(2)}) %collective-permute-start.12) | collective-permute-done | bytes 4128 | tf_op jit(solution)/shard_map/ppermute | solution.py:589
  58.2 2.2 %shard_map.131 = (f32[16,4,32,128]{3,2,1,0:T(8,128)}, f32[16,64]{1,0:T(8,128)}) custom-call(s32[1]{0:T(128)} %bitcast.me, f32[1024,128]{1,0:T(8,128)S(1)} %get-tuple-element.83.image, f32[1024,128]{1,0:T(8,128)S(1)} %collective-permute-done.9.borrowed, bf16[512,2048]{1,0:T(8,128)(2,1)S(1)} %shard_map.126.own_basis.basis, ...), custom_call_target="tpu_custom_call" | custom-call | flops 200000000 | bytes 6291456 | tf_op jit(solution)/shard_map/pallas_call | solution.py:572
  (22 shorter events, 3.3 us)
Async XLA Ops:
  2.8 1.4 %collective-permute-start = (f32[152,128]{1,0:T(8,128)S(1)}, f32[152,128]{1,0:T(8,128)S(1)}, u32[]{:S(2)}, u32[]{:S(2)}) collective-permute-start(f32[152,128]{1,0:T(8,128)S(1)} %get-tuple-element.49.own), channel_id=1, source_target_pairs={{0,1},{1,0},{2,3},{3,2},{4,5},{5,4},{6,7},{7,6},{8,9},{9,8},{10,11... | collective-permute-start | bytes 233480 | tf_op jit(solution)/shard_map/ppermute | solution.py:589
  4.3 2.3 %collective-permute-start.1 = (f32[1536,128]{1,0:T(8,128)S(1)}, f32[1536,128]{1,0:T(8,128)S(1)}, u32[]{:S(2)}, u32[]{:S(2)}) collective-permute-start(f32[1536,128]{1,0:T(8,128)S(1)} %get-tuple-element.52), channel_id=1, source_target_pairs={{0,1},{1,0},{2,3},{3,2},{4,5},{5,4},{6,7},{7,6},{8,9},{9,8},{10,11... | collective-permute-start | bytes 2359304 | tf_op jit(solution)/shard_map/ppermute | solution.py:589
  4.6 5.4 %collective-permute-start.2 = (f32[304,128]{1,0:T(8,128)S(1)}, f32[304,128]{1,0:T(8,128)S(1)}, u32[]{:S(2)}, u32[]{:S(2)}) collective-permute-start(f32[304,128]{1,0:T(8,128)S(1)} %pad_maximum_fusion), channel_id=1, source_target_pairs={{1,2},{2,1},{3,4},{4,3},{5,6},{6,5},{7,8},{8,7},{9,10},{10,9},{11,... | collective-permute-start | bytes 466952 | tf_op jit(solution)/shard_map/ppermute | solution.py:647
  10.1 3.9 %collective-permute-start.3 = (f32[304,128]{1,0:T(8,128)S(1)}, f32[304,128]{1,0:T(8,128)S(1)}, u32[]{:S(2)}, u32[]{:S(2)}) collective-permute-start(f32[304,128]{1,0:T(8,128)S(1)} %collective-permute-done.2.passed), channel_id=1, source_target_pairs={{0,1},{1,0},{2,3},{3,2},{4,5},{5,4},{6,7},{7,6},{8,9},{9,8},{10,11... | collective-permute-start | bytes 466952 | tf_op jit(solution)/shard_map/ppermute | solution.py:589
  14.0 18.1 %collective-permute-start.7 = (f32[8192,128]{1,0:T(8,128)}, f32[8192,128]{1,0:T(8,128)S(1)}, u32[]{:S(2)}, u32[]{:S(2)}) collective-permute-start(f32[8192,128]{1,0:T(8,128)} %bitcast.12), channel_id=1, source_target_pairs={{0,1},{1,0},{2,3},{3,2},{4,5},{5,4},{6,7},{7,6},{8,9},{9,8},{10,11... | collective-permute-start | bytes 12582920 | tf_op jit(solution)/shard_map/ppermute | solution.py:589
  14.3 7.7 %copy-start = (f32[64,4,32,128]{3,2,1,0:T(8,128)S(1)}, f32[64,4,32,128]{3,2,1,0:T(8,128)}, u32[]{:S(2)}) copy-start(f32[64,4,32,128]{3,2,1,0:T(8,128)} %param.15) | copy-start | bytes 12582916
  19.2 5.6 %collective-permute-start.4 = (f32[144,128]{1,0:T(8,128)S(1)}, f32[144,128]{1,0:T(8,128)S(1)}, u32[]{:S(2)}, u32[]{:S(2)}) collective-permute-start(f32[144,128]{1,0:T(8,128)S(1)} %get-tuple-element.60.when), channel_id=1, source_target_pairs={{0,2},{1,3},{2,0},{3,1},{4,6},{5,7},{6,4},{7,5},{8,10},{9,11},{10,... | collective-permute-start | bytes 221192 | tf_op jit(solution)/shard_map/ppermute | solution.py:589
  24.8 4.4 %collective-permute-start.5 = (f32[144,128]{1,0:T(8,128)S(1)}, f32[144,128]{1,0:T(8,128)S(1)}, u32[]{:S(2)}, u32[]{:S(2)}) collective-permute-start(f32[144,128]{1,0:T(8,128)S(1)} %add.12.when), channel_id=1, source_target_pairs={{0,4},{1,5},{2,6},{3,7},{4,0},{5,1},{6,2},{7,3},{8,12},{9,13},{10,... | collective-permute-start | bytes 221192 | tf_op jit(solution)/shard_map/ppermute | solution.py:589
  29.2 6.1 %collective-permute-start.6 = (f32[144,128]{1,0:T(8,128)S(1)}, f32[144,128]{1,0:T(8,128)S(1)}, u32[]{:S(2)}, u32[]{:S(2)}) collective-permute-start(f32[144,128]{1,0:T(8,128)S(1)} %add.13.when), channel_id=1, source_target_pairs={{0,8},{1,9},{2,10},{3,11},{4,12},{5,13},{6,14},{7,15},{8,0},{9,1},... | collective-permute-start | bytes 221192 | tf_op jit(solution)/shard_map/ppermute | solution.py:589
  44.9 1.2 %collective-permute-start.8 = (f32[8,64]{1,0:T(8,128)S(1)}, f32[8,64]{1,0:T(8,128)S(1)}, u32[]{:S(2)}, u32[]{:S(2)}) collective-permute-start(f32[8,64]{1,0:T(8,128)S(1)} %get-tuple-element.85), channel_id=1, source_target_pairs={{0,1},{1,0},{2,3},{3,2},{4,5},{5,4},{6,7},{7,6},{8,9},{9,8},{10,11... | collective-permute-start | bytes 6152 | tf_op jit(solution)/shard_map/ppermute | solution.py:589
  46.1 12.1 %collective-permute-start.9 = (f32[1024,128]{1,0:T(8,128)S(1)}, f32[1024,128]{1,0:T(8,128)S(1)}, u32[]{:S(2)}, u32[]{:S(2)}) collective-permute-start(f32[1024,128]{1,0:T(8,128)S(1)} %get-tuple-element.86), channel_id=1, source_target_pairs={{0,1},{1,0},{2,3},{3,2},{4,5},{5,4},{6,7},{7,6},{8,9},{9,8},{10,11... | collective-permute-start | bytes 1572872 | tf_op jit(solution)/shard_map/ppermute | solution.py:589
  46.2 3.7 %collective-permute-start.10 = (f32[16,64]{1,0:T(8,128)S(1)}, f32[16,64]{1,0:T(8,128)S(1)}, u32[]{:S(2)}, u32[]{:S(2)}) collective-permute-start(f32[16,64]{1,0:T(8,128)S(1)} %pad_maximum_fusion.1), channel_id=1, source_target_pairs={{0,2},{1,3},{2,0},{3,1},{4,6},{5,7},{6,4},{7,5},{8,10},{9,11},{10,... | collective-permute-start | bytes 12296 | tf_op jit(solution)/shard_map/ppermute | solution.py:589
  49.9 5.4 %collective-permute-start.11 = (f32[16,64]{1,0:T(8,128)S(1)}, f32[16,64]{1,0:T(8,128)S(1)}, u32[]{:S(2)}, u32[]{:S(2)}) collective-permute-start(f32[16,64]{1,0:T(8,128)S(1)} %add.15.rest_3_), channel_id=1, source_target_pairs={{0,12},{1,13},{2,14},{3,15},{4,8},{5,9},{6,10},{7,11},{8,4},{9,5},... | collective-permute-start | bytes 12296 | tf_op jit(solution)/shard_map/ppermute | solution.py:589
  53.6 4.5 %collective-permute-start.12 = (f32[16,64]{1,0:T(8,128)S(1)}, f32[16,64]{1,0:T(8,128)S(1)}, u32[]{:S(2)}, u32[]{:S(2)}) collective-permute-start(f32[16,64]{1,0:T(8,128)S(1)} %add.15.rest_3_), channel_id=1, source_target_pairs={{0,8},{1,9},{2,10},{3,11},{4,12},{5,13},{6,14},{7,15},{8,0},{9,1},... | collective-permute-start | bytes 12296 | tf_op jit(solution)/shard_map/ppermute | solution.py:589
  53.6 4.5 %collective-permute-start.13 = (f32[16,64]{1,0:T(8,128)S(1)}, f32[16,64]{1,0:T(8,128)S(1)}, u32[]{:S(2)}, u32[]{:S(2)}) collective-permute-start(f32[16,64]{1,0:T(8,128)S(1)} %add.15.rest_3_), channel_id=1, source_target_pairs={{0,4},{1,5},{2,6},{3,7},{4,0},{5,1},{6,2},{7,3},{8,12},{9,13},{10,... | collective-permute-start | bytes 12296 | tf_op jit(solution)/shard_map/ppermute | solution.py:589

commit v12 on v11

--- a/solution.py
+++ b/solution.py
@@ -373,10 +373,15 @@
     def body(group, carry):
         here = window(basis, (first + group) * 8, basis.shape[0] - 15 * 8)
         there = window(out, group * rank, rank)
-        for step in range(8):
-            high, low = split(here[pl.ds(step, rank, stride=HALF), :])
-            there[:, step * 256 : step * 256 + HALF] = high
-            there[:, step * 256 + HALF : (step + 1) * 256] = low
+        for start in range(0, rank, 16):
+            blocks = []
+            for block in (start, start + 8):
+                rows = [here[k * HALF : k * HALF + 8, :] for k in range(block, block + 8)]
+                blocks.append(jnp.swapaxes(jnp.stack(rows, axis=0), 0, 1))
+            for step in range(8):
+                high, low = split(jnp.concatenate([block[step] for block in blocks], axis=0))
+                there[start : start + 16, step * 256 : step * 256 + HALF] = high
+                there[start : start + 16, step * 256 + HALF : (step + 1) * 256] = low
         return carry
 
     lax.fori_loop(0, 8, body, 0)
@@ -425,7 +430,7 @@
         high_ref[rows, :] = high
         low_ref[rows, :] = value - high
 
-    for tile in range(TILES):
+    def product(tile):
         left = lefts[tile]
         rows = slice(tile * fields, (tile + 1) * fields)
         line, high, low = line_ref[rows, :], high_ref[rows, :], low_ref[rows, :]
@@ -436,7 +441,9 @@
                 both = [jnp.where(which, part, 0.0) for which in chosen]
                 left[row, side] = jnp.concatenate(both, axis=0).astype(BF16)
         hot = hot_ref[tile * entries : (tile + 1) * entries, :]
-        value = jnp.dot(left[...], jnp.concatenate([hot, hot], axis=0), preferred_element_type=F32)
+        return jnp.dot(left[...], jnp.concatenate([hot, hot], axis=0), preferred_element_type=F32)
+
+    def inject(tile, value):
         for i in range(32):
             for step in range(4):
                 layer, y = tile * LAYERS + i // 8, i % 8 * 4 + step
@@ -449,6 +456,12 @@
                 inner_two[row : row + fields, :] = speed * now
         if 1 <= tile <= 4:
             along_z(inner_two, tile * LAYERS, LAYERS, fields, band_ref, z_term, (tile - 1) * cells * fields)
+
+    values = product(0)
+    for tile in range(TILES):
+        after = product(tile + 1) if tile + 1 < TILES else None
+        inject(tile, values)
+        values = after
 
     def step_one(index, carry):
         pair, chunk = index // 4, index % 4
@@ -512,27 +525,24 @@
             for x in range(LAYERS):
                 columns = pieces[x // 2][at((x % 2 * 4 + chunk) * rank, rank), :]
                 parts = image_parts[at((side * LAYERS + x) * 2 * fields, 2 * fields), :]
-                total = total + lax.dot_general(columns, parts, NT, preferred_element_type=F32)
+                total = total + lax.dot_general(parts, columns, NT, preferred_element_type=F32)
         return total
 
-    total = lax.fori_loop(0, 4, step_two, jnp.zeros((rank, 2 * fields), F32))
-    both = jnp.concatenate([total[:, :fields] + total[:, fields:], jnp.zeros((rank, HALF - fields), F32)], axis=1)
-    coeffs[...] = jnp.transpose(both)[:fields, :]
+    total = lax.fori_loop(0, 4, step_two, jnp.zeros((2 * fields, rank), F32))
+    coeffs[...] = total[:fields, :] + total[fields:, :]
     kept[...] = image[at(mine * LAYERS * flat, LAYERS * flat), :]
     lent[...] = image[at((1 - mine) * LAYERS * flat, LAYERS * flat), :]
 
 
-def remainder(fields, me, image, borrowed, basis, basis_two, *rest):
-    *shares, out, coeffs, natural, sem = rest
+def remainder(fields, me, image, borrowed, basis, basis_two, found, told, out, coeffs, natural, sem):
     rank = coeffs.shape[1]
     half = fields // 2
     mine = me[0] % 2
-    while len(shares) > 1:
-        shares = [shares[i][...] + shares[i + 1][...] for i in range(0, len(shares), 2)]
-    total = shares[0][...]
-    coeffs[at(mine * half, half), :] = total[:half, :]
-    coeffs[at((1 - mine) * half, half), :] = total[half:, :]
-    parts = jnp.concatenate(split(total), axis=0)
+    total = jnp.where(mine == 1, found[...], told[...])
+    coeffs[half:, :] = total[:half, :]
+    coeffs[:half, :] = total[half:, :]
+    ordered = jnp.where(mine == 1, total, jnp.concatenate([total[half:, :], total[:half, :]], axis=0))
+    parts = jnp.concatenate(split(ordered), axis=0)
     whole = natural.reshape(out.shape)
     first, second = (window(natural, side * half * HALF, half * HALF) for side in (mine, 1 - mine))
 
@@ -582,6 +592,11 @@
 
 def struct(*shape, dtype=F32):
     return jax.ShapeDtypeStruct(shape, dtype)
+
+
+def odd_swapped(array, axis, bits):
+    count = lax.axis_size(axis)
+    return lax.ppermute(array, axis, [(i, i ^ bits) for i in range(1, count, 2)])
 
 
 def swapped(array, axis, bits):
@@ -744,17 +759,20 @@
         scalars=1,
         room=30,
     )
-    coeffs = jnp.concatenate([coeffs, swapped(coeffs, "space", 1)], axis=0)
+    even = [(i, i + 1) for i in range(0, peers, 2)]
+    coeffs = jnp.concatenate([coeffs, lax.ppermute(coeffs, "space", even)], axis=0)
     lent, coeffs = lax.optimization_barrier((lent, coeffs))
     borrowed = swapped(lent, "space", 1)
     bits = 2
     while bits * 4 < peers:
-        coeffs = coeffs + swapped(coeffs, "space", bits)
+        coeffs = coeffs + odd_swapped(coeffs, "space", bits)
         bits *= 2
-    shares = [swapped(coeffs, "space", bits * i) for i in (3, 2, 1)] + [coeffs]
+    shares = [odd_swapped(coeffs, "space", bits * i) for i in (3, 2, 1)] + [coeffs]
+    coeffs = (shares[0] + shares[1]) + (shares[2] + shares[3])
+    told = lax.ppermute(coeffs, "space", [(j, i) for i, j in even])
     hess_probe, coeffs = call(
         functools.partial(remainder, 2 * fields),
-        (me, kept, borrowed, *columns[:2], *shares),
+        (me, kept, borrowed, *columns[:2], coeffs, told),
         [struct(*probes.shape), struct(2 * fields, rank)],
         [pltpu.VMEM((2 * fields * cells, HALF), F32), pltpu.SemaphoreType.DMA((LAYERS,))],
         200_000_000,

time: 60.5 us -> 67 us (1.11)
  waiting for transfers between devices: 11.7 us -> 23.1 us
  Pallas kernels: 28.7 us -> 24.2 us
    ppermute x0 -> x6, waiting for transfers between devices: none -> 15.7 us  [the longest x1 14.9 us: local(): told = lax.ppermute(coeffs, 'space', [(j, i) for i, j in even])]
    ppermute x13 -> x8, starting transfers between devices: 17.8 us -> 12 us  [swapped(): return lax.ppermute(array, axis, [(i, i ^ bits) for i in range(count)])]
    ppermute x0 -> x6, starting transfers between devices: none -> 5.22 us  [the longest x4 2.63 us: odd_swapped(): lax.ppermute(array, axis, [(i, i ^ bits) for i in range(1, count, 2)])]
    pallas_call x10, Pallas kernels: 28.7 us -> 24.2 us  [call(): pl.pallas_call(kernel, out_shape=out_shape, in_specs=[smem] * scalars + [...]
    ppermute x13 -> x8, waiting for transfers between devices: 11.7 us -> 7.38 us  [swapped(): return lax.ppermute(array, axis, [(i, i ^ bits) for i in range(count)])]
  transfers between devices with their start and end apart: 14 -> 15, of which waited for: 9 -> 8; matrix products, arithmetic and copies ran while one was open for 0% -> 0% of each run, Pallas kernels for 26% -> 18%
where the time goes in v12:
time: 67 us; the launch traced here: 66.8 us
  Pallas kernels  24.2 us (36%)
  waiting for transfers between devices  23.1 us (34%)
  starting transfers between devices  17.9 us (27%)
  between operations  1.46 us (2%)
    pallas_call x10, Pallas kernels, call(): pl.pallas_call(kernel, out_shape=out_shape, in_specs=[smem] * scalars + [...  24.2 us
    ppermute x1, waiting for transfers between devices, local(): told = lax.ppermute(coeffs, 'space', [(j, i) for i, j in even])  14.9 us
    ppermute x8, starting transfers between devices, swapped(): return lax.ppermute(array, axis, [(i, i ^ bits) for i in range(count)])  12 us
    ppermute x8, waiting for transfers between devices, swapped(): return lax.ppermute(array, axis, [(i, i ^ bits) for i in range(count)])  7.38 us
    ppermute x4, starting transfers between devices, odd_swapped(): lax.ppermute(array, axis, [(i, i ^ bits) for i in range(1, count, 2)])  2.63 us
  transfers between devices with their start and end apart: 15, of which 8 were waited for; matrix products, arithmetic and copies ran while one was open for 0% of the time, Pallas kernels for 18%

profile of v12, /device:TPU:0, one launch (start us, length us, event | category | flops | bytes accessed | tf_op | source)
XLA Modules:
  0.0 66.8 jit_solution(4751703936844120029)
XLA Ops:
  1.3 1.6 %shard_map.122 = (f32[152,128]{1,0:T(8,128)S(1)}, f32[1024,128]{1,0:T(8,128)S(1)}, f32[384,128]{1,0:T(8,128)S(1)}, f32[128,128]{1,0:T(8,128)S(1)}, f32[1536,128]...) custom-call(s32[1]{0:T(128)S(6)} %copy.13.count, s32[1]{0:T(128)} %bitcast.me, f32[2048,128]{1,0:T(8,128)} %bitcast.15, ...), custom_call_target="tpu_custom_call" | custom-call | flops 100000 | bytes 2097152 | tf_op jit(solution)/shard_map/pallas_call | solution.py:582
  3.4 0.9 %collective-permute-done.partner = f32[152,128]{1,0:T(8,128)S(1)} collective-permute-done((f32[152,128]{1,0:T(8,128)S(1)}, f32[152,128]{1,0:T(8,128)S(1)}, u32[]{:S(2)}, u32[]{:S(2)}) %collective-permute-start) | collective-permute-done | bytes 77856 | tf_op jit(solution)/shard_map/ppermute | solution.py:604
  5.3 1.2 %collective-permute-done.1.borrowed = f32[1536,128]{1,0:T(8,128)S(1)} collective-permute-done((f32[1536,128]{1,0:T(8,128)S(1)}, f32[1536,128]{1,0:T(8,128)S(1)}, u32[]{:S(2)}, u32[]{:S(2)}) %collective-permute-start.1) | collective-permute-done | bytes 786464 | tf_op jit(solution)/shard_map/ppermute | solution.py:604
  6.6 3.5 %shard_map.123 = (f32[2048,128]{1,0:T(8,128)S(1)}, f32[2560,128]{1,0:T(8,128)S(1)}, f32[2560,128]{1,0:T(8,128)S(1)}, f32[2048,128]{1,0:T(8,128)S(1)}, f32[768,128]{1,0:T(8,128)S(1)}, /*index=5*/f32[256,128]{1,0:T(8,128)S(1)}) custom-call(s32[1]{0:T(128)} %bitcast.me, f32[1024,128]{1,0:T(8,128)S(1)} %get-tuple-element.46.probes, ...), custom_call_target="tpu_custom_call" | custom-call | flops 600000000 | bytes 6291456 | tf_op jit(solution)/shard_map/pallas_call | solution.py:582
  10.1 2.9 %collective-permute-start.3 = (f32[304,128]{1,0:T(8,128)S(1)}, f32[304,128]{1,0:T(8,128)S(1)}, u32[]{:S(2)}, u32[]{:S(2)}) collective-permute-start(f32[304,128]{1,0:T(8,128)S(1)} %collective-permute-done.2.passed), channel_id=1, source_target_pairs={{0,1},{1,0},{2,3},{3,2},{4,5},{5,4},{6,7},{7,6},{8,9},{9,8},{10,11... | collective-permute-start | bytes 466952 | tf_op jit(solution)/shard_map/ppermute | solution.py:604
  12.9 1.0 %collective-permute-done.3.across = f32[304,128]{1,0:T(8,128)S(1)} collective-permute-done((f32[304,128]{1,0:T(8,128)S(1)}, f32[304,128]{1,0:T(8,128)S(1)}, u32[]{:S(2)}, u32[]{:S(2)}) %collective-permute-start.3) | collective-permute-done | bytes 155680 | tf_op jit(solution)/shard_map/ppermute | solution.py:604
  14.3 4.9 %shard_map.124 = (f32[144,128]{1,0:T(8,128)S(1)}, f32[48,512]{1,0:T(8,128)S(1)}, bf16[768,512]{1,0:T(8,128)(2,1)S(1)}, f32[768,128]{1,0:T(8,128)S(1)}, s32[48,51...) custom-call(s32[1]{0:T(128)} %bitcast.me, f32[2560,128]{1,0:T(8,128)S(1)} %get-tuple-element.54.first, ...), custom_call_target="tpu_custom_call" | custom-call | flops 3000000000 | bytes 6291456 | tf_op jit(solution)/shard_map/pallas_call | solution.py:582
  19.2 2.8 %collective-permute-start.4 = (f32[144,128]{1,0:T(8,128)S(1)}, f32[144,128]{1,0:T(8,128)S(1)}, u32[]{:S(2)}, u32[]{:S(2)}) collective-permute-start(f32[144,128]{1,0:T(8,128)S(1)} %get-tuple-element.60.when), channel_id=1, source_target_pairs={{0,2},{1,3},{2,0},{3,1},{4,6},{5,7},{6,4},{7,5},{8,10},{9,11},{10,... | collective-permute-start | bytes 221192 | tf_op jit(solution)/shard_map/ppermute | solution.py:604
  22.0 0.7 %shard_map.126.own_basis.basis = bf16[512,2048]{1,0:T(8,128)(2,1)S(1)} custom-call(f32[8192,128]{1,0:T(8,128)S(1)} %bitcast.13, f32[144,128]{1,0:T(8,128)S(1)} %get-tuple-element.60.when), custom_call_target="tpu_custom_call" | custom-call | flops 10000000 | bytes 4194304 | tf_op jit(solution)/shard_map/pallas_call | solution.py:582
  22.7 0.8 %shard_map.125.hot_ref = bf16[3072,512]{1,0:T(8,128)(2,1)S(1)} custom-call(f32[48,512]{1,0:T(8,128)S(1)} %get-tuple-element.61.place_ref, f32[144,128]{1,0:T(8,128)S(1)} %get-tuple-element.60.when), custom_call_target="tpu_custom_call" | custom-call | flops 10000000 | bytes 4194304 | tf_op jit(solution)/shard_map/pallas_call | solution.py:582
  23.5 1.3 %collective-permute-done.4 = f32[144,128]{1,0:T(8,128)S(1)} collective-permute-done((f32[144,128]{1,0:T(8,128)S(1)}, f32[144,128]{1,0:T(8,128)S(1)}, u32[]{:S(2)}, u32[]{:S(2)}) %collective-permute-start.4) | collective-permute-done | bytes 73760 | tf_op jit(solution)/shard_map/ppermute | solution.py:604
  24.8 1.9 %collective-permute-start.5 = (f32[144,128]{1,0:T(8,128)S(1)}, f32[144,128]{1,0:T(8,128)S(1)}, u32[]{:S(2)}, u32[]{:S(2)}) collective-permute-start(f32[144,128]{1,0:T(8,128)S(1)} %add.21.when), channel_id=1, source_target_pairs={{0,4},{1,5},{2,6},{3,7},{4,0},{5,1},{6,2},{7,3},{8,12},{9,13},{10,... | collective-permute-start | bytes 221192 | tf_op jit(solution)/shard_map/ppermute | solution.py:604
  26.7 0.7 %shard_map.127.own_basis_two.basis_two = bf16[512,2048]{1,0:T(8,128)(2,1)S(1)} custom-call(f32[8192,128]{1,0:T(8,128)S(1)} %bitcast.14, f32[144,128]{1,0:T(8,128)S(1)} %add.21.when), custom_call_target="tpu_custom_call" | custom-call | flops 10000000 | bytes 4194304 | tf_op jit(solution)/shard_map/pallas_call | solution.py:582
  27.4 1.8 %collective-permute-done.5 = f32[144,128]{1,0:T(8,128)S(1)} collective-permute-done((f32[144,128]{1,0:T(8,128)S(1)}, f32[144,128]{1,0:T(8,128)S(1)}, u32[]{:S(2)}, u32[]{:S(2)}) %collective-permute-start.5) | collective-permute-done | bytes 73760 | tf_op jit(solution)/shard_map/ppermute | solution.py:604
  29.2 2.9 %collective-permute-start.6 = (f32[144,128]{1,0:T(8,128)S(1)}, f32[144,128]{1,0:T(8,128)S(1)}, u32[]{:S(2)}, u32[]{:S(2)}) collective-permute-start(f32[144,128]{1,0:T(8,128)S(1)} %add.22.when), channel_id=1, source_target_pairs={{0,8},{1,9},{2,10},{3,11},{4,12},{5,13},{6,14},{7,15},{8,0},{9,1},... | collective-permute-start | bytes 221192 | tf_op jit(solution)/shard_map/ppermute | solution.py:604
  32.1 0.7 %shard_map.129.other_basis_two = bf16[512,2048]{1,0:T(8,128)(2,1)S(1)} custom-call(f32[8192,128]{1,0:T(8,128)S(1)} %collective-permute-done.7.basis, f32[144,128]{1,0:T(8,128)S(1)} %add.22.when), custom_call_target="tpu_custom_call" | custom-call | flops 10000000 | bytes 4194304 | tf_op jit(solution)/shard_map/pallas_call | solution.py:582
  32.8 0.7 %shard_map.128.other_basis = bf16[512,2048]{1,0:T(8,128)(2,1)S(1)} custom-call(f32[8192,128]{1,0:T(8,128)S(1)} %collective-permute-done.7.basis, f32[144,128]{1,0:T(8,128)S(1)} %add.22.when), custom_call_target="tpu_custom_call" | custom-call | flops 10000000 | bytes 4194304 | tf_op jit(solution)/shard_map/pallas_call | solution.py:582
  33.5 1.0 %collective-permute-done.6 = f32[144,128]{1,0:T(8,128)S(1)} collective-permute-done((f32[144,128]{1,0:T(8,128)S(1)}, f32[144,128]{1,0:T(8,128)S(1)}, u32[]{:S(2)}, u32[]{:S(2)}) %collective-permute-start.6) | collective-permute-done | bytes 73760 | tf_op jit(solution)/shard_map/ppermute | solution.py:604
  34.6 8.6 %shard_map.130 = (f32[1024,128]{1,0:T(8,128)S(1)}, f32[1024,128]{1,0:T(8,128)S(1)}, f32[8,64]{1,0:T(8,128)S(1)}) custom-call(s32[1]{0:T(128)} %bitcast.me, f32[144,128]{1,0:T(8,128)S(1)} %add.23.table, bf16[3072,512]{1,0:T(8,128)(2,1)S(1)} %shard_map.125.hot_ref, bf16[768,512]{1,0:T(8,128)(2,1)S(1)} %get-tuple-element.71.slot_ref, ...), custom_call_target="tpu_custom_call" | custom-call | flops 5000000000 | bytes 10485760 | tf_op jit(solution)/shard_map/pallas_call | solution.py:582
  43.2 1.3 %collective-permute-start.8 = (f32[8,64]{1,0:T(8,128)S(1)}, f32[8,64]{1,0:T(8,128)S(1)}, u32[]{:S(2)}, u32[]{:S(2)}) collective-permute-start(f32[8,64]{1,0:T(8,128)S(1)} %get-tuple-element.85), channel_id=1, source_target_pairs={{0,1},{2,3},{4,5},{6,7},{8,9},{10,11},{12,13},{14,15},{16,17},{18,... | collective-permute-start | bytes 6152 | tf_op jit(solution)/shard_map/ppermute | solution.py:763
  44.5 0.8 %collective-permute-done.8 = f32[8,64]{1,0:T(8,128)S(1)} collective-permute-done((f32[8,64]{1,0:T(8,128)S(1)}, f32[8,64]{1,0:T(8,128)S(1)}, u32[]{:S(2)}, u32[]{:S(2)}) %collective-permute-start.8) | collective-permute-done | bytes 2080 | tf_op jit(solution)/shard_map/ppermute | solution.py:763
  48.4 1.3 %collective-permute-start.14 = (f32[16,64]{1,0:T(8,128)S(1)}, f32[16,64]{1,0:T(8,128)S(1)}, u32[]{:S(2)}, u32[]{:S(2)}) collective-permute-start(f32[16,64]{1,0:T(8,128)S(1)} %add_add_fusion.found), channel_id=1, source_target_pairs={{1,0},{3,2},{5,4},{7,6},{9,8},{11,10},{13,12},{15,14},{17,16},{19,... | collective-permute-start | bytes 12296 | tf_op jit(solution)/shard_map/ppermute | solution.py:772
  49.7 14.9 %collective-permute-done.14.told = f32[16,64]{1,0:T(8,128)S(1)} collective-permute-done((f32[16,64]{1,0:T(8,128)S(1)}, f32[16,64]{1,0:T(8,128)S(1)}, u32[]{:S(2)}, u32[]{:S(2)}) %collective-permute-start.14) | collective-permute-done | bytes 4128 | tf_op jit(solution)/shard_map/ppermute | solution.py:772
  64.6 2.2 %shard_map.131 = (f32[16,4,32,128]{3,2,1,0:T(8,128)}, f32[16,64]{1,0:T(8,128)}) custom-call(s32[1]{0:T(128)} %bitcast.me, f32[1024,128]{1,0:T(8,128)S(1)} %get-tuple-element.83.image, f32[1024,128]{1,0:T(8,128)S(1)} %collective-permute-done.9.borrowed, bf16[512,2048]{1,0:T(8,128)(2,1)S(1)} %shard_map.126.own_basis.basis, ...), custom_call_target="tpu_custom_call" | custom-call | flops 200000000 | bytes 6291456 | tf_op jit(solution)/shard_map/pallas_call | solution.py:582
  (25 shorter events, 5.0 us)
Async XLA Ops:
  2.8 1.4 %collective-permute-start = (f32[152,128]{1,0:T(8,128)S(1)}, f32[152,128]{1,0:T(8,128)S(1)}, u32[]{:S(2)}, u32[]{:S(2)}) collective-permute-start(f32[152,128]{1,0:T(8,128)S(1)} %get-tuple-element.49.own), channel_id=1, source_target_pairs={{0,1},{1,0},{2,3},{3,2},{4,5},{5,4},{6,7},{7,6},{8,9},{9,8},{10,11... | collective-permute-start | bytes 233480 | tf_op jit(solution)/shard_map/ppermute | solution.py:604
  4.3 2.3 %collective-permute-start.1 = (f32[1536,128]{1,0:T(8,128)S(1)}, f32[1536,128]{1,0:T(8,128)S(1)}, u32[]{:S(2)}, u32[]{:S(2)}) collective-permute-start(f32[1536,128]{1,0:T(8,128)S(1)} %get-tuple-element.52), channel_id=1, source_target_pairs={{0,1},{1,0},{2,3},{3,2},{4,5},{5,4},{6,7},{7,6},{8,9},{9,8},{10,11... | collective-permute-start | bytes 2359304 | tf_op jit(solution)/shard_map/ppermute | solution.py:604
  4.6 5.4 %collective-permute-start.2 = (f32[304,128]{1,0:T(8,128)S(1)}, f32[304,128]{1,0:T(8,128)S(1)}, u32[]{:S(2)}, u32[]{:S(2)}) collective-permute-start(f32[304,128]{1,0:T(8,128)S(1)} %pad_maximum_fusion), channel_id=1, source_target_pairs={{1,2},{2,1},{3,4},{4,3},{5,6},{6,5},{7,8},{8,7},{9,10},{10,9},{11,... | collective-permute-start | bytes 466952 | tf_op jit(solution)/shard_map/ppermute | solution.py:662
  10.1 3.9 %collective-permute-start.3 = (f32[304,128]{1,0:T(8,128)S(1)}, f32[304,128]{1,0:T(8,128)S(1)}, u32[]{:S(2)}, u32[]{:S(2)}) collective-permute-start(f32[304,128]{1,0:T(8,128)S(1)} %collective-permute-done.2.passed), channel_id=1, source_target_pairs={{0,1},{1,0},{2,3},{3,2},{4,5},{5,4},{6,7},{7,6},{8,9},{9,8},{10,11... | collective-permute-start | bytes 466952 | tf_op jit(solution)/shard_map/ppermute | solution.py:604
  14.0 18.1 %collective-permute-start.7 = (f32[8192,128]{1,0:T(8,128)}, f32[8192,128]{1,0:T(8,128)S(1)}, u32[]{:S(2)}, u32[]{:S(2)}) collective-permute-start(f32[8192,128]{1,0:T(8,128)} %bitcast.12), channel_id=1, source_target_pairs={{0,1},{1,0},{2,3},{3,2},{4,5},{5,4},{6,7},{7,6},{8,9},{9,8},{10,11... | collective-permute-start | bytes 12582920 | tf_op jit(solution)/shard_map/ppermute | solution.py:604
  14.3 7.7 %copy-start = (f32[64,4,32,128]{3,2,1,0:T(8,128)S(1)}, f32[64,4,32,128]{3,2,1,0:T(8,128)}, u32[]{:S(2)}) copy-start(f32[64,4,32,128]{3,2,1,0:T(8,128)} %param.15) | copy-start | bytes 12582916
  19.2 5.6 %collective-permute-start.4 = (f32[144,128]{1,0:T(8,128)S(1)}, f32[144,128]{1,0:T(8,128)S(1)}, u32[]{:S(2)}, u32[]{:S(2)}) collective-permute-start(f32[144,128]{1,0:T(8,128)S(1)} %get-tuple-element.60.when), channel_id=1, source_target_pairs={{0,2},{1,3},{2,0},{3,1},{4,6},{5,7},{6,4},{7,5},{8,10},{9,11},{10,... | collective-permute-start | bytes 221192 | tf_op jit(solution)/shard_map/ppermute | solution.py:604
  24.8 4.4 %collective-permute-start.5 = (f32[144,128]{1,0:T(8,128)S(1)}, f32[144,128]{1,0:T(8,128)S(1)}, u32[]{:S(2)}, u32[]{:S(2)}) collective-permute-start(f32[144,128]{1,0:T(8,128)S(1)} %add.21.when), channel_id=1, source_target_pairs={{0,4},{1,5},{2,6},{3,7},{4,0},{5,1},{6,2},{7,3},{8,12},{9,13},{10,... | collective-permute-start | bytes 221192 | tf_op jit(solution)/shard_map/ppermute | solution.py:604
  29.2 5.3 %collective-permute-start.6 = (f32[144,128]{1,0:T(8,128)S(1)}, f32[144,128]{1,0:T(8,128)S(1)}, u32[]{:S(2)}, u32[]{:S(2)}) collective-permute-start(f32[144,128]{1,0:T(8,128)S(1)} %add.22.when), channel_id=1, source_target_pairs={{0,8},{1,9},{2,10},{3,11},{4,12},{5,13},{6,14},{7,15},{8,0},{9,1},... | collective-permute-start | bytes 221192 | tf_op jit(solution)/shard_map/ppermute | solution.py:604
  43.2 2.1 %collective-permute-start.8 = (f32[8,64]{1,0:T(8,128)S(1)}, f32[8,64]{1,0:T(8,128)S(1)}, u32[]{:S(2)}, u32[]{:S(2)}) collective-permute-start(f32[8,64]{1,0:T(8,128)S(1)} %get-tuple-element.85), channel_id=1, source_target_pairs={{0,1},{2,3},{4,5},{6,7},{8,9},{10,11},{12,13},{14,15},{16,17},{18,... | collective-permute-start | bytes 6152 | tf_op jit(solution)/shard_map/ppermute | solution.py:763
  45.3 19.3 %collective-permute-start.9 = (f32[1024,128]{1,0:T(8,128)S(1)}, f32[1024,128]{1,0:T(8,128)S(1)}, u32[]{:S(2)}, u32[]{:S(2)}) collective-permute-start(f32[1024,128]{1,0:T(8,128)S(1)} %get-tuple-element.86), channel_id=1, source_target_pairs={{0,1},{1,0},{2,3},{3,2},{4,5},{5,4},{6,7},{7,6},{8,9},{9,8},{10,11... | collective-permute-start | bytes 1572872 | tf_op jit(solution)/shard_map/ppermute | solution.py:604
  45.6 0.7 collective-permute-start.10
  46.3 2.0 %collective-permute-start.11 = (f32[16,64]{1,0:T(8,128)S(1)}, f32[16,64]{1,0:T(8,128)S(1)}, u32[]{:S(2)}, u32[]{:S(2)}) collective-permute-start(f32[16,64]{1,0:T(8,128)S(1)} %add.24), channel_id=1, source_target_pairs={{1,13},{3,15},{5,9},{7,11},{9,5},{11,7},{13,1},{15,3},{17,29},{19,... | collective-permute-start | bytes 12296 | tf_op jit(solution)/shard_map/ppermute | solution.py:599
  47.0 1.4 %collective-permute-start.12 = (f32[16,64]{1,0:T(8,128)S(1)}, f32[16,64]{1,0:T(8,128)S(1)}, u32[]{:S(2)}, u32[]{:S(2)}) collective-permute-start(f32[16,64]{1,0:T(8,128)S(1)} %add.24), channel_id=1, source_target_pairs={{1,9},{3,11},{5,13},{7,15},{9,1},{11,3},{13,5},{15,7},{17,25},{19,... | collective-permute-start | bytes 12296 | tf_op jit(solution)/shard_map/ppermute | solution.py:599
  47.7 0.7 %collective-permute-start.13 = (f32[16,64]{1,0:T(8,128)S(1)}, f32[16,64]{1,0:T(8,128)S(1)}, u32[]{:S(2)}, u32[]{:S(2)}) collective-permute-start(f32[16,64]{1,0:T(8,128)S(1)} %add.24), channel_id=1, source_target_pairs={{1,5},{3,7},{5,1},{7,3},{9,13},{11,15},{13,9},{15,11},{17,21},{19,... | collective-permute-start | bytes 12296 | tf_op jit(solution)/shard_map/ppermute | solution.py:599
  48.4 16.2 %collective-permute-start.14 = (f32[16,64]{1,0:T(8,128)S(1)}, f32[16,64]{1,0:T(8,128)S(1)}, u32[]{:S(2)}, u32[]{:S(2)}) collective-permute-start(f32[16,64]{1,0:T(8,128)S(1)} %add_add_fusion.found), channel_id=1, source_target_pairs={{1,0},{3,2},{5,4},{7,6},{9,8},{11,10},{13,12},{15,14},{17,16},{19,... | collective-permute-start | bytes 12296 | tf_op jit(solution)/shard_map/ppermute | solution.py:772

commit v13 on v12

--- a/solution.py
+++ b/solution.py
@@ -225,7 +225,7 @@
 def forward_window(
     fields, peers, me, first, second, third, own, partner, passed, across, band_ref,
     table, place_ref, slot_ref, speed_ref, line_ref, owner_ref, weight_ref,
-    cell_ref, below, above, z_term, total_ref, *samples,
+    cell_ref, wide_ref, below, above, z_term, total_ref, *samples,
 ):
     entries = line_ref.shape[1]
     cells = LAYERS * 32
@@ -236,8 +236,8 @@
     clear_margins(above, LAYERS, fields)
     total_ref[...] = jnp.zeros_like(total_ref)
     mine, theirs = own[...], partner[...]
-    low = jnp.where(odd, across[...], passed[...])
-    high = jnp.where(odd, passed[...], across[...])
+    low = jnp.where(me[0] < 2, 0.0, jnp.where(odd, across[...], passed[...]))
+    high = jnp.where(me[0] >= peers - 2, 0.0, jnp.where(odd, passed[...], across[...]))
     tiles = (
         low[length:, :],
         low[0:length, :],
@@ -259,8 +259,9 @@
         hot = jnp.where(slot_place == slot, 1.0, 0.0)
         slot_ref[tile * HALF : (tile + 1) * HALF, :] = hot.astype(BF16)
         rows = slice(tile * fields, (tile + 1) * fields)
-        line_ref[rows, :] = jnp.broadcast_to(lax.shift_right_logical(cell, 9), (fields, entries))
-        place_ref[rows, :] = jnp.broadcast_to(jnp.bitwise_and(cell, PLACES - 1), (fields, entries)).astype(F32)
+        line_ref[rows, :] = jnp.broadcast_to(lax.shift_right_logical(cell, 8), (fields, entries))
+        wide_ref[rows, :] = jnp.broadcast_to(lax.shift_right_logical(cell, 9), (fields, entries))
+        place_ref[rows, :] = jnp.broadcast_to(jnp.bitwise_and(cell, 255), (fields, entries)).astype(F32)
         owner_ref[rows, :] = jnp.broadcast_to(owner, (fields, entries))
         weight_ref[rows, :] = jnp.broadcast_to(weight, (fields, entries))
 
@@ -334,7 +335,7 @@
             picked = jnp.dot(jnp.concatenate(split(sample[...]), axis=0), hot, preferred_element_type=F32)
             picked = picked[: 16 * fields, :] + picked[16 * fields :, :]
             rows = slice(tile * fields, (tile + 1) * fields)
-            line = line_ref[rows, :]
+            line = wide_ref[rows, :]
             total = total_ref[rows, :]
             for i in range(16):
                 chosen = line == i // 4 * 8 + chunk * 4 + i % 4
@@ -393,7 +394,7 @@
     for tile in range(TILES):
         row = place_ref[tile * fields : tile * fields + 1, :]
         column = jnp.transpose(jnp.broadcast_to(row, (HALF, entries))).astype(jnp.int32)
-        for part in range(PLACES // HALF):
+        for part in range(2):
             hot = jnp.where(column == lane + part * HALF, 1.0, 0.0).astype(BF16)
             hot_ref[tile * entries : (tile + 1) * entries, part * HALF : (part + 1) * HALF] = hot
 
@@ -434,7 +435,7 @@
         left = lefts[tile]
         rows = slice(tile * fields, (tile + 1) * fields)
         line, high, low = line_ref[rows, :], high_ref[rows, :], low_ref[rows, :]
-        for i in range(0, 32, 2):
+        for i in range(0, 64, 2):
             chosen = [line == i, line == i + 1]
             row = slice(i * fields, (i + 2) * fields)
             for part, side in ((high, slice(0, entries)), (low, slice(entries, 2 * entries))):
@@ -444,9 +445,9 @@
         return jnp.dot(left[...], jnp.concatenate([hot, hot], axis=0), preferred_element_type=F32)
 
     def inject(tile, value):
-        for i in range(32):
-            for step in range(4):
-                layer, y = tile * LAYERS + i // 8, i % 8 * 4 + step
+        for i in range(64):
+            for step in range(2):
+                layer, y = tile * LAYERS + i // 16, i % 16 * 2 + step
                 now = value[i * fields : (i + 1) * fields, step * HALF : (step + 1) * HALF]
                 if 1 <= tile <= 4:
                     row = ((layer - LAYERS) * 32 + y) * fields
@@ -534,15 +535,17 @@
     lent[...] = image[at((1 - mine) * LAYERS * flat, LAYERS * flat), :]
 
 
-def remainder(fields, me, image, borrowed, basis, basis_two, found, told, out, coeffs, natural, sem):
+def remainder(fields, me, image, borrowed, basis, basis_two, *rest):
+    *shares, out, coeffs, natural, sem = rest
     rank = coeffs.shape[1]
     half = fields // 2
     mine = me[0] % 2
-    total = jnp.where(mine == 1, found[...], told[...])
-    coeffs[half:, :] = total[:half, :]
-    coeffs[:half, :] = total[half:, :]
-    ordered = jnp.where(mine == 1, total, jnp.concatenate([total[half:, :], total[:half, :]], axis=0))
-    parts = jnp.concatenate(split(ordered), axis=0)
+    while len(shares) > 1:
+        shares = [shares[i][...] + shares[i + 1][...] for i in range(0, len(shares), 2)]
+    total = shares[0][...]
+    coeffs[at(mine * half, half), :] = total[:half, :]
+    coeffs[at((1 - mine) * half, half), :] = total[half:, :]
+    parts = jnp.concatenate(split(total), axis=0)
     whole = natural.reshape(out.shape)
     first, second = (window(natural, side * half * HALF, half * HALF) for side in (mine, 1 - mine))
 
@@ -592,11 +595,6 @@
 
 def struct(*shape, dtype=F32):
     return jax.ShapeDtypeStruct(shape, dtype)
-
-
-def odd_swapped(array, axis, bits):
-    count = lax.axis_size(axis)
-    return lax.ppermute(array, axis, [(i, i ^ bits) for i in range(1, count, 2)])
 
 
 def swapped(array, axis, bits):
@@ -662,7 +660,7 @@
     passed = lax.ppermute(
         jnp.concatenate([own, partner], axis=0),
         "space",
-        [pair for i in range(1, peers - 1, 2) for pair in ((i, i + 1), (i + 1, i))],
+        [pair for i in range(1, peers - 1, 2) for pair in ((i, i + 1), (i + 1, i))] + [(0, 0), (peers - 1, peers - 1)],
     )
 
     turned, first, second, third, push, damping = call(
@@ -699,6 +697,7 @@
         ],
         [
             pltpu.VMEM((TILES * PLACES, entries), BF16),
+            pltpu.VMEM((TILES * fields, entries), jnp.int32),
             pltpu.VMEM((LAYERS * slab, HALF), F32),
             pltpu.VMEM((LAYERS * slab, HALF), F32),
             pltpu.VMEM((PAIR * flat, HALF), F32),
@@ -728,7 +727,7 @@
             (turned_hot,) = call(
                 functools.partial(turn_places, fields),
                 (place, table),
-                [struct(TILES * entries, PLACES, dtype=BF16)],
+                [struct(TILES * entries, 256, dtype=BF16)],
                 [],
                 10_000_000,
                 4 * 2**20,
@@ -752,27 +751,24 @@
             pltpu.VMEM((PAIR * flat, HALF), F32),
             pltpu.VMEM((peers * fields, HALF), F32),
         ]
-        + [pltpu.VMEM((32 * fields, 2 * entries), BF16)] * TILES
+        + [pltpu.VMEM((64 * fields, 2 * entries), BF16)] * TILES
         + [pltpu.VMEM((2 * PAIR * fields, 2048), BF16)],
         5_000_000_000,
         10 * 2**20,
         scalars=1,
         room=30,
     )
-    even = [(i, i + 1) for i in range(0, peers, 2)]
-    coeffs = jnp.concatenate([coeffs, lax.ppermute(coeffs, "space", even)], axis=0)
+    coeffs = jnp.concatenate([coeffs, swapped(coeffs, "space", 1)], axis=0)
     lent, coeffs = lax.optimization_barrier((lent, coeffs))
     borrowed = swapped(lent, "space", 1)
     bits = 2
     while bits * 4 < peers:
-        coeffs = coeffs + odd_swapped(coeffs, "space", bits)
+        coeffs = coeffs + swapped(coeffs, "space", bits)
         bits *= 2
-    shares = [odd_swapped(coeffs, "space", bits * i) for i in (3, 2, 1)] + [coeffs]
-    coeffs = (shares[0] + shares[1]) + (shares[2] + shares[3])
-    told = lax.ppermute(coeffs, "space", [(j, i) for i, j in even])
+    shares = [swapped(coeffs, "space", bits * i) for i in (3, 2, 1)] + [coeffs]
     hess_probe, coeffs = call(
         functools.partial(remainder, 2 * fields),
-        (me, kept, borrowed, *columns[:2], coeffs, told),
+        (me, kept, borrowed, *columns[:2], *shares),
         [struct(*probes.shape), struct(2 * fields, rank)],
         [pltpu.VMEM((2 * fields * cells, HALF), F32), pltpu.SemaphoreType.DMA((LAYERS,))],
         200_000_000,

time: 67 us -> 59.6 us (0.89)
  waiting for transfers between devices: 23.1 us -> 14.7 us
  starting transfers between devices: 17.9 us -> 19.4 us
    ppermute x6 -> x0, waiting for transfers between devices: 15.7 us -> none  [the longest x1 14.9 us: local(): told = lax.ppermute(coeffs, 'space', [(j, i) for i, j in even])]
    ppermute x8 -> x13, waiting for transfers between devices: 7.38 us -> 14.7 us  [swapped(): return lax.ppermute(array, axis, [(i, i ^ bits) for i in range(count)])]
    ppermute x8 -> x13, starting transfers between devices: 12 us -> 18.8 us  [swapped(): return lax.ppermute(array, axis, [(i, i ^ bits) for i in range(count)])]
    ppermute x6 -> x0, starting transfers between devices: 5.22 us -> none  [the longest x4 2.63 us: odd_swapped(): lax.ppermute(array, axis, [(i, i ^ bits) for i in range(1, count, 2)])]
  transfers between devices with their start and end apart: 15 -> 14, of which waited for: 8 -> 10; matrix products, arithmetic and copies ran while one was open for 0% -> 0% of each run, Pallas kernels for 18% -> 19%
where the time goes in v13:
time: 59.6 us; the launch traced here: 59.5 us
  Pallas kernels  23.9 us (40%)
  starting transfers between devices  19.4 us (33%)
  waiting for transfers between devices  14.7 us (25%)
  between operations  1.38 us (2%)
    pallas_call x10, Pallas kernels, call(): pl.pallas_call(kernel, out_shape=out_shape, in_specs=[smem] * scalars + [...  23.9 us
    ppermute x13, starting transfers between devices, swapped(): return lax.ppermute(array, axis, [(i, i ^ bits) for i in range(count)])  18.8 us
    ppermute x13, waiting for transfers between devices, swapped(): return lax.ppermute(array, axis, [(i, i ^ bits) for i in range(count)])  14.7 us
  transfers between devices with their start and end apart: 14, of which 10 were waited for; matrix products, arithmetic and copies ran while one was open for 0% of the time, Pallas kernels for 19%

profile of v13, /device:TPU:0, one launch (start us, length us, event | category | flops | bytes accessed | tf_op | source)
XLA Modules:
  0.0 59.5 jit_solution(12570389170811056709)
XLA Ops:
  1.3 1.6 %shard_map.122 = (f32[152,128]{1,0:T(8,128)S(1)}, f32[1024,128]{1,0:T(8,128)S(1)}, f32[384,128]{1,0:T(8,128)S(1)}, f32[128,128]{1,0:T(8,128)S(1)}, f32[1536,128]...) custom-call(s32[1]{0:T(128)S(6)} %copy.13.count, s32[1]{0:T(128)} %bitcast.me, f32[2048,128]{1,0:T(8,128)} %bitcast.15, ...), custom_call_target="tpu_custom_call" | custom-call | flops 100000 | bytes 2097152 | tf_op jit(solution)/shard_map/pallas_call | solution.py:585
  3.4 0.9 %collective-permute-done.partner = f32[152,128]{1,0:T(8,128)S(1)} collective-permute-done((f32[152,128]{1,0:T(8,128)S(1)}, f32[152,128]{1,0:T(8,128)S(1)}, u32[]{:S(2)}, u32[]{:S(2)}) %collective-permute-start) | collective-permute-done | bytes 77856 | tf_op jit(solution)/shard_map/ppermute | solution.py:602
  5.3 1.2 %collective-permute-done.1.borrowed = f32[1536,128]{1,0:T(8,128)S(1)} collective-permute-done((f32[1536,128]{1,0:T(8,128)S(1)}, f32[1536,128]{1,0:T(8,128)S(1)}, u32[]{:S(2)}, u32[]{:S(2)}) %collective-permute-start.1) | collective-permute-done | bytes 786464 | tf_op jit(solution)/shard_map/ppermute | solution.py:602
  6.6 3.5 %shard_map.123 = (f32[2048,128]{1,0:T(8,128)S(1)}, f32[2560,128]{1,0:T(8,128)S(1)}, f32[2560,128]{1,0:T(8,128)S(1)}, f32[2048,128]{1,0:T(8,128)S(1)}, f32[768,128]{1,0:T(8,128)S(1)}, /*index=5*/f32[256,128]{1,0:T(8,128)S(1)}) custom-call(s32[1]{0:T(128)} %bitcast.me, f32[1024,128]{1,0:T(8,128)S(1)} %get-tuple-element.46.probes, ...), custom_call_target="tpu_custom_call" | custom-call | flops 600000000 | bytes 6291456 | tf_op jit(solution)/shard_map/pallas_call | solution.py:585
  10.1 2.9 %collective-permute-start.3 = (f32[304,128]{1,0:T(8,128)S(1)}, f32[304,128]{1,0:T(8,128)S(1)}, u32[]{:S(2)}, u32[]{:S(2)}) collective-permute-start(f32[304,128]{1,0:T(8,128)S(1)} %collective-permute-done.2.passed), channel_id=1, source_target_pairs={{0,1},{1,0},{2,3},{3,2},{4,5},{5,4},{6,7},{7,6},{8,9},{9,8},{10,11... | collective-permute-start | bytes 466952 | tf_op jit(solution)/shard_map/ppermute | solution.py:602
  12.9 1.0 %collective-permute-done.3.across = f32[304,128]{1,0:T(8,128)S(1)} collective-permute-done((f32[304,128]{1,0:T(8,128)S(1)}, f32[304,128]{1,0:T(8,128)S(1)}, u32[]{:S(2)}, u32[]{:S(2)}) %collective-permute-start.3) | collective-permute-done | bytes 155680 | tf_op jit(solution)/shard_map/ppermute | solution.py:602
  14.3 4.9 %shard_map.124 = (f32[144,128]{1,0:T(8,128)S(1)}, f32[48,512]{1,0:T(8,128)S(1)}, bf16[768,512]{1,0:T(8,128)(2,1)S(1)}, f32[768,128]{1,0:T(8,128)S(1)}, s32[48,51...) custom-call(s32[1]{0:T(128)} %bitcast.me, f32[2560,128]{1,0:T(8,128)S(1)} %get-tuple-element.54.first, ...), custom_call_target="tpu_custom_call" | custom-call | flops 3000000000 | bytes 6291456 | tf_op jit(solution)/shard_map/pallas_call | solution.py:585
  19.2 2.8 %collective-permute-start.4 = (f32[144,128]{1,0:T(8,128)S(1)}, f32[144,128]{1,0:T(8,128)S(1)}, u32[]{:S(2)}, u32[]{:S(2)}) collective-permute-start(f32[144,128]{1,0:T(8,128)S(1)} %get-tuple-element.60.when), channel_id=1, source_target_pairs={{0,2},{1,3},{2,0},{3,1},{4,6},{5,7},{6,4},{7,5},{8,10},{9,11},{10,... | collective-permute-start | bytes 221192 | tf_op jit(solution)/shard_map/ppermute | solution.py:602
  22.0 0.7 %shard_map.126.own_basis.basis = bf16[512,2048]{1,0:T(8,128)(2,1)S(1)} custom-call(f32[8192,128]{1,0:T(8,128)S(1)} %bitcast.13, f32[144,128]{1,0:T(8,128)S(1)} %get-tuple-element.60.when), custom_call_target="tpu_custom_call" | custom-call | flops 10000000 | bytes 4194304 | tf_op jit(solution)/shard_map/pallas_call | solution.py:585
  23.2 1.6 %collective-permute-done.4 = f32[144,128]{1,0:T(8,128)S(1)} collective-permute-done((f32[144,128]{1,0:T(8,128)S(1)}, f32[144,128]{1,0:T(8,128)S(1)}, u32[]{:S(2)}, u32[]{:S(2)}) %collective-permute-start.4) | collective-permute-done | bytes 73760 | tf_op jit(solution)/shard_map/ppermute | solution.py:602
  24.8 1.9 %collective-permute-start.5 = (f32[144,128]{1,0:T(8,128)S(1)}, f32[144,128]{1,0:T(8,128)S(1)}, u32[]{:S(2)}, u32[]{:S(2)}) collective-permute-start(f32[144,128]{1,0:T(8,128)S(1)} %add.12.when), channel_id=1, source_target_pairs={{0,4},{1,5},{2,6},{3,7},{4,0},{5,1},{6,2},{7,3},{8,12},{9,13},{10,... | collective-permute-start | bytes 221192 | tf_op jit(solution)/shard_map/ppermute | solution.py:602
  26.7 0.7 %shard_map.127.own_basis_two.basis_two = bf16[512,2048]{1,0:T(8,128)(2,1)S(1)} custom-call(f32[8192,128]{1,0:T(8,128)S(1)} %bitcast.14, f32[144,128]{1,0:T(8,128)S(1)} %add.12.when), custom_call_target="tpu_custom_call" | custom-call | flops 10000000 | bytes 4194304 | tf_op jit(solution)/shard_map/pallas_call | solution.py:585
  27.4 1.9 %collective-permute-done.5 = f32[144,128]{1,0:T(8,128)S(1)} collective-permute-done((f32[144,128]{1,0:T(8,128)S(1)}, f32[144,128]{1,0:T(8,128)S(1)}, u32[]{:S(2)}, u32[]{:S(2)}) %collective-permute-start.5) | collective-permute-done | bytes 73760 | tf_op jit(solution)/shard_map/ppermute | solution.py:602
  29.3 2.9 %collective-permute-start.6 = (f32[144,128]{1,0:T(8,128)S(1)}, f32[144,128]{1,0:T(8,128)S(1)}, u32[]{:S(2)}, u32[]{:S(2)}) collective-permute-start(f32[144,128]{1,0:T(8,128)S(1)} %add.13.when), channel_id=1, source_target_pairs={{0,8},{1,9},{2,10},{3,11},{4,12},{5,13},{6,14},{7,15},{8,0},{9,1},... | collective-permute-start | bytes 221192 | tf_op jit(solution)/shard_map/ppermute | solution.py:602
  32.9 0.7 %shard_map.128.other_basis = bf16[512,2048]{1,0:T(8,128)(2,1)S(1)} custom-call(f32[8192,128]{1,0:T(8,128)S(1)} %collective-permute-done.7.basis, f32[144,128]{1,0:T(8,128)S(1)} %add.13.when), custom_call_target="tpu_custom_call" | custom-call | flops 10000000 | bytes 4194304 | tf_op jit(solution)/shard_map/pallas_call | solution.py:585
  33.5 1.0 %collective-permute-done.6 = f32[144,128]{1,0:T(8,128)S(1)} collective-permute-done((f32[144,128]{1,0:T(8,128)S(1)}, f32[144,128]{1,0:T(8,128)S(1)}, u32[]{:S(2)}, u32[]{:S(2)}) %collective-permute-start.6) | collective-permute-done | bytes 73760 | tf_op jit(solution)/shard_map/ppermute | solution.py:602
  34.6 8.6 %shard_map.130 = (f32[1024,128]{1,0:T(8,128)S(1)}, f32[1024,128]{1,0:T(8,128)S(1)}, f32[8,64]{1,0:T(8,128)S(1)}) custom-call(s32[1]{0:T(128)} %bitcast.me, f32[144,128]{1,0:T(8,128)S(1)} %add.14.table, bf16[3072,256]{1,0:T(8,128)(2,1)S(1)} %shard_map.125.hot_ref, bf16[768,512]{1,0:T(8,128)(2,1)S(1)} %get-tuple-element.71.slot_ref, ...), custom_call_target="tpu_custom_call" | custom-call | flops 5000000000 | bytes 10485760 | tf_op jit(solution)/shard_map/pallas_call | solution.py:585
  43.2 1.2 %collective-permute-done.8 = f32[8,64]{1,0:T(8,128)S(1)} collective-permute-done((f32[8,64]{1,0:T(8,128)S(1)}, f32[8,64]{1,0:T(8,128)S(1)}, u32[]{:S(2)}, u32[]{:S(2)}) %collective-permute-start.8) | collective-permute-done | bytes 2080 | tf_op jit(solution)/shard_map/ppermute | solution.py:602
  44.6 1.7 %collective-permute-start.10 = (f32[16,64]{1,0:T(8,128)S(1)}, f32[16,64]{1,0:T(8,128)S(1)}, u32[]{:S(2)}, u32[]{:S(2)}) collective-permute-start(f32[16,64]{1,0:T(8,128)S(1)} %pad_maximum_fusion.1), channel_id=1, source_target_pairs={{0,2},{1,3},{2,0},{3,1},{4,6},{5,7},{6,4},{7,5},{8,10},{9,11},{10,... | collective-permute-start | bytes 12296 | tf_op jit(solution)/shard_map/ppermute | solution.py:602
  46.3 1.9 %collective-permute-done.10 = f32[16,64]{1,0:T(8,128)S(1)} collective-permute-done((f32[16,64]{1,0:T(8,128)S(1)}, f32[16,64]{1,0:T(8,128)S(1)}, u32[]{:S(2)}, u32[]{:S(2)}) %collective-permute-start.10) | collective-permute-done | bytes 4128 | tf_op jit(solution)/shard_map/ppermute | solution.py:602
  48.2 4.5 %collective-permute-start.11 = (f32[16,64]{1,0:T(8,128)S(1)}, f32[16,64]{1,0:T(8,128)S(1)}, u32[]{:S(2)}, u32[]{:S(2)}) collective-permute-start(f32[16,64]{1,0:T(8,128)S(1)} %add.15.rest_3_), channel_id=1, source_target_pairs={{0,12},{1,13},{2,14},{3,15},{4,8},{5,9},{6,10},{7,11},{8,4},{9,5},... | collective-permute-start | bytes 12296 | tf_op jit(solution)/shard_map/ppermute | solution.py:602
  53.3 1.1 %collective-permute-done.11.rest_0_ = f32[16,64]{1,0:T(8,128)S(1)} collective-permute-done((f32[16,64]{1,0:T(8,128)S(1)}, f32[16,64]{1,0:T(8,128)S(1)}, u32[]{:S(2)}, u32[]{:S(2)}) %collective-permute-start.11) | collective-permute-done | bytes 4128 | tf_op jit(solution)/shard_map/ppermute | solution.py:602
  54.4 2.9 %collective-permute-done.12.rest_1_ = f32[16,64]{1,0:T(8,128)S(1)} collective-permute-done((f32[16,64]{1,0:T(8,128)S(1)}, f32[16,64]{1,0:T(8,128)S(1)}, u32[]{:S(2)}, u32[]{:S(2)}) %collective-permute-start.12) | collective-permute-done | bytes 4128 | tf_op jit(solution)/shard_map/ppermute | solution.py:602
  57.3 2.2 %shard_map.131 = (f32[16,4,32,128]{3,2,1,0:T(8,128)}, f32[16,64]{1,0:T(8,128)}) custom-call(s32[1]{0:T(128)} %bitcast.me, f32[1024,128]{1,0:T(8,128)S(1)} %get-tuple-element.83.image, f32[1024,128]{1,0:T(8,128)S(1)} %collective-permute-done.9.borrowed, bf16[512,2048]{1,0:T(8,128)(2,1)S(1)} %shard_map.126.own_basis.basis, ...), custom_call_target="tpu_custom_call" | custom-call | flops 200000000 | bytes 6291456 | tf_op jit(solution)/shard_map/pallas_call | solution.py:585
  (22 shorter events, 3.9 us)
Async XLA Ops:
  2.8 1.4 %collective-permute-start = (f32[152,128]{1,0:T(8,128)S(1)}, f32[152,128]{1,0:T(8,128)S(1)}, u32[]{:S(2)}, u32[]{:S(2)}) collective-permute-start(f32[152,128]{1,0:T(8,128)S(1)} %get-tuple-element.49.own), channel_id=1, source_target_pairs={{0,1},{1,0},{2,3},{3,2},{4,5},{5,4},{6,7},{7,6},{8,9},{9,8},{10,11... | collective-permute-start | bytes 233480 | tf_op jit(solution)/shard_map/ppermute | solution.py:602
  4.3 2.3 %collective-permute-start.1 = (f32[1536,128]{1,0:T(8,128)S(1)}, f32[1536,128]{1,0:T(8,128)S(1)}, u32[]{:S(2)}, u32[]{:S(2)}) collective-permute-start(f32[1536,128]{1,0:T(8,128)S(1)} %get-tuple-element.52), channel_id=1, source_target_pairs={{0,1},{1,0},{2,3},{3,2},{4,5},{5,4},{6,7},{7,6},{8,9},{9,8},{10,11... | collective-permute-start | bytes 2359304 | tf_op jit(solution)/shard_map/ppermute | solution.py:602
  4.6 5.4 %collective-permute-start.2 = (f32[304,128]{1,0:T(8,128)S(1)}, f32[304,128]{1,0:T(8,128)S(1)}, u32[]{:S(2)}, u32[]{:S(2)}) collective-permute-start(f32[304,128]{1,0:T(8,128)S(1)} %pad_maximum_fusion), channel_id=1, source_target_pairs={{1,2},{2,1},{3,4},{4,3},{5,6},{6,5},{7,8},{8,7},{9,10},{10,9},{11,... | collective-permute-start | bytes 466952 | tf_op jit(solution)/shard_map/ppermute | solution.py:660
  10.1 3.9 %collective-permute-start.3 = (f32[304,128]{1,0:T(8,128)S(1)}, f32[304,128]{1,0:T(8,128)S(1)}, u32[]{:S(2)}, u32[]{:S(2)}) collective-permute-start(f32[304,128]{1,0:T(8,128)S(1)} %collective-permute-done.2.passed), channel_id=1, source_target_pairs={{0,1},{1,0},{2,3},{3,2},{4,5},{5,4},{6,7},{7,6},{8,9},{9,8},{10,11... | collective-permute-start | bytes 466952 | tf_op jit(solution)/shard_map/ppermute | solution.py:602
  14.0 18.2 %collective-permute-start.7 = (f32[8192,128]{1,0:T(8,128)}, f32[8192,128]{1,0:T(8,128)S(1)}, u32[]{:S(2)}, u32[]{:S(2)}) collective-permute-start(f32[8192,128]{1,0:T(8,128)} %bitcast.12), channel_id=1, source_target_pairs={{0,1},{1,0},{2,3},{3,2},{4,5},{5,4},{6,7},{7,6},{8,9},{9,8},{10,11... | collective-permute-start | bytes 12582920 | tf_op jit(solution)/shard_map/ppermute | solution.py:602
  14.3 7.7 %copy-start = (f32[64,4,32,128]{3,2,1,0:T(8,128)S(1)}, f32[64,4,32,128]{3,2,1,0:T(8,128)}, u32[]{:S(2)}) copy-start(f32[64,4,32,128]{3,2,1,0:T(8,128)} %param.15) | copy-start | bytes 12582916
  19.2 5.6 %collective-permute-start.4 = (f32[144,128]{1,0:T(8,128)S(1)}, f32[144,128]{1,0:T(8,128)S(1)}, u32[]{:S(2)}, u32[]{:S(2)}) collective-permute-start(f32[144,128]{1,0:T(8,128)S(1)} %get-tuple-element.60.when), channel_id=1, source_target_pairs={{0,2},{1,3},{2,0},{3,1},{4,6},{5,7},{6,4},{7,5},{8,10},{9,11},{10,... | collective-permute-start | bytes 221192 | tf_op jit(solution)/shard_map/ppermute | solution.py:602
  24.8 4.4 %collective-permute-start.5 = (f32[144,128]{1,0:T(8,128)S(1)}, f32[144,128]{1,0:T(8,128)S(1)}, u32[]{:S(2)}, u32[]{:S(2)}) collective-permute-start(f32[144,128]{1,0:T(8,128)S(1)} %add.12.when), channel_id=1, source_target_pairs={{0,4},{1,5},{2,6},{3,7},{4,0},{5,1},{6,2},{7,3},{8,12},{9,13},{10,... | collective-permute-start | bytes 221192 | tf_op jit(solution)/shard_map/ppermute | solution.py:602
  29.3 5.3 %collective-permute-start.6 = (f32[144,128]{1,0:T(8,128)S(1)}, f32[144,128]{1,0:T(8,128)S(1)}, u32[]{:S(2)}, u32[]{:S(2)}) collective-permute-start(f32[144,128]{1,0:T(8,128)S(1)} %add.13.when), channel_id=1, source_target_pairs={{0,8},{1,9},{2,10},{3,11},{4,12},{5,13},{6,14},{7,15},{8,0},{9,1},... | collective-permute-start | bytes 221192 | tf_op jit(solution)/shard_map/ppermute | solution.py:602
  43.2 1.2 %collective-permute-start.8 = (f32[8,64]{1,0:T(8,128)S(1)}, f32[8,64]{1,0:T(8,128)S(1)}, u32[]{:S(2)}, u32[]{:S(2)}) collective-permute-start(f32[8,64]{1,0:T(8,128)S(1)} %get-tuple-element.85), channel_id=1, source_target_pairs={{0,1},{1,0},{2,3},{3,2},{4,5},{5,4},{6,7},{7,6},{8,9},{9,8},{10,11... | collective-permute-start | bytes 6152 | tf_op jit(solution)/shard_map/ppermute | solution.py:602
  44.4 12.9 %collective-permute-start.9 = (f32[1024,128]{1,0:T(8,128)S(1)}, f32[1024,128]{1,0:T(8,128)S(1)}, u32[]{:S(2)}, u32[]{:S(2)}) collective-permute-start(f32[1024,128]{1,0:T(8,128)S(1)} %get-tuple-element.86), channel_id=1, source_target_pairs={{0,1},{1,0},{2,3},{3,2},{4,5},{5,4},{6,7},{7,6},{8,9},{9,8},{10,11... | collective-permute-start | bytes 1572872 | tf_op jit(solution)/shard_map/ppermute | solution.py:602
  44.6 3.7 %collective-permute-start.10 = (f32[16,64]{1,0:T(8,128)S(1)}, f32[16,64]{1,0:T(8,128)S(1)}, u32[]{:S(2)}, u32[]{:S(2)}) collective-permute-start(f32[16,64]{1,0:T(8,128)S(1)} %pad_maximum_fusion.1), channel_id=1, source_target_pairs={{0,2},{1,3},{2,0},{3,1},{4,6},{5,7},{6,4},{7,5},{8,10},{9,11},{10,... | collective-permute-start | bytes 12296 | tf_op jit(solution)/shard_map/ppermute | solution.py:602
  48.2 6.2 %collective-permute-start.11 = (f32[16,64]{1,0:T(8,128)S(1)}, f32[16,64]{1,0:T(8,128)S(1)}, u32[]{:S(2)}, u32[]{:S(2)}) collective-permute-start(f32[16,64]{1,0:T(8,128)S(1)} %add.15.rest_3_), channel_id=1, source_target_pairs={{0,12},{1,13},{2,14},{3,15},{4,8},{5,9},{6,10},{7,11},{8,4},{9,5},... | collective-permute-start | bytes 12296 | tf_op jit(solution)/shard_map/ppermute | solution.py:602
  52.8 4.5 %collective-permute-start.12 = (f32[16,64]{1,0:T(8,128)S(1)}, f32[16,64]{1,0:T(8,128)S(1)}, u32[]{:S(2)}, u32[]{:S(2)}) collective-permute-start(f32[16,64]{1,0:T(8,128)S(1)} %add.15.rest_3_), channel_id=1, source_target_pairs={{0,8},{1,9},{2,10},{3,11},{4,12},{5,13},{6,14},{7,15},{8,0},{9,1},... | collective-permute-start | bytes 12296 | tf_op jit(solution)/shard_map/ppermute | solution.py:602
  52.8 4.5 %collective-permute-start.13 = (f32[16,64]{1,0:T(8,128)S(1)}, f32[16,64]{1,0:T(8,128)S(1)}, u32[]{:S(2)}, u32[]{:S(2)}) collective-permute-start(f32[16,64]{1,0:T(8,128)S(1)} %add.15.rest_3_), channel_id=1, source_target_pairs={{0,4},{1,5},{2,6},{3,7},{4,0},{5,1},{6,2},{7,3},{8,12},{9,13},{10,... | collective-permute-start | bytes 12296 | tf_op jit(solution)/shard_map/ppermute | solution.py:602

commit v14 on v13

--- a/solution.py
+++ b/solution.py
@@ -46,6 +46,13 @@
     return get
 
 
+def half_of(me):
+    value = me[0]
+    for by in (4, 2, 1):
+        value = jnp.bitwise_xor(value, lax.shift_right_logical(value, by))
+    return jnp.bitwise_and(value, 1)
+
+
 def spread(ref, row, fields):
     return jnp.broadcast_to(ref[pl.ds(row, 1), :], (fields, HALF))
 
@@ -85,7 +92,7 @@
     rows = cell.shape[0]
     cells = kappa.shape[0]
     half = probes_out.shape[0]
-    mine = me[0] % 2
+    mine = half_of(me)
     other = probes.at[pl.ds(pl.multiple_of((1 - mine) * half, 8), half)]
     small = [
         pltpu.make_async_copy(kappa, statics.at[pl.ds(0, cells)], sem.at[0]),
@@ -492,7 +499,7 @@
     along_z(inner_one, LAYERS, PAIR, fields, band_ref, z_term)
     mine = me[0] % 2
 
-    def step_two(chunk, total):
+    def step_two_chunk(chunk, which):
         skip = chunk * 8 * fields
         here = window(inner_one, skip, 2 * PAIR * slab - ahead)
         two_rows, one_rows = (window(ref, LAYERS * flat + skip, PAIR * flat - ahead) for ref in (outer_two, outer_one))
@@ -519,17 +526,23 @@
                     value = value + spread(damping, cell, fields) * there[row, :]
                     out[row, :] = value
                     high = value.astype(BF16).astype(F32)
-                    rows, lane = slice(x * 2 * fields, (x + 1) * 2 * fields), y * 256
+                    start, lane = (x * 2 + which) * 2 * fields, y * 256
+                    rows = slice(start, start + 2 * fields)
                     image_parts[rows, lane : lane + HALF] = jnp.concatenate([high, value - high], axis=0).astype(BF16)
                     image_parts[rows, lane + HALF : lane + 256] = jnp.concatenate([high, nothing], axis=0).astype(BF16)
+
+    def step_two(pair, total):
+        for which in range(2):
+            step_two_chunk(pair * 2 + which, which)
         for side, pieces in ((mine, (own_basis, own_basis_two)), (1 - mine, (other_basis, other_basis_two))):
             for x in range(LAYERS):
-                columns = pieces[x // 2][at((x % 2 * 4 + chunk) * rank, rank), :]
-                parts = image_parts[at((side * LAYERS + x) * 2 * fields, 2 * fields), :]
+                columns = pieces[x // 2][at((x % 2 * 4 + pair * 2) * rank, 2 * rank), :]
+                parts = image_parts[at((side * LAYERS + x) * 4 * fields, 4 * fields), :]
                 total = total + lax.dot_general(parts, columns, NT, preferred_element_type=F32)
         return total
 
-    total = lax.fori_loop(0, 4, step_two, jnp.zeros((2 * fields, rank), F32))
+    total = lax.fori_loop(0, 2, step_two, jnp.zeros((4 * fields, 2 * rank), F32))
+    total = total[: 2 * fields, :rank] + total[2 * fields :, rank:]
     coeffs[...] = total[:fields, :] + total[fields:, :]
     kept[...] = image[at(mine * LAYERS * flat, LAYERS * flat), :]
     lent[...] = image[at((1 - mine) * LAYERS * flat, LAYERS * flat), :]
@@ -539,7 +552,7 @@
     *shares, out, coeffs, natural, sem = rest
     rank = coeffs.shape[1]
     half = fields // 2
-    mine = me[0] % 2
+    mine = half_of(me)
     while len(shares) > 1:
         shares = [shares[i][...] + shares[i + 1][...] for i in range(0, len(shares), 2)]
     total = shares[0][...]
@@ -712,7 +725,7 @@
     columns = []
     bits = 2
     while bits < peers:
-        arrived = swapped(table, "space", bits)
+        arrived = swapped(table, "space", bits + 1)
         for i in ((0,), (1,), (2, 3))[len(columns)] if len(columns) < 3 else ():
             (some,) = call(
                 functools.partial(basis_parts, 8 * (i % 2)),
@@ -752,7 +765,7 @@
             pltpu.VMEM((peers * fields, HALF), F32),
         ]
         + [pltpu.VMEM((64 * fields, 2 * entries), BF16)] * TILES
-        + [pltpu.VMEM((2 * PAIR * fields, 2048), BF16)],
+        + [pltpu.VMEM((4 * PAIR * fields, 2048), BF16)],
         5_000_000_000,
         10 * 2**20,
         scalars=1,
@@ -762,10 +775,10 @@
     lent, coeffs = lax.optimization_barrier((lent, coeffs))
     borrowed = swapped(lent, "space", 1)
     bits = 2
-    while bits * 4 < peers:
-        coeffs = coeffs + swapped(coeffs, "space", bits)
+    while bits * 2 < peers:
+        coeffs = coeffs + swapped(coeffs, "space", bits + 1)
         bits *= 2
-    shares = [swapped(coeffs, "space", bits * i) for i in (3, 2, 1)] + [coeffs]
+    shares = [coeffs, swapped(coeffs, "space", bits + 1)]
     hess_probe, coeffs = call(
         functools.partial(remainder, 2 * fields),
         (me, kept, borrowed, *columns[:2], *shares),

time: 59.6 us -> 58.6 us (0.983)
  waiting for transfers between devices: 14.7 us -> 12.8 us
    ppermute x13 -> x12, waiting for transfers between devices: 14.7 us -> 12.8 us  [swapped(): return lax.ppermute(array, axis, [(i, i ^ bits) for i in range(count)])]
    ppermute x13 -> x12, starting transfers between devices: 18.8 us -> 19.3 us  [swapped(): return lax.ppermute(array, axis, [(i, i ^ bits) for i in range(count)])]
  transfers between devices with their start and end apart: 14 -> 13, of which waited for: 10 -> 10; matrix products, arithmetic and copies ran while one was open for 0% -> 0% of each run, Pallas kernels for 19% -> 20%
where the time goes in v14:
time: 58.6 us; the launch traced here: 58.5 us
  Pallas kernels  24.3 us (41%)
  starting transfers between devices  19.9 us (34%)
  waiting for transfers between devices  12.8 us (22%)
  between operations  1.36 us (2%)
    pallas_call x10, Pallas kernels, call(): pl.pallas_call(kernel, out_shape=out_shape, in_specs=[smem] * scalars + [...  24.3 us
    ppermute x12, starting transfers between devices, swapped(): return lax.ppermute(array, axis, [(i, i ^ bits) for i in range(count)])  19.3 us
    ppermute x12, waiting for transfers between devices, swapped(): return lax.ppermute(array, axis, [(i, i ^ bits) for i in range(count)])  12.8 us
  transfers between devices with their start and end apart: 13, of which 10 were waited for; matrix products, arithmetic and copies ran while one was open for 0% of the time, Pallas kernels for 20%

profile of v14, /device:TPU:0, one launch (start us, length us, event | category | flops | bytes accessed | tf_op | source)
XLA Modules:
  0.0 58.5 jit_solution(15993706319665977359)
XLA Ops:
  1.3 1.6 %shard_map.122 = (f32[152,128]{1,0:T(8,128)S(1)}, f32[1024,128]{1,0:T(8,128)S(1)}, f32[384,128]{1,0:T(8,128)S(1)}, f32[128,128]{1,0:T(8,128)S(1)}, f32[1536,128]...) custom-call(s32[1]{0:T(128)S(6)} %copy.13.count, s32[1]{0:T(128)} %bitcast.me, f32[2048,128]{1,0:T(8,128)} %bitcast.15, ...), custom_call_target="tpu_custom_call" | custom-call | flops 100000 | bytes 2097152 | tf_op jit(solution)/shard_map/pallas_call | solution.py:598
  3.4 0.9 %collective-permute-done.partner = f32[152,128]{1,0:T(8,128)S(1)} collective-permute-done((f32[152,128]{1,0:T(8,128)S(1)}, f32[152,128]{1,0:T(8,128)S(1)}, u32[]{:S(2)}, u32[]{:S(2)}) %collective-permute-start) | collective-permute-done | bytes 77856 | tf_op jit(solution)/shard_map/ppermute | solution.py:615
  5.3 1.2 %collective-permute-done.1.borrowed = f32[1536,128]{1,0:T(8,128)S(1)} collective-permute-done((f32[1536,128]{1,0:T(8,128)S(1)}, f32[1536,128]{1,0:T(8,128)S(1)}, u32[]{:S(2)}, u32[]{:S(2)}) %collective-permute-start.1) | collective-permute-done | bytes 786464 | tf_op jit(solution)/shard_map/ppermute | solution.py:615
  6.6 3.5 %shard_map.123 = (f32[2048,128]{1,0:T(8,128)S(1)}, f32[2560,128]{1,0:T(8,128)S(1)}, f32[2560,128]{1,0:T(8,128)S(1)}, f32[2048,128]{1,0:T(8,128)S(1)}, f32[768,128]{1,0:T(8,128)S(1)}, /*index=5*/f32[256,128]{1,0:T(8,128)S(1)}) custom-call(s32[1]{0:T(128)} %bitcast.me, f32[1024,128]{1,0:T(8,128)S(1)} %get-tuple-element.46.probes, ...), custom_call_target="tpu_custom_call" | custom-call | flops 600000000 | bytes 6291456 | tf_op jit(solution)/shard_map/pallas_call | solution.py:598
  10.1 2.9 %collective-permute-start.3 = (f32[304,128]{1,0:T(8,128)S(1)}, f32[304,128]{1,0:T(8,128)S(1)}, u32[]{:S(2)}, u32[]{:S(2)}) collective-permute-start(f32[304,128]{1,0:T(8,128)S(1)} %collective-permute-done.2.passed), channel_id=1, source_target_pairs={{0,1},{1,0},{2,3},{3,2},{4,5},{5,4},{6,7},{7,6},{8,9},{9,8},{10,11... | collective-permute-start | bytes 466952 | tf_op jit(solution)/shard_map/ppermute | solution.py:615
  12.9 1.0 %collective-permute-done.3.across = f32[304,128]{1,0:T(8,128)S(1)} collective-permute-done((f32[304,128]{1,0:T(8,128)S(1)}, f32[304,128]{1,0:T(8,128)S(1)}, u32[]{:S(2)}, u32[]{:S(2)}) %collective-permute-start.3) | collective-permute-done | bytes 155680 | tf_op jit(solution)/shard_map/ppermute | solution.py:615
  14.3 4.9 %shard_map.124 = (f32[144,128]{1,0:T(8,128)S(1)}, f32[48,512]{1,0:T(8,128)S(1)}, bf16[768,512]{1,0:T(8,128)(2,1)S(1)}, f32[768,128]{1,0:T(8,128)S(1)}, s32[48,51...) custom-call(s32[1]{0:T(128)} %bitcast.me, f32[2560,128]{1,0:T(8,128)S(1)} %get-tuple-element.54.first, ...), custom_call_target="tpu_custom_call" | custom-call | flops 3000000000 | bytes 6291456 | tf_op jit(solution)/shard_map/pallas_call | solution.py:598
  19.2 2.8 %collective-permute-start.4 = (f32[144,128]{1,0:T(8,128)S(1)}, f32[144,128]{1,0:T(8,128)S(1)}, u32[]{:S(2)}, u32[]{:S(2)}) collective-permute-start(f32[144,128]{1,0:T(8,128)S(1)} %get-tuple-element.60.when), channel_id=1, source_target_pairs={{0,3},{1,2},{2,1},{3,0},{4,7},{5,6},{6,5},{7,4},{8,11},{9,10},{10,... | collective-permute-start | bytes 221192 | tf_op jit(solution)/shard_map/ppermute | solution.py:615
  23.2 1.3 %collective-permute-done.4 = f32[144,128]{1,0:T(8,128)S(1)} collective-permute-done((f32[144,128]{1,0:T(8,128)S(1)}, f32[144,128]{1,0:T(8,128)S(1)}, u32[]{:S(2)}, u32[]{:S(2)}) %collective-permute-start.4) | collective-permute-done | bytes 73760 | tf_op jit(solution)/shard_map/ppermute | solution.py:615
  24.5 1.8 %collective-permute-start.5 = (f32[144,128]{1,0:T(8,128)S(1)}, f32[144,128]{1,0:T(8,128)S(1)}, u32[]{:S(2)}, u32[]{:S(2)}) collective-permute-start(f32[144,128]{1,0:T(8,128)S(1)} %add.15.when), channel_id=1, source_target_pairs={{0,5},{1,4},{2,7},{3,6},{4,1},{5,0},{6,3},{7,2},{8,13},{9,12},{10,... | collective-permute-start | bytes 221192 | tf_op jit(solution)/shard_map/ppermute | solution.py:615
  27.0 1.7 %collective-permute-done.5 = f32[144,128]{1,0:T(8,128)S(1)} collective-permute-done((f32[144,128]{1,0:T(8,128)S(1)}, f32[144,128]{1,0:T(8,128)S(1)}, u32[]{:S(2)}, u32[]{:S(2)}) %collective-permute-start.5) | collective-permute-done | bytes 73760 | tf_op jit(solution)/shard_map/ppermute | solution.py:615
  28.7 3.0 %collective-permute-start.6 = (f32[144,128]{1,0:T(8,128)S(1)}, f32[144,128]{1,0:T(8,128)S(1)}, u32[]{:S(2)}, u32[]{:S(2)}) collective-permute-start(f32[144,128]{1,0:T(8,128)S(1)} %add.16.when), channel_id=1, source_target_pairs={{0,9},{1,8},{2,11},{3,10},{4,13},{5,12},{6,15},{7,14},{8,1},{9,0},... | collective-permute-start | bytes 221192 | tf_op jit(solution)/shard_map/ppermute | solution.py:615
  32.4 0.7 %shard_map.128.other_basis = bf16[512,2048]{1,0:T(8,128)(2,1)S(1)} custom-call(f32[8192,128]{1,0:T(8,128)S(1)} %collective-permute-done.7.basis, f32[144,128]{1,0:T(8,128)S(1)} %add.16.when), custom_call_target="tpu_custom_call" | custom-call | flops 10000000 | bytes 4194304 | tf_op jit(solution)/shard_map/pallas_call | solution.py:598
  33.1 1.0 %collective-permute-done.6 = f32[144,128]{1,0:T(8,128)S(1)} collective-permute-done((f32[144,128]{1,0:T(8,128)S(1)}, f32[144,128]{1,0:T(8,128)S(1)}, u32[]{:S(2)}, u32[]{:S(2)}) %collective-permute-start.6) | collective-permute-done | bytes 73760 | tf_op jit(solution)/shard_map/ppermute | solution.py:615
  34.1 9.0 %shard_map.130 = (f32[1024,128]{1,0:T(8,128)S(1)}, f32[1024,128]{1,0:T(8,128)S(1)}, f32[8,64]{1,0:T(8,128)S(1)}) custom-call(s32[1]{0:T(128)} %bitcast.me, f32[144,128]{1,0:T(8,128)S(1)} %add.17.table, bf16[3072,256]{1,0:T(8,128)(2,1)S(1)} %shard_map.125.hot_ref, bf16[768,512]{1,0:T(8,128)(2,1)S(1)} %get-tuple-element.71.slot_ref, ...), custom_call_target="tpu_custom_call" | custom-call | flops 5000000000 | bytes 10485760 | tf_op jit(solution)/shard_map/pallas_call | solution.py:598
  43.0 1.9 %collective-permute-start.8 = (f32[8,64]{1,0:T(8,128)S(1)}, f32[8,64]{1,0:T(8,128)S(1)}, u32[]{:S(2)}, u32[]{:S(2)}) collective-permute-start(f32[8,64]{1,0:T(8,128)S(1)} %get-tuple-element.85), channel_id=1, source_target_pairs={{0,1},{1,0},{2,3},{3,2},{4,5},{5,4},{6,7},{7,6},{8,9},{9,8},{10,11... | collective-permute-start | bytes 6152 | tf_op jit(solution)/shard_map/ppermute | solution.py:615
  44.9 0.8 %collective-permute-done.8 = f32[8,64]{1,0:T(8,128)S(1)} collective-permute-done((f32[8,64]{1,0:T(8,128)S(1)}, f32[8,64]{1,0:T(8,128)S(1)}, u32[]{:S(2)}, u32[]{:S(2)}) %collective-permute-start.8) | collective-permute-done | bytes 2080 | tf_op jit(solution)/shard_map/ppermute | solution.py:615
  46.1 1.4 %collective-permute-start.10 = (f32[16,64]{1,0:T(8,128)S(1)}, f32[16,64]{1,0:T(8,128)S(1)}, u32[]{:S(2)}, u32[]{:S(2)}) collective-permute-start(f32[16,64]{1,0:T(8,128)S(1)} %pad_maximum_fusion.1), channel_id=1, source_target_pairs={{0,3},{1,2},{2,1},{3,0},{4,7},{5,6},{6,5},{7,4},{8,11},{9,10},{10,... | collective-permute-start | bytes 12296 | tf_op jit(solution)/shard_map/ppermute | solution.py:615
  47.5 1.7 %collective-permute-done.10 = f32[16,64]{1,0:T(8,128)S(1)} collective-permute-done((f32[16,64]{1,0:T(8,128)S(1)}, f32[16,64]{1,0:T(8,128)S(1)}, u32[]{:S(2)}, u32[]{:S(2)}) %collective-permute-start.10) | collective-permute-done | bytes 4128 | tf_op jit(solution)/shard_map/ppermute | solution.py:615
  49.2 1.3 %collective-permute-start.11 = (f32[16,64]{1,0:T(8,128)S(1)}, f32[16,64]{1,0:T(8,128)S(1)}, u32[]{:S(2)}, u32[]{:S(2)}) collective-permute-start(f32[16,64]{1,0:T(8,128)S(1)} %add.18), channel_id=1, source_target_pairs={{0,5},{1,4},{2,7},{3,6},{4,1},{5,0},{6,3},{7,2},{8,13},{9,12},{10,... | collective-permute-start | bytes 12296 | tf_op jit(solution)/shard_map/ppermute | solution.py:615
  50.5 1.8 %collective-permute-done.11 = f32[16,64]{1,0:T(8,128)S(1)} collective-permute-done((f32[16,64]{1,0:T(8,128)S(1)}, f32[16,64]{1,0:T(8,128)S(1)}, u32[]{:S(2)}, u32[]{:S(2)}) %collective-permute-start.11) | collective-permute-done | bytes 4128 | tf_op jit(solution)/shard_map/ppermute | solution.py:615
  52.3 2.7 %collective-permute-start.12 = (f32[16,64]{1,0:T(8,128)S(1)}, f32[16,64]{1,0:T(8,128)S(1)}, u32[]{:S(2)}, u32[]{:S(2)}) collective-permute-start(f32[16,64]{1,0:T(8,128)S(1)} %add.19.rest_0_), channel_id=1, source_target_pairs={{0,9},{1,8},{2,11},{3,10},{4,13},{5,12},{6,15},{7,14},{8,1},{9,0},... | collective-permute-start | bytes 12296 | tf_op jit(solution)/shard_map/ppermute | solution.py:615
  54.9 1.4 %collective-permute-done.12.rest_1_ = f32[16,64]{1,0:T(8,128)S(1)} collective-permute-done((f32[16,64]{1,0:T(8,128)S(1)}, f32[16,64]{1,0:T(8,128)S(1)}, u32[]{:S(2)}, u32[]{:S(2)}) %collective-permute-start.12) | collective-permute-done | bytes 4128 | tf_op jit(solution)/shard_map/ppermute | solution.py:615
  56.3 2.2 %shard_map.131 = (f32[16,4,32,128]{3,2,1,0:T(8,128)}, f32[16,64]{1,0:T(8,128)}) custom-call(s32[1]{0:T(128)} %bitcast.me, f32[1024,128]{1,0:T(8,128)S(1)} %get-tuple-element.83.image, f32[1024,128]{1,0:T(8,128)S(1)} %collective-permute-done.9.borrowed, bf16[512,2048]{1,0:T(8,128)(2,1)S(1)} %shard_map.126.own_basis.basis, ...), custom_call_target="tpu_custom_call" | custom-call | flops 200000000 | bytes 6291456 | tf_op jit(solution)/shard_map/pallas_call | solution.py:598
  (21 shorter events, 4.9 us)
Async XLA Ops:
  2.8 1.4 %collective-permute-start = (f32[152,128]{1,0:T(8,128)S(1)}, f32[152,128]{1,0:T(8,128)S(1)}, u32[]{:S(2)}, u32[]{:S(2)}) collective-permute-start(f32[152,128]{1,0:T(8,128)S(1)} %get-tuple-element.49.own), channel_id=1, source_target_pairs={{0,1},{1,0},{2,3},{3,2},{4,5},{5,4},{6,7},{7,6},{8,9},{9,8},{10,11... | collective-permute-start | bytes 233480 | tf_op jit(solution)/shard_map/ppermute | solution.py:615
  4.3 2.3 %collective-permute-start.1 = (f32[1536,128]{1,0:T(8,128)S(1)}, f32[1536,128]{1,0:T(8,128)S(1)}, u32[]{:S(2)}, u32[]{:S(2)}) collective-permute-start(f32[1536,128]{1,0:T(8,128)S(1)} %get-tuple-element.52), channel_id=1, source_target_pairs={{0,1},{1,0},{2,3},{3,2},{4,5},{5,4},{6,7},{7,6},{8,9},{9,8},{10,11... | collective-permute-start | bytes 2359304 | tf_op jit(solution)/shard_map/ppermute | solution.py:615
  4.6 5.4 %collective-permute-start.2 = (f32[304,128]{1,0:T(8,128)S(1)}, f32[304,128]{1,0:T(8,128)S(1)}, u32[]{:S(2)}, u32[]{:S(2)}) collective-permute-start(f32[304,128]{1,0:T(8,128)S(1)} %pad_maximum_fusion), channel_id=1, source_target_pairs={{1,2},{2,1},{3,4},{4,3},{5,6},{6,5},{7,8},{8,7},{9,10},{10,9},{11,... | collective-permute-start | bytes 466952 | tf_op jit(solution)/shard_map/ppermute | solution.py:673
  10.1 3.9 %collective-permute-start.3 = (f32[304,128]{1,0:T(8,128)S(1)}, f32[304,128]{1,0:T(8,128)S(1)}, u32[]{:S(2)}, u32[]{:S(2)}) collective-permute-start(f32[304,128]{1,0:T(8,128)S(1)} %collective-permute-done.2.passed), channel_id=1, source_target_pairs={{0,1},{1,0},{2,3},{3,2},{4,5},{5,4},{6,7},{7,6},{8,9},{9,8},{10,11... | collective-permute-start | bytes 466952 | tf_op jit(solution)/shard_map/ppermute | solution.py:615
  14.0 17.7 %collective-permute-start.7 = (f32[8192,128]{1,0:T(8,128)}, f32[8192,128]{1,0:T(8,128)S(1)}, u32[]{:S(2)}, u32[]{:S(2)}) collective-permute-start(f32[8192,128]{1,0:T(8,128)} %bitcast.12), channel_id=1, source_target_pairs={{0,1},{1,0},{2,3},{3,2},{4,5},{5,4},{6,7},{7,6},{8,9},{9,8},{10,11... | collective-permute-start | bytes 12582920 | tf_op jit(solution)/shard_map/ppermute | solution.py:615
  14.3 7.7 %copy-start = (f32[64,4,32,128]{3,2,1,0:T(8,128)S(1)}, f32[64,4,32,128]{3,2,1,0:T(8,128)}, u32[]{:S(2)}) copy-start(f32[64,4,32,128]{3,2,1,0:T(8,128)} %param.15) | copy-start | bytes 12582916
  19.2 5.3 %collective-permute-start.4 = (f32[144,128]{1,0:T(8,128)S(1)}, f32[144,128]{1,0:T(8,128)S(1)}, u32[]{:S(2)}, u32[]{:S(2)}) collective-permute-start(f32[144,128]{1,0:T(8,128)S(1)} %get-tuple-element.60.when), channel_id=1, source_target_pairs={{0,3},{1,2},{2,1},{3,0},{4,7},{5,6},{6,5},{7,4},{8,11},{9,10},{10,... | collective-permute-start | bytes 221192 | tf_op jit(solution)/shard_map/ppermute | solution.py:615
  24.5 4.2 %collective-permute-start.5 = (f32[144,128]{1,0:T(8,128)S(1)}, f32[144,128]{1,0:T(8,128)S(1)}, u32[]{:S(2)}, u32[]{:S(2)}) collective-permute-start(f32[144,128]{1,0:T(8,128)S(1)} %add.15.when), channel_id=1, source_target_pairs={{0,5},{1,4},{2,7},{3,6},{4,1},{5,0},{6,3},{7,2},{8,13},{9,12},{10,... | collective-permute-start | bytes 221192 | tf_op jit(solution)/shard_map/ppermute | solution.py:615
  28.7 5.3 %collective-permute-start.6 = (f32[144,128]{1,0:T(8,128)S(1)}, f32[144,128]{1,0:T(8,128)S(1)}, u32[]{:S(2)}, u32[]{:S(2)}) collective-permute-start(f32[144,128]{1,0:T(8,128)S(1)} %add.16.when), channel_id=1, source_target_pairs={{0,9},{1,8},{2,11},{3,10},{4,13},{5,12},{6,15},{7,14},{8,1},{9,0},... | collective-permute-start | bytes 221192 | tf_op jit(solution)/shard_map/ppermute | solution.py:615
  43.0 2.7 %collective-permute-start.8 = (f32[8,64]{1,0:T(8,128)S(1)}, f32[8,64]{1,0:T(8,128)S(1)}, u32[]{:S(2)}, u32[]{:S(2)}) collective-permute-start(f32[8,64]{1,0:T(8,128)S(1)} %get-tuple-element.85), channel_id=1, source_target_pairs={{0,1},{1,0},{2,3},{3,2},{4,5},{5,4},{6,7},{7,6},{8,9},{9,8},{10,11... | collective-permute-start | bytes 6152 | tf_op jit(solution)/shard_map/ppermute | solution.py:615
  45.8 10.5 %collective-permute-start.9 = (f32[1024,128]{1,0:T(8,128)S(1)}, f32[1024,128]{1,0:T(8,128)S(1)}, u32[]{:S(2)}, u32[]{:S(2)}) collective-permute-start(f32[1024,128]{1,0:T(8,128)S(1)} %get-tuple-element.86), channel_id=1, source_target_pairs={{0,1},{1,0},{2,3},{3,2},{4,5},{5,4},{6,7},{7,6},{8,9},{9,8},{10,11... | collective-permute-start | bytes 1572872 | tf_op jit(solution)/shard_map/ppermute | solution.py:615
  46.1 3.1 %collective-permute-start.10 = (f32[16,64]{1,0:T(8,128)S(1)}, f32[16,64]{1,0:T(8,128)S(1)}, u32[]{:S(2)}, u32[]{:S(2)}) collective-permute-start(f32[16,64]{1,0:T(8,128)S(1)} %pad_maximum_fusion.1), channel_id=1, source_target_pairs={{0,3},{1,2},{2,1},{3,0},{4,7},{5,6},{6,5},{7,4},{8,11},{9,10},{10,... | collective-permute-start | bytes 12296 | tf_op jit(solution)/shard_map/ppermute | solution.py:615
  49.2 3.1 %collective-permute-start.11 = (f32[16,64]{1,0:T(8,128)S(1)}, f32[16,64]{1,0:T(8,128)S(1)}, u32[]{:S(2)}, u32[]{:S(2)}) collective-permute-start(f32[16,64]{1,0:T(8,128)S(1)} %add.18), channel_id=1, source_target_pairs={{0,5},{1,4},{2,7},{3,6},{4,1},{5,0},{6,3},{7,2},{8,13},{9,12},{10,... | collective-permute-start | bytes 12296 | tf_op jit(solution)/shard_map/ppermute | solution.py:615
  52.3 4.0 %collective-permute-start.12 = (f32[16,64]{1,0:T(8,128)S(1)}, f32[16,64]{1,0:T(8,128)S(1)}, u32[]{:S(2)}, u32[]{:S(2)}) collective-permute-start(f32[16,64]{1,0:T(8,128)S(1)} %add.19.rest_0_), channel_id=1, source_target_pairs={{0,9},{1,8},{2,11},{3,10},{4,13},{5,12},{6,15},{7,14},{8,1},{9,0},... | collective-permute-start | bytes 12296 | tf_op jit(solution)/shard_map/ppermute | solution.py:615

commit v15 on v14

--- a/solution.py
+++ b/solution.py
@@ -411,7 +411,7 @@
     prior_ref, band_ref, own_basis, own_basis_two, other_basis, other_basis_two, kept, lent, coeffs,
     high_ref, low_ref, inner_two, outer_two, inner_one, outer_one, z_term, image, scaled, *scratch,
 ):
-    *lefts, image_parts = scratch
+    left, image_parts = scratch
     entries = line_ref.shape[1]
     cells = LAYERS * 32
     rank = own_basis.shape[0] // 8
@@ -422,10 +422,10 @@
     for owner in range(peers):
         rows = slice(owner * fields, (owner + 1) * fields)
         scaled[rows, :] = table[rows, :] * table[peers * fields + owner : peers * fields + owner + 1, :]
-    for tile in range(TILES):
-        rows = slice(tile * fields, (tile + 1) * fields)
+    def weigh(tile, carry):
+        rows = at(tile * fields, fields)
         owner = owner_ref[rows, :]
-        hot = slot_ref[tile * HALF : (tile + 1) * HALF, :]
+        hot = slot_ref[at(tile * HALF, HALF), :]
         hot = jnp.concatenate([hot, hot], axis=0)
         total = jnp.zeros((fields, entries), F32)
         for group in range(peers // 16):
@@ -437,10 +437,12 @@
         high = value.astype(BF16).astype(F32)
         high_ref[rows, :] = high
         low_ref[rows, :] = value - high
-
-    def product(tile):
-        left = lefts[tile]
-        rows = slice(tile * fields, (tile + 1) * fields)
+        return carry
+
+    lax.fori_loop(0, TILES, weigh, 0)
+
+    def inject(tile, carry):
+        rows = at(tile * fields, fields)
         line, high, low = line_ref[rows, :], high_ref[rows, :], low_ref[rows, :]
         for i in range(0, 64, 2):
             chosen = [line == i, line == i + 1]
@@ -448,34 +450,35 @@
             for part, side in ((high, slice(0, entries)), (low, slice(entries, 2 * entries))):
                 both = [jnp.where(which, part, 0.0) for which in chosen]
                 left[row, side] = jnp.concatenate(both, axis=0).astype(BF16)
-        hot = hot_ref[tile * entries : (tile + 1) * entries, :]
-        return jnp.dot(left[...], jnp.concatenate([hot, hot], axis=0), preferred_element_type=F32)
-
-    def inject(tile, value):
+        hot = hot_ref[at(tile * entries, entries), :]
+        value = jnp.dot(left[...], jnp.concatenate([hot, hot], axis=0), preferred_element_type=F32)
+        two = window(outer_two, tile * LAYERS * flat, LAYERS * flat)
+        out = window(inner_two, tile * LAYERS * slab, LAYERS * slab)
+        speed = window(speed_ref, tile * cells, cells)
         for i in range(64):
             for step in range(2):
-                layer, y = tile * LAYERS + i // 16, i % 16 * 2 + step
+                x, y = i // 16, i % 16 * 2 + step
                 now = value[i * fields : (i + 1) * fields, step * HALF : (step + 1) * HALF]
-                if 1 <= tile <= 4:
-                    row = ((layer - LAYERS) * 32 + y) * fields
-                    outer_two[row : row + fields, :] = now
-                speed = spread(speed_ref, layer * 32 + y, fields)
-                row = layer * slab + (REACH + y) * fields
-                inner_two[row : row + fields, :] = speed * now
-        if 1 <= tile <= 4:
-            along_z(inner_two, tile * LAYERS, LAYERS, fields, band_ref, z_term, (tile - 1) * cells * fields)
-
-    values = product(0)
-    for tile in range(TILES):
-        after = product(tile + 1) if tile + 1 < TILES else None
-        inject(tile, values)
-        values = after
+                cell = x * 32 + y
+                two[cell * fields : (cell + 1) * fields, :] = now
+                row = x * slab + (REACH + y) * fields
+                out[row : row + fields, :] = spread(speed, cell, fields) * now
+        return carry
+
+    lax.fori_loop(0, TILES, inject, 0)
+
+    def terms(tile, carry):
+        along_z(inner_two, (tile + 1) * LAYERS, LAYERS, fields, band_ref, z_term, tile * cells * fields)
+        return carry
+
+    lax.fori_loop(0, 4, terms, 0)
 
     def step_one(index, carry):
         pair, chunk = index // 4, index % 4
         start, skip = pair * PAIR * slab + chunk * 8 * fields, pair * PAIR * flat + chunk * 8 * fields
         here = window(inner_two, start, 2 * PAIR * slab - ahead)
-        two, one, z_part = (window(ref, skip, PAIR * flat - ahead) for ref in (outer_two, outer_one, z_term))
+        one, z_part = (window(ref, skip, PAIR * flat - ahead) for ref in (outer_one, z_term))
+        two = window(outer_two, LAYERS * flat + skip, PAIR * flat - ahead)
         out = window(inner_one, start, PAIR * slab - ahead)
         speed = window(speed_ref, cells + pair * 2 * cells + chunk * 8, 2 * cells - 24)
 
@@ -499,10 +502,11 @@
     along_z(inner_one, LAYERS, PAIR, fields, band_ref, z_term)
     mine = me[0] % 2
 
-    def step_two_chunk(chunk, which):
+    def step_two(chunk, total):
         skip = chunk * 8 * fields
         here = window(inner_one, skip, 2 * PAIR * slab - ahead)
-        two_rows, one_rows = (window(ref, LAYERS * flat + skip, PAIR * flat - ahead) for ref in (outer_two, outer_one))
+        two_rows = window(outer_two, 2 * LAYERS * flat + skip, PAIR * flat - ahead)
+        one_rows = window(outer_one, LAYERS * flat + skip, PAIR * flat - ahead)
         z_part, there, out = (window(ref, skip, PAIR * flat - ahead) for ref in (z_term, turned, image))
         push = window(push_ref, chunk * 8, 6 * cells - 24)
         damping = window(prior_ref, chunk * 8, 2 * cells - 24)
@@ -526,23 +530,17 @@
                     value = value + spread(damping, cell, fields) * there[row, :]
                     out[row, :] = value
                     high = value.astype(BF16).astype(F32)
-                    start, lane = (x * 2 + which) * 2 * fields, y * 256
-                    rows = slice(start, start + 2 * fields)
+                    rows, lane = slice(x * 2 * fields, (x + 1) * 2 * fields), y * 256
                     image_parts[rows, lane : lane + HALF] = jnp.concatenate([high, value - high], axis=0).astype(BF16)
                     image_parts[rows, lane + HALF : lane + 256] = jnp.concatenate([high, nothing], axis=0).astype(BF16)
-
-    def step_two(pair, total):
-        for which in range(2):
-            step_two_chunk(pair * 2 + which, which)
         for side, pieces in ((mine, (own_basis, own_basis_two)), (1 - mine, (other_basis, other_basis_two))):
             for x in range(LAYERS):
-                columns = pieces[x // 2][at((x % 2 * 4 + pair * 2) * rank, 2 * rank), :]
-                parts = image_parts[at((side * LAYERS + x) * 4 * fields, 4 * fields), :]
+                columns = pieces[x // 2][at((x % 2 * 4 + chunk) * rank, rank), :]
+                parts = image_parts[at((side * LAYERS + x) * 2 * fields, 2 * fields), :]
                 total = total + lax.dot_general(parts, columns, NT, preferred_element_type=F32)
         return total
 
-    total = lax.fori_loop(0, 2, step_two, jnp.zeros((4 * fields, 2 * rank), F32))
-    total = total[: 2 * fields, :rank] + total[2 * fields :, rank:]
+    total = lax.fori_loop(0, 4, step_two, jnp.zeros((2 * fields, rank), F32))
     coeffs[...] = total[:fields, :] + total[fields:, :]
     kept[...] = image[at(mine * LAYERS * flat, LAYERS * flat), :]
     lent[...] = image[at((1 - mine) * LAYERS * flat, LAYERS * flat), :]
@@ -757,15 +755,15 @@
             pltpu.VMEM((TILES * fields, entries), F32),
             pltpu.VMEM((TILES * fields, entries), F32),
             pltpu.VMEM((TILES * LAYERS * slab, HALF), F32),
-            pltpu.VMEM((2 * PAIR * flat, HALF), F32),
+            pltpu.VMEM((TILES * LAYERS * flat, HALF), F32),
             pltpu.VMEM((2 * PAIR * slab, HALF), F32),
             pltpu.VMEM((2 * PAIR * flat, HALF), F32),
             pltpu.VMEM((2 * PAIR * flat, HALF), F32),
             pltpu.VMEM((PAIR * flat, HALF), F32),
             pltpu.VMEM((peers * fields, HALF), F32),
         ]
-        + [pltpu.VMEM((64 * fields, 2 * entries), BF16)] * TILES
-        + [pltpu.VMEM((4 * PAIR * fields, 2048), BF16)],
+        + [pltpu.VMEM((64 * fields, 2 * entries), BF16)]
+        + [pltpu.VMEM((2 * PAIR * fields, 2048), BF16)],
         5_000_000_000,
         10 * 2**20,
         scalars=1,

time: 58.6 us -> 60.3 us (1.029)
  Pallas kernels: 24.3 us -> 25.9 us
    pallas_call x10, Pallas kernels: 24.3 us -> 25.9 us  [call(): pl.pallas_call(kernel, out_shape=out_shape, in_specs=[smem] * scalars + [...]
  transfers between devices with their start and end apart: 13 -> 13, of which waited for: 10 -> 10; matrix products, arithmetic and copies ran while one was open for 0% -> 0% of each run, Pallas kernels for 20% -> 19%
where the time goes in v15:
time: 60.3 us; the launch traced here: 60.1 us
  Pallas kernels  25.9 us (43%)
  starting transfers between devices  20 us (33%)
  waiting for transfers between devices  12.8 us (21%)
  between operations  1.37 us (2%)
    pallas_call x10, Pallas kernels, call(): pl.pallas_call(kernel, out_shape=out_shape, in_specs=[smem] * scalars + [...  25.9 us
    ppermute x12, starting transfers between devices, swapped(): return lax.ppermute(array, axis, [(i, i ^ bits) for i in range(count)])  19.3 us
    ppermute x12, waiting for transfers between devices, swapped(): return lax.ppermute(array, axis, [(i, i ^ bits) for i in range(count)])  12.8 us
  transfers between devices with their start and end apart: 13, of which 10 were waited for; matrix products, arithmetic and copies ran while one was open for 0% of the time, Pallas kernels for 19%

profile of v15, /device:TPU:0, one launch (start us, length us, event | category | flops | bytes accessed | tf_op | source)
XLA Modules:
  0.0 60.1 jit_solution(4590630653222479471)
XLA Ops:
  1.3 1.6 %shard_map.122 = (f32[152,128]{1,0:T(8,128)S(1)}, f32[1024,128]{1,0:T(8,128)S(1)}, f32[384,128]{1,0:T(8,128)S(1)}, f32[128,128]{1,0:T(8,128)S(1)}, f32[1536,128]...) custom-call(s32[1]{0:T(128)S(6)} %copy.13.count, s32[1]{0:T(128)} %bitcast.me, f32[2048,128]{1,0:T(8,128)} %bitcast.15, ...), custom_call_target="tpu_custom_call" | custom-call | flops 100000 | bytes 2097152 | tf_op jit(solution)/shard_map/pallas_call | solution.py:596
  3.4 0.9 %collective-permute-done.partner = f32[152,128]{1,0:T(8,128)S(1)} collective-permute-done((f32[152,128]{1,0:T(8,128)S(1)}, f32[152,128]{1,0:T(8,128)S(1)}, u32[]{:S(2)}, u32[]{:S(2)}) %collective-permute-start) | collective-permute-done | bytes 77856 | tf_op jit(solution)/shard_map/ppermute | solution.py:613
  5.3 1.2 %collective-permute-done.1.borrowed = f32[1536,128]{1,0:T(8,128)S(1)} collective-permute-done((f32[1536,128]{1,0:T(8,128)S(1)}, f32[1536,128]{1,0:T(8,128)S(1)}, u32[]{:S(2)}, u32[]{:S(2)}) %collective-permute-start.1) | collective-permute-done | bytes 786464 | tf_op jit(solution)/shard_map/ppermute | solution.py:613
  6.6 3.5 %shard_map.123 = (f32[2048,128]{1,0:T(8,128)S(1)}, f32[2560,128]{1,0:T(8,128)S(1)}, f32[2560,128]{1,0:T(8,128)S(1)}, f32[2048,128]{1,0:T(8,128)S(1)}, f32[768,128]{1,0:T(8,128)S(1)}, /*index=5*/f32[256,128]{1,0:T(8,128)S(1)}) custom-call(s32[1]{0:T(128)} %bitcast.me, f32[1024,128]{1,0:T(8,128)S(1)} %get-tuple-element.46.probes, ...), custom_call_target="tpu_custom_call" | custom-call | flops 600000000 | bytes 6291456 | tf_op jit(solution)/shard_map/pallas_call | solution.py:596
  10.1 2.9 %collective-permute-start.3 = (f32[304,128]{1,0:T(8,128)S(1)}, f32[304,128]{1,0:T(8,128)S(1)}, u32[]{:S(2)}, u32[]{:S(2)}) collective-permute-start(f32[304,128]{1,0:T(8,128)S(1)} %collective-permute-done.2.passed), channel_id=1, source_target_pairs={{0,1},{1,0},{2,3},{3,2},{4,5},{5,4},{6,7},{7,6},{8,9},{9,8},{10,11... | collective-permute-start | bytes 466952 | tf_op jit(solution)/shard_map/ppermute | solution.py:613
  12.9 1.0 %collective-permute-done.3.across = f32[304,128]{1,0:T(8,128)S(1)} collective-permute-done((f32[304,128]{1,0:T(8,128)S(1)}, f32[304,128]{1,0:T(8,128)S(1)}, u32[]{:S(2)}, u32[]{:S(2)}) %collective-permute-start.3) | collective-permute-done | bytes 155680 | tf_op jit(solution)/shard_map/ppermute | solution.py:613
  14.3 4.9 %shard_map.124 = (f32[144,128]{1,0:T(8,128)S(1)}, f32[48,512]{1,0:T(8,128)S(1)}, bf16[768,512]{1,0:T(8,128)(2,1)S(1)}, f32[768,128]{1,0:T(8,128)S(1)}, s32[48,51...) custom-call(s32[1]{0:T(128)} %bitcast.me, f32[2560,128]{1,0:T(8,128)S(1)} %get-tuple-element.54.first, ...), custom_call_target="tpu_custom_call" | custom-call | flops 3000000000 | bytes 6291456 | tf_op jit(solution)/shard_map/pallas_call | solution.py:596
  19.2 2.8 %collective-permute-start.4 = (f32[144,128]{1,0:T(8,128)S(1)}, f32[144,128]{1,0:T(8,128)S(1)}, u32[]{:S(2)}, u32[]{:S(2)}) collective-permute-start(f32[144,128]{1,0:T(8,128)S(1)} %get-tuple-element.60.when), channel_id=1, source_target_pairs={{0,3},{1,2},{2,1},{3,0},{4,7},{5,6},{6,5},{7,4},{8,11},{9,10},{10,... | collective-permute-start | bytes 221192 | tf_op jit(solution)/shard_map/ppermute | solution.py:613
  23.2 1.3 %collective-permute-done.4 = f32[144,128]{1,0:T(8,128)S(1)} collective-permute-done((f32[144,128]{1,0:T(8,128)S(1)}, f32[144,128]{1,0:T(8,128)S(1)}, u32[]{:S(2)}, u32[]{:S(2)}) %collective-permute-start.4) | collective-permute-done | bytes 73760 | tf_op jit(solution)/shard_map/ppermute | solution.py:613
  24.5 1.8 %collective-permute-start.5 = (f32[144,128]{1,0:T(8,128)S(1)}, f32[144,128]{1,0:T(8,128)S(1)}, u32[]{:S(2)}, u32[]{:S(2)}) collective-permute-start(f32[144,128]{1,0:T(8,128)S(1)} %add.15.when), channel_id=1, source_target_pairs={{0,5},{1,4},{2,7},{3,6},{4,1},{5,0},{6,3},{7,2},{8,13},{9,12},{10,... | collective-permute-start | bytes 221192 | tf_op jit(solution)/shard_map/ppermute | solution.py:613
  27.0 1.7 %collective-permute-done.5 = f32[144,128]{1,0:T(8,128)S(1)} collective-permute-done((f32[144,128]{1,0:T(8,128)S(1)}, f32[144,128]{1,0:T(8,128)S(1)}, u32[]{:S(2)}, u32[]{:S(2)}) %collective-permute-start.5) | collective-permute-done | bytes 73760 | tf_op jit(solution)/shard_map/ppermute | solution.py:613
  28.7 3.0 %collective-permute-start.6 = (f32[144,128]{1,0:T(8,128)S(1)}, f32[144,128]{1,0:T(8,128)S(1)}, u32[]{:S(2)}, u32[]{:S(2)}) collective-permute-start(f32[144,128]{1,0:T(8,128)S(1)} %add.16.when), channel_id=1, source_target_pairs={{0,9},{1,8},{2,11},{3,10},{4,13},{5,12},{6,15},{7,14},{8,1},{9,0},... | collective-permute-start | bytes 221192 | tf_op jit(solution)/shard_map/ppermute | solution.py:613
  32.4 0.7 %shard_map.128.other_basis = bf16[512,2048]{1,0:T(8,128)(2,1)S(1)} custom-call(f32[8192,128]{1,0:T(8,128)S(1)} %collective-permute-done.7.basis, f32[144,128]{1,0:T(8,128)S(1)} %add.16.when), custom_call_target="tpu_custom_call" | custom-call | flops 10000000 | bytes 4194304 | tf_op jit(solution)/shard_map/pallas_call | solution.py:596
  33.1 1.0 %collective-permute-done.6 = f32[144,128]{1,0:T(8,128)S(1)} collective-permute-done((f32[144,128]{1,0:T(8,128)S(1)}, f32[144,128]{1,0:T(8,128)S(1)}, u32[]{:S(2)}, u32[]{:S(2)}) %collective-permute-start.6) | collective-permute-done | bytes 73760 | tf_op jit(solution)/shard_map/ppermute | solution.py:613
  34.1 10.6 %shard_map.130 = (f32[1024,128]{1,0:T(8,128)S(1)}, f32[1024,128]{1,0:T(8,128)S(1)}, f32[8,64]{1,0:T(8,128)S(1)}) custom-call(s32[1]{0:T(128)} %bitcast.me, f32[144,128]{1,0:T(8,128)S(1)} %add.17.table, bf16[3072,256]{1,0:T(8,128)(2,1)S(1)} %shard_map.125.hot_ref, bf16[768,512]{1,0:T(8,128)(2,1)S(1)} %get-tuple-element.71.slot_ref, ...), custom_call_target="tpu_custom_call" | custom-call | flops 5000000000 | bytes 10485760 | tf_op jit(solution)/shard_map/pallas_call | solution.py:596
  44.7 1.9 %collective-permute-start.8 = (f32[8,64]{1,0:T(8,128)S(1)}, f32[8,64]{1,0:T(8,128)S(1)}, u32[]{:S(2)}, u32[]{:S(2)}) collective-permute-start(f32[8,64]{1,0:T(8,128)S(1)} %get-tuple-element.85), channel_id=1, source_target_pairs={{0,1},{1,0},{2,3},{3,2},{4,5},{5,4},{6,7},{7,6},{8,9},{9,8},{10,11... | collective-permute-start | bytes 6152 | tf_op jit(solution)/shard_map/ppermute | solution.py:613
  46.6 0.8 %collective-permute-done.8 = f32[8,64]{1,0:T(8,128)S(1)} collective-permute-done((f32[8,64]{1,0:T(8,128)S(1)}, f32[8,64]{1,0:T(8,128)S(1)}, u32[]{:S(2)}, u32[]{:S(2)}) %collective-permute-start.8) | collective-permute-done | bytes 2080 | tf_op jit(solution)/shard_map/ppermute | solution.py:613
  47.8 1.4 %collective-permute-start.10 = (f32[16,64]{1,0:T(8,128)S(1)}, f32[16,64]{1,0:T(8,128)S(1)}, u32[]{:S(2)}, u32[]{:S(2)}) collective-permute-start(f32[16,64]{1,0:T(8,128)S(1)} %pad_maximum_fusion.1), channel_id=1, source_target_pairs={{0,3},{1,2},{2,1},{3,0},{4,7},{5,6},{6,5},{7,4},{8,11},{9,10},{10,... | collective-permute-start | bytes 12296 | tf_op jit(solution)/shard_map/ppermute | solution.py:613
  49.1 1.7 %collective-permute-done.10 = f32[16,64]{1,0:T(8,128)S(1)} collective-permute-done((f32[16,64]{1,0:T(8,128)S(1)}, f32[16,64]{1,0:T(8,128)S(1)}, u32[]{:S(2)}, u32[]{:S(2)}) %collective-permute-start.10) | collective-permute-done | bytes 4128 | tf_op jit(solution)/shard_map/ppermute | solution.py:613
  50.9 1.3 %collective-permute-start.11 = (f32[16,64]{1,0:T(8,128)S(1)}, f32[16,64]{1,0:T(8,128)S(1)}, u32[]{:S(2)}, u32[]{:S(2)}) collective-permute-start(f32[16,64]{1,0:T(8,128)S(1)} %add.18), channel_id=1, source_target_pairs={{0,5},{1,4},{2,7},{3,6},{4,1},{5,0},{6,3},{7,2},{8,13},{9,12},{10,... | collective-permute-start | bytes 12296 | tf_op jit(solution)/shard_map/ppermute | solution.py:613
  52.2 1.8 %collective-permute-done.11 = f32[16,64]{1,0:T(8,128)S(1)} collective-permute-done((f32[16,64]{1,0:T(8,128)S(1)}, f32[16,64]{1,0:T(8,128)S(1)}, u32[]{:S(2)}, u32[]{:S(2)}) %collective-permute-start.11) | collective-permute-done | bytes 4128 | tf_op jit(solution)/shard_map/ppermute | solution.py:613
  53.9 2.7 %collective-permute-start.12 = (f32[16,64]{1,0:T(8,128)S(1)}, f32[16,64]{1,0:T(8,128)S(1)}, u32[]{:S(2)}, u32[]{:S(2)}) collective-permute-start(f32[16,64]{1,0:T(8,128)S(1)} %add.19.rest_0_), channel_id=1, source_target_pairs={{0,9},{1,8},{2,11},{3,10},{4,13},{5,12},{6,15},{7,14},{8,1},{9,0},... | collective-permute-start | bytes 12296 | tf_op jit(solution)/shard_map/ppermute | solution.py:613
  56.6 1.4 %collective-permute-done.12.rest_1_ = f32[16,64]{1,0:T(8,128)S(1)} collective-permute-done((f32[16,64]{1,0:T(8,128)S(1)}, f32[16,64]{1,0:T(8,128)S(1)}, u32[]{:S(2)}, u32[]{:S(2)}) %collective-permute-start.12) | collective-permute-done | bytes 4128 | tf_op jit(solution)/shard_map/ppermute | solution.py:613
  58.0 2.2 %shard_map.131 = (f32[16,4,32,128]{3,2,1,0:T(8,128)}, f32[16,64]{1,0:T(8,128)}) custom-call(s32[1]{0:T(128)} %bitcast.me, f32[1024,128]{1,0:T(8,128)S(1)} %get-tuple-element.83.image, f32[1024,128]{1,0:T(8,128)S(1)} %collective-permute-done.9.borrowed, bf16[512,2048]{1,0:T(8,128)(2,1)S(1)} %shard_map.126.own_basis.basis, ...), custom_call_target="tpu_custom_call" | custom-call | flops 200000000 | bytes 6291456 | tf_op jit(solution)/shard_map/pallas_call | solution.py:596
  (21 shorter events, 4.9 us)
Async XLA Ops:
  2.8 1.4 %collective-permute-start = (f32[152,128]{1,0:T(8,128)S(1)}, f32[152,128]{1,0:T(8,128)S(1)}, u32[]{:S(2)}, u32[]{:S(2)}) collective-permute-start(f32[152,128]{1,0:T(8,128)S(1)} %get-tuple-element.49.own), channel_id=1, source_target_pairs={{0,1},{1,0},{2,3},{3,2},{4,5},{5,4},{6,7},{7,6},{8,9},{9,8},{10,11... | collective-permute-start | bytes 233480 | tf_op jit(solution)/shard_map/ppermute | solution.py:613
  4.3 2.3 %collective-permute-start.1 = (f32[1536,128]{1,0:T(8,128)S(1)}, f32[1536,128]{1,0:T(8,128)S(1)}, u32[]{:S(2)}, u32[]{:S(2)}) collective-permute-start(f32[1536,128]{1,0:T(8,128)S(1)} %get-tuple-element.52), channel_id=1, source_target_pairs={{0,1},{1,0},{2,3},{3,2},{4,5},{5,4},{6,7},{7,6},{8,9},{9,8},{10,11... | collective-permute-start | bytes 2359304 | tf_op jit(solution)/shard_map/ppermute | solution.py:613
  4.6 5.4 %collective-permute-start.2 = (f32[304,128]{1,0:T(8,128)S(1)}, f32[304,128]{1,0:T(8,128)S(1)}, u32[]{:S(2)}, u32[]{:S(2)}) collective-permute-start(f32[304,128]{1,0:T(8,128)S(1)} %pad_maximum_fusion), channel_id=1, source_target_pairs={{1,2},{2,1},{3,4},{4,3},{5,6},{6,5},{7,8},{8,7},{9,10},{10,9},{11,... | collective-permute-start | bytes 466952 | tf_op jit(solution)/shard_map/ppermute | solution.py:671
  10.1 3.9 %collective-permute-start.3 = (f32[304,128]{1,0:T(8,128)S(1)}, f32[304,128]{1,0:T(8,128)S(1)}, u32[]{:S(2)}, u32[]{:S(2)}) collective-permute-start(f32[304,128]{1,0:T(8,128)S(1)} %collective-permute-done.2.passed), channel_id=1, source_target_pairs={{0,1},{1,0},{2,3},{3,2},{4,5},{5,4},{6,7},{7,6},{8,9},{9,8},{10,11... | collective-permute-start | bytes 466952 | tf_op jit(solution)/shard_map/ppermute | solution.py:613
  14.0 17.7 %collective-permute-start.7 = (f32[8192,128]{1,0:T(8,128)}, f32[8192,128]{1,0:T(8,128)S(1)}, u32[]{:S(2)}, u32[]{:S(2)}) collective-permute-start(f32[8192,128]{1,0:T(8,128)} %bitcast.12), channel_id=1, source_target_pairs={{0,1},{1,0},{2,3},{3,2},{4,5},{5,4},{6,7},{7,6},{8,9},{9,8},{10,11... | collective-permute-start | bytes 12582920 | tf_op jit(solution)/shard_map/ppermute | solution.py:613
  14.3 7.7 %copy-start = (f32[64,4,32,128]{3,2,1,0:T(8,128)S(1)}, f32[64,4,32,128]{3,2,1,0:T(8,128)}, u32[]{:S(2)}) copy-start(f32[64,4,32,128]{3,2,1,0:T(8,128)} %param.15) | copy-start | bytes 12582916
  19.2 5.3 %collective-permute-start.4 = (f32[144,128]{1,0:T(8,128)S(1)}, f32[144,128]{1,0:T(8,128)S(1)}, u32[]{:S(2)}, u32[]{:S(2)}) collective-permute-start(f32[144,128]{1,0:T(8,128)S(1)} %get-tuple-element.60.when), channel_id=1, source_target_pairs={{0,3},{1,2},{2,1},{3,0},{4,7},{5,6},{6,5},{7,4},{8,11},{9,10},{10,... | collective-permute-start | bytes 221192 | tf_op jit(solution)/shard_map/ppermute | solution.py:613
  24.5 4.2 %collective-permute-start.5 = (f32[144,128]{1,0:T(8,128)S(1)}, f32[144,128]{1,0:T(8,128)S(1)}, u32[]{:S(2)}, u32[]{:S(2)}) collective-permute-start(f32[144,128]{1,0:T(8,128)S(1)} %add.15.when), channel_id=1, source_target_pairs={{0,5},{1,4},{2,7},{3,6},{4,1},{5,0},{6,3},{7,2},{8,13},{9,12},{10,... | collective-permute-start | bytes 221192 | tf_op jit(solution)/shard_map/ppermute | solution.py:613
  28.7 5.3 %collective-permute-start.6 = (f32[144,128]{1,0:T(8,128)S(1)}, f32[144,128]{1,0:T(8,128)S(1)}, u32[]{:S(2)}, u32[]{:S(2)}) collective-permute-start(f32[144,128]{1,0:T(8,128)S(1)} %add.16.when), channel_id=1, source_target_pairs={{0,9},{1,8},{2,11},{3,10},{4,13},{5,12},{6,15},{7,14},{8,1},{9,0},... | collective-permute-start | bytes 221192 | tf_op jit(solution)/shard_map/ppermute | solution.py:613
  44.7 2.8 %collective-permute-start.8 = (f32[8,64]{1,0:T(8,128)S(1)}, f32[8,64]{1,0:T(8,128)S(1)}, u32[]{:S(2)}, u32[]{:S(2)}) collective-permute-start(f32[8,64]{1,0:T(8,128)S(1)} %get-tuple-element.85), channel_id=1, source_target_pairs={{0,1},{1,0},{2,3},{3,2},{4,5},{5,4},{6,7},{7,6},{8,9},{9,8},{10,11... | collective-permute-start | bytes 6152 | tf_op jit(solution)/shard_map/ppermute | solution.py:613
  47.4 10.5 %collective-permute-start.9 = (f32[1024,128]{1,0:T(8,128)S(1)}, f32[1024,128]{1,0:T(8,128)S(1)}, u32[]{:S(2)}, u32[]{:S(2)}) collective-permute-start(f32[1024,128]{1,0:T(8,128)S(1)} %get-tuple-element.86), channel_id=1, source_target_pairs={{0,1},{1,0},{2,3},{3,2},{4,5},{5,4},{6,7},{7,6},{8,9},{9,8},{10,11... | collective-permute-start | bytes 1572872 | tf_op jit(solution)/shard_map/ppermute | solution.py:613
  47.8 3.1 %collective-permute-start.10 = (f32[16,64]{1,0:T(8,128)S(1)}, f32[16,64]{1,0:T(8,128)S(1)}, u32[]{:S(2)}, u32[]{:S(2)}) collective-permute-start(f32[16,64]{1,0:T(8,128)S(1)} %pad_maximum_fusion.1), channel_id=1, source_target_pairs={{0,3},{1,2},{2,1},{3,0},{4,7},{5,6},{6,5},{7,4},{8,11},{9,10},{10,... | collective-permute-start | bytes 12296 | tf_op jit(solution)/shard_map/ppermute | solution.py:613
  50.9 3.1 %collective-permute-start.11 = (f32[16,64]{1,0:T(8,128)S(1)}, f32[16,64]{1,0:T(8,128)S(1)}, u32[]{:S(2)}, u32[]{:S(2)}) collective-permute-start(f32[16,64]{1,0:T(8,128)S(1)} %add.18), channel_id=1, source_target_pairs={{0,5},{1,4},{2,7},{3,6},{4,1},{5,0},{6,3},{7,2},{8,13},{9,12},{10,... | collective-permute-start | bytes 12296 | tf_op jit(solution)/shard_map/ppermute | solution.py:613
  53.9 4.0 %collective-permute-start.12 = (f32[16,64]{1,0:T(8,128)S(1)}, f32[16,64]{1,0:T(8,128)S(1)}, u32[]{:S(2)}, u32[]{:S(2)}) collective-permute-start(f32[16,64]{1,0:T(8,128)S(1)} %add.19.rest_0_), channel_id=1, source_target_pairs={{0,9},{1,8},{2,11},{3,10},{4,13},{5,12},{6,15},{7,14},{8,1},{9,0},... | collective-permute-start | bytes 12296 | tf_op jit(solution)/shard_map/ppermute | solution.py:613

commit v16 on v14

--- a/solution.py
+++ b/solution.py
@@ -232,7 +232,7 @@
 def forward_window(
     fields, peers, me, first, second, third, own, partner, passed, across, band_ref,
     table, place_ref, slot_ref, speed_ref, line_ref, owner_ref, weight_ref,
-    cell_ref, wide_ref, below, above, z_term, total_ref, *samples,
+    cell_ref, wide_ref, statics, below, above, z_term, total_ref, *samples,
 ):
     entries = line_ref.shape[1]
     cells = LAYERS * 32
@@ -257,20 +257,25 @@
     slot_place = lax.broadcasted_iota(jnp.int32, (HALF, entries), 0)
     for tile, value in enumerate(tiles):
         speed_ref[tile * cells : (tile + 1) * cells, :] = value[0:cells, :]
-        cell = entry_row(value, cells).astype(jnp.int32)
-        owner = entry_row(value, cells + 4).astype(jnp.int32)
-        slot = entry_row(value, cells + 8).astype(jnp.int32)
-        weight = entry_row(value, cells + 12)
+        statics[tile * 16 : (tile + 1) * 16, :] = value[cells : cells + 16, :]
+
+    def describe(tile, carry):
+        value = statics[at(tile * 16), :]
+        cell, owner, slot = (entry_row(value, i * 4).astype(jnp.int32) for i in range(3))
+        weight = entry_row(value, 12)
         hot = jnp.where(place == jnp.bitwise_and(cell, PLACES - 1), 1.0, 0.0)
-        cell_ref[tile * PLACES : (tile + 1) * PLACES, :] = hot.astype(BF16)
+        cell_ref[at(tile * PLACES, PLACES), :] = hot.astype(BF16)
         hot = jnp.where(slot_place == slot, 1.0, 0.0)
-        slot_ref[tile * HALF : (tile + 1) * HALF, :] = hot.astype(BF16)
-        rows = slice(tile * fields, (tile + 1) * fields)
+        slot_ref[at(tile * HALF, HALF), :] = hot.astype(BF16)
+        rows = at(tile * fields, fields)
         line_ref[rows, :] = jnp.broadcast_to(lax.shift_right_logical(cell, 8), (fields, entries))
         wide_ref[rows, :] = jnp.broadcast_to(lax.shift_right_logical(cell, 9), (fields, entries))
         place_ref[rows, :] = jnp.broadcast_to(jnp.bitwise_and(cell, 255), (fields, entries)).astype(F32)
         owner_ref[rows, :] = jnp.broadcast_to(owner, (fields, entries))
         weight_ref[rows, :] = jnp.broadcast_to(weight, (fields, entries))
+        return carry
+
+    lax.fori_loop(0, TILES, describe, 0)
 
     def outward(chunk, carry):
         ahead = 24 * fields
@@ -462,8 +467,8 @@
                 speed = spread(speed_ref, layer * 32 + y, fields)
                 row = layer * slab + (REACH + y) * fields
                 inner_two[row : row + fields, :] = speed * now
-        if 1 <= tile <= 4:
-            along_z(inner_two, tile * LAYERS, LAYERS, fields, band_ref, z_term, (tile - 1) * cells * fields)
+        if 2 <= tile:
+            along_z(inner_two, (tile - 1) * LAYERS, LAYERS, fields, band_ref, z_term, (tile - 2) * cells * fields)
 
     values = product(0)
     for tile in range(TILES):
@@ -499,7 +504,7 @@
     along_z(inner_one, LAYERS, PAIR, fields, band_ref, z_term)
     mine = me[0] % 2
 
-    def step_two_chunk(chunk, which):
+    def step_two(chunk, total):
         skip = chunk * 8 * fields
         here = window(inner_one, skip, 2 * PAIR * slab - ahead)
         two_rows, one_rows = (window(ref, LAYERS * flat + skip, PAIR * flat - ahead) for ref in (outer_two, outer_one))
@@ -526,23 +531,17 @@
                     value = value + spread(damping, cell, fields) * there[row, :]
                     out[row, :] = value
                     high = value.astype(BF16).astype(F32)
-                    start, lane = (x * 2 + which) * 2 * fields, y * 256
-                    rows = slice(start, start + 2 * fields)
+                    rows, lane = slice(x * 2 * fields, (x + 1) * 2 * fields), y * 256
                     image_parts[rows, lane : lane + HALF] = jnp.concatenate([high, value - high], axis=0).astype(BF16)
                     image_parts[rows, lane + HALF : lane + 256] = jnp.concatenate([high, nothing], axis=0).astype(BF16)
-
-    def step_two(pair, total):
-        for which in range(2):
-            step_two_chunk(pair * 2 + which, which)
         for side, pieces in ((mine, (own_basis, own_basis_two)), (1 - mine, (other_basis, other_basis_two))):
             for x in range(LAYERS):
-                columns = pieces[x // 2][at((x % 2 * 4 + pair * 2) * rank, 2 * rank), :]
-                parts = image_parts[at((side * LAYERS + x) * 4 * fields, 4 * fields), :]
+                columns = pieces[x // 2][at((x % 2 * 4 + chunk) * rank, rank), :]
+                parts = image_parts[at((side * LAYERS + x) * 2 * fields, 2 * fields), :]
                 total = total + lax.dot_general(parts, columns, NT, preferred_element_type=F32)
         return total
 
-    total = lax.fori_loop(0, 2, step_two, jnp.zeros((4 * fields, 2 * rank), F32))
-    total = total[: 2 * fields, :rank] + total[2 * fields :, rank:]
+    total = lax.fori_loop(0, 4, step_two, jnp.zeros((2 * fields, rank), F32))
     coeffs[...] = total[:fields, :] + total[fields:, :]
     kept[...] = image[at(mine * LAYERS * flat, LAYERS * flat), :]
     lent[...] = image[at((1 - mine) * LAYERS * flat, LAYERS * flat), :]
@@ -711,6 +710,7 @@
         [
             pltpu.VMEM((TILES * PLACES, entries), BF16),
             pltpu.VMEM((TILES * fields, entries), jnp.int32),
+            pltpu.VMEM((TILES * 16, HALF), F32),
             pltpu.VMEM((LAYERS * slab, HALF), F32),
             pltpu.VMEM((LAYERS * slab, HALF), F32),
             pltpu.VMEM((PAIR * flat, HALF), F32),
@@ -765,7 +765,7 @@
             pltpu.VMEM((peers * fields, HALF), F32),
         ]
         + [pltpu.VMEM((64 * fields, 2 * entries), BF16)] * TILES
-        + [pltpu.VMEM((4 * PAIR * fields, 2048), BF16)],
+        + [pltpu.VMEM((2 * PAIR * fields, 2048), BF16)],
         5_000_000_000,
         10 * 2**20,
         scalars=1,

time: 58.6 us -> 58.4 us (level)
  no operation moved by 1% of the time
where the time goes in v16:
time: 58.4 us; the launch traced here: 58.2 us
  Pallas kernels  24 us (41%)
  starting transfers between devices  20 us (34%)
  waiting for transfers between devices  12.8 us (22%)
  between operations  1.37 us (2%)
    pallas_call x10, Pallas kernels, call(): pl.pallas_call(kernel, out_shape=out_shape, in_specs=[smem] * scalars + [...  24 us
    ppermute x12, starting transfers between devices, swapped(): return lax.ppermute(array, axis, [(i, i ^ bits) for i in range(count)])  19.3 us
    ppermute x12, waiting for transfers between devices, swapped(): return lax.ppermute(array, axis, [(i, i ^ bits) for i in range(count)])  12.8 us
  transfers between devices with their start and end apart: 13, of which 10 were waited for; matrix products, arithmetic and copies ran while one was open for 0% of the time, Pallas kernels for 20%

profile of v16, /device:TPU:0, one launch (start us, length us, event | category | flops | bytes accessed | tf_op | source)
XLA Modules:
  0.0 58.2 jit_solution(14551743953501016241)
XLA Ops:
  1.3 1.6 %shard_map.122 = (f32[152,128]{1,0:T(8,128)S(1)}, f32[1024,128]{1,0:T(8,128)S(1)}, f32[384,128]{1,0:T(8,128)S(1)}, f32[128,128]{1,0:T(8,128)S(1)}, f32[1536,128]...) custom-call(s32[1]{0:T(128)S(6)} %copy.13.count, s32[1]{0:T(128)} %bitcast.me, f32[2048,128]{1,0:T(8,128)} %bitcast.15, ...), custom_call_target="tpu_custom_call" | custom-call | flops 100000 | bytes 2097152 | tf_op jit(solution)/shard_map/pallas_call | solution.py:597
  3.4 0.9 %collective-permute-done.partner = f32[152,128]{1,0:T(8,128)S(1)} collective-permute-done((f32[152,128]{1,0:T(8,128)S(1)}, f32[152,128]{1,0:T(8,128)S(1)}, u32[]{:S(2)}, u32[]{:S(2)}) %collective-permute-start) | collective-permute-done | bytes 77856 | tf_op jit(solution)/shard_map/ppermute | solution.py:614
  5.3 1.2 %collective-permute-done.1.borrowed = f32[1536,128]{1,0:T(8,128)S(1)} collective-permute-done((f32[1536,128]{1,0:T(8,128)S(1)}, f32[1536,128]{1,0:T(8,128)S(1)}, u32[]{:S(2)}, u32[]{:S(2)}) %collective-permute-start.1) | collective-permute-done | bytes 786464 | tf_op jit(solution)/shard_map/ppermute | solution.py:614
  6.6 3.5 %shard_map.123 = (f32[2048,128]{1,0:T(8,128)S(1)}, f32[2560,128]{1,0:T(8,128)S(1)}, f32[2560,128]{1,0:T(8,128)S(1)}, f32[2048,128]{1,0:T(8,128)S(1)}, f32[768,128]{1,0:T(8,128)S(1)}, /*index=5*/f32[256,128]{1,0:T(8,128)S(1)}) custom-call(s32[1]{0:T(128)} %bitcast.me, f32[1024,128]{1,0:T(8,128)S(1)} %get-tuple-element.46.probes, ...), custom_call_target="tpu_custom_call" | custom-call | flops 600000000 | bytes 6291456 | tf_op jit(solution)/shard_map/pallas_call | solution.py:597
  10.1 2.9 %collective-permute-start.3 = (f32[304,128]{1,0:T(8,128)S(1)}, f32[304,128]{1,0:T(8,128)S(1)}, u32[]{:S(2)}, u32[]{:S(2)}) collective-permute-start(f32[304,128]{1,0:T(8,128)S(1)} %collective-permute-done.2.passed), channel_id=1, source_target_pairs={{0,1},{1,0},{2,3},{3,2},{4,5},{5,4},{6,7},{7,6},{8,9},{9,8},{10,11... | collective-permute-start | bytes 466952 | tf_op jit(solution)/shard_map/ppermute | solution.py:614
  12.9 1.0 %collective-permute-done.3.across = f32[304,128]{1,0:T(8,128)S(1)} collective-permute-done((f32[304,128]{1,0:T(8,128)S(1)}, f32[304,128]{1,0:T(8,128)S(1)}, u32[]{:S(2)}, u32[]{:S(2)}) %collective-permute-start.3) | collective-permute-done | bytes 155680 | tf_op jit(solution)/shard_map/ppermute | solution.py:614
  14.3 5.0 %shard_map.124 = (f32[144,128]{1,0:T(8,128)S(1)}, f32[48,512]{1,0:T(8,128)S(1)}, bf16[768,512]{1,0:T(8,128)(2,1)S(1)}, f32[768,128]{1,0:T(8,128)S(1)}, s32[48,51...) custom-call(s32[1]{0:T(128)} %bitcast.me, f32[2560,128]{1,0:T(8,128)S(1)} %get-tuple-element.54.first, ...), custom_call_target="tpu_custom_call" | custom-call | flops 3000000000 | bytes 6291456 | tf_op jit(solution)/shard_map/pallas_call | solution.py:597
  19.3 2.8 %collective-permute-start.4 = (f32[144,128]{1,0:T(8,128)S(1)}, f32[144,128]{1,0:T(8,128)S(1)}, u32[]{:S(2)}, u32[]{:S(2)}) collective-permute-start(f32[144,128]{1,0:T(8,128)S(1)} %get-tuple-element.60.when), channel_id=1, source_target_pairs={{0,3},{1,2},{2,1},{3,0},{4,7},{5,6},{6,5},{7,4},{8,11},{9,10},{10,... | collective-permute-start | bytes 221192 | tf_op jit(solution)/shard_map/ppermute | solution.py:614
  23.3 1.3 %collective-permute-done.4 = f32[144,128]{1,0:T(8,128)S(1)} collective-permute-done((f32[144,128]{1,0:T(8,128)S(1)}, f32[144,128]{1,0:T(8,128)S(1)}, u32[]{:S(2)}, u32[]{:S(2)}) %collective-permute-start.4) | collective-permute-done | bytes 73760 | tf_op jit(solution)/shard_map/ppermute | solution.py:614
  24.6 1.8 %collective-permute-start.5 = (f32[144,128]{1,0:T(8,128)S(1)}, f32[144,128]{1,0:T(8,128)S(1)}, u32[]{:S(2)}, u32[]{:S(2)}) collective-permute-start(f32[144,128]{1,0:T(8,128)S(1)} %add.15.when), channel_id=1, source_target_pairs={{0,5},{1,4},{2,7},{3,6},{4,1},{5,0},{6,3},{7,2},{8,13},{9,12},{10,... | collective-permute-start | bytes 221192 | tf_op jit(solution)/shard_map/ppermute | solution.py:614
  27.2 1.7 %collective-permute-done.5 = f32[144,128]{1,0:T(8,128)S(1)} collective-permute-done((f32[144,128]{1,0:T(8,128)S(1)}, f32[144,128]{1,0:T(8,128)S(1)}, u32[]{:S(2)}, u32[]{:S(2)}) %collective-permute-start.5) | collective-permute-done | bytes 73760 | tf_op jit(solution)/shard_map/ppermute | solution.py:614
  28.8 3.0 %collective-permute-start.6 = (f32[144,128]{1,0:T(8,128)S(1)}, f32[144,128]{1,0:T(8,128)S(1)}, u32[]{:S(2)}, u32[]{:S(2)}) collective-permute-start(f32[144,128]{1,0:T(8,128)S(1)} %add.16.when), channel_id=1, source_target_pairs={{0,9},{1,8},{2,11},{3,10},{4,13},{5,12},{6,15},{7,14},{8,1},{9,0},... | collective-permute-start | bytes 221192 | tf_op jit(solution)/shard_map/ppermute | solution.py:614
  32.5 0.7 %shard_map.128.other_basis = bf16[512,2048]{1,0:T(8,128)(2,1)S(1)} custom-call(f32[8192,128]{1,0:T(8,128)S(1)} %collective-permute-done.7.basis, f32[144,128]{1,0:T(8,128)S(1)} %add.16.when), custom_call_target="tpu_custom_call" | custom-call | flops 10000000 | bytes 4194304 | tf_op jit(solution)/shard_map/pallas_call | solution.py:597
  33.2 1.0 %collective-permute-done.6 = f32[144,128]{1,0:T(8,128)S(1)} collective-permute-done((f32[144,128]{1,0:T(8,128)S(1)}, f32[144,128]{1,0:T(8,128)S(1)}, u32[]{:S(2)}, u32[]{:S(2)}) %collective-permute-start.6) | collective-permute-done | bytes 73760 | tf_op jit(solution)/shard_map/ppermute | solution.py:614
  34.2 8.6 %shard_map.130 = (f32[1024,128]{1,0:T(8,128)S(1)}, f32[1024,128]{1,0:T(8,128)S(1)}, f32[8,64]{1,0:T(8,128)S(1)}) custom-call(s32[1]{0:T(128)} %bitcast.me, f32[144,128]{1,0:T(8,128)S(1)} %add.17.table, bf16[3072,256]{1,0:T(8,128)(2,1)S(1)} %shard_map.125.hot_ref, bf16[768,512]{1,0:T(8,128)(2,1)S(1)} %get-tuple-element.71.slot_ref, ...), custom_call_target="tpu_custom_call" | custom-call | flops 5000000000 | bytes 10485760 | tf_op jit(solution)/shard_map/pallas_call | solution.py:597
  42.7 1.9 %collective-permute-start.8 = (f32[8,64]{1,0:T(8,128)S(1)}, f32[8,64]{1,0:T(8,128)S(1)}, u32[]{:S(2)}, u32[]{:S(2)}) collective-permute-start(f32[8,64]{1,0:T(8,128)S(1)} %get-tuple-element.85), channel_id=1, source_target_pairs={{0,1},{1,0},{2,3},{3,2},{4,5},{5,4},{6,7},{7,6},{8,9},{9,8},{10,11... | collective-permute-start | bytes 6152 | tf_op jit(solution)/shard_map/ppermute | solution.py:614
  44.7 0.8 %collective-permute-done.8 = f32[8,64]{1,0:T(8,128)S(1)} collective-permute-done((f32[8,64]{1,0:T(8,128)S(1)}, f32[8,64]{1,0:T(8,128)S(1)}, u32[]{:S(2)}, u32[]{:S(2)}) %collective-permute-start.8) | collective-permute-done | bytes 2080 | tf_op jit(solution)/shard_map/ppermute | solution.py:614
  45.9 1.4 %collective-permute-start.10 = (f32[16,64]{1,0:T(8,128)S(1)}, f32[16,64]{1,0:T(8,128)S(1)}, u32[]{:S(2)}, u32[]{:S(2)}) collective-permute-start(f32[16,64]{1,0:T(8,128)S(1)} %pad_maximum_fusion.1), channel_id=1, source_target_pairs={{0,3},{1,2},{2,1},{3,0},{4,7},{5,6},{6,5},{7,4},{8,11},{9,10},{10,... | collective-permute-start | bytes 12296 | tf_op jit(solution)/shard_map/ppermute | solution.py:614
  47.2 1.7 %collective-permute-done.10 = f32[16,64]{1,0:T(8,128)S(1)} collective-permute-done((f32[16,64]{1,0:T(8,128)S(1)}, f32[16,64]{1,0:T(8,128)S(1)}, u32[]{:S(2)}, u32[]{:S(2)}) %collective-permute-start.10) | collective-permute-done | bytes 4128 | tf_op jit(solution)/shard_map/ppermute | solution.py:614
  48.9 1.3 %collective-permute-start.11 = (f32[16,64]{1,0:T(8,128)S(1)}, f32[16,64]{1,0:T(8,128)S(1)}, u32[]{:S(2)}, u32[]{:S(2)}) collective-permute-start(f32[16,64]{1,0:T(8,128)S(1)} %add.18), channel_id=1, source_target_pairs={{0,5},{1,4},{2,7},{3,6},{4,1},{5,0},{6,3},{7,2},{8,13},{9,12},{10,... | collective-permute-start | bytes 12296 | tf_op jit(solution)/shard_map/ppermute | solution.py:614
  50.2 1.8 %collective-permute-done.11 = f32[16,64]{1,0:T(8,128)S(1)} collective-permute-done((f32[16,64]{1,0:T(8,128)S(1)}, f32[16,64]{1,0:T(8,128)S(1)}, u32[]{:S(2)}, u32[]{:S(2)}) %collective-permute-start.11) | collective-permute-done | bytes 4128 | tf_op jit(solution)/shard_map/ppermute | solution.py:614
  52.0 2.6 %collective-permute-start.12 = (f32[16,64]{1,0:T(8,128)S(1)}, f32[16,64]{1,0:T(8,128)S(1)}, u32[]{:S(2)}, u32[]{:S(2)}) collective-permute-start(f32[16,64]{1,0:T(8,128)S(1)} %add.19.rest_0_), channel_id=1, source_target_pairs={{0,9},{1,8},{2,11},{3,10},{4,13},{5,12},{6,15},{7,14},{8,1},{9,0},... | collective-permute-start | bytes 12296 | tf_op jit(solution)/shard_map/ppermute | solution.py:614
  54.7 1.4 %collective-permute-done.12.rest_1_ = f32[16,64]{1,0:T(8,128)S(1)} collective-permute-done((f32[16,64]{1,0:T(8,128)S(1)}, f32[16,64]{1,0:T(8,128)S(1)}, u32[]{:S(2)}, u32[]{:S(2)}) %collective-permute-start.12) | collective-permute-done | bytes 4128 | tf_op jit(solution)/shard_map/ppermute | solution.py:614
  56.0 2.2 %shard_map.131 = (f32[16,4,32,128]{3,2,1,0:T(8,128)}, f32[16,64]{1,0:T(8,128)}) custom-call(s32[1]{0:T(128)} %bitcast.me, f32[1024,128]{1,0:T(8,128)S(1)} %get-tuple-element.83.image, f32[1024,128]{1,0:T(8,128)S(1)} %collective-permute-done.9.borrowed, bf16[512,2048]{1,0:T(8,128)(2,1)S(1)} %shard_map.126.own_basis.basis, ...), custom_call_target="tpu_custom_call" | custom-call | flops 200000000 | bytes 6291456 | tf_op jit(solution)/shard_map/pallas_call | solution.py:597
  (21 shorter events, 4.9 us)
Async XLA Ops:
  2.8 1.4 %collective-permute-start = (f32[152,128]{1,0:T(8,128)S(1)}, f32[152,128]{1,0:T(8,128)S(1)}, u32[]{:S(2)}, u32[]{:S(2)}) collective-permute-start(f32[152,128]{1,0:T(8,128)S(1)} %get-tuple-element.49.own), channel_id=1, source_target_pairs={{0,1},{1,0},{2,3},{3,2},{4,5},{5,4},{6,7},{7,6},{8,9},{9,8},{10,11... | collective-permute-start | bytes 233480 | tf_op jit(solution)/shard_map/ppermute | solution.py:614
  4.3 2.3 %collective-permute-start.1 = (f32[1536,128]{1,0:T(8,128)S(1)}, f32[1536,128]{1,0:T(8,128)S(1)}, u32[]{:S(2)}, u32[]{:S(2)}) collective-permute-start(f32[1536,128]{1,0:T(8,128)S(1)} %get-tuple-element.52), channel_id=1, source_target_pairs={{0,1},{1,0},{2,3},{3,2},{4,5},{5,4},{6,7},{7,6},{8,9},{9,8},{10,11... | collective-permute-start | bytes 2359304 | tf_op jit(solution)/shard_map/ppermute | solution.py:614
  4.6 5.4 %collective-permute-start.2 = (f32[304,128]{1,0:T(8,128)S(1)}, f32[304,128]{1,0:T(8,128)S(1)}, u32[]{:S(2)}, u32[]{:S(2)}) collective-permute-start(f32[304,128]{1,0:T(8,128)S(1)} %pad_maximum_fusion), channel_id=1, source_target_pairs={{1,2},{2,1},{3,4},{4,3},{5,6},{6,5},{7,8},{8,7},{9,10},{10,9},{11,... | collective-permute-start | bytes 466952 | tf_op jit(solution)/shard_map/ppermute | solution.py:672
  10.1 3.9 %collective-permute-start.3 = (f32[304,128]{1,0:T(8,128)S(1)}, f32[304,128]{1,0:T(8,128)S(1)}, u32[]{:S(2)}, u32[]{:S(2)}) collective-permute-start(f32[304,128]{1,0:T(8,128)S(1)} %collective-permute-done.2.passed), channel_id=1, source_target_pairs={{0,1},{1,0},{2,3},{3,2},{4,5},{5,4},{6,7},{7,6},{8,9},{9,8},{10,11... | collective-permute-start | bytes 466952 | tf_op jit(solution)/shard_map/ppermute | solution.py:614
  14.0 17.8 %collective-permute-start.7 = (f32[8192,128]{1,0:T(8,128)}, f32[8192,128]{1,0:T(8,128)S(1)}, u32[]{:S(2)}, u32[]{:S(2)}) collective-permute-start(f32[8192,128]{1,0:T(8,128)} %bitcast.12), channel_id=1, source_target_pairs={{0,1},{1,0},{2,3},{3,2},{4,5},{5,4},{6,7},{7,6},{8,9},{9,8},{10,11... | collective-permute-start | bytes 12582920 | tf_op jit(solution)/shard_map/ppermute | solution.py:614
  14.3 7.8 %copy-start = (f32[64,4,32,128]{3,2,1,0:T(8,128)S(1)}, f32[64,4,32,128]{3,2,1,0:T(8,128)}, u32[]{:S(2)}) copy-start(f32[64,4,32,128]{3,2,1,0:T(8,128)} %param.15) | copy-start | bytes 12582916
  19.3 5.3 %collective-permute-start.4 = (f32[144,128]{1,0:T(8,128)S(1)}, f32[144,128]{1,0:T(8,128)S(1)}, u32[]{:S(2)}, u32[]{:S(2)}) collective-permute-start(f32[144,128]{1,0:T(8,128)S(1)} %get-tuple-element.60.when), channel_id=1, source_target_pairs={{0,3},{1,2},{2,1},{3,0},{4,7},{5,6},{6,5},{7,4},{8,11},{9,10},{10,... | collective-permute-start | bytes 221192 | tf_op jit(solution)/shard_map/ppermute | solution.py:614
  24.6 4.2 %collective-permute-start.5 = (f32[144,128]{1,0:T(8,128)S(1)}, f32[144,128]{1,0:T(8,128)S(1)}, u32[]{:S(2)}, u32[]{:S(2)}) collective-permute-start(f32[144,128]{1,0:T(8,128)S(1)} %add.15.when), channel_id=1, source_target_pairs={{0,5},{1,4},{2,7},{3,6},{4,1},{5,0},{6,3},{7,2},{8,13},{9,12},{10,... | collective-permute-start | bytes 221192 | tf_op jit(solution)/shard_map/ppermute | solution.py:614
  28.8 5.3 %collective-permute-start.6 = (f32[144,128]{1,0:T(8,128)S(1)}, f32[144,128]{1,0:T(8,128)S(1)}, u32[]{:S(2)}, u32[]{:S(2)}) collective-permute-start(f32[144,128]{1,0:T(8,128)S(1)} %add.16.when), channel_id=1, source_target_pairs={{0,9},{1,8},{2,11},{3,10},{4,13},{5,12},{6,15},{7,14},{8,1},{9,0},... | collective-permute-start | bytes 221192 | tf_op jit(solution)/shard_map/ppermute | solution.py:614
  42.7 2.8 %collective-permute-start.8 = (f32[8,64]{1,0:T(8,128)S(1)}, f32[8,64]{1,0:T(8,128)S(1)}, u32[]{:S(2)}, u32[]{:S(2)}) collective-permute-start(f32[8,64]{1,0:T(8,128)S(1)} %get-tuple-element.85), channel_id=1, source_target_pairs={{0,1},{1,0},{2,3},{3,2},{4,5},{5,4},{6,7},{7,6},{8,9},{9,8},{10,11... | collective-permute-start | bytes 6152 | tf_op jit(solution)/shard_map/ppermute | solution.py:614
  45.5 10.5 %collective-permute-start.9 = (f32[1024,128]{1,0:T(8,128)S(1)}, f32[1024,128]{1,0:T(8,128)S(1)}, u32[]{:S(2)}, u32[]{:S(2)}) collective-permute-start(f32[1024,128]{1,0:T(8,128)S(1)} %get-tuple-element.86), channel_id=1, source_target_pairs={{0,1},{1,0},{2,3},{3,2},{4,5},{5,4},{6,7},{7,6},{8,9},{9,8},{10,11... | collective-permute-start | bytes 1572872 | tf_op jit(solution)/shard_map/ppermute | solution.py:614
  45.9 3.1 %collective-permute-start.10 = (f32[16,64]{1,0:T(8,128)S(1)}, f32[16,64]{1,0:T(8,128)S(1)}, u32[]{:S(2)}, u32[]{:S(2)}) collective-permute-start(f32[16,64]{1,0:T(8,128)S(1)} %pad_maximum_fusion.1), channel_id=1, source_target_pairs={{0,3},{1,2},{2,1},{3,0},{4,7},{5,6},{6,5},{7,4},{8,11},{9,10},{10,... | collective-permute-start | bytes 12296 | tf_op jit(solution)/shard_map/ppermute | solution.py:614
  48.9 3.1 %collective-permute-start.11 = (f32[16,64]{1,0:T(8,128)S(1)}, f32[16,64]{1,0:T(8,128)S(1)}, u32[]{:S(2)}, u32[]{:S(2)}) collective-permute-start(f32[16,64]{1,0:T(8,128)S(1)} %add.18), channel_id=1, source_target_pairs={{0,5},{1,4},{2,7},{3,6},{4,1},{5,0},{6,3},{7,2},{8,13},{9,12},{10,... | collective-permute-start | bytes 12296 | tf_op jit(solution)/shard_map/ppermute | solution.py:614
  52.0 4.0 %collective-permute-start.12 = (f32[16,64]{1,0:T(8,128)S(1)}, f32[16,64]{1,0:T(8,128)S(1)}, u32[]{:S(2)}, u32[]{:S(2)}) collective-permute-start(f32[16,64]{1,0:T(8,128)S(1)} %add.19.rest_0_), channel_id=1, source_target_pairs={{0,9},{1,8},{2,11},{3,10},{4,13},{5,12},{6,15},{7,14},{8,1},{9,0},... | collective-permute-start | bytes 12296 | tf_op jit(solution)/shard_map/ppermute | solution.py:614
